TPU v7x, 32 devices: a whole 2x2x4 slice. The times are simulated.
32 devices in a mesh: dp: 8 (over z, y), mp: 4 (over x, core).
Axes of the slice: x: 2, y: 2, z: 4, core: 2. Of those that a mesh axis runs over, the one named last changes fastest.
Arguments:
- targets: bfloat16 [8, 256, 1024], P('dp'), may hold values from -6 to 6
- labels: int32 [8, 256], replicated, may hold values from 0 to 50175
- passages: bfloat16 [16, 256, 1024], P('dp'), may hold values from -6 to 6
- slot_question: int32 [32], replicated, may hold values from 0 to 7, as said below
- slot_passage: int32 [32], P('dp'), may hold values from 0 to 1, as said below
- score_table: float32 [64], replicated, may hold values from -4 to 4
- score_index: int32 [32], replicated, may hold values from 0 to 63
- query_weight: bfloat16 [1024, 1024], P(None, 'mp'), may hold values from -0.1875 to 0.1875
- query_bias: bfloat16 [1024], P('mp'), may hold values from -1.1953125 to 1.1953125
- key_weight: bfloat16 [1024, 1024], P(None, 'mp'), may hold values from -0.1875 to 0.1875
- value_weight: bfloat16 [1024, 1024], P(None, 'mp'), may hold values from -0.1875 to 0.1875
- value_bias: bfloat16 [1024], P('mp'), may hold values from -1.1953125 to 1.1953125
- output_weight: bfloat16 [1024, 1024], P('mp'), may hold values from -0.75 to 0.75
- output_bias: bfloat16 [1024], replicated, may hold values from -1.1953125 to 1.1953125
- first_gain: bfloat16 [1024], replicated, may hold values from 0.5 to 1.5
- first_shift: bfloat16 [1024], replicated, may hold values from -1.1953125 to 1.1953125
- probe_weight: bfloat16 [1024, 1024], P(None, 'mp'), may hold values from -0.1875 to 0.1875
- probe_bias: bfloat16 [1024], P('mp'), may hold values from -1.1953125 to 1.1953125
- address_weight: bfloat16 [1024, 1024], P(None, 'mp'), may hold values from -0.1875 to 0.1875
- content_weight: bfloat16 [1024, 1024], P(None, 'mp'), may hold values from -0.1875 to 0.1875
- content_bias: bfloat16 [1024], P('mp'), may hold values from -1.1953125 to 1.1953125
- merged_weight: bfloat16 [1024, 1024], P('mp'), may hold values from -0.75 to 0.75
- merged_bias: bfloat16 [1024], replicated, may hold values from -1.1953125 to 1.1953125
- second_gain: bfloat16 [1024], replicated, may hold values from 0.5 to 1.5
- second_shift: bfloat16 [1024], replicated, may hold values from -1.1953125 to 1.1953125
- expand_weight: bfloat16 [1024, 4096], P(None, 'mp'), may hold values from -0.1875 to 0.1875
- expand_bias: bfloat16 [4096], P('mp'), may hold values from -1.1953125 to 1.1953125
- shrink_weight: bfloat16 [4096, 1024], P('mp'), may hold values from -0.09375 to 0.09375
- shrink_bias: bfloat16 [1024], replicated, may hold values from -1.1953125 to 1.1953125
- third_gain: bfloat16 [1024], replicated, may hold values from 0.5 to 1.5
- third_shift: bfloat16 [1024], replicated, may hold values from -1.1953125 to 1.1953125
- embedding: bfloat16 [50176, 1024], P('mp'), may hold values from -0.375 to 0.375
Outputs:
- objective: float32 [], replicated
- targets_slope: float32 [8, 256, 1024], P('dp')
- passages_slope: float32 [16, 256, 1024], P('dp')
- query_slope: float32 [1024, 1024], P('dp', 'mp')
- bias_query: float32 [1024], P(('mp', 'dp'))
- key_slope: float32 [1024, 1024], P('dp', 'mp')
- value_slope: float32 [1024, 1024], P('dp', 'mp')
- bias_value: float32 [1024], P(('mp', 'dp'))
- output_slope: float32 [1024, 1024], P('mp', 'dp')
- bias_output: float32 [1024], P('dp')
- first_gain_slope: float32 [1024], P('dp')
- first_shift_slope: float32 [1024], P('dp')
- probe_slope: float32 [1024, 1024], P('dp', 'mp')
- bias_probe: float32 [1024], P(('mp', 'dp'))
- address_slope: float32 [1024, 1024], P('dp', 'mp')
- content_slope: float32 [1024, 1024], P('dp', 'mp')
- bias_content: float32 [1024], P(('mp', 'dp'))
- merged_slope: float32 [1024, 1024], P('mp', 'dp')
- bias_merged: float32 [1024], P('dp')
- second_gain_slope: float32 [1024], P('dp')
- second_shift_slope: float32 [1024], P('dp')
- expand_slope: float32 [1024, 4096], P('dp', 'mp')
- bias_expand: float32 [4096], P(('mp', 'dp'))
- shrink_slope: float32 [4096, 1024], P('mp', 'dp')
- bias_shrink: float32 [1024], P('dp')
- third_gain_slope: float32 [1024], P('dp')
- third_shift_slope: float32 [1024], P('dp')
- embedding_slope: float32 [50176, 1024], P('mp', 'dp')
Inputs may be any that keep to these rules, and one draw needn't show every extreme that they name: `slot_question`: each question is named by exactly 4 slots. `slot_passage`: among the 4 slots of one dp index (aligned blocks), every one of that index's 2 passages is named at least once.
All inputs are finite; a program needn't handle non-finite values.
Results may differ from a plain program's by a relative error of at most 0.03.
Values may be sent and summed in bfloat16 or wider, within the bound.
No kernel may reach another device: no remote copies, remote signals or barrier semaphores. Data moves between devices by JAX's collectives and lax.ppermute only.
A program may use at most 320 MiB of HBM per device.

v0:
```python
import jax
import jax.numpy as jnp
from jax import lax
from jax.sharding import PartitionSpec as P

HD = 64


EPSILON = 1e-05
ENTROPY_WEIGHT = 0.5


def layer_norm(hidden, gain, shift):
    center = hidden - jnp.mean(hidden, -1, keepdims=True)
    spread = jnp.mean(center * center, -1, keepdims=True)
    return center * lax.rsqrt(spread + EPSILON) * gain + shift


def norm_backward(hidden, gain, shift, upstream):
    unused_value, pullback = jax.vjp(layer_norm, hidden, gain, shift)
    return pullback(upstream)


def exact_gelu(inputs):
    return jax.nn.gelu(inputs, approximate=False)


def gelu_backward(inputs, upstream):
    unused_value, pullback = jax.vjp(exact_gelu, inputs)
    return pullback(upstream)[0]


def matmul(left, right):
    return jnp.dot(left, right, preferred_element_type=jnp.float32)


def inner_rows(left, right):
    return lax.dot_general(
        left, right, (((0,), (0,)), ((), ())), preferred_element_type=jnp.float32
    )


def outer_rows(left, right):
    return lax.dot_general(
        left, right, (((1,), (1,)), ((), ())), preferred_element_type=jnp.float32
    )


def model_sum(partial_term):
    return lax.psum(partial_term.astype(jnp.bfloat16), "mp").astype(jnp.float32)


def score_block(queries, addresses, causal):
    scores = (
        jnp.einsum("plhe,pmhe->phlm", queries, addresses, preferred_element_type=jnp.float32)
        * 0.125
    )
    if causal:
        row_place = lax.broadcasted_iota(jnp.int32, scores.shape, 2)
        col_place = lax.broadcasted_iota(jnp.int32, scores.shape, 3)
        scores = jnp.where(row_place >= col_place, scores, -1000000000.0)
    return scores


def attend_forward(queries, addresses, contents, causal):
    scores = score_block(queries, addresses, causal)
    top = jnp.max(scores, -1, keepdims=True)
    expo = jnp.exp(scores - top)
    total = jnp.sum(expo, -1, keepdims=True)
    weights = (expo / total).astype(jnp.bfloat16)
    mixed = jnp.einsum("phlm,pmhe->plhe", weights, contents, preferred_element_type=jnp.float32)
    return (mixed.astype(jnp.bfloat16), top + jnp.log(total))


def attend_backward(queries, addresses, contents, log_total, upstream, causal):
    weights = jnp.exp(score_block(queries, addresses, causal) - log_total)
    weight_delta = jnp.einsum(
        "plhe,pmhe->phlm", upstream, contents, preferred_element_type=jnp.float32
    )
    score_delta = (
        weights * (weight_delta - jnp.sum(weights * weight_delta, -1, keepdims=True))
    ).astype(jnp.bfloat16)
    query_delta = (
        jnp.einsum("phlm,pmhe->plhe", score_delta, addresses, preferred_element_type=jnp.float32)
        * 0.125
    )
    address_delta = (
        jnp.einsum("phlm,plhe->pmhe", score_delta, queries, preferred_element_type=jnp.float32)
        * 0.125
    )
    content_delta = jnp.einsum(
        "phlm,plhe->pmhe",
        weights.astype(jnp.bfloat16),
        upstream,
        preferred_element_type=jnp.float32,
    )
    return (query_delta.astype(jnp.bfloat16), address_delta, content_delta)


def marginal_objective(seq_values, doc_scores, member, length):
    joint = doc_scores + seq_values / length
    masked = jnp.where(member, joint[None, :], -1e30)
    top = jnp.max(masked, 1, keepdims=True)
    unscaled = jnp.where(member, jnp.exp(masked - top), 0.0)
    total = jnp.sum(unscaled, 1, keepdims=True)
    marginal = top[:, 0] + jnp.log(total[:, 0])
    posterior = unscaled / total
    entropy = -jnp.sum(jnp.where(member, posterior * (joint[None, :] - marginal[:, None]), 0.0), 1)
    return jnp.mean(-marginal + ENTROPY_WEIGHT * entropy)


def on_device(
    targets,
    labels,
    passages,
    slot_question,
    slot_passage,
    score_table,
    score_index,
    query_weight,
    query_bias,
    key_weight,
    value_weight,
    value_bias,
    output_weight,
    output_bias,
    first_gain,
    first_shift,
    probe_weight,
    probe_bias,
    address_weight,
    content_weight,
    content_bias,
    merged_weight,
    merged_bias,
    second_gain,
    second_shift,
    expand_weight,
    expand_bias,
    shrink_weight,
    shrink_bias,
    third_gain,
    third_shift,
    embedding,
):
    bfloat = jnp.bfloat16
    single = jnp.float32
    device = lax.axis_index("dp")
    spread_rows = lax.all_to_all(targets, "dp", split_axis=1, concat_axis=0, tiled=True)
    questions, row_share, model_width = spread_rows.shape
    pair_count = slot_passage.shape[0]
    slot_count = slot_question.shape[0]
    length = targets.shape[1]
    total_rows = pair_count * length
    store_count, passage_length = (passages.shape[0], passages.shape[1])
    vocab_share = embedding.shape[0]
    heads_local = query_weight.shape[1] // HD

    def split_heads(flat):
        return flat.reshape(pair_count, -1, heads_local, HD)

    outgoing = jnp.take(spread_rows, slot_question, axis=0)
    arrived = lax.all_to_all(outgoing, "dp", split_axis=0, concat_axis=1, tiled=True)
    inputs_low = arrived.reshape(total_rows, model_width)
    my_questions = lax.dynamic_slice_in_dim(slot_question, device * pair_count, pair_count)
    pair_labels = jnp.take(labels, my_questions, axis=0).reshape(total_rows)
    self_queries = (matmul(inputs_low, query_weight) + query_bias).astype(bfloat)
    self_addresses = matmul(inputs_low, key_weight).astype(bfloat)
    self_contents = (matmul(inputs_low, value_weight) + value_bias).astype(bfloat)
    self_mixed, self_total = attend_forward(
        split_heads(self_queries), split_heads(self_addresses), split_heads(self_contents), True
    )
    self_flat = self_mixed.reshape(total_rows, -1)
    first_in = inputs_low + (model_sum(matmul(self_flat, output_weight)) + output_bias)
    first_norm = layer_norm(first_in, first_gain.astype(single), first_shift.astype(single))
    first_low = first_norm.astype(bfloat)
    passage_rows = passages.reshape(-1, model_width)
    stored_addresses = matmul(passage_rows, address_weight).astype(bfloat)
    stored_contents = (matmul(passage_rows, content_weight) + content_bias).astype(bfloat)
    chooser = (slot_passage[:, None] == jnp.arange(store_count, dtype=jnp.int32)[None, :]).astype(
        bfloat
    )

    def select(stored):
        picked = matmul(chooser, stored.reshape(store_count, -1))
        return split_heads(picked.astype(bfloat))

    probe_low = (matmul(first_low, probe_weight) + probe_bias).astype(bfloat)
    picked_addresses = select(stored_addresses)
    picked_contents = select(stored_contents)
    cross_mixed, cross_total = attend_forward(
        split_heads(probe_low), picked_addresses, picked_contents, False
    )
    cross_flat = cross_mixed.reshape(total_rows, -1)
    second_in = first_norm + (model_sum(matmul(cross_flat, merged_weight)) + merged_bias)
    second_norm = layer_norm(second_in, second_gain.astype(single), second_shift.astype(single))
    second_low = second_norm.astype(bfloat)
    expanded = matmul(second_low, expand_weight) + expand_bias
    activated = exact_gelu(expanded).astype(bfloat)
    third_in = second_norm + (model_sum(matmul(activated, shrink_weight)) + shrink_bias)
    third_norm = layer_norm(third_in, third_gain.astype(single), third_shift.astype(single))
    third_low = third_norm.astype(bfloat)
    logits = outer_rows(third_low, embedding)
    local_top = jnp.max(logits, -1)
    local_total = jnp.sum(jnp.exp(logits - local_top[:, None]), -1)
    local_index = pair_labels - lax.axis_index("mp") * vocab_share
    inside = (local_index >= 0) & (local_index < vocab_share)
    clipped = jnp.clip(local_index, 0, vocab_share - 1)
    local_target = jnp.where(inside, jnp.take_along_axis(logits, clipped[:, None], 1)[:, 0], 0.0)
    global_top = lax.pmax(local_top, "mp")
    global_total, target_logit = lax.psum(
        (local_total * jnp.exp(local_top - global_top), local_target), "mp"
    )
    log_norm = global_top + jnp.log(global_total)
    pair_likelihood = jnp.sum((target_logit - log_norm).reshape(pair_count, length), -1)
    every_likelihood = lax.all_gather(pair_likelihood, "dp", axis=0, tiled=True)
    doc_scores = jnp.take(score_table, score_index)
    member = slot_question[None, :] == jnp.arange(questions, dtype=jnp.int32)[:, None]

    def scored(values_all):
        return marginal_objective(values_all, doc_scores, member, length)

    objective, pullback = jax.vjp(scored, every_likelihood)
    likelihood_delta = pullback(jnp.ones_like(objective) * (questions * length))[0]
    pair_delta = lax.dynamic_slice_in_dim(likelihood_delta, device * pair_count, pair_count)
    row_delta = jnp.broadcast_to(pair_delta[:, None], (pair_count, length)).reshape(total_rows)
    columns = lax.broadcasted_iota(jnp.int32, logits.shape, 1)
    hit_table = jnp.where(columns == local_index[:, None], 1.0, 0.0)
    logit_delta = (row_delta[:, None] * (hit_table - jnp.exp(logits - log_norm[:, None]))).astype(
        bfloat
    )
    embedding_slope = inner_rows(logit_delta, third_low)
    third_delta = model_sum(matmul(logit_delta, embedding))
    third_back = norm_backward(
        third_in, third_gain.astype(single), third_shift.astype(single), third_delta
    )
    feed_delta = third_back[0].astype(bfloat)
    bias_shrink = jnp.sum(feed_delta, 0, dtype=single)
    shrink_slope = inner_rows(activated, feed_delta)
    expanded_delta = gelu_backward(expanded, outer_rows(feed_delta, shrink_weight)).astype(bfloat)
    bias_expand = jnp.sum(expanded_delta, 0, dtype=single)
    expand_slope = inner_rows(second_low, expanded_delta)
    second_delta = third_back[0] + model_sum(outer_rows(expanded_delta, expand_weight))
    second_back = norm_backward(
        second_in, second_gain.astype(single), second_shift.astype(single), second_delta
    )
    recall_delta = second_back[0].astype(bfloat)
    bias_merged = jnp.sum(recall_delta, 0, dtype=single)
    merged_slope = inner_rows(cross_flat, recall_delta)
    mixed_delta = outer_rows(recall_delta, merged_weight).astype(bfloat)
    probe_delta, picked_address_delta, picked_content_delta = attend_backward(
        split_heads(probe_low),
        picked_addresses,
        picked_contents,
        cross_total,
        split_heads(mixed_delta),
        False,
    )
    chooser_single = chooser.astype(single)
    address_delta = (
        jnp.dot(
            chooser_single.T,
            picked_address_delta.reshape(pair_count, -1),
            precision=lax.Precision.HIGHEST,
        )
        .astype(bfloat)
        .reshape(store_count * passage_length, -1)
    )
    content_delta = (
        jnp.dot(
            chooser_single.T,
            picked_content_delta.reshape(pair_count, -1),
            precision=lax.Precision.HIGHEST,
        )
        .astype(bfloat)
        .reshape(store_count * passage_length, -1)
    )
    probe_flat = probe_delta.reshape(total_rows, -1)
    bias_probe = jnp.sum(probe_flat, 0, dtype=single)
    probe_slope = inner_rows(first_low, probe_flat)
    address_slope = inner_rows(passage_rows, address_delta)
    content_slope = inner_rows(passage_rows, content_delta)
    bias_content = jnp.sum(content_delta, 0, dtype=single)
    passage_sum, probe_sum = (
        lax.psum(
            (
                outer_rows(address_delta, address_weight)
                + outer_rows(content_delta, content_weight)
            ).astype(jnp.bfloat16),
            "mp",
        ).astype(jnp.float32),
        lax.psum(outer_rows(probe_flat, probe_weight).astype(jnp.bfloat16), "mp").astype(
            jnp.float32
        ),
    )
    first_delta = second_back[0] + probe_sum
    first_back = norm_backward(
        first_in, first_gain.astype(single), first_shift.astype(single), first_delta
    )
    self_delta = first_back[0].astype(bfloat)
    bias_output = jnp.sum(self_delta, 0, dtype=single)
    output_slope = inner_rows(self_flat, self_delta)
    self_mixed_delta = outer_rows(self_delta, output_weight).astype(bfloat)
    query_delta, address_raw, content_raw = attend_backward(
        split_heads(self_queries),
        split_heads(self_addresses),
        split_heads(self_contents),
        self_total,
        split_heads(self_mixed_delta),
        True,
    )
    query_flat = query_delta.reshape(total_rows, -1)
    key_flat = address_raw.reshape(total_rows, -1).astype(bfloat)
    value_flat = content_raw.reshape(total_rows, -1).astype(bfloat)
    query_slope = inner_rows(inputs_low, query_flat)
    bias_query = jnp.sum(query_flat, 0, dtype=single)
    key_slope = inner_rows(inputs_low, key_flat)
    value_slope = inner_rows(inputs_low, value_flat)
    bias_value = jnp.sum(value_flat, 0, dtype=single)
    input_delta = first_back[0] + model_sum(
        outer_rows(query_flat, query_weight)
        + outer_rows(key_flat, key_weight)
        + outer_rows(value_flat, value_weight)
    )
    sendback = input_delta.astype(bfloat).reshape(pair_count, length, model_width)
    returned = lax.all_to_all(sendback, "dp", split_axis=1, concat_axis=0, tiled=True)
    question_share = matmul(member.astype(bfloat), returned.reshape(slot_count, -1)).reshape(
        questions, row_share, model_width
    )
    targets_slope = lax.all_to_all(
        question_share.astype(jnp.bfloat16), "dp", split_axis=0, concat_axis=1, tiled=True
    ).astype(question_share.dtype)
    passages_slope = passage_sum.reshape(passages.shape)
    reduced = (
        lax.psum_scatter(query_slope, "dp", scatter_dimension=0, tiled=True),
        lax.psum_scatter(bias_query, "dp", scatter_dimension=0, tiled=True),
        lax.psum_scatter(key_slope, "dp", scatter_dimension=0, tiled=True),
        lax.psum_scatter(value_slope, "dp", scatter_dimension=0, tiled=True),
        lax.psum_scatter(bias_value, "dp", scatter_dimension=0, tiled=True),
        lax.psum_scatter(output_slope, "dp", scatter_dimension=1, tiled=True),
        lax.psum_scatter(bias_output, "dp", scatter_dimension=0, tiled=True),
        lax.psum_scatter(first_back[1], "dp", scatter_dimension=0, tiled=True),
        lax.psum_scatter(first_back[2], "dp", scatter_dimension=0, tiled=True),
        lax.psum_scatter(probe_slope, "dp", scatter_dimension=0, tiled=True),
        lax.psum_scatter(bias_probe, "dp", scatter_dimension=0, tiled=True),
        lax.psum_scatter(address_slope, "dp", scatter_dimension=0, tiled=True),
        lax.psum_scatter(content_slope, "dp", scatter_dimension=0, tiled=True),
        lax.psum_scatter(bias_content, "dp", scatter_dimension=0, tiled=True),
        lax.psum_scatter(merged_slope, "dp", scatter_dimension=1, tiled=True),
        lax.psum_scatter(bias_merged, "dp", scatter_dimension=0, tiled=True),
        lax.psum_scatter(second_back[1], "dp", scatter_dimension=0, tiled=True),
        lax.psum_scatter(second_back[2], "dp", scatter_dimension=0, tiled=True),
        lax.psum_scatter(expand_slope, "dp", scatter_dimension=0, tiled=True),
        lax.psum_scatter(bias_expand, "dp", scatter_dimension=0, tiled=True),
        lax.psum_scatter(shrink_slope, "dp", scatter_dimension=1, tiled=True),
        lax.psum_scatter(bias_shrink, "dp", scatter_dimension=0, tiled=True),
        lax.psum_scatter(third_back[1], "dp", scatter_dimension=0, tiled=True),
        lax.psum_scatter(third_back[2], "dp", scatter_dimension=0, tiled=True),
        lax.psum_scatter(embedding_slope, "dp", scatter_dimension=1, tiled=True),
    )
    return (
        objective,
        targets_slope,
        passages_slope,
        reduced[0],
        reduced[1],
        reduced[2],
        reduced[3],
        reduced[4],
        reduced[5],
        reduced[6],
        reduced[7],
        reduced[8],
        reduced[9],
        reduced[10],
        reduced[11],
        reduced[12],
        reduced[13],
        reduced[14],
        reduced[15],
        reduced[16],
        reduced[17],
        reduced[18],
        reduced[19],
        reduced[20],
        reduced[21],
        reduced[22],
        reduced[23],
        reduced[24],
    )


def solution(mesh):
    return jax.shard_map(
        on_device,
        mesh=mesh,
        in_specs=(
            P("dp", None, None),
            P(),
            P("dp", None, None),
            P(),
            P("dp"),
            P(),
            P(),
            P(None, "mp"),
            P("mp"),
            P(None, "mp"),
            P(None, "mp"),
            P("mp"),
            P("mp", None),
            P(),
            P(),
            P(),
            P(None, "mp"),
            P("mp"),
            P(None, "mp"),
            P(None, "mp"),
            P("mp"),
            P("mp", None),
            P(),
            P(),
            P(),
            P(None, "mp"),
            P("mp"),
            P("mp", None),
            P(),
            P(),
            P(),
            P("mp", None),
        ),
        out_specs=(
            P(),
            P("dp", None, None),
            P("dp", None, None),
            P("dp", "mp"),
            P(("mp", "dp")),
            P("dp", "mp"),
            P("dp", "mp"),
            P(("mp", "dp")),
            P("mp", "dp"),
            P("dp"),
            P("dp"),
            P("dp"),
            P("dp", "mp"),
            P(("mp", "dp")),
            P("dp", "mp"),
            P("dp", "mp"),
            P(("mp", "dp")),
            P("mp", "dp"),
            P("dp"),
            P("dp"),
            P("dp"),
            P("dp", "mp"),
            P(("mp", "dp")),
            P("mp", "dp"),
            P("dp"),
            P("dp"),
            P("dp"),
            P("mp", "dp"),
        ),
        check_vma=False,
    )
```

profile of v0, /device:TPU:0, one launch (start us, length us, event | category | flops | bytes accessed | tf_op | source)
XLA Modules:
  0.0 2343.8 jit_solution(3394192510936872219)
XLA Ops:
  9.8 4.5 reduce.3
  16.5 7.3 all-to-all-start
  23.8 14.4 all-to-all-done
  46.6 4.5 all-to-all-start.1
  51.4 47.5 %all-to-all-done.1 = bf16[32,32,1024]{2,1,0:T(8,128)(2,1)} async-done(((bf16[32,32,1024]{2,1,0:T(8,128)(2,1)}), bf16[32,32,1024]{2,1,0:T(8,128)(2,1)}, u32[]{:S(2)}, u32[]{:S(2)}) %all-to-all-start.1) | async-done | bytes 2097184 | tf_op jit(solution)/shard_map/all_to_all | solution.py:163
  139.5 38.3 %all-reduce.26.cloned.1.call-done = bf16[1024,1024]{1,0:T(8,128)(2,1)} async-done(((bf16[1024,1024]{1,0:T(8,128)(2,1)}), bf16[1024,1024]{1,0:T(8,128)(2,1)}) %all-reduce.26.cloned.1.call-update) | async-done | bytes 2097168 | tf_op jit(solution)/shard_map/psum | solution.py:50
  196.5 50.5 %all-reduce.28.cloned.1.call-done = bf16[1024,1024]{1,0:T(8,128)(2,1)} async-done(((bf16[1024,1024]{1,0:T(8,128)(2,1)}), bf16[1024,1024]{1,0:T(8,128)(2,1)}) %all-reduce.28.cloned.1.call-update) | async-done | bytes 2097168 | tf_op jit(solution)/shard_map/psum | solution.py:50
  247.0 4.1 fusion.105
  251.7 13.1 multiply_convert_fusion.3
  266.1 3.7 convolution_convert_fusion.6
  272.1 49.4 %all-reduce.30.cloned.1.call-done = bf16[1024,1024]{1,0:T(8,128)(2,1)} async-done(((bf16[1024,1024]{1,0:T(8,128)(2,1)}), bf16[1024,1024]{1,0:T(8,128)(2,1)}) %all-reduce.30.cloned.1.call-update) | async-done | bytes 2097168 | tf_op jit(solution)/shard_map/psum | solution.py:50
  321.5 3.8 fusion.103
  327.9 38.8 %fusion.108 = (f32[1024]{0:T(1024)S(1)}, f32[1024,12544]{1,0:T(8,128)}) fusion(bf16[12544,1024]{1,0:T(8,128)(2,1)} %param.63, f32[1024,1024]{1,0:T(8,128)} %copy-done.13, f32[1024]{0:T(1024)S(1)} %convert_element_type.312, f32[1024]{0:T(1024)S(1)} %convert_element_type.311, f32[1024]{0:T(1024)S(1)} %fusion.77, f32[1024]{0:T(1024)S(1)} %broadcast_multiply_fusion), kind=kOutput, calls=%fused_computation.236 | convolution fusion | flops 26324762624 | bytes 81285120 | tf_op jit(solution)/shard_map/dot_general | solution.py:44
  366.6 5.8 pmax.7
  372.4 20.1 exponential_reduce_fusion
  392.5 15.9 gather_fusion.3
  408.4 5.9 all-reduce.16
  414.7 22.0 all-reduce
  438.3 26.1 %multiply_convert_fusion = bf16[1024,12544]{1,0:T(8,128)(2,1)} fusion(f32[1024,12544]{1,0:T(8,128)} %get-tuple-element.266, f32[1024]{0:T(1024)S(1)} %get-tuple-element.245, s32[1024]{0:T(1024)S(1)} %bitcast.253, f32[1024]{0:T(1024)S(1)} %bitcast.254), kind=kLoop, calls=%fused_computation.8 | loop fusion | flops 77070336 | bytes 77082624 | tf_op jit(solution)/shard_map/convert_element_type | solution.py:229
  464.4 33.8 %convolution_convert_fusion.9 = bf16[1024,1024]{1,0:T(8,128)(2,1)} fusion(bf16[1024,12544]{1,0:T(8,128)(2,1)} %multiply_convert_fusion, bf16[12544,1024]{1,0:T(8,128)(2,1)} %param.63), kind=kOutput, calls=%fused_computation.100 | convolution fusion | flops 26307723264 | bytes 53477376 | tf_op jit(solution)/shard_map/dot_general | solution.py:34
  498.2 47.4 %all-reduce.32.cloned.1.call-done = bf16[1024,1024]{1,0:T(8,128)(2,1)} async-done(((bf16[1024,1024]{1,0:T(8,128)(2,1)}), bf16[1024,1024]{1,0:T(8,128)(2,1)}) %all-reduce.32.cloned.1.call-update) | async-done | bytes 2097168 | tf_op jit(solution)/shard_map/psum | solution.py:50
  545.6 5.0 fusion.4
  557.3 4.6 convert_reduce_fusion.2
  563.4 3.7 convolution_convert_fusion.5
  567.6 51.1 %all-reduce.34.cloned.1.call-done = bf16[1024,1024]{1,0:T(8,128)(2,1)} async-done(((bf16[1024,1024]{1,0:T(8,128)(2,1)}), bf16[1024,1024]{1,0:T(8,128)(2,1)}) %all-reduce.34.cloned.1.call-update) | async-done | bytes 2097168 | tf_op jit(solution)/shard_map/psum | solution.py:50
  618.7 5.8 multiply_reduce_fusion
  636.0 3.5 multiply_reduce_fusion.4
  669.2 30.8 %all-reduce.36.cloned.1.call-done = bf16[1024,1024]{1,0:T(8,128)(2,1)} async-done(((bf16[1024,1024]{1,0:T(8,128)(2,1)}), bf16[1024,1024]{1,0:T(8,128)(2,1)}) %all-reduce.36.cloned.1.call-update) | async-done | bytes 2097168 | tf_op jit(solution)/shard_map/psum | solution.py:292
  700.1 6.3 multiply_reduce_fusion.1
  735.4 3.5 fusion.116
  739.0 3.5 fusion.117
  742.6 3.5 fusion.112
  746.1 3.4 fusion.113
  756.5 7.6 fusion.93
  764.2 6.8 fusion.118
  771.6 38.9 %fusion.91 = f32[12544,1024]{1,0:T(8,128)} fusion(bf16[1024,12544]{1,0:T(8,128)(2,1)} %multiply_convert_fusion, f32[1024,1024]{1,0:T(8,128)} %copy-done.13, f32[1024]{0:T(1024)S(1)} %copy-done.96, f32[1024]{0:T(1024)S(1)} %convert_element_type.311, f32[1024]{0:T(1024)S(1)} %fusion.77, f32[1024]{0:T(1024)S(1)} %broadcast_multiply_fusion), kind=kOutput, calls=%fused_computation.222 | convolution fusion | flops 26311917568 | bytes 81281024 | tf_op jit(solution)/shard_map/dot_general | solution.py:38
  815.6 61.5 %all_to_all.51 = bf16[4,256,1024]{2,0,1:T(4,128)(2,1)S(1)} all-to-all(bf16[4,256,1024]{2,0,1:T(4,128)(2,1)S(1)} %copy.301), channel_id=1, replica_groups=mesh['dp'=8,'mp'=4] {'dp'}, dimensions={1} | all-to-all | bytes 4194304 | tf_op jit(solution)/shard_map/all_to_all | solution.py:326
  881.5 3.7 all-to-all-start.3
  888.2 41.7 %all-reduce.15 = (f32[256]{0:T(256)S(1)}, f32[256]{0:T(256)S(1)}, f32[1024]{0:T(1024)S(1)}, f32[1024]{0:T(1024)S(1)}, f32[1024]{0:T(1024)S(1)}, /*index=5*/f32[2...) all-reduce(f32[256]{0:T(256)S(1)} %reduce_sum.421, ...), channel_id=3, replica_groups=mesh['dp'=8,'mp'=4] {'dp'}, use_global_device_ids=true, to_apply=%region_44.45.clone | all-reduce | flops 11264 | bytes 90112
  947.9 60.8 %reduce-scatter.20.cloned.1.call-done = f32[128,256]{1,0:T(8,128)} async-done(((f32[1024,256]{1,0:T(8,128)}), f32[128,256]{1,0:T(8,128)}) %reduce-scatter.20.cloned.1.call-update) | async-done | bytes 131088 | tf_op jit(solution)/shard_map/reduce_scatter | solution.py:344
  1008.8 67.4 %reduce-scatter.26.cloned.1.call-done = f32[256,128]{1,0:T(8,128)} async-done(((f32[256,1024]{1,0:T(8,128)}), f32[256,128]{1,0:T(8,128)}) %reduce-scatter.26.cloned.1.call-update) | async-done | bytes 131088 | tf_op jit(solution)/shard_map/reduce_scatter | solution.py:349
  1076.1 66.4 %reduce-scatter.12.cloned.1.call-done = f32[128,256]{1,0:T(8,128)} async-done(((f32[1024,256]{1,0:T(8,128)}), f32[128,256]{1,0:T(8,128)}) %reduce-scatter.12.cloned.1.call-update) | async-done | bytes 131088 | tf_op jit(solution)/shard_map/reduce_scatter | solution.py:335
  1142.5 66.9 %reduce-scatter.14.cloned.1.call-done = f32[128,256]{1,0:T(8,128)} async-done(((f32[1024,256]{1,0:T(8,128)}), f32[128,256]{1,0:T(8,128)}) %reduce-scatter.14.cloned.1.call-update) | async-done | bytes 131088 | tf_op jit(solution)/shard_map/reduce_scatter | solution.py:337
  1209.4 66.2 %reduce-scatter.16.cloned.1.call-done = f32[128,256]{1,0:T(8,128)} async-done(((f32[1024,256]{1,0:T(8,128)}), f32[128,256]{1,0:T(8,128)}) %reduce-scatter.16.cloned.1.call-update) | async-done | bytes 131088 | tf_op jit(solution)/shard_map/reduce_scatter | solution.py:338
  1275.5 67.1 %reduce-scatter.18.cloned.1.call-done = f32[256,128]{1,0:T(8,128)} async-done(((f32[256,1024]{1,0:T(8,128)}), f32[256,128]{1,0:T(8,128)}) %reduce-scatter.18.cloned.1.call-update) | async-done | bytes 131088 | tf_op jit(solution)/shard_map/reduce_scatter | solution.py:340
  1342.6 91.0 %reduce-scatter.28.cloned.1.call-done = f32[128,1024]{1,0:T(8,128)} async-done(((f32[1024,1024]{1,0:T(8,128)}), f32[128,1024]{1,0:T(8,128)}) %reduce-scatter.28.cloned.1.call-update) | async-done | bytes 524304 | tf_op jit(solution)/shard_map/reduce_scatter | solution.py:353
  1433.6 92.6 %reduce-scatter.30.cloned.1.call-done = f32[1024,128]{1,0:T(8,128)} async-done(((f32[1024,1024]{1,0:T(8,128)}), f32[1024,128]{1,0:T(8,128)}) %reduce-scatter.30.cloned.1.call-update) | async-done | bytes 524304 | tf_op jit(solution)/shard_map/reduce_scatter | solution.py:355
  1526.2 809.4 %reduce-scatter.32.cloned.1.call-done = f32[12544,128]{1,0:T(8,128)} async-done(((f32[12544,1024]{1,0:T(8,128)}), f32[12544,128]{1,0:T(8,128)}) %reduce-scatter.32.cloned.1.call-update) | async-done | bytes 6422544 | tf_op jit(solution)/shard_map/reduce_scatter | solution.py:359
  (478 shorter events, 194.1 us)
Async XLA Ops:
  7.2 244.5 %copy-start = (bf16[1024,1024]{1,0:T(8,128)(2,1)S(1)}, bf16[1024,1024]{1,0:T(8,128)(2,1)}, u32[]{:S(2)}) copy-start(bf16[1024,1024]{1,0:T(8,128)(2,1)} %param.57) | copy-start | bytes 6291460
  7.2 16.5 copy-start.91
  16.5 21.8 all-to-all-start
  46.6 55.4 %copy-start.46 = (bf16[1024,256]{1,0:T(8,128)(2,1)S(1)}, bf16[1024,256]{1,0:T(8,128)(2,1)}, u32[]{:S(2)}) copy-start(bf16[1024,256]{1,0:T(8,128)(2,1)} %param.42) | copy-start | bytes 1572868
  46.6 52.3 %all-to-all-start.1 = ((bf16[32,32,1024]{2,1,0:T(8,128)(2,1)}), bf16[32,32,1024]{2,1,0:T(8,128)(2,1)}, u32[]{:S(2)}, u32[]{:S(2)}) async-start(bf16[32,32,1024]{2,1,0:T(8,128)(2,1)} %broadcast_select_fusion), calls=%async_computation.1 | async-start | bytes 4194304 | tf_op jit(solution)/shard_map/all_to_all | solution.py:163
  51.1 126.7 %all-reduce.26.cloned.1.call-start = ((), (), s32[]{:S(2)}) async-start(), calls=%async_computation.15 | async-start | bytes 4194304 | tf_op jit(solution)/shard_map/psum | solution.py:50
  127.3 119.7 %all-reduce.28.cloned.1.call-start = ((), (), s32[]{:S(2)}) async-start(), calls=%async_computation.16 | async-start | bytes 4194304 | tf_op jit(solution)/shard_map/psum | solution.py:50
  133.8 113.2 %copy-start.61 = (f32[1024]{0:T(1024)}, f32[1024]{0:T(1024)S(1)}, u32[]{:S(2)}) copy-start(f32[1024]{0:T(1024)S(1)} %convert_element_type.287) | copy-start | bytes 12292
  133.8 113.1 %copy-start.54 = (f32[1024]{0:T(1024)}, f32[1024]{0:T(1024)S(1)}, u32[]{:S(2)}) copy-start(f32[1024]{0:T(1024)S(1)} %convert_element_type.286) | copy-start | bytes 12292
  139.5 49.6 %copy-start.29 = (bf16[4,256,4,64]{1,3,2,0:T(8,128)(2,1)}, bf16[4,256,4,64]{1,3,2,0:T(8,128)(2,1)S(1)}, u32[]{:S(2)}) copy-start(bf16[4,256,4,64]{1,3,2,0:T(8,128)(2,1)S(1)} %copy.279) | copy-start | bytes 1572868
  181.3 65.7 %copy-start.56 = (f32[1024]{0:T(1024)}, f32[1024]{0:T(1024)S(1)}, u32[]{:S(2)}) copy-start(f32[1024]{0:T(1024)S(1)} %broadcast_multiply_fusion.2) | copy-start | bytes 12292
  182.4 64.5 %copy-start.63 = (f32[1024]{0:T(1024)}, f32[1024]{0:T(1024)S(1)}, u32[]{:S(2)}) copy-start(f32[1024]{0:T(1024)S(1)} %fusion.75) | copy-start | bytes 12292
  195.4 126.1 %all-reduce.30.cloned.1.call-start = ((), (), s32[]{:S(2)}) async-start(), calls=%async_computation.17 | async-start | bytes 4194304 | tf_op jit(solution)/shard_map/psum | solution.py:50
  195.6 56.0 %copy-start.97 = (f32[1024]{0:T(1024)}, f32[1024]{0:T(1024)S(1)}, u32[]{:S(2)}) copy-start(f32[1024]{0:T(1024)S(1)} %convert_element_type.306) | copy-start | bytes 12292
  195.7 125.8 %copy-start.83 = (f32[1024]{0:T(1024)}, f32[1024]{0:T(1024)S(1)}, u32[]{:S(2)}) copy-start(f32[1024]{0:T(1024)S(1)} %convert_element_type.304) | copy-start | bytes 12292
  195.7 125.8 %copy-start.73 = (f32[1024]{0:T(1024)}, f32[1024]{0:T(1024)S(1)}, u32[]{:S(2)}) copy-start(f32[1024]{0:T(1024)S(1)} %convert_element_type.303) | copy-start | bytes 12292
  195.8 132.1 %copy-start.95 = (f32[1024]{0:T(1024)}, f32[1024]{0:T(1024)S(1)}, u32[]{:S(2)}) copy-start(f32[1024]{0:T(1024)S(1)} %convert_element_type.312) | copy-start | bytes 12292
  251.0 70.4 %copy-start.65 = (f32[1024]{0:T(1024)}, f32[1024]{0:T(1024)S(1)}, u32[]{:S(2)}) copy-start(f32[1024]{0:T(1024)S(1)} %broadcast_multiply_fusion.1) | copy-start | bytes 12292
  251.7 69.8 %copy-start.75 = (f32[1024]{0:T(1024)}, f32[1024]{0:T(1024)S(1)}, u32[]{:S(2)}) copy-start(f32[1024]{0:T(1024)S(1)} %fusion.76) | copy-start | bytes 12292
  251.7 14.4 copy-start.115
  269.9 275.7 %all-reduce.32.cloned.1.call-start = ((), (), s32[]{:S(2)}) async-start(), calls=%async_computation.18 | async-start | bytes 4194304 | tf_op jit(solution)/shard_map/psum | solution.py:50
  327.8 38.8 %copy-start.81 = (f32[1024]{0:T(1024)}, f32[1024]{0:T(1024)S(1)}, u32[]{:S(2)}) copy-start(f32[1024]{0:T(1024)S(1)} %multiply_reduce_fusion.6) | copy-start | bytes 12292
  437.0 27.4 %copy-start.93 = (f32[8]{0:T(128)}, f32[8]{0:T(128)S(1)}, u32[]{:S(2)}) copy-start(f32[8]{0:T(128)S(1)} %get-tuple-element.258) | copy-start | bytes 100
  498.2 52.4 %copy-start.82 = (f32[1024]{0:T(1024)S(1)}, f32[1024]{0:T(1024)}, u32[]{:S(2)}) copy-start(f32[1024]{0:T(1024)} %copy-done.81) | copy-start | bytes 12292
  498.2 120.5 %all-reduce.34.cloned.1.call-start = ((), (), s32[]{:S(2)}) async-start(), calls=%async_computation.19 | async-start | bytes 4194304 | tf_op jit(solution)/shard_map/psum | solution.py:50
  563.3 55.4 %copy-start.66 = (f32[1024]{0:T(1024)S(1)}, f32[1024]{0:T(1024)}, u32[]{:S(2)}) copy-start(f32[1024]{0:T(1024)} %copy-done.65) | copy-start | bytes 12292
  563.3 55.4 %copy-start.74 = (f32[1024]{0:T(1024)S(1)}, f32[1024]{0:T(1024)}, u32[]{:S(2)}) copy-start(f32[1024]{0:T(1024)} %copy-done.73) | copy-start | bytes 12292
  563.3 55.4 %copy-start.76 = (f32[1024]{0:T(1024)S(1)}, f32[1024]{0:T(1024)}, u32[]{:S(2)}) copy-start(f32[1024]{0:T(1024)} %copy-done.75) | copy-start | bytes 12292
  567.1 132.9 %all-reduce.36.cloned.1.call-start = ((), (), s32[]{:S(2)}) async-start(), calls=%async_computation.20 | async-start | bytes 4194304 | tf_op jit(solution)/shard_map/psum | solution.py:292
  567.6 56.9 %copy-start.80 = (f32[1024]{0:T(1024)S(1)}, f32[1024]{0:T(1024)}, u32[]{:S(2)}) copy-start(f32[1024]{0:T(1024)} %copy-done.79) | copy-start | bytes 12292
  648.4 162.2 %all-reduce.38.cloned.1.call-start = ((), (), s32[]{:S(2)}) async-start(), calls=%async_computation.32 | async-start | bytes 6291456 | tf_op jit(solution)/shard_map/psum | solution.py:50
  661.8 38.2 %copy-start.55 = (f32[1024]{0:T(1024)S(1)}, f32[1024]{0:T(1024)}, u32[]{:S(2)}) copy-start(f32[1024]{0:T(1024)} %copy-done.54) | copy-start | bytes 12292
  661.8 38.2 %copy-start.57 = (f32[1024]{0:T(1024)S(1)}, f32[1024]{0:T(1024)}, u32[]{:S(2)}) copy-start(f32[1024]{0:T(1024)} %copy-done.56) | copy-start | bytes 12292
  661.8 38.2 %copy-start.62 = (f32[1024]{0:T(1024)S(1)}, f32[1024]{0:T(1024)}, u32[]{:S(2)}) copy-start(f32[1024]{0:T(1024)} %copy-done.61) | copy-start | bytes 12292
  661.8 38.2 %copy-start.64 = (f32[1024]{0:T(1024)S(1)}, f32[1024]{0:T(1024)}, u32[]{:S(2)}) copy-start(f32[1024]{0:T(1024)} %copy-done.63) | copy-start | bytes 12292
  669.2 37.2 %copy-start.78 = (f32[1024]{0:T(1024)S(1)}, f32[1024]{0:T(1024)}, u32[]{:S(2)}) copy-start(f32[1024]{0:T(1024)} %copy-done.77) | copy-start | bytes 12292
  729.7 208.4 %reduce-scatter.22.cloned.1.call-start = ((), (), s32[]{:S(2)}) async-start(), calls=%async_computation.26 | async-start | bytes 1179648 | tf_op jit(solution)/shard_map/reduce_scatter | solution.py:346
  732.5 209.8 %reduce-scatter.24.cloned.1.call-start = ((), (), s32[]{:S(2)}) async-start(), calls=%async_computation.27 | async-start | bytes 1179648 | tf_op jit(solution)/shard_map/reduce_scatter | solution.py:347
  735.3 273.4 %reduce-scatter.20.cloned.1.call-start = ((), (), s32[]{:S(2)}) async-start(), calls=%async_computation.25 | async-start | bytes 1179648 | tf_op jit(solution)/shard_map/reduce_scatter | solution.py:344
  738.9 337.2 %reduce-scatter.26.cloned.1.call-start = ((), (), s32[]{:S(2)}) async-start(), calls=%async_computation.28 | async-start | bytes 1179648 | tf_op jit(solution)/shard_map/reduce_scatter | solution.py:349
  742.5 400.0 %reduce-scatter.12.cloned.1.call-start = ((), (), s32[]{:S(2)}) async-start(), calls=%async_computation.21 | async-start | bytes 1179648 | tf_op jit(solution)/shard_map/reduce_scatter | solution.py:335
  746.1 463.3 %reduce-scatter.14.cloned.1.call-start = ((), (), s32[]{:S(2)}) async-start(), calls=%async_computation.22 | async-start | bytes 1179648 | tf_op jit(solution)/shard_map/reduce_scatter | solution.py:337
  749.5 526.0 %reduce-scatter.16.cloned.1.call-start = ((), (), s32[]{:S(2)}) async-start(), calls=%async_computation.23 | async-start | bytes 1179648 | tf_op jit(solution)/shard_map/reduce_scatter | solution.py:338
  753.0 589.6 %reduce-scatter.18.cloned.1.call-start = ((), (), s32[]{:S(2)}) async-start(), calls=%async_computation.24 | async-start | bytes 1179648 | tf_op jit(solution)/shard_map/reduce_scatter | solution.py:340
  756.4 677.2 %reduce-scatter.28.cloned.1.call-start = ((), (), s32[]{:S(2)}) async-start(), calls=%async_computation.29 | async-start | bytes 4718592 | tf_op jit(solution)/shard_map/reduce_scatter | solution.py:353
  764.1 762.1 %reduce-scatter.30.cloned.1.call-start = ((), (), s32[]{:S(2)}) async-start(), calls=%async_computation.30 | async-start | bytes 4718592 | tf_op jit(solution)/shard_map/reduce_scatter | solution.py:355
  770.9 1564.7 %reduce-scatter.32.cloned.1.call-start = ((), (), s32[]{:S(2)}) async-start(), calls=%async_computation.31 | async-start | bytes 57802752 | tf_op jit(solution)/shard_map/reduce_scatter | solution.py:359
  881.5 65.3 %all-to-all-start.3 = ((bf16[8,32,1024]{2,1,0:T(8,128)(2,1)}), bf16[8,32,1024]{2,1,0:T(8,128)(2,1)S(1)}, u32[]{:S(2)}, u32[]{:S(2)}) async-start(bf16[8,32,1024]{2,1,0:T(8,128)(2,1)} %copy.305), calls=%async_computation.3 | async-start | bytes 1048576 | tf_op jit(solution)/shard_map/all_to_all | solution.py:330
  (98 other events, 418.2 us)
Sparse Core Ops, SparseCore 0:
  127.4 50.4 all-reduce.25
  195.5 51.4 all-reduce.27
  270.0 51.4 all-reduce.29
  498.3 47.2 all-reduce.31
  567.2 51.4 all-reduce.33
  648.5 51.4 all-reduce.35
  729.8 68.6 all-reduce.37
  802.6 70.1 reduce-scatter.21
  876.5 65.7 reduce-scatter.23
  946.2 62.5 reduce-scatter.19
  1013.1 62.9 reduce-scatter.25
  1080.0 62.4 reduce-scatter.11
  1146.9 62.4 reduce-scatter.13
  1213.2 62.2 reduce-scatter.15
  1279.7 62.8 reduce-scatter.17
  1346.7 86.8 reduce-scatter.27
  1438.1 88.0 reduce-scatter.29
  1530.5 805.0 reduce-scatter.31
where the time goes:
time: 2350 us; the launch traced here: 2340 us
  waiting for transfers between devices  1720 us (73%)
  matrix products  230 us (10%)
  blocking collectives  137 us (6%)
  local copies, waits for them, and re-layouts  111 us (5%)
  other arithmetic  108 us (5%)
    reduce_scatter x1, waiting for transfers between devices, on_device(): lax.psum_scatter(embedding_slope, 'dp', scatter_dimension=1, tiled=True)  809 us
    psum x6, waiting for transfers between devices, model_sum(): return lax.psum(partial_term.astype(jnp.bfloat16), 'mp').astype(jnp.float32)  237 us
    reduce_scatter x1, waiting for transfers between devices, on_device(): lax.psum_scatter(shrink_slope, 'dp', scatter_dimension=1, tiled=True)  92.6 us
    reduce_scatter x1, waiting for transfers between devices, on_device(): lax.psum_scatter(expand_slope, 'dp', scatter_dimension=0, tiled=True)  91 us
    dot_general x11, matrix products, inner_rows(): lax.dot_general(left, right, (((0,), (0,)), ((), ())), preferred_element_...  79.4 us
    dot_general x14, matrix products, matmul(): return jnp.dot(left, right, preferred_element_type=jnp.float32)  70.6 us
    reduce_scatter x1, waiting for transfers between devices, on_device(): lax.psum_scatter(merged_slope, 'dp', scatter_dimension=1, tiled=True)  67.4 us
    reduce_scatter x1, waiting for transfers between devices, on_device(): lax.psum_scatter(output_slope, 'dp', scatter_dimension=1, tiled=True)  67.1 us
  transfers between devices with their start and end apart: 21, of which 18 were waited for; matrix products, arithmetic and copies ran while one was open for 6% of the time, Pallas kernels for 0%

commit v1 on v0

v1 whole, which is shorter than its diff:
```python
import functools

import jax
import jax.numpy as jnp
from jax import lax
from jax.sharding import PartitionSpec as P

HD = 64
LANES = 128
EPSILON = 1e-05
ENTROPY_WEIGHT = 0.5
bfloat = jnp.bfloat16
single = jnp.float32


def norm_forward(hidden, gain, shift):
    center = hidden - jnp.mean(hidden, -1, keepdims=True)
    spread = jnp.mean(center * center, -1, keepdims=True)
    return center * lax.rsqrt(spread + EPSILON) * gain + shift


def norm_backward(hidden, gain, upstream):
    center = hidden - jnp.mean(hidden, -1, keepdims=True)
    spread = jnp.mean(center * center, -1, keepdims=True)
    inverse = lax.rsqrt(spread + EPSILON)
    normal = center * inverse
    scaled = upstream * gain
    delta = inverse * (
        scaled
        - jnp.mean(scaled, -1, keepdims=True)
        - normal * jnp.mean(scaled * normal, -1, keepdims=True)
    )
    return delta, jnp.sum(upstream * normal, 0), jnp.sum(upstream, 0)


def exact_gelu(inputs):
    return jax.nn.gelu(inputs, approximate=False)


def gelu_backward(inputs, upstream):
    unused_value, pullback = jax.vjp(exact_gelu, inputs)
    return pullback(upstream)[0]


def matmul(left, right):
    return jnp.dot(left, right, preferred_element_type=single)


def inner_rows(left, right):
    return lax.dot_general(left, right, (((0,), (0,)), ((), ())), preferred_element_type=single)


def outer_rows(left, right):
    return lax.dot_general(left, right, (((1,), (1,)), ((), ())), preferred_element_type=single)


def bits_of(count):
    bits = []
    while (1 << len(bits)) < count:
        bits.append(1 << len(bits))
    return bits


def swap(value, axis, count, bit):
    return lax.ppermute(value, axis, [(i, i ^ bit) for i in range(count)])


def relative_of(order):
    table = [0]
    for bit in order:
        table = table + [r ^ bit for r in table]
    return table


def gather_blocks(own, axis, count, order):
    held = own[None]
    for bit in order:
        held = jnp.concatenate([held, swap(held, axis, count, bit)], 0)
    return held


def scatter_blocks(parts, axis, count, order):
    for bit in reversed(order):
        half = parts.shape[0] // 2
        arrived = swap(parts[half:].astype(bfloat), axis, count, bit)
        parts = parts[:half] + arrived.astype(single)
    return parts[0]


def total_over(value, axis, count, order):
    for bit in order:
        value = value + swap(value, axis, count, bit)
    return value


def xor_take(table, me, array, axis):
    return jnp.take(array, me ^ jnp.asarray(table, jnp.int32), axis=axis, mode="clip")


def places(table):
    inverse = [0] * len(table)
    for position, relative in enumerate(table):
        inverse[relative] = position
    return inverse


def natural_order(table, me, array, axis):
    count = len(table)
    order = jnp.asarray(places(table), jnp.int32)[me ^ jnp.arange(count, dtype=jnp.int32)]
    return jnp.take(array, order, axis=axis, mode="clip")


def score_block(queries, addresses, causal):
    scores = (
        jnp.einsum("plhe,pmhe->phlm", queries, addresses, preferred_element_type=single) * 0.125
    )
    if causal:
        row_place = lax.broadcasted_iota(jnp.int32, scores.shape, 2)
        col_place = lax.broadcasted_iota(jnp.int32, scores.shape, 3)
        scores = jnp.where(row_place >= col_place, scores, -1000000000.0)
    return scores


def attend_forward(queries, addresses, contents, causal):
    scores = score_block(queries, addresses, causal)
    top = jnp.max(scores, -1, keepdims=True)
    expo = jnp.exp(scores - top)
    total = jnp.sum(expo, -1, keepdims=True)
    weights = (expo / total).astype(bfloat)
    mixed = jnp.einsum("phlm,pmhe->plhe", weights, contents, preferred_element_type=single)
    return (mixed.astype(bfloat), top + jnp.log(total))


def attend_backward(queries, addresses, contents, log_total, upstream, causal):
    weights = jnp.exp(score_block(queries, addresses, causal) - log_total)
    weight_delta = jnp.einsum("plhe,pmhe->phlm", upstream, contents, preferred_element_type=single)
    score_delta = (
        weights * (weight_delta - jnp.sum(weights * weight_delta, -1, keepdims=True))
    ).astype(bfloat)
    query_delta = (
        jnp.einsum("phlm,pmhe->plhe", score_delta, addresses, preferred_element_type=single) * 0.125
    )
    address_delta = (
        jnp.einsum("phlm,plhe->pmhe", score_delta, queries, preferred_element_type=single) * 0.125
    )
    content_delta = jnp.einsum(
        "phlm,plhe->pmhe", weights.astype(bfloat), upstream, preferred_element_type=single
    )
    return query_delta, address_delta, content_delta


def marginal_objective(seq_values, doc_scores, member, length):
    joint = doc_scores + seq_values / length
    masked = jnp.where(member, joint[None, :], -1e30)
    top = jnp.max(masked, 1, keepdims=True)
    unscaled = jnp.where(member, jnp.exp(masked - top), 0.0)
    total = jnp.sum(unscaled, 1, keepdims=True)
    marginal = top[:, 0] + jnp.log(total[:, 0])
    posterior = unscaled / total
    entropy = -jnp.sum(jnp.where(member, posterior * (joint[None, :] - marginal[:, None]), 0.0), 1)
    return jnp.mean(-marginal + ENTROPY_WEIGHT * entropy)


def on_device(
    dp,
    mp,
    targets,
    labels,
    passages,
    slot_question,
    slot_passage,
    score_table,
    score_index,
    query_weight,
    query_bias,
    key_weight,
    value_weight,
    value_bias,
    output_weight,
    output_bias,
    first_gain,
    first_shift,
    probe_weight,
    probe_bias,
    address_weight,
    content_weight,
    content_bias,
    merged_weight,
    merged_bias,
    second_gain,
    second_shift,
    expand_weight,
    expand_bias,
    shrink_weight,
    shrink_bias,
    third_gain,
    third_shift,
    embedding,
):
    group = lax.axis_index("dp")
    member_index = lax.axis_index("mp")
    own_questions, length, width = targets.shape
    questions = own_questions * dp
    pair_count = slot_passage.shape[0]
    store_count, passage_length = (passages.shape[0], passages.shape[1])
    vocab_share = embedding.shape[0]
    heads_local = query_weight.shape[1] // HD
    local_width = query_weight.shape[1]
    quarter = length // mp

    mp_order = bits_of(mp)[::-1]
    mp_table = relative_of(mp_order)
    dp_bits = bits_of(dp)
    dp_order = dp_bits[::-1]
    dp_table = relative_of(dp_order)

    def split_heads(flat, count):
        return flat.reshape(count, -1, heads_local, HD)

    def to_own(rows, count):
        natural = rows.reshape((count, mp, quarter) + rows.shape[2:])
        return jnp.moveaxis(xor_take(mp_table, member_index, natural, 1), 1, 0)

    def to_natural(rows, count):
        shaped = rows.reshape((mp, count, quarter) + rows.shape[1:])
        return jnp.moveaxis(natural_order(mp_table, member_index, shaped, 0), 0, 1)

    def mp_scatter(rows, count):
        return scatter_blocks(rows.reshape(mp, count * quarter, width), "mp", mp, mp_order)

    def mp_gather(rows):
        return gather_blocks(rows, "mp", mp, mp_order).reshape((-1,) + rows.shape[1:])

    gains = [value.astype(single) for value in (first_gain, second_gain, third_gain)]
    shifts = [value.astype(single) for value in (first_shift, second_shift, third_shift)]

    inputs = targets.reshape(own_questions * length, width)
    self_queries = (matmul(inputs, query_weight) + query_bias).astype(bfloat)
    self_addresses = matmul(inputs, key_weight).astype(bfloat)
    self_contents = (matmul(inputs, value_weight) + value_bias).astype(bfloat)
    self_mixed, self_total = attend_forward(
        split_heads(self_queries, own_questions),
        split_heads(self_addresses, own_questions),
        split_heads(self_contents, own_questions),
        True,
    )
    self_flat = self_mixed.reshape(own_questions * length, local_width)
    self_own = to_own(self_mixed.reshape(own_questions, length, local_width), own_questions)
    inputs_own = lax.dynamic_slice_in_dim(targets, member_index * quarter, quarter, 1)
    first_in = inputs_own.reshape(-1, width) + (
        mp_scatter(matmul(self_own.reshape(-1, local_width), output_weight), own_questions)
        + output_bias
    )
    first_norm = norm_forward(first_in, gains[0], shifts[0])
    first_low = first_norm.astype(bfloat)
    first_full = mp_gather(first_low)
    probe_own = (matmul(first_full, probe_weight) + probe_bias).astype(bfloat)

    def to_slots(value):
        gathered = gather_blocks(value, "dp", dp, dp_order)
        gathered = jnp.moveaxis(gathered, 2, 1).reshape((questions,) + value.shape[:1] + value.shape[2:])
        where = jnp.asarray(places(dp_table), jnp.int32)[group ^ (my_questions // own_questions)]
        return jnp.take(gathered, where * own_questions + my_questions % own_questions, axis=0, mode="clip")

    my_questions = lax.dynamic_slice_in_dim(slot_question, group * pair_count, pair_count)
    first_slots = to_slots(first_low.reshape(1, own_questions, quarter * width))
    first_slots = first_slots.reshape(pair_count * quarter, width)
    probe_slots = to_slots(probe_own.reshape(mp, own_questions, quarter * local_width))
    probe_slots = probe_slots.reshape(pair_count, length, local_width)

    passage_rows = passages.reshape(-1, width)
    stored_addresses = matmul(passage_rows, address_weight).astype(bfloat)
    stored_contents = (matmul(passage_rows, content_weight) + content_bias).astype(bfloat)

    def select(stored):
        picked = jnp.take(stored.reshape(store_count, -1), slot_passage, axis=0, mode="clip")
        return split_heads(picked, pair_count)

    picked_addresses = select(stored_addresses)
    picked_contents = select(stored_contents)
    cross_mixed, cross_total = attend_forward(
        split_heads(probe_slots, pair_count), picked_addresses, picked_contents, False
    )

    def slots_inside(rows):
        return jnp.moveaxis(rows.reshape(pair_count, mp, quarter, -1), 1, 0).reshape(
            mp * pair_count * quarter, -1
        )

    def slots_outside(rows):
        return jnp.moveaxis(rows.reshape(mp, pair_count, quarter, -1), 0, 1).reshape(
            pair_count, length, -1
        )

    cross_flat = slots_inside(cross_mixed)
    second_in = first_slots + (mp_scatter(matmul(cross_flat, merged_weight), pair_count) + merged_bias)
    second_norm = norm_forward(second_in, gains[1], shifts[1])
    second_low = mp_gather(second_norm.astype(bfloat))
    expanded = matmul(second_low, expand_weight) + expand_bias
    activated = exact_gelu(expanded).astype(bfloat)
    third_in = second_norm + (mp_scatter(matmul(activated, shrink_weight), pair_count) + shrink_bias)
    third_norm = norm_forward(third_in, gains[2], shifts[2])
    third_low = mp_gather(third_norm.astype(bfloat))

    pair_labels = to_own(jnp.take(labels, my_questions, axis=0, mode="clip"), pair_count).reshape(-1)
    local_index = pair_labels - member_index * vocab_share
    inside = (local_index >= 0) & (local_index < vocab_share)
    clipped = jnp.clip(local_index, 0, vocab_share - 1)
    label_rows = jnp.take(embedding, clipped, axis=0, mode="clip")
    logits = outer_rows(third_low, embedding)
    local_top = jnp.max(logits, -1)
    local_total = jnp.sum(jnp.exp(logits - local_top[:, None]), -1)
    local_target = jnp.where(
        inside, jnp.sum(third_low.astype(single) * label_rows.astype(single), -1), 0.0
    )
    top, total, target_logit = local_top, local_total, local_target
    stats = to_natural(jnp.stack([top, total, target_logit], -1), pair_count)
    for bit in mp_order[::-1]:
        other = swap(stats, "mp", mp, bit)
        high = jnp.maximum(stats[..., 0], other[..., 0])
        sums = stats[..., 1] * jnp.exp(stats[..., 0] - high) + other[..., 1] * jnp.exp(
            other[..., 0] - high
        )
        stats = jnp.stack([high, sums, stats[..., 2] + other[..., 2]], -1)
    row_log = stats[..., 0] + jnp.log(stats[..., 1])
    pair_likelihood = jnp.sum((stats[..., 2] - row_log).reshape(pair_count, length), -1)
    every_likelihood = natural_order(
        dp_table, group, gather_blocks(pair_likelihood, "dp", dp, dp_order), 0
    ).reshape(-1)
    log_norm = to_own(row_log.reshape(pair_count, length), pair_count).reshape(-1)
    doc_scores = jnp.take(score_table, score_index)
    member = slot_question[None, :] == jnp.arange(questions, dtype=jnp.int32)[:, None]

    def scored(values_all):
        return marginal_objective(values_all, doc_scores, member, length)

    objective, pullback = jax.vjp(scored, every_likelihood)
    likelihood_delta = pullback(jnp.ones_like(objective) * (questions * length))[0]
    pair_delta = lax.dynamic_slice_in_dim(likelihood_delta, group * pair_count, pair_count)
    row_delta = jnp.broadcast_to(pair_delta[None, :, None], (mp, pair_count, quarter)).reshape(-1)
    columns = lax.broadcasted_iota(jnp.int32, logits.shape, 1)
    hit_table = jnp.where(columns == local_index[:, None], 1.0, 0.0)
    logit_delta = (row_delta[:, None] * (hit_table - jnp.exp(logits - log_norm[:, None]))).astype(
        bfloat
    )

    fast = width % (dp * LANES) == 0

    def permuted(right, order):
        blocks = right.reshape(right.shape[0], dp, width // dp)
        return xor_take(relative_of(order), group, blocks, 1).reshape(right.shape)

    def slope_sum(pairs, order):
        if not fast:
            slope = jnp.concatenate([inner_rows(left, right) for left, right in pairs], 0)
            return lax.psum_scatter(slope, "dp", scatter_dimension=1, tiled=True)
        pairs = [(left, permuted(right, order)) for left, right in pairs]
        held = None
        span = width
        for bit in reversed(order):
            half = span // 2
            sent = [inner_rows(left, right[:, half:span]) for left, right in pairs]
            sent = sent[0] if len(sent) == 1 else jnp.concatenate(sent, 0)
            if held is not None:
                sent = sent + held[:, half:].astype(single)
                held = held[:, :half]
            arrived = swap(sent.astype(bfloat), "dp", dp, bit)
            held = arrived if held is None else held.astype(single) + arrived.astype(single)
            span = half
        kept = [inner_rows(left, right[:, :span]) for left, right in pairs]
        kept = kept[0] if len(kept) == 1 else jnp.concatenate(kept, 0)
        return kept + held.astype(single)

    order_a = dp_bits[::-1]
    order_b = order_a if dp < 4 else [dp_bits[-1], dp_bits[0]] + dp_bits[1:-1]
    unit = vocab_share // 7 if vocab_share % 7 == 0 else vocab_share
    cuts = [0, 2 * unit, 4 * unit, 6 * unit, vocab_share] if unit < vocab_share else [0, unit]
    embedding_parts = []
    for index in range(len(cuts) - 1):
        piece = logit_delta[:, cuts[index] : cuts[index + 1]]
        embedding_parts.append(slope_sum([(piece, third_low)], order_b if index == 1 else order_a))
    embedding_slope = jnp.concatenate(embedding_parts, 0)

    third_delta = mp_scatter(matmul(logit_delta, embedding), pair_count)
    third_back = norm_backward(third_in, gains[2], third_delta)
    feed_low = third_back[0].astype(bfloat)
    feed_delta = mp_gather(feed_low)
    expanded_delta = gelu_backward(expanded, outer_rows(feed_delta, shrink_weight)).astype(bfloat)
    bias_expand = jnp.sum(expanded_delta, 0, dtype=single)
    second_delta = third_back[0] + mp_scatter(outer_rows(expanded_delta, expand_weight), pair_count)
    second_back = norm_backward(second_in, gains[1], second_delta)
    recall_low = second_back[0].astype(bfloat)
    recall_delta = mp_gather(recall_low)
    mixed_delta = outer_rows(recall_delta, merged_weight).astype(bfloat)
    probe_delta, picked_address_delta, picked_content_delta = attend_backward(
        split_heads(probe_slots, pair_count),
        picked_addresses,
        picked_contents,
        cross_total,
        split_heads(slots_outside(mixed_delta), pair_count),
        False,
    )

    def to_questions(value):
        natural = jnp.arange(dp, dtype=jnp.int32)[:, None] * 0 + (
            (group ^ jnp.asarray(dp_table, jnp.int32))[:, None] * own_questions
            + jnp.arange(own_questions, dtype=jnp.int32)[None, :]
        )
        binned = sum(
            jnp.where((natural == my_questions[s])[..., None], value[s][None, None, :], 0.0)
            for s in range(pair_count)
        )
        return scatter_blocks(binned, "dp", dp, dp_order)

    state_delta = to_questions(second_back[0].reshape(pair_count, quarter * width))
    state_delta = state_delta.reshape(own_questions * quarter, width)
    probe_sum = to_questions(probe_delta.reshape(pair_count, length * local_width))
    probe_flat = jnp.moveaxis(
        probe_sum.reshape(own_questions, mp, quarter, local_width), 1, 0
    ).reshape(-1, local_width).astype(bfloat)

    def by_passage(value):
        flat = value.reshape(pair_count, -1)
        return jnp.stack(
            [
                sum(jnp.where(slot_passage[s] == p, flat[s], 0.0) for s in range(pair_count))
                for p in range(store_count)
            ]
        ).astype(bfloat).reshape(store_count * passage_length, local_width)

    address_delta = by_passage(picked_address_delta)
    content_delta = by_passage(picked_content_delta)
    bias_content = jnp.sum(content_delta, 0, dtype=single)
    passages_slope = lax.psum(
        (outer_rows(address_delta, address_weight) + outer_rows(content_delta, content_weight)).astype(bfloat),
        "mp",
    ).astype(single).reshape(passages.shape)

    bias_probe = jnp.sum(probe_flat, 0, dtype=single)
    first_delta = state_delta + mp_scatter(outer_rows(probe_flat, probe_weight), own_questions)
    first_back = norm_backward(first_in, gains[0], first_delta)
    self_low = first_back[0].astype(bfloat)
    self_delta = to_natural(mp_gather(self_low), own_questions).reshape(-1, width)
    self_mixed_delta = outer_rows(self_delta, output_weight).astype(bfloat)
    query_delta, address_raw, content_raw = attend_backward(
        split_heads(self_queries, own_questions),
        split_heads(self_addresses, own_questions),
        split_heads(self_contents, own_questions),
        self_total,
        split_heads(self_mixed_delta, own_questions),
        True,
    )
    query_flat = query_delta.reshape(-1, local_width).astype(bfloat)
    key_flat = address_raw.reshape(-1, local_width).astype(bfloat)
    value_flat = content_raw.reshape(-1, local_width).astype(bfloat)
    bias_query = jnp.sum(query_flat, 0, dtype=single)
    bias_value = jnp.sum(value_flat, 0, dtype=single)
    partial = (
        outer_rows(query_flat, query_weight)
        + outer_rows(key_flat, key_weight)
        + outer_rows(value_flat, value_weight)
    )
    partial_own = to_own(partial.reshape(own_questions, length, width), own_questions)
    input_delta = first_back[0] + mp_scatter(partial_own, own_questions)
    targets_slope = to_natural(mp_gather(input_delta.astype(bfloat)), own_questions)
    targets_slope = targets_slope.reshape(targets.shape).astype(single)

    feed_slopes = slope_sum([(activated, feed_delta), (expanded_delta, second_low)], order_a)
    cross_slopes = slope_sum(
        [
            (cross_flat, recall_delta),
            (address_delta, passage_rows),
            (content_delta, passage_rows),
        ],
        order_a,
    )
    self_slopes = slope_sum(
        [
            (probe_flat, first_full),
            (self_flat, self_delta),
            (query_flat, inputs),
            (key_flat, inputs),
            (value_flat, inputs),
        ],
        order_a,
    )
    hidden = expanded.shape[1]
    shrink_slope = feed_slopes[:hidden]
    expand_slope = feed_slopes[hidden:].T
    merged_slope = cross_slopes[:local_width]
    address_slope = cross_slopes[local_width : 2 * local_width].T
    content_slope = cross_slopes[2 * local_width :].T
    probe_slope = self_slopes[:local_width].T
    output_slope = self_slopes[local_width : 2 * local_width]
    query_slope = self_slopes[2 * local_width : 3 * local_width].T
    key_slope = self_slopes[3 * local_width : 4 * local_width].T
    value_slope = self_slopes[4 * local_width :].T

    shared = total_over(
        jnp.stack(
            [
                jnp.sum(self_low, 0, dtype=single),
                first_back[1],
                first_back[2],
                jnp.sum(recall_low, 0, dtype=single),
                second_back[1],
                second_back[2],
                jnp.sum(feed_low, 0, dtype=single),
                third_back[1],
                third_back[2],
            ]
        ),
        "mp",
        mp,
        mp_order,
    )
    vectors = jnp.concatenate(
        [
            value.reshape(-1, dp, value.shape[-1] // dp).swapaxes(0, 1).reshape(dp, -1)
            for value in (shared, bias_expand, bias_query, bias_value, bias_probe, bias_content)
        ],
        1,
    )
    vectors = scatter_blocks(xor_take(dp_table, group, vectors, 0), "dp", dp, dp_order)
    span = width // dp
    (
        bias_output,
        first_gain_slope,
        first_shift_slope,
        bias_merged,
        second_gain_slope,
        second_shift_slope,
        bias_shrink,
        third_gain_slope,
        third_shift_slope,
    ) = (vectors[i * span : (i + 1) * span] for i in range(9))
    vectors = vectors[9 * span :]
    bias_expand = vectors[: hidden // dp]
    vectors = vectors[hidden // dp :]
    bias_query, bias_value, bias_probe, bias_content = (
        vectors[i * (local_width // dp) : (i + 1) * (local_width // dp)] for i in range(4)
    )
    return (
        objective,
        targets_slope,
        passages_slope,
        query_slope,
        bias_query,
        key_slope,
        value_slope,
        bias_value,
        output_slope,
        bias_output,
        first_gain_slope,
        first_shift_slope,
        probe_slope,
        bias_probe,
        address_slope,
        content_slope,
        bias_content,
        merged_slope,
        bias_merged,
        second_gain_slope,
        second_shift_slope,
        expand_slope,
        bias_expand,
        shrink_slope,
        bias_shrink,
        third_gain_slope,
        third_shift_slope,
        embedding_slope,
    )


def solution(mesh):
    return jax.shard_map(
        functools.partial(on_device, mesh.shape["dp"], mesh.shape["mp"]),
        mesh=mesh,
        in_specs=(
            P("dp", None, None),
            P(),
            P("dp", None, None),
            P(),
            P("dp"),
            P(),
            P(),
            P(None, "mp"),
            P("mp"),
            P(None, "mp"),
            P(None, "mp"),
            P("mp"),
            P("mp", None),
            P(),
            P(),
            P(),
            P(None, "mp"),
            P("mp"),
            P(None, "mp"),
            P(None, "mp"),
            P("mp"),
            P("mp", None),
            P(),
            P(),
            P(),
            P(None, "mp"),
            P("mp"),
            P("mp", None),
            P(),
            P(),
            P(),
            P("mp", None),
        ),
        out_specs=(
            P(),
            P("dp", None, None),
            P("dp", None, None),
            P("dp", "mp"),
            P(("mp", "dp")),
            P("dp", "mp"),
            P("dp", "mp"),
            P(("mp", "dp")),
            P("mp", "dp"),
            P("dp"),
            P("dp"),
            P("dp"),
            P("dp", "mp"),
            P(("mp", "dp")),
            P("dp", "mp"),
            P("dp", "mp"),
            P(("mp", "dp")),
            P("mp", "dp"),
            P("dp"),
            P("dp"),
            P("dp"),
            P("dp", "mp"),
            P(("mp", "dp")),
            P("mp", "dp"),
            P("dp"),
            P("dp"),
            P("dp"),
            P("mp", "dp"),
        ),
        check_vma=False,
    )
```

time: 2350 us -> 1030 us (0.44)
  waiting for transfers between devices: 1720 us -> 275 us
  blocking collectives: 137 us -> 0 us
  local copies, waits for them, and re-layouts: 111 us -> 208 us
  starting transfers between devices: 17.8 us -> 78.8 us
  other arithmetic: 108 us -> 165 us
  matrix products: 230 us -> 268 us
    reduce_scatter x11 -> x0, waiting for transfers between devices: 1390 us -> none  [the longest x1 809 us: on_device(): lax.psum_scatter(embedding_slope, 'dp', scatter_dimension=1, tiled=True)]
    ppermute x0 -> x71, waiting for transfers between devices: none -> 275 us  [swap(): return lax.ppermute(value, axis, [(i, i ^ bit) for i in range(count)])]
    psum x7 -> x1, waiting for transfers between devices: 267 us -> 0.01 us  [on_device(): lax.psum((outer_rows(address_delta, address_weight) + outer_rows(content_...]
    ppermute x0 -> x71, starting transfers between devices: none -> 78.7 us  [swap(): return lax.ppermute(value, axis, [(i, i ^ bit) for i in range(count)])]
    gather x3 -> x36, local copies, waits for them, and re-layouts: 18.4 us -> 92.9 us  [the longest x23 58.2 us: xor_take(): jnp.take(array, me ^ jnp.asarray(table, jnp.int32), axis=axis, mode='clip')]
    dot_general x11 -> x56, matrix products: 79.4 us -> 147 us  [inner_rows(): lax.dot_general(left, right, (((0,), (0,)), ((), ())), preferred_element_...]
    unnamed x2 -> x0, blocking collectives: 63.7 us -> none
    all_to_all x3 -> x0, waiting for transfers between devices: 62 us -> none  [the longest x1 47.5 us: on_device(): lax.all_to_all(outgoing, 'dp', split_axis=0, concat_axis=1, tiled=True)]
  transfers between devices with their start and end apart: 21 -> 72, of which waited for: 18 -> 34; matrix products, arithmetic and copies ran while one was open for 6% -> 43% of each run, Pallas kernels for 0% -> 0%
where the time goes in v1:
time: 1030 us; the launch traced here: 1020 us
  waiting for transfers between devices  275 us (27%)
  matrix products  268 us (26%)
  local copies, waits for them, and re-layouts  208 us (20%)
  other arithmetic  165 us (16%)
  starting transfers between devices  78.8 us (8%)
  between operations  24.6 us (2%)
    ppermute x71, waiting for transfers between devices, swap(): return lax.ppermute(value, axis, [(i, i ^ bit) for i in range(count)])  275 us
    dot_general x56, matrix products, inner_rows(): lax.dot_general(left, right, (((0,), (0,)), ((), ())), preferred_element_...  147 us
    ppermute x71, starting transfers between devices, swap(): return lax.ppermute(value, axis, [(i, i ^ bit) for i in range(count)])  78.7 us
    gather x23, local copies, waits for them, and re-layouts, xor_take(): jnp.take(array, me ^ jnp.asarray(table, jnp.int32), axis=axis, mode='clip')  58.2 us
    dot_general x11, matrix products, matmul(): return jnp.dot(left, right, preferred_element_type=single)  55.2 us
    dot_general x11, matrix products, outer_rows(): lax.dot_general(left, right, (((1,), (1,)), ((), ())), preferred_element_...  53.8 us
    unnamed x421, local copies, waits for them, and re-layouts  34.7 us
    convert_element_type x1, other arithmetic, on_device(): (row_delta[:, None] * (hit_table - jnp.exp(logits - log_norm[:, None])))....  26.6 us
  transfers between devices with their start and end apart: 72, of which 34 were waited for; matrix products, arithmetic and copies ran while one was open for 43% of the time, Pallas kernels for 0%

profile of v1, /device:TPU:0, one launch (start us, length us, event | category | flops | bytes accessed | tf_op | source)
XLA Modules:
  0.0 1019.0 jit_solution(982705494193933391)
XLA Ops:
  67.7 5.5 collective-permute-done.8
  76.1 5.9 collective-permute-done.2
  83.4 4.3 collective-permute-done.9
  116.2 9.1 collective-permute-done.4
  140.4 11.5 %collective-permute-done.12 = bf16[1,256,1024]{2,1,0:T(8,128)(2,1)S(1)} collective-permute-done((bf16[1,256,1024]{2,1,0:T(8,128)(2,1)S(1)}, bf16[1,256,1024]{2,1,0:T(8,128)(2,1)S(1)}, u32[]{:S(2)}, u32[]{:S(2)}) %collective-permute-start.12) | collective-permute-done | bytes 524320 | tf_op jit(solution)/shard_map/ppermute | solution.py:65
  154.9 12.5 %multiply_convert_fusion.2 = (bf16[1024,1024]{1,0:T(8,128)(2,1)S(1)}, f32[1024,1024]{1,0:T(8,128)}, f32[1024,1024]{1,0:T(8,128)}) fusion(f32[1024]{0:T(1024)S(1)} %convert_element_type.644, bf16[1024,1024]{1,0:T(8,128)(2,1)S(1)} %bitcast.452, bf16[1024,1024]{1,0:T(8,128)(2,1)S(1)} %copy-done), kind=kOutput, calls=%fused_computation.64 | convolution fusion | flops 2216689664 | bytes 14684160 | tf_op jit(solution)/shard_map/dot_general | solution.py:46
  182.1 11.6 %collective-permute-done.15 = bf16[1,256,1024]{2,1,0:T(8,128)(2,1)} collective-permute-done((bf16[1,256,1024]{2,1,0:T(8,128)(2,1)}, bf16[1,256,1024]{2,1,0:T(8,128)(2,1)}, u32[]{:S(2)}, u32[]{:S(2)}) %collective-permute-start.15) | collective-permute-done | bytes 524320 | tf_op jit(solution)/shard_map/ppermute | solution.py:65
  200.9 12.0 %collective-permute-done.16 = bf16[1,256,1024]{2,1,0:T(8,128)(2,1)S(1)} collective-permute-done((bf16[1,256,1024]{2,1,0:T(8,128)(2,1)S(1)}, bf16[1,256,1024]{2,1,0:T(8,128)(2,1)S(1)}, u32[]{:S(2)}, u32[]{:S(2)}) %collective-permute-start.16) | collective-permute-done | bytes 524320 | tf_op jit(solution)/shard_map/ppermute | solution.py:65
  214.0 17.6 %gather_fusion.9 = bf16[1024,1024]{1,0:T(8,128)(2,1)} fusion(bf16[12544,1024]{1,0:T(8,128)(2,1)} %param.90, s32[1024]{0:T(1024)S(1)} %broadcast_clamp_fusion.1), kind=kCustom, calls=%fused_computation.9 | custom fusion | bytes 4198400 | tf_op jit(solution)/shard_map/jit(_take)/gather | solution.py:309
  240.3 37.6 %fusion.252 = (f32[1024]{0:T(1024)S(1)}, f32[1024,12544]{1,0:T(8,128)}) fusion(bf16[1024,1024]{1,0:T(8,128)(2,1)} %bitcast.430, bf16[12544,1024]{1,0:T(8,128)(2,1)} %param.90), kind=kOutput, calls=%fused_computation.565 | convolution fusion | flops 26319519744 | bytes 79171584 | tf_op jit(solution)/shard_map/dot_general | solution.py:54
  278.0 20.1 %exponential_reduce_fusion = f32[1024]{0:T(1024)S(1)} fusion(f32[1024,12544]{1,0:T(8,128)} %get-tuple-element.277, f32[1024]{0:T(1024)S(1)} %get-tuple-element.276), kind=kLoop, calls=%fused_computation.30 | loop fusion | flops 25689088 | bytes 51388416 | tf_op jit(solution)/shard_map/reduce_sum | solution.py:312
  327.0 4.0 copy.316
  334.9 3.8 gather_fusion.26
  338.7 3.9 copy.318
  346.3 4.0 copy.320
  364.6 26.6 %multiply_convert_fusion = bf16[1024,12544]{1,0:T(8,128)(2,1)} fusion(f32[1024,12544]{1,0:T(8,128)} %get-tuple-element.277, f32[1024]{0:T(1024)S(1)} %sub.344, s32[1024]{0:T(1024)S(1)} %sub.339, f32[1024]{0:T(1024)S(1)} %mul.507), kind=kLoop, calls=%fused_computation.28 | loop fusion | flops 77070336 | bytes 77082624 | tf_op jit(solution)/shard_map/convert_element_type | solution.py:343
  391.2 32.2 %fusion.256 = f32[1024,1024]{1,0:T(8,128)S(1)} fusion(bf16[1024,12544]{1,0:T(8,128)(2,1)} %multiply_convert_fusion, bf16[12544,1024]{1,0:T(8,128)(2,1)} %param.90), kind=kOutput, calls=%fused_computation.569 | convolution fusion | flops 26306674688 | bytes 55574528 | tf_op jit(solution)/shard_map/dot_general | solution.py:46
  426.5 4.2 convolution_convert_fusion.3
  432.3 8.6 convolution_convert_fusion
  442.7 8.8 convolution_convert_fusion.2
  456.6 17.2 %collective-permute-done.68 = bf16[1792,512]{1,0:T(8,128)(2,1)S(1)} collective-permute-done((bf16[1792,512]{1,0:T(8,128)(2,1)S(1)}, bf16[1792,512]{1,0:T(8,128)(2,1)S(1)}, u32[]{:S(2)}, u32[]{:S(2)}) %collective-permute-start.68) | collective-permute-done | bytes 1835040 | tf_op jit(solution)/shard_map/ppermute | solution.py:65
  473.7 4.9 add_convert_fusion.5
  480.7 8.7 convolution_convert_fusion.1
  495.6 6.6 collective-permute-done.69
  503.6 4.7 fusion.79
  512.8 4.7 convert_reduce_fusion
  528.5 4.3 copy.314
  549.6 33.0 %collective-permute-done.70 = bf16[1792,128]{1,0:T(8,128)(2,1)} collective-permute-done((bf16[1792,128]{1,0:T(8,128)(2,1)}, bf16[1792,128]{1,0:T(8,128)(2,1)}, u32[]{:S(2)}, u32[]{:S(2)}) %collective-permute-start.70) | collective-permute-done | bytes 458784 | tf_op jit(solution)/shard_map/ppermute | solution.py:65
  584.1 4.3 fusion.80
  588.5 5.2 add_convert_fusion.1
  597.3 5.5 add_convert_fusion.2
  606.3 24.9 %collective-permute-done.59 = bf16[3584,512]{1,0:T(8,128)(2,1)} collective-permute-done((bf16[3584,512]{1,0:T(8,128)(2,1)}, bf16[3584,512]{1,0:T(8,128)(2,1)}, u32[]{:S(2)}, u32[]{:S(2)}) %collective-permute-start.59) | collective-permute-done | bytes 3670048 | tf_op jit(solution)/shard_map/ppermute | solution.py:65
  631.1 5.2 add_convert_fusion.3
  647.3 4.5 collective-permute-done.32
  652.0 24.1 %collective-permute-done.56 = bf16[2048,512]{1,0:T(8,128)(2,1)} collective-permute-done((bf16[2048,512]{1,0:T(8,128)(2,1)}, bf16[2048,512]{1,0:T(8,128)(2,1)}, u32[]{:S(2)}, u32[]{:S(2)}) %collective-permute-start.56) | collective-permute-done | bytes 2097184 | tf_op jit(solution)/shard_map/ppermute | solution.py:65
  683.1 4.3 fusion.42
  690.3 21.7 %collective-permute-done.63 = bf16[3584,256]{1,0:T(8,128)(2,1)} collective-permute-done((bf16[3584,256]{1,0:T(8,128)(2,1)}, bf16[3584,256]{1,0:T(8,128)(2,1)}, u32[]{:S(2)}, u32[]{:S(2)}) %collective-permute-start.63) | collective-permute-done | bytes 1835040 | tf_op jit(solution)/shard_map/ppermute | solution.py:65
  714.5 4.3 fusion.44
  724.2 4.6 fusion.46
  780.3 4.0 copy.310
  802.9 5.8 fusion.43
  811.4 5.6 fusion.45
  817.0 5.6 fusion.47
  822.7 9.2 pad_maximum_fusion
  854.6 12.7 %collective-permute-done.36 = bf16[1,1,65536]{2,0,1:T(2,128)(2,1)S(1)} collective-permute-done((bf16[1,1,65536]{2,0,1:T(2,128)(2,1)S(1)}, bf16[1,1,65536]{2,0,1:T(2,128)(2,1)S(1)}, u32[]{:S(2)}, u32[]{:S(2)}) %collective-permute-start.36) | collective-permute-done | bytes 131104 | tf_op jit(solution)/shard_map/ppermute | solution.py:65
  937.2 26.6 %collective-permute-done.50 = bf16[4,1408]{1,0:T(4,128)(2,1)S(1)} collective-permute-done((bf16[4,1408]{1,0:T(4,128)(2,1)S(1)}, bf16[4,1408]{1,0:T(4,128)(2,1)S(1)}, u32[]{:S(2)}, u32[]{:S(2)}) %collective-permute-start.50) | collective-permute-done | bytes 11296 | tf_op jit(solution)/shard_map/ppermute | solution.py:65
  984.9 4.8 collective-permute-done.46
  998.1 7.5 collective-permute-done.47
  (926 shorter events, 476.3 us)
Async XLA Ops:
  7.2 833.9 %all-reduce.2.cloned.1.call-start = ((), (), s32[]{:S(2)}) async-start(), calls=%async_computation | async-start | bytes 2097152 | tf_op jit(solution)/shard_map/psum | solution.py:434
  36.8 25.7 %collective-permute-start.7 = (bf16[1,4,1,16384]{3,1,2,0:T(4,128)(2,1)S(1)}, bf16[1,4,1,16384]{3,1,2,0:T(4,128)(2,1)}, u32[]{:S(2)}, u32[]{:S(2)}) collective-permute-start(bf16[1,4,1,16384]{3,1,2,0:T(4,128)(2,1)S(1)} %broadcast_in_dim_reshape.2), channel_id=1, source_target_pairs={{0,16},{4,20},{8,24},{12,28},{16,0},{20,4},{24,8},{28,12},{1,17},{... | collective-permute-start | bytes 393224 | tf_op jit(solution)/shard_map/ppermute | solution.py:65
  67.3 14.7 %collective-permute-start.2 = (bf16[1,1,1,65536]{3,0,2,1:T(2,128)(2,1)S(1)}, bf16[1,1,1,65536]{3,0,2,1:T(2,128)(2,1)S(1)}, u32[]{:S(2)}, u32[]{:S(2)}) collective-permute-start(bf16[1,1,1,65536]{3,0,2,1:T(2,128)(2,1)S(1)} %add_convert_fusion.13), channel_id=1, source_target_pairs={{0,16},{4,20},{8,24},{12,28},{16,0},{20,4},{24,8},{28,12},{1,17},{... | collective-permute-start | bytes 393224 | tf_op jit(solution)/shard_map/ppermute | solution.py:65
  74.5 13.2 %collective-permute-start.9 = (bf16[4,4,1,16384]{3,1,2,0:T(4,128)(2,1)S(1)}, bf16[4,4,1,16384]{3,1,2,0:T(4,128)(2,1)S(1)}, u32[]{:S(2)}, u32[]{:S(2)}) collective-permute-start(bf16[4,4,1,16384]{3,1,2,0:T(4,128)(2,1)S(1)} %pad_maximum_fusion.13), channel_id=1, source_target_pairs={{0,4},{4,0},{8,12},{12,8},{16,20},{20,16},{24,28},{28,24},{1,5},{5... | collective-permute-start | bytes 1572872 | tf_op jit(solution)/shard_map/ppermute | solution.py:65
  83.4 25.7 %collective-permute-start.3 = (bf16[2,1,1,65536]{3,0,2,1:T(2,128)(2,1)}, bf16[2,1,1,65536]{3,0,2,1:T(2,128)(2,1)}, u32[]{:S(2)}, u32[]{:S(2)}) collective-permute-start(bf16[2,1,1,65536]{3,0,2,1:T(2,128)(2,1)} %pad_maximum_fusion.16), channel_id=1, source_target_pairs={{0,8},{4,12},{8,0},{12,4},{16,24},{20,28},{24,16},{28,20},{1,9},{5... | collective-permute-start | bytes 786440 | tf_op jit(solution)/shard_map/ppermute | solution.py:65
  111.6 13.7 %collective-permute-start.4 = (bf16[4,1,1,65536]{3,0,2,1:T(4,128)(2,1)S(1)}, bf16[4,1,1,65536]{3,0,2,1:T(4,128)(2,1)S(1)}, u32[]{:S(2)}, u32[]{:S(2)}) collective-permute-start(bf16[4,1,1,65536]{3,0,2,1:T(4,128)(2,1)S(1)} %pad_maximum_fusion.11), channel_id=1, source_target_pairs={{0,4},{4,0},{8,12},{12,8},{16,20},{20,16},{24,28},{28,24},{1,5},{5... | collective-permute-start | bytes 1572872 | tf_op jit(solution)/shard_map/ppermute | solution.py:65
  114.7 19.2 %collective-permute-start.11 = (bf16[1,256,1024]{2,1,0:T(8,128)(2,1)}, bf16[1,256,1024]{2,1,0:T(8,128)(2,1)}, u32[]{:S(2)}, u32[]{:S(2)}) collective-permute-start(bf16[1,256,1024]{2,1,0:T(8,128)(2,1)} %slice.1523), channel_id=1, source_target_pairs={{0,2},{1,3},{2,0},{3,1},{4,6},{5,7},{6,4},{7,5},{8,10},{9,11},{10,... | collective-permute-start | bytes 1572872 | tf_op jit(solution)/shard_map/ppermute | solution.py:65
  139.0 12.9 %collective-permute-start.12 = (bf16[1,256,1024]{2,1,0:T(8,128)(2,1)S(1)}, bf16[1,256,1024]{2,1,0:T(8,128)(2,1)S(1)}, u32[]{:S(2)}, u32[]{:S(2)}) collective-permute-start(bf16[1,256,1024]{2,1,0:T(8,128)(2,1)S(1)} %get-tuple-element.207), channel_id=1, source_target_pairs={{0,2},{1,3},{2,0},{3,1},{4,6},{5,7},{6,4},{7,5},{8,10},{9,11},{10,... | collective-permute-start | bytes 1572872 | tf_op jit(solution)/shard_map/ppermute | solution.py:65
  179.2 14.5 %collective-permute-start.15 = (bf16[1,256,1024]{2,1,0:T(8,128)(2,1)}, bf16[1,256,1024]{2,1,0:T(8,128)(2,1)}, u32[]{:S(2)}, u32[]{:S(2)}) collective-permute-start(bf16[1,256,1024]{2,1,0:T(8,128)(2,1)} %slice.1522), channel_id=1, source_target_pairs={{0,2},{1,3},{2,0},{3,1},{4,6},{5,7},{6,4},{7,5},{8,10},{9,11},{10,... | collective-permute-start | bytes 1572872 | tf_op jit(solution)/shard_map/ppermute | solution.py:65
  199.5 13.4 %collective-permute-start.16 = (bf16[1,256,1024]{2,1,0:T(8,128)(2,1)S(1)}, bf16[1,256,1024]{2,1,0:T(8,128)(2,1)S(1)}, u32[]{:S(2)}, u32[]{:S(2)}) collective-permute-start(bf16[1,256,1024]{2,1,0:T(8,128)(2,1)S(1)} %get-tuple-element.201), channel_id=1, source_target_pairs={{0,2},{1,3},{2,0},{3,1},{4,6},{5,7},{6,4},{7,5},{8,10},{9,11},{10,... | collective-permute-start | bytes 1572872 | tf_op jit(solution)/shard_map/ppermute | solution.py:65
  214.0 22.6 %collective-permute-start.17 = (bf16[2,256,1024]{2,1,0:T(8,128)(2,1)}, bf16[2,256,1024]{2,1,0:T(8,128)(2,1)}, u32[]{:S(2)}, u32[]{:S(2)}) collective-permute-start(bf16[2,256,1024]{2,1,0:T(8,128)(2,1)} %pad_maximum_fusion.7), channel_id=1, source_target_pairs={{0,1},{1,0},{2,3},{3,2},{4,5},{5,4},{6,7},{7,6},{8,9},{9,8},{10,11... | collective-permute-start | bytes 3145736 | tf_op jit(solution)/shard_map/ppermute | solution.py:65
  298.8 18.5 %collective-permute-start.18 = (f32[4,4,64,3]{2,0,1,3:T(4,128)S(1)}, f32[4,4,64,3]{2,0,1,3:T(4,128)S(1)}, u32[]{:S(2)}, u32[]{:S(2)}) collective-permute-start(f32[4,4,64,3]{2,0,1,3:T(4,128)S(1)} %copy.278), channel_id=1, source_target_pairs={{0,1},{1,0},{2,3},{3,2},{4,5},{5,4},{6,7},{7,6},{8,9},{9,8},{10,11... | collective-permute-start | bytes 36872 | tf_op jit(solution)/shard_map/ppermute | solution.py:65
  317.4 32.8 %collective-permute-start.19 = (f32[4,4,64,3]{2,0,1,3:T(4,128)S(1)}, f32[4,4,64,3]{2,0,1,3:T(4,128)S(1)}, u32[]{:S(2)}, u32[]{:S(2)}) collective-permute-start(f32[4,4,64,3]{2,0,1,3:T(4,128)S(1)} %pad_maximum_fusion.24), channel_id=1, source_target_pairs={{0,2},{1,3},{2,0},{3,1},{4,6},{5,7},{6,4},{7,5},{8,10},{9,11},{10,... | collective-permute-start | bytes 36872 | tf_op jit(solution)/shard_map/ppermute | solution.py:65
  423.6 17.9 %collective-permute-start.23 = (bf16[2,256,1024]{2,1,0:T(8,128)(2,1)S(1)}, bf16[2,256,1024]{2,1,0:T(8,128)(2,1)S(1)}, u32[]{:S(2)}, u32[]{:S(2)}) collective-permute-start(bf16[2,256,1024]{2,1,0:T(8,128)(2,1)S(1)} %bitcast.567), channel_id=1, source_target_pairs={{0,1},{1,0},{2,3},{3,2},{4,5},{5,4},{6,7},{7,6},{8,9},{9,8},{10,11... | collective-permute-start | bytes 3145736 | tf_op jit(solution)/shard_map/ppermute | solution.py:65
  430.7 43.0 %collective-permute-start.68 = (bf16[1792,512]{1,0:T(8,128)(2,1)S(1)}, bf16[1792,512]{1,0:T(8,128)(2,1)S(1)}, u32[]{:S(2)}, u32[]{:S(2)}) collective-permute-start(bf16[1792,512]{1,0:T(8,128)(2,1)S(1)} %convolution_convert_fusion.3), channel_id=1, source_target_pairs={{0,4},{4,0},{8,12},{12,8},{16,20},{20,16},{24,28},{28,24},{1,5},{5... | collective-permute-start | bytes 5505032 | tf_op jit(solution)/shard_map/ppermute | solution.py:65
  440.9 147.5 %collective-permute-start.65 = (bf16[3584,512]{1,0:T(8,128)(2,1)}, bf16[3584,512]{1,0:T(8,128)(2,1)}, u32[]{:S(2)}, u32[]{:S(2)}) collective-permute-start(bf16[3584,512]{1,0:T(8,128)(2,1)} %convolution_convert_fusion), channel_id=1, source_target_pairs={{0,4},{4,0},{8,12},{12,8},{16,20},{20,16},{24,28},{28,24},{1,5},{5... | collective-permute-start | bytes 11010056 | tf_op jit(solution)/shard_map/ppermute | solution.py:65
  442.0 11.1 %collective-permute-start.24 = (bf16[1,256,1024]{2,1,0:T(8,128)(2,1)S(1)}, bf16[1,256,1024]{2,1,0:T(8,128)(2,1)S(1)}, u32[]{:S(2)}, u32[]{:S(2)}) collective-permute-start(bf16[1,256,1024]{2,1,0:T(8,128)(2,1)S(1)} %slice.1521), channel_id=1, source_target_pairs={{0,2},{1,3},{2,0},{3,1},{4,6},{5,7},{6,4},{7,5},{8,10},{9,11},{10,... | collective-permute-start | bytes 1572872 | tf_op jit(solution)/shard_map/ppermute | solution.py:65
  456.0 36.2 %collective-permute-start.25 = (bf16[1,256,1024]{2,1,0:T(8,128)(2,1)}, bf16[1,256,1024]{2,1,0:T(8,128)(2,1)}, u32[]{:S(2)}, u32[]{:S(2)}) collective-permute-start(bf16[1,256,1024]{2,1,0:T(8,128)(2,1)} %fusion.235), channel_id=1, source_target_pairs={{0,2},{1,3},{2,0},{3,1},{4,6},{5,7},{6,4},{7,5},{8,10},{9,11},{10,... | collective-permute-start | bytes 1572872 | tf_op jit(solution)/shard_map/ppermute | solution.py:65
  478.6 23.6 %collective-permute-start.69 = (bf16[1792,256]{1,0:T(8,128)(2,1)}, bf16[1792,256]{1,0:T(8,128)(2,1)}, u32[]{:S(2)}, u32[]{:S(2)}) collective-permute-start(bf16[1792,256]{1,0:T(8,128)(2,1)} %add_convert_fusion.5), channel_id=1, source_target_pairs={{0,8},{4,12},{8,0},{12,4},{16,24},{20,28},{24,16},{28,20},{1,9},{5... | collective-permute-start | bytes 2752520 | tf_op jit(solution)/shard_map/ppermute | solution.py:65
  489.3 108.0 %collective-permute-start.62 = (bf16[3584,512]{1,0:T(8,128)(2,1)}, bf16[3584,512]{1,0:T(8,128)(2,1)}, u32[]{:S(2)}, u32[]{:S(2)}) collective-permute-start(bf16[3584,512]{1,0:T(8,128)(2,1)} %convolution_convert_fusion.1), channel_id=1, source_target_pairs={{0,8},{4,12},{8,0},{12,4},{16,24},{20,28},{24,16},{28,20},{1,9},{5... | collective-permute-start | bytes 11010056 | tf_op jit(solution)/shard_map/ppermute | solution.py:65
  489.4 141.8 %collective-permute-start.59 = (bf16[3584,512]{1,0:T(8,128)(2,1)}, bf16[3584,512]{1,0:T(8,128)(2,1)}, u32[]{:S(2)}, u32[]{:S(2)}) collective-permute-start(bf16[3584,512]{1,0:T(8,128)(2,1)} %convolution_convert_fusion.2), channel_id=1, source_target_pairs={{0,4},{4,0},{8,12},{12,8},{16,20},{20,16},{24,28},{28,24},{1,5},{5... | collective-permute-start | bytes 11010056 | tf_op jit(solution)/shard_map/ppermute | solution.py:65
  493.5 17.8 %collective-permute-start.26 = (bf16[2,256,1024]{2,1,0:T(8,128)(2,1)S(1)}, bf16[2,256,1024]{2,1,0:T(8,128)(2,1)S(1)}, u32[]{:S(2)}, u32[]{:S(2)}) collective-permute-start(bf16[2,256,1024]{2,1,0:T(8,128)(2,1)S(1)} %pad_maximum_fusion.8), channel_id=1, source_target_pairs={{0,1},{1,0},{2,3},{3,2},{4,5},{5,4},{6,7},{7,6},{8,9},{9,8},{10,11... | collective-permute-start | bytes 3145736 | tf_op jit(solution)/shard_map/ppermute | solution.py:65
  508.4 74.2 %collective-permute-start.70 = (bf16[1792,128]{1,0:T(8,128)(2,1)}, bf16[1792,128]{1,0:T(8,128)(2,1)}, u32[]{:S(2)}, u32[]{:S(2)}) collective-permute-start(bf16[1792,128]{1,0:T(8,128)(2,1)} %fusion.79), channel_id=1, source_target_pairs={{0,16},{4,20},{8,24},{12,28},{16,0},{20,4},{24,8},{28,12},{1,17},{... | collective-permute-start | bytes 1376264 | tf_op jit(solution)/shard_map/ppermute | solution.py:65
  522.4 80.9 %collective-permute-start.27 = (bf16[2,256,1024]{2,1,0:T(8,128)(2,1)}, bf16[2,256,1024]{2,1,0:T(8,128)(2,1)}, u32[]{:S(2)}, u32[]{:S(2)}) collective-permute-start(bf16[2,256,1024]{2,1,0:T(8,128)(2,1)} %bitcast.45), channel_id=1, source_target_pairs={{0,1},{1,0},{2,3},{3,2},{4,5},{5,4},{6,7},{7,6},{8,9},{9,8},{10,11... | collective-permute-start | bytes 3145736 | tf_op jit(solution)/shard_map/ppermute | solution.py:65
  582.6 93.5 %collective-permute-start.56 = (bf16[2048,512]{1,0:T(8,128)(2,1)}, bf16[2048,512]{1,0:T(8,128)(2,1)}, u32[]{:S(2)}, u32[]{:S(2)}) collective-permute-start(bf16[2048,512]{1,0:T(8,128)(2,1)} %pad_maximum_fusion.5), channel_id=1, source_target_pairs={{0,4},{4,0},{8,12},{12,8},{16,20},{20,16},{24,28},{28,24},{1,5},{5... | collective-permute-start | bytes 6291464 | tf_op jit(solution)/shard_map/ppermute | solution.py:65
  593.7 87.0 %collective-permute-start.66 = (bf16[3584,256]{1,0:T(8,128)(2,1)}, bf16[3584,256]{1,0:T(8,128)(2,1)}, u32[]{:S(2)}, u32[]{:S(2)}) collective-permute-start(bf16[3584,256]{1,0:T(8,128)(2,1)} %add_convert_fusion.1), channel_id=1, source_target_pairs={{0,8},{4,12},{8,0},{12,4},{16,24},{20,28},{24,16},{28,20},{1,9},{5... | collective-permute-start | bytes 5505032 | tf_op jit(solution)/shard_map/ppermute | solution.py:65
  602.8 109.2 %collective-permute-start.63 = (bf16[3584,256]{1,0:T(8,128)(2,1)}, bf16[3584,256]{1,0:T(8,128)(2,1)}, u32[]{:S(2)}, u32[]{:S(2)}) collective-permute-start(bf16[3584,256]{1,0:T(8,128)(2,1)} %add_convert_fusion.2), channel_id=1, source_target_pairs={{0,4},{4,0},{8,12},{12,8},{16,20},{20,16},{24,28},{28,24},{1,5},{5... | collective-permute-start | bytes 5505032 | tf_op jit(solution)/shard_map/ppermute | solution.py:65
  605.6 32.7 %collective-permute-start.28 = (bf16[1,256,1024]{2,1,0:T(8,128)(2,1)S(1)}, bf16[1,256,1024]{2,1,0:T(8,128)(2,1)S(1)}, u32[]{:S(2)}, u32[]{:S(2)}) collective-permute-start(bf16[1,256,1024]{2,1,0:T(8,128)(2,1)S(1)} %slice.1520), channel_id=1, source_target_pairs={{0,2},{1,3},{2,0},{3,1},{4,6},{5,7},{6,4},{7,5},{8,10},{9,11},{10,... | collective-permute-start | bytes 1572872 | tf_op jit(solution)/shard_map/ppermute | solution.py:65
  636.3 85.3 %collective-permute-start.60 = (bf16[3584,256]{1,0:T(8,128)(2,1)}, bf16[3584,256]{1,0:T(8,128)(2,1)}, u32[]{:S(2)}, u32[]{:S(2)}) collective-permute-start(bf16[3584,256]{1,0:T(8,128)(2,1)} %add_convert_fusion.3), channel_id=1, source_target_pairs={{0,8},{4,12},{8,0},{12,4},{16,24},{20,28},{24,16},{28,20},{1,9},{5... | collective-permute-start | bytes 5505032 | tf_op jit(solution)/shard_map/ppermute | solution.py:65
  651.9 76.9 %collective-permute-start.33 = (bf16[2,256,1024]{2,1,0:T(8,128)(2,1)S(1)}, bf16[2,256,1024]{2,1,0:T(8,128)(2,1)S(1)}, u32[]{:S(2)}, u32[]{:S(2)}) collective-permute-start(bf16[2,256,1024]{2,1,0:T(8,128)(2,1)S(1)} %pad_maximum_fusion.9), channel_id=1, source_target_pairs={{0,1},{1,0},{2,3},{3,2},{4,5},{5,4},{6,7},{7,6},{8,9},{9,8},{10,11... | collective-permute-start | bytes 3145736 | tf_op jit(solution)/shard_map/ppermute | solution.py:65
  678.6 116.4 %collective-permute-start.57 = (bf16[2048,256]{1,0:T(8,128)(2,1)}, bf16[2048,256]{1,0:T(8,128)(2,1)}, u32[]{:S(2)}, u32[]{:S(2)}) collective-permute-start(bf16[2048,256]{1,0:T(8,128)(2,1)} %fusion.38), channel_id=1, source_target_pairs={{0,8},{4,12},{8,0},{12,4},{16,24},{20,28},{24,16},{28,20},{1,9},{5... | collective-permute-start | bytes 3145736 | tf_op jit(solution)/shard_map/ppermute | solution.py:65
  687.4 114.5 %collective-permute-start.67 = (bf16[3584,128]{1,0:T(8,128)(2,1)}, bf16[3584,128]{1,0:T(8,128)(2,1)}, u32[]{:S(2)}, u32[]{:S(2)}) collective-permute-start(bf16[3584,128]{1,0:T(8,128)(2,1)} %fusion.42), channel_id=1, source_target_pairs={{0,16},{4,20},{8,24},{12,28},{16,0},{20,4},{24,8},{28,12},{1,17},{... | collective-permute-start | bytes 2752520 | tf_op jit(solution)/shard_map/ppermute | solution.py:65
  718.8 89.9 %collective-permute-start.64 = (bf16[3584,128]{1,0:T(8,128)(2,1)}, bf16[3584,128]{1,0:T(8,128)(2,1)}, u32[]{:S(2)}, u32[]{:S(2)}) collective-permute-start(bf16[3584,128]{1,0:T(8,128)(2,1)} %fusion.44), channel_id=1, source_target_pairs={{0,16},{4,20},{8,24},{12,28},{16,0},{20,4},{24,8},{28,12},{1,17},{... | collective-permute-start | bytes 2752520 | tf_op jit(solution)/shard_map/ppermute | solution.py:65
  728.8 88.2 %collective-permute-start.61 = (bf16[3584,128]{1,0:T(8,128)(2,1)}, bf16[3584,128]{1,0:T(8,128)(2,1)}, u32[]{:S(2)}, u32[]{:S(2)}) collective-permute-start(bf16[3584,128]{1,0:T(8,128)(2,1)} %fusion.46), channel_id=1, source_target_pairs={{0,16},{4,20},{8,24},{12,28},{16,0},{20,4},{24,8},{28,12},{1,17},{... | collective-permute-start | bytes 2752520 | tf_op jit(solution)/shard_map/ppermute | solution.py:65
  768.5 63.3 %collective-permute-start.29 = (bf16[4,1,65536]{2,0,1:T(4,128)(2,1)}, bf16[4,1,65536]{2,0,1:T(4,128)(2,1)}, u32[]{:S(2)}, u32[]{:S(2)}) collective-permute-start(bf16[4,1,65536]{2,0,1:T(4,128)(2,1)} %slice.1519), channel_id=1, source_target_pairs={{0,4},{4,0},{8,12},{12,8},{16,20},{20,16},{24,28},{28,24},{1,5},{5... | collective-permute-start | bytes 1572872 | tf_op jit(solution)/shard_map/ppermute | solution.py:65
  795.1 41.4 %collective-permute-start.34 = (bf16[4,1,65536]{2,0,1:T(4,128)(2,1)S(1)}, bf16[4,1,65536]{2,0,1:T(4,128)(2,1)S(1)}, u32[]{:S(2)}, u32[]{:S(2)}) collective-permute-start(bf16[4,1,65536]{2,0,1:T(4,128)(2,1)S(1)} %copy-done.112), channel_id=1, source_target_pairs={{0,4},{4,0},{8,12},{12,8},{16,20},{20,16},{24,28},{28,24},{1,5},{5... | collective-permute-start | bytes 1572872 | tf_op jit(solution)/shard_map/ppermute | solution.py:65
  801.9 48.8 %collective-permute-start.53 = (bf16[768,512]{1,0:T(8,128)(2,1)}, bf16[768,512]{1,0:T(8,128)(2,1)}, u32[]{:S(2)}, u32[]{:S(2)}) collective-permute-start(bf16[768,512]{1,0:T(8,128)(2,1)} %pad_maximum_fusion.10), channel_id=1, source_target_pairs={{0,4},{4,0},{8,12},{12,8},{16,20},{20,16},{24,28},{28,24},{1,5},{5... | collective-permute-start | bytes 2359304 | tf_op jit(solution)/shard_map/ppermute | solution.py:65
  808.7 29.1 %collective-permute-start.58 = (bf16[2048,128]{1,0:T(8,128)(2,1)S(1)}, bf16[2048,128]{1,0:T(8,128)(2,1)S(1)}, u32[]{:S(2)}, u32[]{:S(2)}) collective-permute-start(bf16[2048,128]{1,0:T(8,128)(2,1)S(1)} %fusion.68), channel_id=1, source_target_pairs={{0,16},{4,20},{8,24},{12,28},{16,0},{20,4},{24,8},{28,12},{1,17},{... | collective-permute-start | bytes 1572872 | tf_op jit(solution)/shard_map/ppermute | solution.py:65
  834.4 9.6 collective-permute-start.30
  846.2 26.8 %collective-permute-start.31 = (bf16[1,1,65536]{2,0,1:T(2,128)(2,1)}, bf16[1,1,65536]{2,0,1:T(2,128)(2,1)}, u32[]{:S(2)}, u32[]{:S(2)}) collective-permute-start(bf16[1,1,65536]{2,0,1:T(2,128)(2,1)} %slice.1531), channel_id=1, source_target_pairs={{0,16},{4,20},{8,24},{12,28},{16,0},{20,4},{24,8},{28,12},{1,17},{... | collective-permute-start | bytes 393224 | tf_op jit(solution)/shard_map/ppermute | solution.py:65
  848.2 19.1 %collective-permute-start.36 = (bf16[1,1,65536]{2,0,1:T(2,128)(2,1)S(1)}, bf16[1,1,65536]{2,0,1:T(2,128)(2,1)S(1)}, u32[]{:S(2)}, u32[]{:S(2)}) collective-permute-start(bf16[1,1,65536]{2,0,1:T(2,128)(2,1)S(1)} %slice.1530), channel_id=1, source_target_pairs={{0,16},{4,20},{8,24},{12,28},{16,0},{20,4},{24,8},{28,12},{1,17},{... | collective-permute-start | bytes 393224 | tf_op jit(solution)/shard_map/ppermute | solution.py:65
  852.6 25.9 %collective-permute-start.54 = (bf16[768,256]{1,0:T(8,128)(2,1)}, bf16[768,256]{1,0:T(8,128)(2,1)}, u32[]{:S(2)}, u32[]{:S(2)}) collective-permute-start(bf16[768,256]{1,0:T(8,128)(2,1)} %fusion.85), channel_id=1, source_target_pairs={{0,8},{4,12},{8,0},{12,4},{16,24},{20,28},{24,16},{28,20},{1,9},{5... | collective-permute-start | bytes 1179656 | tf_op jit(solution)/shard_map/ppermute | solution.py:65
  881.4 11.7 %collective-permute-start.55 = (bf16[768,128]{1,0:T(8,128)(2,1)}, bf16[768,128]{1,0:T(8,128)(2,1)}, u32[]{:S(2)}, u32[]{:S(2)}) collective-permute-start(bf16[768,128]{1,0:T(8,128)(2,1)} %fusion.122), channel_id=1, source_target_pairs={{0,16},{4,20},{8,24},{12,28},{16,0},{20,4},{24,8},{28,12},{1,17},{... | collective-permute-start | bytes 589832 | tf_op jit(solution)/shard_map/ppermute | solution.py:65
  913.9 58.3 %collective-permute-start.41 = (bf16[2,64,1024]{2,1,0:T(8,128)(2,1)}, bf16[2,64,1024]{2,1,0:T(8,128)(2,1)}, u32[]{:S(2)}, u32[]{:S(2)}) collective-permute-start(bf16[2,64,1024]{2,1,0:T(8,128)(2,1)} %fusion.124), channel_id=1, source_target_pairs={{0,1},{1,0},{2,3},{3,2},{4,5},{5,4},{6,7},{7,6},{8,9},{9,8},{10,11... | collective-permute-start | bytes 786440 | tf_op jit(solution)/shard_map/ppermute | solution.py:65
  932.5 42.2 %collective-permute-start.45 = (bf16[1280,512]{1,0:T(8,128)(2,1)}, bf16[1280,512]{1,0:T(8,128)(2,1)}, u32[]{:S(2)}, u32[]{:S(2)}) collective-permute-start(bf16[1280,512]{1,0:T(8,128)(2,1)} %fusion.57), channel_id=1, source_target_pairs={{0,4},{4,0},{8,12},{12,8},{16,20},{20,16},{24,28},{28,24},{1,5},{5... | collective-permute-start | bytes 3932168 | tf_op jit(solution)/shard_map/ppermute | solution.py:65
  935.4 28.3 %collective-permute-start.50 = (bf16[4,1408]{1,0:T(4,128)(2,1)S(1)}, bf16[4,1408]{1,0:T(4,128)(2,1)S(1)}, u32[]{:S(2)}, u32[]{:S(2)}) collective-permute-start(bf16[4,1408]{1,0:T(4,128)(2,1)S(1)} %slice.1533), channel_id=1, source_target_pairs={{0,4},{4,0},{8,12},{12,8},{16,20},{20,16},{24,28},{28,24},{1,5},{5... | collective-permute-start | bytes 33800 | tf_op jit(solution)/shard_map/ppermute | solution.py:65
  976.0 13.8 %collective-permute-start.46 = (bf16[1280,256]{1,0:T(8,128)(2,1)S(1)}, bf16[1280,256]{1,0:T(8,128)(2,1)S(1)}, u32[]{:S(2)}, u32[]{:S(2)}) collective-permute-start(bf16[1280,256]{1,0:T(8,128)(2,1)S(1)} %add_convert_fusion.6), channel_id=1, source_target_pairs={{0,8},{4,12},{8,0},{12,4},{16,24},{20,28},{24,16},{28,20},{1,9},{5... | collective-permute-start | bytes 1966088 | tf_op jit(solution)/shard_map/ppermute | solution.py:65
  991.8 13.8 %collective-permute-start.47 = (bf16[1280,128]{1,0:T(8,128)(2,1)}, bf16[1280,128]{1,0:T(8,128)(2,1)}, u32[]{:S(2)}, u32[]{:S(2)}) collective-permute-start(bf16[1280,128]{1,0:T(8,128)(2,1)} %fusion.86), channel_id=1, source_target_pairs={{0,16},{4,20},{8,24},{12,28},{16,0},{20,4},{24,8},{28,12},{1,17},{... | collective-permute-start | bytes 983048 | tf_op jit(solution)/shard_map/ppermute | solution.py:65
  (226 other events, 2395.3 us)
Sparse Core Ops, SparseCore 0:
  772.7 36.3 all-reduce.1

commit v2 on v1

v2 whole, which is shorter than its diff:
```python
import functools

import jax
import jax.numpy as jnp
from jax import lax
from jax.experimental import pallas as pl
from jax.experimental.pallas import tpu as pltpu
from jax.sharding import PartitionSpec as P

HD = 64
LANES = 128
EPSILON = 1e-05
ENTROPY_WEIGHT = 0.5
BRIEF = pl.CostEstimate(flops=0, bytes_accessed=0, transcendentals=0)
bfloat = jnp.bfloat16
single = jnp.float32


def matmul(left, right):
    return jnp.dot(left, right, preferred_element_type=single)


def inner_rows(left, right):
    return lax.dot_general(left, right, (((0,), (0,)), ((), ())), preferred_element_type=single)


def outer_rows(left, right):
    return lax.dot_general(left, right, (((1,), (1,)), ((), ())), preferred_element_type=single)


def bits_of(count):
    bits = []
    while (1 << len(bits)) < count:
        bits.append(1 << len(bits))
    return bits


def swap(value, axis, count, bit):
    return lax.ppermute(value, axis, [(i, i ^ bit) for i in range(count)])


def relative_of(order):
    table = [0]
    for bit in order:
        table = table + [r ^ bit for r in table]
    return table


def gather_blocks(own, axis, count, order):
    held = own[None]
    for bit in order:
        held = jnp.concatenate([held, swap(held, axis, count, bit)], 0)
    return held


def scatter_blocks(parts, axis, count, order):
    for bit in reversed(order):
        half = parts.shape[0] // 2
        arrived = swap(parts[half:].astype(bfloat), axis, count, bit)
        parts = parts[:half] + arrived.astype(single)
    return parts[0]


def tie(*values):
    return lax.optimization_barrier(values)


def gather_both(owns, axis, count, orders):
    helds = [own[None] for own in owns]
    for bits in zip(*orders):
        arrived = tie(*(swap(held, axis, count, bit) for held, bit in zip(helds, bits)))
        helds = [jnp.concatenate([held, more], 0) for held, more in zip(helds, arrived)]
    return helds


def scatter_both_steps(values, axis, count, orders, through):
    for bits in zip(*(order[::-1] for order in orders)):
        sent = through(*(value[0] for value in values))
        arrived = [swap(value, axis, count, bit) for value, bit in zip(sent, bits)]
        yield None
        arrived = through(*arrived)
        if bits[0] == orders[0][0]:
            yield [(value[1], more) for value, more in zip(values, arrived)]
        else:
            values = [add_halves(value[1], more) for value, more in zip(values, arrived)]


def total_over(value, axis, count, order):
    for bit in order:
        value = value + swap(value, axis, count, bit)
    return value


def xor_take(table, me, array, axis):
    return jnp.take(array, me ^ jnp.asarray(table, jnp.int32), axis=axis, mode="clip")


def places(table):
    inverse = [0] * len(table)
    for position, relative in enumerate(table):
        inverse[relative] = position
    return inverse


def natural_order(table, me, array, axis):
    count = len(table)
    order = jnp.asarray(places(table), jnp.int32)[me ^ jnp.arange(count, dtype=jnp.int32)]
    return jnp.take(array, order, axis=axis, mode="clip")


VMEM = pl.BlockSpec(memory_space=pltpu.VMEM)


def run_whole(kernel, name, outs, *operands, scratch=()):
    return pl.pallas_call(
        kernel,
        in_specs=[VMEM] * len(operands),
        out_specs=[VMEM] * len(outs),
        out_shape=[jax.ShapeDtypeStruct(shape, dtype) for shape, dtype in outs],
        scratch_shapes=list(scratch),
        compiler_params=pltpu.CompilerParams(vmem_limit_bytes=56 * 1024 * 1024),
        cost_estimate=BRIEF,
        name=name,
    )(*operands)


def row(vector):
    return vector.reshape(1, -1).astype(single)


def norm_forward_kernel(kept_ref, arrived_ref, state_ref, bias_ref, gain_ref, shift_ref, in_ref, out_ref, low_ref):
    hidden = (
        state_ref[...].astype(single)
        + (kept_ref[...].astype(single) + arrived_ref[...].astype(single))
        + bias_ref[...]
    )
    in_ref[...] = hidden
    center = hidden - jnp.mean(hidden, -1, keepdims=True)
    spread = jnp.mean(center * center, -1, keepdims=True)
    normal = center * lax.rsqrt(spread + EPSILON) * gain_ref[...] + shift_ref[...]
    out_ref[...] = normal
    low_ref[...] = normal.astype(bfloat)


def norm_forward(kept, arrived, state, bias, gain, shift):
    shape = state.shape
    return run_whole(
        norm_forward_kernel,
        "norm_forward",
        [(shape, single), (shape, single), (shape, bfloat)],
        kept.reshape(shape),
        arrived.reshape(shape),
        state,
        row(bias),
        row(gain),
        row(shift),
    )


def norm_backward_kernel(count, *refs):
    hidden_ref, gain_ref, out_ref, low_ref, sums_ref = refs[count:]
    upstream = refs[0][...].astype(single)
    for ref in refs[1:count]:
        upstream = upstream + ref[...].astype(single)
    hidden = hidden_ref[...]
    center = hidden - jnp.mean(hidden, -1, keepdims=True)
    spread = jnp.mean(center * center, -1, keepdims=True)
    inverse = lax.rsqrt(spread + EPSILON)
    normal = center * inverse
    scaled = upstream * gain_ref[...]
    delta = inverse * (
        scaled
        - jnp.mean(scaled, -1, keepdims=True)
        - normal * jnp.mean(scaled * normal, -1, keepdims=True)
    )
    low = delta.astype(bfloat)
    out_ref[...] = delta
    low_ref[...] = low
    sums_ref[0:1, :] = jnp.sum(low.astype(single), 0, keepdims=True)
    sums_ref[1:2, :] = jnp.sum(upstream * normal, 0, keepdims=True)
    sums_ref[2:3, :] = jnp.sum(upstream, 0, keepdims=True)


def norm_backward(parts, hidden, gain):
    shape = hidden.shape
    return run_whole(
        functools.partial(norm_backward_kernel, len(parts)),
        "norm_backward",
        [(shape, single), (shape, bfloat), ((3, shape[1]), single)],
        *(part.reshape(shape) for part in parts),
        hidden,
        row(gain),
    )


def erf_gelu(value):
    phi = 0.5 * (1.0 + lax.erf(value * 0.7071067811865476))
    return value * phi, phi


def join(pieces, full_ref):
    rows = pieces[0].shape[0]
    for index, piece in enumerate(pieces):
        full_ref[index * rows : (index + 1) * rows, :] = piece[...]


def feed_forward_kernel(count, *refs):
    expand_ref, bias_ref, shrink_ref, full_ref, hidden_ref, act_ref, sent_ref, kept_ref = refs[count:]
    join(refs[:count], full_ref)
    half = sent_ref.shape[0]
    for index in (1, 0):
        part = slice(index * half, (index + 1) * half)
        hidden = matmul(full_ref[part, :], expand_ref[...]) + bias_ref[...]
        hidden_ref[part, :] = hidden
        act = erf_gelu(hidden)[0].astype(bfloat)
        act_ref[part, :] = act
        out = matmul(act, shrink_ref[...])
        if index == 0:
            kept_ref[...] = out
        else:
            sent_ref[...] = out.astype(bfloat)


def feed_forward(pieces, expand, bias, shrink):
    rows, width = len(pieces) * pieces[0].shape[0], pieces[0].shape[1]
    hidden = expand.shape[1]
    return run_whole(
        functools.partial(feed_forward_kernel, len(pieces)),
        "feed_forward",
        [
            ((rows, width), bfloat),
            ((rows, hidden), single),
            ((rows, hidden), bfloat),
            ((rows // 2, width), bfloat),
            ((rows // 2, width), single),
        ],
        *pieces,
        expand,
        row(bias),
        shrink,
    )


def feed_backward_kernel(count, *refs):
    expand_ref, shrink_ref, hidden_ref, full_ref, delta_ref, sums_ref, sent_ref, kept_ref = refs[count:]
    join(refs[:count], full_ref)
    half = sent_ref.shape[0]
    sums = jnp.zeros(sums_ref.shape, single)
    for index in (1, 0):
        part = slice(index * half, (index + 1) * half)
        upstream = outer_rows(full_ref[part, :], shrink_ref[...])
        hidden = hidden_ref[part, :]
        slope = erf_gelu(hidden)[1] + hidden * jnp.exp(-0.5 * hidden * hidden) * 0.3989422804014327
        delta = (upstream * slope).astype(bfloat)
        delta_ref[part, :] = delta
        sums = sums + jnp.sum(delta.astype(single), 0, keepdims=True)
        out = outer_rows(delta, expand_ref[...])
        if index == 0:
            kept_ref[...] = out
        else:
            sent_ref[...] = out.astype(bfloat)
    sums_ref[...] = sums


def feed_backward(pieces, expand, shrink, hidden):
    rows, width = len(pieces) * pieces[0].shape[0], pieces[0].shape[1]
    return run_whole(
        functools.partial(feed_backward_kernel, len(pieces)),
        "feed_backward",
        [
            ((rows, width), bfloat),
            (hidden.shape, bfloat),
            ((1, hidden.shape[1]), single),
            ((rows // 2, width), bfloat),
            ((rows // 2, width), single),
        ],
        *pieces,
        expand,
        shrink,
        hidden,
    )


def project_kernel(count, transposed, *refs):
    weight_ref, bias_ref, full_ref, out_ref = refs[count:]
    join(refs[:count], full_ref)
    out = (outer_rows if transposed else matmul)(full_ref[...], weight_ref[...])
    out_ref[...] = (out + bias_ref[...]).astype(bfloat)


def project(pieces, weight, bias, transposed=False):
    rows, width = len(pieces) * pieces[0].shape[0], pieces[0].shape[1]
    return run_whole(
        functools.partial(project_kernel, len(pieces), transposed),
        "project",
        [((rows, width), bfloat), ((rows, bias.shape[0]), bfloat)],
        *pieces,
        weight,
        row(bias),
    )


def halves_kernel(count, transposed, *refs):
    lefts, weights, (sent_ref, kept_ref) = refs[:count], refs[count : 2 * count], refs[2 * count :]
    half = sent_ref.shape[0]
    product = outer_rows if transposed else matmul
    for part, out in ((slice(half, 2 * half), sent_ref), (slice(0, half), kept_ref)):
        total = product(lefts[0][part, :], weights[0][...])
        for left, weight in zip(lefts[1:], weights[1:]):
            total = total + product(left[part, :], weight[...])
        out[...] = total.astype(out.dtype)


def product_halves(lefts, weights, transposed=False):
    half = lefts[0].shape[0] // 2
    width = weights[0].shape[0] if transposed else weights[0].shape[1]
    return run_whole(
        functools.partial(halves_kernel, len(lefts), transposed),
        "product_halves",
        [((half, width), bfloat), ((half, width), single)],
        *lefts,
        *weights,
    )


def add_halves_kernel(kept_ref, arrived_ref, sent_ref, left_ref):
    half = kept_ref.shape[0] // 2
    sent_ref[...] = (kept_ref[half:, :].astype(single) + arrived_ref[half:, :].astype(single)).astype(bfloat)
    left_ref[...] = kept_ref[:half, :].astype(single) + arrived_ref[:half, :].astype(single)


def add_halves(kept, arrived):
    half, width = kept.shape[0] // 2, kept.shape[1]
    return run_whole(
        add_halves_kernel,
        "add_halves",
        [((half, width), bfloat), ((half, width), single)],
        kept,
        arrived,
    )


def add_columns_kernel(kept_ref, arrived_ref, sent_ref, left_ref):
    half = sent_ref.shape[1]
    total = kept_ref[...].astype(single) + arrived_ref[...].astype(single)
    sent_ref[...] = total[:, half:].astype(bfloat)
    left_ref[...] = total[:, :half].astype(bfloat)


def add_columns(kept, arrived):
    rows, width = kept.shape
    block = rows
    for count in (8, 7, 6, 5, 4, 3, 2):
        if rows % (16 * count) == 0:
            block = rows // count
            break
    whole = pl.BlockSpec((block, width), lambda i: (i, 0))
    half = pl.BlockSpec((block, width // 2), lambda i: (i, 0))
    return pl.pallas_call(
        add_columns_kernel,
        grid=(rows // block,),
        in_specs=[whole, whole],
        out_specs=[half, half],
        out_shape=[jax.ShapeDtypeStruct((rows, width // 2), bfloat)] * 2,
        cost_estimate=BRIEF,
        name="add_columns",
    )(kept, arrived)


def bin_rows_kernel(bins_ref, value_ref, sent_ref, kept_ref, sums):
    sums[...] = jnp.zeros_like(sums)
    for slot in range(value_ref.shape[0]):
        sums[bins_ref[slot]] += value_ref[slot]
    half = sent_ref.shape[0]
    sent_ref[...] = sums[half:].astype(bfloat)
    kept_ref[...] = sums[:half]


def bin_rows(value, bins, count):
    shape = (count // 2,) + value.shape[1:]
    return pl.pallas_call(
        bin_rows_kernel,
        in_specs=[pl.BlockSpec(memory_space=pltpu.SMEM), VMEM],
        out_specs=[VMEM, VMEM],
        out_shape=[jax.ShapeDtypeStruct(shape, bfloat), jax.ShapeDtypeStruct(shape, single)],
        scratch_shapes=[pltpu.VMEM((count,) + value.shape[1:], single)],
        compiler_params=pltpu.CompilerParams(vmem_limit_bytes=56 * 1024 * 1024),
        cost_estimate=BRIEF,
        name="bin_rows",
    )(bins, value)


def vocab_tile(vocab_share):
    for tile in (1792, 896, 512, 256, 128):
        if vocab_share % tile == 0:
            return tile
    return vocab_share


def vocab_forward_kernel(state_ref, table_ref, label_ref, weight_ref, sum_ref, mixed_ref, tops_ref, top):
    step = pl.program_id(0)
    rows = state_ref.shape[0]
    tile = table_ref.shape[0]
    block = min(rows, 1024)

    @pl.when(step == 0)
    def start():
        top[...] = jnp.full_like(top, -jnp.inf)
        sum_ref[...] = jnp.zeros_like(sum_ref)
        mixed_ref[...] = jnp.zeros_like(mixed_ref)
        tops_ref[...] = jnp.zeros_like(tops_ref)

    repeat = lambda value, count: jnp.concatenate([value] * count, 1) if count > 1 else value
    spans = tile // LANES
    for index in range(rows // block):
        part = pl.ds(index * block, block)
        logits = outer_rows(state_ref[part, :], table_ref[...])
        old = top[part, :]
        new = jnp.maximum(old, jnp.max(logits, -1, keepdims=True))
        lanes = lax.broadcasted_iota(jnp.int32, new.shape, 1)
        offset = label_ref[part, :] - step * tile
        shrink = jnp.exp(old - new)
        top[part, :] = new
        tops_ref[part, :] = jnp.where(lanes == step, new, tops_ref[part, :])
        sums = sum_ref[part, :] * shrink
        low = []
        for span in range(spans):
            weights = jnp.exp(logits[:, span * LANES : (span + 1) * LANES] - new)
            weights = jnp.where(lanes + span * LANES == offset, 0.0, weights)
            sums = sums + weights
            low.append(weights.astype(bfloat))
        sum_ref[part, :] = sums
        low = jnp.concatenate(low, 1)
        weight_ref[part, :] = low
        mixed_ref[part, :] = mixed_ref[part, :] * repeat(shrink, mixed_ref.shape[1] // LANES) + matmul(
            low, table_ref[...]
        )


def vocab_forward(states, table, label):
    rows, width = states.shape
    entries = table.shape[0]
    tile = vocab_tile(entries)
    whole = lambda *shape: pl.BlockSpec(shape, lambda i: (0,) * len(shape))
    return pl.pallas_call(
        vocab_forward_kernel,
        grid=(entries // tile,),
        in_specs=[
            whole(rows, width),
            pl.BlockSpec((tile, width), lambda i: (i, 0)),
            whole(rows, LANES),
        ],
        out_specs=[
            pl.BlockSpec((rows, tile), lambda i: (0, i)),
            whole(rows, LANES),
            whole(rows, width),
            whole(rows, LANES),
        ],
        out_shape=[
            jax.ShapeDtypeStruct((rows, entries), bfloat),
            jax.ShapeDtypeStruct((rows, LANES), single),
            jax.ShapeDtypeStruct((rows, width), single),
            jax.ShapeDtypeStruct((rows, LANES), single),
        ],
        scratch_shapes=[pltpu.VMEM((rows, LANES), single)],
        compiler_params=pltpu.CompilerParams(
            dimension_semantics=("arbitrary",), vmem_limit_bytes=56 * 1024 * 1024
        ),
        cost_estimate=BRIEF,
        name="vocab_forward",
    )(states, table, label)


def vocab_slope_kernel(first, ratio, order_ref, weight_ref, factor_ref, label_ref, patch_ref, state_ref, sent_ref, kept_ref, moved):
    step = pl.program_id(0)
    tile = weight_ref.shape[1]
    width = state_ref.shape[1]
    blocks = order_ref.shape[0]
    span = width // blocks

    @pl.when(step == 0)
    def start():
        for place in range(blocks):
            source = pl.multiple_of(order_ref[place] * span, span)
            moved[:, place * span : (place + 1) * span] = state_ref[:, pl.ds(source, span)]

    here = step + first
    factors = factor_ref[...]
    lanes = lax.broadcasted_iota(jnp.int32, factors.shape, 1)
    factor = jnp.sum(jnp.where(lanes == here // ratio, factors, 0.0), -1, keepdims=True)
    columns = lax.broadcasted_iota(jnp.int32, weight_ref.shape, 1) + here * tile
    delta = jnp.where(
        columns == label_ref[...], patch_ref[...], weight_ref[...].astype(single) * factor
    ).astype(bfloat)
    half = width // 2
    sent_ref[...] = inner_rows(delta, moved[:, half:]).astype(bfloat)
    kept_ref[...] = inner_rows(delta, moved[:, :half]).astype(bfloat)


def vocab_slope(weights, factors, label, patch, states, order, first, count, tile):
    rows, width = states.shape
    whole = lambda *shape: pl.BlockSpec(shape, lambda i, o: (0,) * len(shape))
    half = pl.BlockSpec((tile, width // 2), lambda i, o: (i, 0))
    return pl.pallas_call(
        functools.partial(vocab_slope_kernel, first, vocab_tile(weights.shape[1]) // tile),
        grid_spec=pltpu.PrefetchScalarGridSpec(
            num_scalar_prefetch=1,
            grid=(count,),
            in_specs=[
                pl.BlockSpec((rows, tile), lambda i, o: (0, i + first)),
                whole(rows, LANES),
                whole(rows, 1),
                whole(rows, 1),
                whole(rows, width),
            ],
            out_specs=[half, half],
            scratch_shapes=[pltpu.VMEM((rows, width), bfloat)],
        ),
        out_shape=[jax.ShapeDtypeStruct((count * tile, width // 2), bfloat)] * 2,
        compiler_params=pltpu.CompilerParams(
            dimension_semantics=("arbitrary",), vmem_limit_bytes=56 * 1024 * 1024
        ),
        cost_estimate=BRIEF,
        name="vocab_slope",
    )(order, weights, factors, label, patch, states)


def slope_group_kernel(count, order_ref, *refs):
    lefts, rights = refs[:count], refs[count : 2 * count]
    sent_ref, kept_ref, moved = refs[2 * count :]
    blocks = order_ref.shape[0]
    width = rights[0].shape[1]
    span, half = width // blocks, width // 2
    base = 0
    for index in range(count):
        rows, entries = lefts[index].shape
        if index == 0 or rights[index] is not rights[index - 1]:
            for place in range(blocks):
                source = pl.multiple_of(order_ref[place] * span, span)
                moved[:rows, place * span : (place + 1) * span] = rights[index][:, pl.ds(source, span)]
        right = moved[:rows, :]
        left = lefts[index][...]
        sent_ref[base : base + entries, :] = inner_rows(left, right[:, half:]).astype(bfloat)
        kept_ref[base : base + entries, :] = inner_rows(left, right[:, :half]).astype(bfloat)
        base += entries


def slope_group(pairs, order):
    width = pairs[0][1].shape[1]
    total = sum(left.shape[1] for left, right in pairs)
    rows = max(left.shape[0] for left, right in pairs)
    lefts = [left for left, right in pairs]
    rights = [right for left, right in pairs]
    whole = pl.BlockSpec(memory_space=pltpu.VMEM)
    return pl.pallas_call(
        functools.partial(slope_group_kernel, len(pairs)),
        in_specs=[pl.BlockSpec(memory_space=pltpu.SMEM)] + [whole] * (2 * len(pairs)),
        out_specs=[whole, whole],
        out_shape=[jax.ShapeDtypeStruct((total, width // 2), bfloat)] * 2,
        scratch_shapes=[pltpu.VMEM((rows, width), bfloat)],
        compiler_params=pltpu.CompilerParams(vmem_limit_bytes=56 * 1024 * 1024),
        cost_estimate=BRIEF,
        name="slope_group",
    )(order, *lefts, *rights)


def head_weights(causal, places, query, address, lanes, head):
    own = (lanes // HD) == head
    scores = outer_rows(jnp.where(own, query, jnp.zeros_like(query)), address) * 0.125
    if causal:
        scores = jnp.where(places[0][:, :1] >= places[1][:1, :], scores, -1000000000.0)
    expo = jnp.exp(scores - jnp.max(scores, -1, keepdims=True))
    return own, expo / jnp.sum(expo, -1, keepdims=True)


def attend_forward_kernel(causal, bins_ref, stores_ref, query_ref, address_ref, content_ref, *refs):
    mixed_ref = refs[-1]
    places = [ref[...] for ref in refs[:-1]]
    length, width = query_ref.shape[1:]
    for pair in range(width // LANES):
        part = slice(pair * LANES, (pair + 1) * LANES)
        query, address, content = query_ref[0, :, part], address_ref[0, :, part], content_ref[0, :, part]
        lanes = lax.broadcasted_iota(jnp.int32, query.shape, 1)
        total = jnp.zeros(query.shape, single)
        for head in range(LANES // HD):
            own, weights = head_weights(causal, places, query, address, lanes, head)
            total = jnp.where(own, matmul(weights.astype(bfloat), content), total)
        shape = (mixed_ref.shape[0], mixed_ref.shape[2], LANES)
        mixed_ref[:, 0, :, part] = total.astype(bfloat).reshape(shape)


def attend_forward(queries, addresses, contents, bins, stores, parts, places=()):
    count = bins.shape[0]
    length, width = queries.shape[1:]
    stored = addresses.shape[1]
    return pl.pallas_call(
        functools.partial(attend_forward_kernel, bool(places)),
        grid_spec=pltpu.PrefetchScalarGridSpec(
            num_scalar_prefetch=2,
            grid=(count,),
            in_specs=[
                pl.BlockSpec((1, length, width), lambda i, b, s: (b[i], 0, 0)),
                pl.BlockSpec((1, stored, width), lambda i, b, s: (s[i], 0, 0)),
                pl.BlockSpec((1, stored, width), lambda i, b, s: (s[i], 0, 0)),
            ]
            + [pl.BlockSpec(place.shape, lambda i, b, s: (0, 0)) for place in places],
            out_specs=pl.BlockSpec((parts, 1, length // parts, width), lambda i, b, s: (0, i, 0, 0)),
        ),
        out_shape=jax.ShapeDtypeStruct((parts, count, length // parts, width), bfloat),
        compiler_params=pltpu.CompilerParams(
            dimension_semantics=("arbitrary",), vmem_limit_bytes=32 * 1024 * 1024
        ),
        cost_estimate=BRIEF,
        name="attend_forward",
    )(bins, stores, queries, addresses, contents, *places)


def attend_backward_kernel(
    causal, bins_ref, stores_ref, sums_ref, query_ref, address_ref, content_ref, upstream_ref, *refs
):
    query_out, address_out, content_out, query_sum, address_sum, content_sum = refs[-6:]
    places = [ref[...] for ref in refs[:-6]]
    step = pl.program_id(0)
    length, width = query_ref.shape[1:]

    @pl.when(step == 0)
    def start():
        query_sum[...] = jnp.zeros_like(query_sum)
        address_sum[...] = jnp.zeros_like(address_sum)
        content_sum[...] = jnp.zeros_like(content_sum)

    for pair in range(width // LANES):
        part = slice(pair * LANES, (pair + 1) * LANES)
        query, address, content = query_ref[0, :, part], address_ref[0, :, part], content_ref[0, :, part]
        upstream = upstream_ref[:, 0, :, part].reshape(length, LANES)
        lanes = lax.broadcasted_iota(jnp.int32, query.shape, 1)
        query_delta = jnp.zeros(query.shape, single)
        address_delta = jnp.zeros(address.shape, single)
        content_delta = jnp.zeros(address.shape, single)
        for head in range(LANES // HD):
            own, weights = head_weights(causal, places, query, address, lanes, head)
            weight_delta = outer_rows(jnp.where(own, upstream, jnp.zeros_like(upstream)), content)
            score_delta = (
                weights * (weight_delta - jnp.sum(weights * weight_delta, -1, keepdims=True))
            ).astype(bfloat)
            query_delta = jnp.where(own, matmul(score_delta, address), query_delta)
            address_delta = jnp.where(own, inner_rows(score_delta, query), address_delta)
            content_delta = jnp.where(own, inner_rows(weights.astype(bfloat), upstream), content_delta)
        query_sum[sums_ref[step], :, part] += query_delta * 0.125
        address_sum[stores_ref[step], :, part] += address_delta * 0.125
        content_sum[stores_ref[step], :, part] += content_delta

    @pl.when(step == pl.num_programs(0) - 1)
    def finish():
        query_out[...] = query_sum[...].astype(bfloat)
        address_out[...] = address_sum[...].astype(bfloat)
        content_out[...] = content_sum[...].astype(bfloat)


def attend_backward(queries, addresses, contents, upstream, bins, stores, sums, places=()):
    count = bins.shape[0]
    length, width = queries.shape[1:]
    stored = addresses.shape[1]
    whole = lambda shape: pl.BlockSpec(shape, lambda i, b, s, t: (0,) * len(shape))
    return pl.pallas_call(
        functools.partial(attend_backward_kernel, bool(places)),
        grid_spec=pltpu.PrefetchScalarGridSpec(
            num_scalar_prefetch=3,
            grid=(count,),
            in_specs=[
                pl.BlockSpec((1, length, width), lambda i, b, s, t: (b[i], 0, 0)),
                pl.BlockSpec((1, stored, width), lambda i, b, s, t: (s[i], 0, 0)),
                pl.BlockSpec((1, stored, width), lambda i, b, s, t: (s[i], 0, 0)),
                pl.BlockSpec((upstream.shape[0], 1) + upstream.shape[2:], lambda i, b, s, t: (0, i, 0, 0)),
            ]
            + [whole(place.shape) for place in places],
            out_specs=[whole(queries.shape), whole(addresses.shape), whole(addresses.shape)],
            scratch_shapes=[
                pltpu.VMEM(queries.shape, single),
                pltpu.VMEM(addresses.shape, single),
                pltpu.VMEM(addresses.shape, single),
            ],
        ),
        out_shape=[
            jax.ShapeDtypeStruct(queries.shape, bfloat),
            jax.ShapeDtypeStruct(addresses.shape, bfloat),
            jax.ShapeDtypeStruct(addresses.shape, bfloat),
        ],
        compiler_params=pltpu.CompilerParams(
            dimension_semantics=("arbitrary",), vmem_limit_bytes=56 * 1024 * 1024
        ),
        cost_estimate=BRIEF,
        name="attend_backward",
    )(bins, stores, sums, queries, addresses, contents, upstream, *places)


def pick_kernel(bins_ref, value_ref, out_ref):
    out_ref[...] = value_ref[...]


def pick(value, bins):
    block = (1,) + value.shape[1:]
    return pl.pallas_call(
        pick_kernel,
        grid_spec=pltpu.PrefetchScalarGridSpec(
            num_scalar_prefetch=1,
            grid=(bins.shape[0],),
            in_specs=[pl.BlockSpec(block, lambda i, b: (b[i], 0, 0))],
            out_specs=pl.BlockSpec(block, lambda i, b: (i, 0, 0)),
        ),
        out_shape=jax.ShapeDtypeStruct(bins.shape + value.shape[1:], value.dtype),
        name="pick",
    )(bins, value)


def finish_kernel(count, *refs):
    base = 0
    for index in range(count):
        rows = refs[index].shape[0]
        refs[-1][base : base + rows, :] = refs[index][...].astype(single) + refs[count + index][
            ...
        ].astype(single)
        base += rows


def finish_sums(kept, arrived):
    total = sum(part.shape[0] for part in kept)
    whole = pl.BlockSpec(memory_space=pltpu.VMEM)
    return pl.pallas_call(
        functools.partial(finish_kernel, len(kept)),
        in_specs=[whole] * (2 * len(kept)),
        out_specs=whole,
        out_shape=jax.ShapeDtypeStruct((total, kept[0].shape[1]), single),
        compiler_params=pltpu.CompilerParams(vmem_limit_bytes=40 * 1024 * 1024),
        name="finish_sums",
    )(*kept, *arrived)


def marginal_objective(seq_values, doc_scores, member, length):
    joint = doc_scores + seq_values / length
    masked = jnp.where(member, joint[None, :], -1e30)
    top = jnp.max(masked, 1, keepdims=True)
    unscaled = jnp.where(member, jnp.exp(masked - top), 0.0)
    total = jnp.sum(unscaled, 1, keepdims=True)
    marginal = top[:, 0] + jnp.log(total[:, 0])
    posterior = unscaled / total
    entropy = -jnp.sum(jnp.where(member, posterior * (joint[None, :] - marginal[:, None]), 0.0), 1)
    return jnp.mean(-marginal + ENTROPY_WEIGHT * entropy)


def on_device(
    dp,
    mp,
    targets,
    labels,
    passages,
    slot_question,
    slot_passage,
    score_table,
    score_index,
    query_weight,
    query_bias,
    key_weight,
    value_weight,
    value_bias,
    output_weight,
    output_bias,
    first_gain,
    first_shift,
    probe_weight,
    probe_bias,
    address_weight,
    content_weight,
    content_bias,
    merged_weight,
    merged_bias,
    second_gain,
    second_shift,
    expand_weight,
    expand_bias,
    shrink_weight,
    shrink_bias,
    third_gain,
    third_shift,
    embedding,
):
    group = lax.axis_index("dp")
    member_index = lax.axis_index("mp")
    own_questions, length, width = targets.shape
    questions = own_questions * dp
    pair_count = slot_passage.shape[0]
    store_count, passage_length = (passages.shape[0], passages.shape[1])
    vocab_share = embedding.shape[0]
    local_width = query_weight.shape[1]
    quarter = length // mp
    assert own_questions == 1

    token = [score_table[0]]

    def through(*values):
        values = tie(*values, token[0])
        token[0] = values[-1]
        return values[:-1] if len(values) > 2 else values[0]

    mp_order = bits_of(mp)[::-1]
    mp_table = relative_of(mp_order)
    dp_bits = bits_of(dp)
    dp_order = dp_bits[::-1]
    dp_table = relative_of(dp_order)

    def to_own(rows, count):
        natural = rows.reshape((count, mp, quarter) + rows.shape[2:])
        return jnp.moveaxis(xor_take(mp_table, member_index, natural, 1), 1, 0)

    def to_natural(rows, count):
        shaped = rows.reshape((mp, count, quarter) + rows.shape[1:])
        return jnp.moveaxis(natural_order(mp_table, member_index, shaped, 0), 0, 1)

    def mp_scatter_steps(halves):
        assert len(mp_order) == 2
        sent, kept = through(*halves)
        arrived = swap(sent, "mp", mp, mp_order[1])
        yield None
        sent, kept = through(*add_halves(kept, through(arrived)))
        arrived = swap(sent, "mp", mp, mp_order[0])
        yield None
        yield kept, through(arrived)

    def mp_gather_steps(own):
        own = through(own)
        held = [own, swap(own, "mp", mp, mp_order[0]), swap(own, "mp", mp, mp_order[1])]
        yield None
        held[1] = through(held[1])
        held.append(swap(held[1], "mp", mp, mp_order[1]))
        yield None
        yield through(*held)

    def last(steps):
        for value in steps:
            pass
        return value

    my_questions = lax.dynamic_slice_in_dim(slot_question, group * pair_count, pair_count)
    every = jnp.arange(own_questions, dtype=jnp.int32)
    quarters = member_index ^ jnp.asarray(mp_table, jnp.int32)
    place = (
        quarters[:, None] * quarter + jnp.arange(quarter, dtype=jnp.int32)[None, :]
    ).reshape(length)
    places_of = (
        jnp.broadcast_to(place[:, None], (length, LANES)),
        jnp.broadcast_to(place[None, :], (8, length)),
    )
    inputs = to_own(targets, own_questions)

    def by_question(rows):
        return jnp.moveaxis(rows.reshape(mp, own_questions, quarter, -1), 0, 1).reshape(
            own_questions, length, -1
        )

    inputs = inputs.reshape(-1, width)
    self_queries = by_question((matmul(inputs, query_weight) + query_bias).astype(bfloat))
    self_addresses = by_question(matmul(inputs, key_weight).astype(bfloat))
    self_contents = by_question((matmul(inputs, value_weight) + value_bias).astype(bfloat))
    self_flat = attend_forward(
        self_queries, self_addresses, self_contents, every, every, mp, places_of
    ).reshape(-1, local_width)
    kept, arrived = last(mp_scatter_steps(product_halves([self_flat], [output_weight])))
    first_in, first_norm, first_low = norm_forward(
        kept, arrived, inputs[:quarter], output_bias, first_gain, first_shift
    )
    first_full, probe_own = project(last(mp_gather_steps(first_low)), probe_weight, probe_bias)
    probe_own = by_question(probe_own)

    def where_slots(order):
        spots = jnp.asarray(places(relative_of(order)), jnp.int32)
        return spots[group ^ (my_questions // own_questions)] * own_questions + (
            my_questions % own_questions
        )

    probe_order = dp_bits[::-1]
    first_order = dp_bits[:1] + dp_bits[:0:-1]
    probe_bins = where_slots(probe_order)
    first_bins = where_slots(first_order)
    probe_all, first_all = gather_both(
        (probe_own, first_low.reshape(own_questions, quarter, width)),
        "dp",
        dp,
        (probe_order, first_order),
    )
    probe_all = probe_all.reshape(questions, length, local_width)
    first_all = first_all.reshape(questions, quarter, width)
    passage_rows = passages.reshape(-1, width)
    stored_addresses = matmul(passage_rows, address_weight).astype(bfloat)
    stored_contents = (matmul(passage_rows, content_weight) + content_bias).astype(bfloat)
    stored_addresses = stored_addresses.reshape(store_count, passage_length, local_width)
    stored_contents = stored_contents.reshape(store_count, passage_length, local_width)
    pair_labels = to_own(jnp.take(labels, my_questions, axis=0, mode="clip"), pair_count).reshape(-1)
    local_index = pair_labels - member_index * vocab_share
    inside = (local_index >= 0) & (local_index < vocab_share)
    label_rows = jnp.take(embedding, jnp.clip(local_index, 0, vocab_share - 1), axis=0, mode="clip")
    probe_all, label_rows = lax.optimization_barrier((probe_all, label_rows))

    cross_flat = attend_forward(
        probe_all, stored_addresses, stored_contents, probe_bins, slot_passage, mp
    ).reshape(-1, local_width)
    first_slots = pick(first_all, first_bins).reshape(-1, width)
    kept, arrived = last(mp_scatter_steps(product_halves([cross_flat], [merged_weight])))
    second_in, second_norm, low = norm_forward(
        kept, arrived, first_slots, merged_bias, second_gain, second_shift
    )
    second_low, expanded, activated, sent, kept = feed_forward(
        last(mp_gather_steps(low)), expand_weight, expand_bias, shrink_weight
    )
    kept, arrived = last(mp_scatter_steps((sent, kept)))
    third_in, third_norm, low = norm_forward(
        kept, arrived, second_norm, shrink_bias, third_gain, third_shift
    )
    third_low = jnp.concatenate(last(mp_gather_steps(low)), 0)

    label_lanes = jnp.broadcast_to(local_index[:, None], (local_index.shape[0], LANES))
    entry_weights, entry_sums, entry_mix, entry_tops = vocab_forward(third_low, embedding, label_lanes)
    entry_tile = vocab_tile(vocab_share)
    local_top = entry_tops[:, vocab_share // entry_tile - 1]
    local_target = jnp.where(
        inside, jnp.sum(third_low.astype(single) * label_rows.astype(single), -1), 0.0
    )
    local_total = jnp.sum(entry_sums, -1) + jnp.where(inside, jnp.exp(local_target - local_top), 0.0)
    stats = jnp.stack([local_top, local_total, local_target]).reshape(3, mp, pair_count, quarter)
    for index, bit in reversed(list(enumerate(mp_order))):
        other = swap(stats, "mp", mp, bit)
        other = jnp.flip(
            other.reshape(3, mp >> (index + 1), 2, 1 << index, pair_count, quarter), 2
        ).reshape(stats.shape)
        high = jnp.maximum(stats[0], other[0])
        sums = stats[1] * jnp.exp(stats[0] - high) + other[1] * jnp.exp(other[0] - high)
        stats = jnp.stack([high, sums, stats[2] + other[2]])
    log_norm = (stats[0] + jnp.log(stats[1])).reshape(-1)
    target_logit = stats[2].reshape(-1)
    pair_likelihood = jnp.sum((target_logit - log_norm).reshape(mp, pair_count, quarter), -1)
    while pair_likelihood.shape[0] > 1:
        pair_likelihood = pair_likelihood[0::2] + pair_likelihood[1::2]
    every_likelihood = natural_order(
        dp_table, group, gather_blocks(pair_likelihood[0], "dp", dp, dp_order), 0
    ).reshape(-1)
    doc_scores = jnp.take(score_table, score_index)
    member = slot_question[None, :] == jnp.arange(questions, dtype=jnp.int32)[:, None]

    def scored(values_all):
        return marginal_objective(values_all, doc_scores, member, length)

    objective, pullback = jax.vjp(scored, every_likelihood)
    likelihood_delta = pullback(jnp.ones_like(objective) * (questions * length))[0]
    pair_delta = lax.dynamic_slice_in_dim(likelihood_delta, group * pair_count, pair_count)
    row_delta = jnp.broadcast_to(pair_delta[None, :, None], (mp, pair_count, quarter)).reshape(-1)
    surplus = row_delta * (1.0 - jnp.exp(target_logit - log_norm))
    factors = -row_delta[:, None] * jnp.exp(entry_tops - log_norm[:, None])
    third_part = (
        jnp.where(inside, surplus, 0.0)[:, None] * label_rows.astype(single)
        - (row_delta * jnp.exp(local_top - log_norm))[:, None] * entry_mix
    )

    fast = width % (dp * LANES) == 0

    def order_table(order):
        if not fast:
            return jnp.arange(width // LANES, dtype=jnp.int32)
        return group ^ jnp.asarray(relative_of(order), jnp.int32)

    token[0] = objective

    class ColumnSum:
        def __init__(self, halves, order):
            self.sent, self.kept = through(*halves)
            self.bits = order[::-1]
            self.arrived = None

        def send(self):
            if fast:
                self.sent = through(self.sent)
                self.arrived = swap(self.sent, "dp", dp, self.bits[0])
                self.bits = self.bits[1:]

        def step(self):
            if not fast or not self.bits:
                return
            self.arrived, self.kept = through(self.arrived, self.kept)
            half = self.kept.shape[1] // 2
            total = self.kept.astype(single) + self.arrived.astype(single)
            self.sent, self.kept = total[:, half:].astype(bfloat), total[:, :half].astype(bfloat)
            self.send()

        def wait(self):
            if fast:
                self.arrived = through(self.arrived)

    def finish(parts):
        if not fast:
            slopes = [
                lax.psum_scatter(
                    jnp.concatenate([part.kept, part.sent], 1), "dp", scatter_dimension=1, tiled=True
                )
                for part in parts
            ]
            return jnp.concatenate(slopes, 0).astype(single)
        assert not any(part.bits for part in parts)
        return finish_sums([part.kept for part in parts], [part.arrived for part in parts])

    order_a = dp_bits[::-1]
    order_b = order_a if dp < 4 else [dp_bits[-1], dp_bits[0]] + dp_bits[1:-1]
    slope_tile = entry_tile // 2 if entry_tile % (2 * LANES) == 0 else entry_tile
    tiles = vocab_share // slope_tile
    cuts = [tiles * i // 14 for i in (0, 3, 6, 10, 14)]
    def table_sum(index, order):
        halves = vocab_slope(
            entry_weights,
            through(factors),
            local_index[:, None],
            surplus[:, None],
            third_low,
            order_table(order),
            cuts[index],
            cuts[index + 1] - cuts[index],
            slope_tile,
        )
        return ColumnSum(halves, order)

    def group_sum(pairs, order):
        pairs = [(through(pairs[0][0]), pairs[0][1])] + pairs[1:]
        return ColumnSum(slope_group(pairs, order_table(order)), order)

    half = third_part.shape[0] // 2
    steps = mp_scatter_steps((third_part[half:].astype(bfloat), third_part[:half]))
    next(steps)
    sum_a1 = table_sum(0, order_a)
    sum_a1.send()
    next(steps)
    sum_b = table_sum(1, order_b)
    sum_b.send()
    third_back, feed_low, third_sums = norm_backward(next(steps), third_in, third_gain)
    steps = mp_gather_steps(feed_low)
    next(steps)
    sum_a2 = table_sum(2, order_a)
    sum_a2.send()
    next(steps)
    feed_delta, expanded_delta, bias_expand, sent, kept = feed_backward(
        next(steps), expand_weight, shrink_weight, expanded
    )
    steps = mp_scatter_steps((sent, kept))
    next(steps)
    next(steps)
    sum_a1.step()
    sum_f = group_sum([(activated, feed_delta), (expanded_delta, second_low)], order_b)
    second_back, recall_low, second_sums = norm_backward(
        next(steps) + (third_back,), second_in, second_gain
    )
    steps = mp_gather_steps(recall_low)
    next(steps)
    sum_b.step()
    sum_a3 = table_sum(3, order_a)
    next(steps)
    recall_delta, mixed_delta = project(
        next(steps), merged_weight, jnp.zeros((local_width,), single), True
    )
    probe_binned, address_delta, content_delta = attend_backward(
        probe_all,
        stored_addresses,
        stored_contents,
        mixed_delta.reshape(mp, pair_count, quarter, local_width),
        probe_bins,
        slot_passage,
        probe_bins,
    )
    address_delta = address_delta.reshape(-1, local_width)
    content_delta = content_delta.reshape(-1, local_width)

    half = questions // 2
    steps = scatter_both_steps(
        (
            (
                probe_binned[half:].reshape(-1, local_width),
                probe_binned[:half].reshape(-1, local_width),
            ),
            tuple(
                value.reshape(-1, width)
                for value in bin_rows(
                    second_back.reshape(pair_count, quarter, width), probe_bins, questions
                )
            ),
        ),
        "dp",
        dp,
        (probe_order, probe_order),
        through,
    )
    next(steps)
    sum_a1.step()
    sum_a2.step()
    sum_a3.send()
    sum_x = group_sum(
        [
            (cross_flat, recall_delta),
            (address_delta, passage_rows),
            (content_delta, passage_rows),
        ],
        order_b,
    )
    next(steps)
    sum_f.send()
    sum_b.step()
    sum_a1.wait()
    for unused in range(len(dp_bits) - 2):
        next(steps)
    sum_a2.step()
    sum_x.send()
    probe_parts, state_parts = next(steps)
    probe_flat = (
        probe_parts[0].astype(single) + probe_parts[1].astype(single)
    ).astype(bfloat)

    bias_content = jnp.sum(content_delta, 0, dtype=single)
    passages_slope = lax.psum(
        (outer_rows(address_delta, address_weight) + outer_rows(content_delta, content_weight)).astype(bfloat),
        "mp",
    ).astype(single).reshape(passages.shape)

    bias_probe = jnp.sum(probe_flat, 0, dtype=single)
    steps = mp_scatter_steps(product_halves([probe_flat], [probe_weight], True))
    next(steps)
    next(steps)
    sum_b.wait()
    first_back, self_low, first_sums = norm_backward(
        next(steps) + tuple(state_parts), first_in, first_gain
    )
    steps = mp_gather_steps(self_low)
    next(steps)
    sum_f.step()
    next(steps)
    self_delta, self_mixed_delta = project(
        next(steps), output_weight, jnp.zeros((local_width,), single), True
    )
    self_deltas = attend_backward(
        self_queries,
        self_addresses,
        self_contents,
        self_mixed_delta.reshape(mp, own_questions, quarter, local_width),
        every,
        every,
        every,
        places_of,
    )
    query_flat, key_flat, value_flat = (
        jnp.moveaxis(delta.reshape(own_questions, mp, quarter, local_width), 1, 0).reshape(
            -1, local_width
        )
        for delta in self_deltas
    )
    steps = mp_scatter_steps(
        product_halves(
            [query_flat, key_flat, value_flat], [query_weight, key_weight, value_weight], True
        )
    )
    shared = total_over(
        jnp.concatenate([first_sums, second_sums, third_sums], 0), "mp", mp, mp_order
    )
    bias_query = jnp.sum(query_flat, 0, dtype=single)
    bias_value = jnp.sum(value_flat, 0, dtype=single)
    quads = jnp.stack([bias_query, bias_value, bias_probe, bias_content])
    quads = quads.reshape(4, dp, local_width // dp).swapaxes(0, 1).reshape(1, width)
    vectors = jnp.concatenate([shared, bias_expand, quads, jnp.zeros((5, width), single)], 0)
    next(steps)
    sum_a3.step()
    next(steps)
    sum_s = group_sum(
        [
            (probe_flat, first_full),
            (self_flat, self_delta),
            (query_flat, inputs),
            (key_flat, inputs),
            (value_flat, inputs),
            (jnp.eye(16, dtype=bfloat), vectors.astype(bfloat)),
        ],
        order_a,
    )
    kept, arrived = next(steps)
    input_low = (kept + arrived.astype(single) + first_back).astype(bfloat)
    steps = mp_gather_steps(input_low)
    next(steps)
    sum_s.send()
    next(steps)
    targets_slope = to_natural(jnp.concatenate(next(steps), 0), own_questions)
    targets_slope = targets_slope.reshape(targets.shape).astype(single)

    sum_a2.wait()
    sum_x.step()
    sum_f.step()
    sum_a3.step()
    sum_s.step()
    sum_x.step()
    sum_s.step()
    sum_f.wait()
    sum_a3.wait()
    sum_x.wait()
    sum_s.wait()
    embedding_slope = finish([sum_a1, sum_b, sum_a2, sum_a3])
    feed_slopes = finish([sum_f])
    cross_slopes = finish([sum_x])
    self_slopes = finish([sum_s])
    hidden = expanded.shape[1]
    shrink_slope = feed_slopes[:hidden]
    expand_slope = feed_slopes[hidden:].T
    merged_slope = cross_slopes[:local_width]
    address_slope = cross_slopes[local_width : 2 * local_width].T
    content_slope = cross_slopes[2 * local_width :].T
    probe_slope = self_slopes[:local_width].T
    output_slope = self_slopes[local_width : 2 * local_width]
    query_slope = self_slopes[2 * local_width : 3 * local_width].T
    key_slope = self_slopes[3 * local_width : 4 * local_width].T
    value_slope = self_slopes[4 * local_width : 5 * local_width].T

    vectors = self_slopes[5 * local_width :]
    (
        bias_output,
        first_gain_slope,
        first_shift_slope,
        bias_merged,
        second_gain_slope,
        second_shift_slope,
        bias_shrink,
        third_gain_slope,
        third_shift_slope,
        bias_expand,
    ) = (vectors[i] for i in range(10))
    bias_query, bias_value, bias_probe, bias_content = vectors[10].reshape(4, local_width // dp)
    return (
        token[0],
        targets_slope,
        passages_slope,
        query_slope,
        bias_query,
        key_slope,
        value_slope,
        bias_value,
        output_slope,
        bias_output,
        first_gain_slope,
        first_shift_slope,
        probe_slope,
        bias_probe,
        address_slope,
        content_slope,
        bias_content,
        merged_slope,
        bias_merged,
        second_gain_slope,
        second_shift_slope,
        expand_slope,
        bias_expand,
        shrink_slope,
        bias_shrink,
        third_gain_slope,
        third_shift_slope,
        embedding_slope,
    )


def solution(mesh):
    return jax.shard_map(
        functools.partial(on_device, mesh.shape["dp"], mesh.shape["mp"]),
        mesh=mesh,
        in_specs=(
            P("dp", None, None),
            P(),
            P("dp", None, None),
            P(),
            P("dp"),
            P(),
            P(),
            P(None, "mp"),
            P("mp"),
            P(None, "mp"),
            P(None, "mp"),
            P("mp"),
            P("mp", None),
            P(),
            P(),
            P(),
            P(None, "mp"),
            P("mp"),
            P(None, "mp"),
            P(None, "mp"),
            P("mp"),
            P("mp", None),
            P(),
            P(),
            P(),
            P(None, "mp"),
            P("mp"),
            P("mp", None),
            P(),
            P(),
            P(),
            P("mp", None),
        ),
        out_specs=(
            P(),
            P("dp", None, None),
            P("dp", None, None),
            P("dp", "mp"),
            P(("mp", "dp")),
            P("dp", "mp"),
            P("dp", "mp"),
            P(("mp", "dp")),
            P("mp", "dp"),
            P("dp"),
            P("dp"),
            P("dp"),
            P("dp", "mp"),
            P(("mp", "dp")),
            P("dp", "mp"),
            P("dp", "mp"),
            P(("mp", "dp")),
            P("mp", "dp"),
            P("dp"),
            P("dp"),
            P("dp"),
            P("dp", "mp"),
            P(("mp", "dp")),
            P("mp", "dp"),
            P("dp"),
            P("dp"),
            P("dp"),
            P("mp", "dp"),
        ),
        check_vma=False,
    )
```

time: 1030 us -> 851 us (0.83)
  Pallas kernels: 0 us -> 266 us
  matrix products: 268 us -> 4.93 us
  local copies, waits for them, and re-layouts: 208 us -> 101 us
  other arithmetic: 165 us -> 69.6 us
  waiting for transfers between devices: 275 us -> 318 us
  starting transfers between devices: 78.8 us -> 66.3 us
    pallas_call x0 -> x44, Pallas kernels: none -> 266 us  [the longest x26 85.9 us: run_whole(): pl.pallas_call(kernel, in_specs=[VMEM] * len(operands), out_specs=[VMEM]...]
    dot_general x68 -> x0, matrix products: 159 us -> none  [the longest x56 147 us: inner_rows(): lax.dot_general(left, right, (((0,), (0,)), ((), ())), preferred_element_...]
    gather x23 -> x2, local copies, waits for them, and re-layouts: 58.2 us -> 2.19 us  [xor_take(): jnp.take(array, me ^ jnp.asarray(table, jnp.int32), axis=axis, mode='clip')]
    dot_general x11 -> x5, matrix products: 55.2 us -> 3.02 us  [matmul(): return jnp.dot(left, right, preferred_element_type=single)]
    dot_general x11 -> x2, matrix products: 53.8 us -> 1.91 us  [outer_rows(): lax.dot_general(left, right, (((1,), (1,)), ((), ())), preferred_element_...]
    ppermute x71 -> x75, waiting for transfers between devices: 275 us -> 318 us  [swap(): return lax.ppermute(value, axis, [(i, i ^ bit) for i in range(count)])]
    convert_element_type x32 -> x15, other arithmetic: 50.1 us -> 8.5 us  [the longest x11 6.55 us: row(): return vector.reshape(1, -1).astype(single)]
    reduce_sum x18 -> x5, other arithmetic: 34.9 us -> 3.48 us  [the longest x1 1.25 us: on_device(): jnp.sum(entry_sums, -1)]
  transfers between devices with their start and end apart: 72 -> 76, of which waited for: 34 -> 39; matrix products, arithmetic and copies ran while one was open for 43% -> 13% of each run, Pallas kernels for 0% -> 19%
where the time goes in v2:
time: 851 us; the launch traced here: 843 us
  waiting for transfers between devices  318 us (37%)
  Pallas kernels  266 us (31%)
  local copies, waits for them, and re-layouts  101 us (12%)
  other arithmetic  69.6 us (8%)
  starting transfers between devices  66.3 us (8%)
  between operations  17.4 us (2%)
    ppermute x75, waiting for transfers between devices, swap(): return lax.ppermute(value, axis, [(i, i ^ bit) for i in range(count)])  318 us
    pallas_call x26, Pallas kernels, run_whole(): pl.pallas_call(kernel, in_specs=[VMEM] * len(operands), out_specs=[VMEM]...  85.9 us
    pallas_call x1, Pallas kernels, vocab_forward(): pl.pallas_call(vocab_forward_kernel, grid=(entries // tile,), in_specs=[w...  68.1 us
    ppermute x75, starting transfers between devices, swap(): return lax.ppermute(value, axis, [(i, i ^ bit) for i in range(count)])  66.2 us
    pallas_call x4, Pallas kernels, vocab_slope(): pl.pallas_call(functools.partial(vocab_slope_kernel, first, vocab_tile(we...  53.6 us
    unnamed x248, local copies, waits for them, and re-layouts  35.9 us
    another operation x16, other arithmetic  28.2 us
    pallas_call x3, Pallas kernels, slope_group(): pl.pallas_call(functools.partial(slope_group_kernel, len(pairs)), in_spec...  20.6 us
  transfers between devices with their start and end apart: 76, of which 39 were waited for; matrix products, arithmetic and copies ran while one was open for 13% of the time, Pallas kernels for 19%

profile of v2, /device:TPU:0, one launch (start us, length us, event | category | flops | bytes accessed | tf_op | source)
XLA Modules:
  0.0 843.4 jit_solution(16987456374110515319)
XLA Ops:
  26.9 3.7 collective-permute-done.1.arrived_ref
  35.0 3.8 collective-permute-done.2.refs_1_
  49.0 6.4 collective-permute-done.5
  58.8 4.0 collective-permute-start.7
  63.7 16.9 %gather_fusion.4 = bf16[1024,1024]{1,0:T(8,128)(2,1)S(1)} fusion(bf16[12544,1024]{1,0:T(8,128)(2,1)} %table_ref.1, s32[1024]{0:T(1024)S(1)} %broadcast_clamp_fusion), kind=kCustom, calls=%fused_computation.4 | custom fusion | bytes 4198400 | tf_op jit(solution)/shard_map/jit(_take)/gather | solution.py:900
  85.2 10.7 %collective-permute-done.10 = bf16[4,1,64,1024]{3,2,0,1:T(8,128)(2,1)S(1)} collective-permute-done((bf16[4,1,64,1024]{3,2,0,1:T(8,128)(2,1)S(1)}, bf16[4,1,64,1024]{3,2,0,1:T(8,128)(2,1)S(1)}, u32[]{:S(2)}, u32[]{:S(2)}) %collective-permute-start.10) | collective-permute-done | bytes 524320 | tf_op jit(solution)/shard_map/ppermute | solution.py:39
  98.2 5.1 attend_forward.3
  104.1 3.3 product_halves.5
  121.2 4.0 pick.1
  125.1 3.6 collective-permute-done.12.arrived_ref
  133.5 11.9 %collective-permute-done.13.refs_1_ = bf16[256,1024]{1,0:T(8,128)(2,1)S(1)} collective-permute-done((bf16[256,1024]{1,0:T(8,128)(2,1)}, bf16[256,1024]{1,0:T(8,128)(2,1)S(1)}, u32[]{:S(2)}, u32[]{:S(2)}) %collective-permute-start.13) | collective-permute-done | bytes 524320 | tf_op jit(solution)/shard_map/ppermute | solution.py:39
  148.0 9.7 %feed_forward.1 = (bf16[1024,1024]{1,0:T(8,128)(2,1)}, f32[1024,1024]{1,0:T(8,128)}, bf16[1024,1024]{1,0:T(8,128)(2,1)}, bf16[512,1024]{1,0:T(8,128)(2,1)}, f32[512,1024]{1,0:T(8,128)}) custom-call(bf16[256,1024]{1,0:T(8,128)(2,1)} %get-tuple-element.415.refs_0_, bf16[256,1024]{1,0:T(8,128)(2,1)} %copy-done.68, bf16[256,1024]{1,0:T(8,128)(2,1)} %copy-done.69, ...), custom_call_target="tpu_custom_call" | custom-call | tf_op jit(solution)/shard_map/feed_forward/pallas_call | solution.py:115
  168.1 10.9 %collective-permute-done.17.arrived_ref = bf16[256,1024]{1,0:T(8,128)(2,1)S(1)} collective-permute-done((bf16[256,1024]{1,0:T(8,128)(2,1)}, bf16[256,1024]{1,0:T(8,128)(2,1)S(1)}, u32[]{:S(2)}, u32[]{:S(2)}) %collective-permute-start.17) | collective-permute-done | bytes 524320 | tf_op jit(solution)/shard_map/ppermute | solution.py:39
  179.8 3.5 norm_forward.5
  184.7 12.0 %collective-permute-done.18 = bf16[256,1024]{1,0:T(8,128)(2,1)} collective-permute-done((bf16[256,1024]{1,0:T(8,128)(2,1)}, bf16[256,1024]{1,0:T(8,128)(2,1)}, u32[]{:S(2)}, u32[]{:S(2)}) %collective-permute-start.18) | collective-permute-done | bytes 524320 | tf_op jit(solution)/shard_map/ppermute | solution.py:39
  204.8 68.1 %vocab_forward.1 = (bf16[1024,12544]{1,0:T(8,128)(2,1)}, f32[1024,128]{1,0:T(8,128)}, f32[1024,1024]{1,0:T(8,128)}, f32[1024,128]{1,0:T(8,128)}) custom-call(bf16[1024,1024]{1,0:T(8,128)(2,1)} %copy-done.26, bf16[12544,1024]{1,0:T(8,128)(2,1)} %table_ref.1, s32[1024,128]{1,0:T(8,128)} %broadcast_in_dim.139.label_ref), custom_call_target="tpu_custom_call" | custom-call | tf_op jit(solution)/shard_map/vocab_forward/pallas_call | solution.py:445
  303.2 4.3 select_reduce_fusion
  313.5 12.1 %vocab_slope.4 = (bf16[2688,512]{1,0:T(8,128)(2,1)}, bf16[2688,512]{1,0:T(8,128)(2,1)}) custom-call(s32[8]{0:T(128)} %get-tuple-element.929.order_ref, bf16[1024,12544]{1,0:T(8,128)(2,1)} %get-tuple-element.437.weight_ref, f32[1024,128]{1,0:T(8,128)} %exponential_multiply_fusion.factor_ref, s32[1024,1]{1,0:T(8,128)} %copy-done.28, ...), custom_call_target="tpu_custom_call" | custom-call | tf_op jit(solution)/shard_map/vocab_slope/pallas_call | solution.py:504
  330.8 12.3 %vocab_slope.5 = (bf16[2688,512]{1,0:T(8,128)(2,1)}, bf16[2688,512]{1,0:T(8,128)(2,1)}) custom-call(s32[8]{0:T(128)} %get-tuple-element.928.order_ref, bf16[1024,12544]{1,0:T(8,128)(2,1)} %get-tuple-element.437.weight_ref, f32[1024,128]{1,0:T(8,128)} %exponential_multiply_fusion.factor_ref, s32[1024,1]{1,0:T(8,128)} %copy-done.28, ...), custom_call_target="tpu_custom_call" | custom-call | tf_op jit(solution)/shard_map/vocab_slope/pallas_call | solution.py:504
  345.3 3.7 norm_backward.3
  349.6 14.7 %vocab_slope.6 = (bf16[3584,512]{1,0:T(8,128)(2,1)}, bf16[3584,512]{1,0:T(8,128)(2,1)}) custom-call(s32[8]{0:T(128)} %get-tuple-element.929.order_ref, bf16[1024,12544]{1,0:T(8,128)(2,1)} %get-tuple-element.437.weight_ref, f32[1024,128]{1,0:T(8,128)} %exponential_multiply_fusion.factor_ref, s32[1024,1]{1,0:T(8,128)} %copy-done.28, ...), custom_call_target="tpu_custom_call" | custom-call | tf_op jit(solution)/shard_map/vocab_slope/pallas_call | solution.py:504
  367.2 11.1 %feed_backward.1 = (bf16[1024,1024]{1,0:T(8,128)(2,1)}, bf16[1024,1024]{1,0:T(8,128)(2,1)}, f32[1,1024]{1,0:T(1,128)}, bf16[512,1024]{1,0:T(8,128)(2,1)}, f32[512,1024]{1,0:T(8,128)}) custom-call(bf16[256,1024]{1,0:T(8,128)(2,1)} %get-tuple-element.475.refs_0_, bf16[256,1024]{1,0:T(8,128)(2,1)} %copy-done.57, bf16[256,1024]{1,0:T(8,128)(2,1)} %copy-done.58, ...), custom_call_target="tpu_custom_call" | custom-call | tf_op jit(solution)/shard_map/feed_backward/pallas_call | solution.py:115
  389.8 9.8 %slope_group.3 = (bf16[2048,512]{1,0:T(8,128)(2,1)}, bf16[2048,512]{1,0:T(8,128)(2,1)}) custom-call(s32[8]{0:T(128)} %get-tuple-element.928.order_ref, bf16[1024,1024]{1,0:T(8,128)(2,1)} %get-tuple-element.500.refs_0_, bf16[1024,1024]{1,0:T(8,128)(2,1)} %get-tuple-element.501.refs_1_, bf16[1024,1024]{1,0:T(8,128)(2,1)} %get-tuple-element.502.refs_2_, ...), custom_call_target="tpu_custom_call" | custom-call | tf_op jit(solution)/shard_map/slope_group/pallas_call | solution.py:555
  402.5 4.0 norm_backward.4
  407.6 34.0 %collective-permute-done.35 = bf16[2688,512]{1,0:T(8,128)(2,1)} collective-permute-done((bf16[2688,512]{1,0:T(8,128)(2,1)}, bf16[2688,512]{1,0:T(8,128)(2,1)}, u32[]{:S(2)}, u32[]{:S(2)}) %collective-permute-start.35) | collective-permute-done | bytes 2752544 | tf_op jit(solution)/shard_map/ppermute | solution.py:39
  444.8 14.5 %vocab_slope.7 = (bf16[3584,512]{1,0:T(8,128)(2,1)}, bf16[3584,512]{1,0:T(8,128)(2,1)}) custom-call(s32[8]{0:T(128)} %get-tuple-element.929.order_ref, bf16[1024,12544]{1,0:T(8,128)(2,1)} %get-tuple-element.437.weight_ref, f32[1024,128]{1,0:T(8,128)} %exponential_multiply_fusion.factor_ref, s32[1024,1]{1,0:T(8,128)} %copy-done.28, ...), custom_call_target="tpu_custom_call" | custom-call | tf_op jit(solution)/shard_map/vocab_slope/pallas_call | solution.py:504
  464.5 3.7 project.4
  468.3 13.1 %attend_backward.2 = (bf16[8,256,256]{2,1,0:T(8,128)(2,1)}, bf16[2,256,256]{2,1,0:T(8,128)(2,1)}, bf16[2,256,256]{2,1,0:T(8,128)(2,1)}) custom-call(s32[4]{0:T(128)} %copy-done.20, s32[4]{0:T(128)} %stores_ref.3, s32[4]{0:T(128)} %copy-done.20, bf16[8,256,256]{2,1,0:T(8,128)(2,1)} %copy-done.1, bf16[2,256,256]{2,1,0:T(8,128)(2,1)} %bitcast.194, ...), custom_call_target="tpu_custom_call" | custom-call | tf_op jit(solution)/shard_map/attend_backward/pallas_call | solution.py:665
  494.8 5.8 slope_group.4
  501.6 6.1 collective-permute-done.38.arrived_ref
  508.1 10.8 %collective-permute-done.39.arrived_ref = bf16[256,1024]{1,0:T(8,128)(2,1)S(1)} collective-permute-done((bf16[256,1024]{1,0:T(8,128)(2,1)}, bf16[256,1024]{1,0:T(8,128)(2,1)S(1)}, u32[]{:S(2)}, u32[]{:S(2)}) %collective-permute-start.39) | collective-permute-done | bytes 524320 | tf_op jit(solution)/shard_map/ppermute | solution.py:39
  529.0 21.2 %collective-permute-done.44.refs_4_ = bf16[2688,128]{1,0:T(8,128)(2,1)S(1)} collective-permute-done((bf16[2688,128]{1,0:T(8,128)(2,1)}, bf16[2688,128]{1,0:T(8,128)(2,1)S(1)}, u32[]{:S(2)}, u32[]{:S(2)}) %collective-permute-start.44) | collective-permute-done | bytes 688160 | tf_op jit(solution)/shard_map/ppermute | solution.py:39
  550.3 3.3 collective-permute-start.51
  553.6 12.5 %collective-permute-done.42.arrived_ref = bf16[512,256]{1,0:T(8,128)(2,1)S(1)} collective-permute-done((bf16[512,256]{1,0:T(8,128)(2,1)}, bf16[512,256]{1,0:T(8,128)(2,1)S(1)}, u32[]{:S(2)}, u32[]{:S(2)}) %collective-permute-start.42) | collective-permute-done | bytes 262176 | tf_op jit(solution)/shard_map/ppermute | solution.py:39
  566.1 5.6 collective-permute-done.43.arrived_ref
  582.1 41.8 %collective-permute-done.46 = bf16[256,256]{1,0:T(8,128)(2,1)S(1)} collective-permute-done((bf16[256,256]{1,0:T(8,128)(2,1)}, bf16[256,256]{1,0:T(8,128)(2,1)S(1)}, u32[]{:S(2)}, u32[]{:S(2)}) %collective-permute-start.46) | collective-permute-done | bytes 131104 | tf_op jit(solution)/shard_map/ppermute | solution.py:39
  634.9 3.7 collective-permute-done.50.refs_1_
  645.6 3.3 collective-permute-start.65
  661.5 4.3 attend_backward.3
  668.0 3.7 product_halves.7
  671.8 4.2 add_convert_fusion
  681.8 5.1 slope_group.5
  688.8 3.8 collective-permute-done.66
  707.0 38.6 %collective-permute-done.62 = bf16[3584,256]{1,0:T(8,128)(2,1)} collective-permute-done((bf16[3584,256]{1,0:T(8,128)(2,1)}, bf16[3584,256]{1,0:T(8,128)(2,1)}, u32[]{:S(2)}, u32[]{:S(2)}) %collective-permute-start.62) | collective-permute-done | bytes 1835040 | tf_op jit(solution)/shard_map/ppermute | solution.py:39
  758.5 17.7 %collective-permute-done.69 = bf16[1296,256]{1,0:T(8,128)(2,1)S(1)} collective-permute-done((bf16[1296,256]{1,0:T(8,128)(2,1)S(1)}, bf16[1296,256]{1,0:T(8,128)(2,1)S(1)}, u32[]{:S(2)}, u32[]{:S(2)}) %collective-permute-start.69) | collective-permute-done | bytes 663584 | tf_op jit(solution)/shard_map/ppermute | solution.py:39
  782.0 29.1 %collective-permute-done.73.refs_7_ = bf16[3584,128]{1,0:T(8,128)(2,1)} collective-permute-done((bf16[3584,128]{1,0:T(8,128)(2,1)}, bf16[3584,128]{1,0:T(8,128)(2,1)}, u32[]{:S(2)}, u32[]{:S(2)}) %collective-permute-start.73) | collective-permute-done | bytes 917536 | tf_op jit(solution)/shard_map/ppermute | solution.py:39
  811.1 4.2 collective-permute-done.72.refs_1_
  824.8 4.5 finish_sums.7
  (582 shorter events, 281.7 us)
Async XLA Ops:
  7.2 688.1 %all-reduce.2.cloned.1.call-start = ((), (), s32[]{:S(2)}) async-start(), calls=%async_computation | async-start | bytes 2097152 | tf_op jit(solution)/shard_map/psum | solution.py:1121
  35.0 7.9 collective-permute-start.3
  45.9 9.5 %collective-permute-start.5 = (bf16[1,1,256,256]{3,2,0,1:T(8,128)(2,1)}, bf16[1,1,256,256]{3,2,0,1:T(8,128)(2,1)S(1)}, u32[]{:S(2)}, u32[]{:S(2)}) collective-permute-start(bf16[1,1,256,256]{3,2,0,1:T(8,128)(2,1)} %bitcast.219), channel_id=1, source_target_pairs={{0,16},{4,20},{8,24},{12,28},{16,0},{20,4},{24,8},{28,12},{1,17},{... | collective-permute-start | bytes 393224 | tf_op jit(solution)/shard_map/ppermute | solution.py:39
  57.2 24.2 %collective-permute-start.8 = (bf16[2,1,64,1024]{3,2,0,1:T(8,128)(2,1)}, bf16[2,1,64,1024]{3,2,0,1:T(8,128)(2,1)}, u32[]{:S(2)}, u32[]{:S(2)}) collective-permute-start(bf16[2,1,64,1024]{3,2,0,1:T(8,128)(2,1)} %pad_maximum_fusion.4), channel_id=1, source_target_pairs={{0,16},{4,20},{8,24},{12,28},{16,0},{20,4},{24,8},{28,12},{1,17},{... | collective-permute-start | bytes 786440 | tf_op jit(solution)/shard_map/ppermute | solution.py:39
  58.8 22.6 %collective-permute-start.7 = (bf16[2,1,256,256]{3,2,0,1:T(8,128)(2,1)}, bf16[2,1,256,256]{3,2,0,1:T(8,128)(2,1)}, u32[]{:S(2)}, u32[]{:S(2)}) collective-permute-start(bf16[2,1,256,256]{3,2,0,1:T(8,128)(2,1)} %pad_maximum_fusion.3), channel_id=1, source_target_pairs={{0,8},{4,12},{8,0},{12,4},{16,24},{20,28},{24,16},{28,20},{1,9},{5... | collective-permute-start | bytes 786440 | tf_op jit(solution)/shard_map/ppermute | solution.py:39
  82.5 13.4 %collective-permute-start.10 = (bf16[4,1,64,1024]{3,2,0,1:T(8,128)(2,1)S(1)}, bf16[4,1,64,1024]{3,2,0,1:T(8,128)(2,1)S(1)}, u32[]{:S(2)}, u32[]{:S(2)}) collective-permute-start(bf16[4,1,64,1024]{3,2,0,1:T(8,128)(2,1)S(1)} %pad_maximum_fusion.1), channel_id=1, source_target_pairs={{0,8},{4,12},{8,0},{12,4},{16,24},{20,28},{24,16},{28,20},{1,9},{5... | collective-permute-start | bytes 1572872 | tf_op jit(solution)/shard_map/ppermute | solution.py:39
  83.7 13.4 %collective-permute-start.9 = (bf16[4,1,256,256]{3,2,0,1:T(8,128)(2,1)S(1)}, bf16[4,1,256,256]{3,2,0,1:T(8,128)(2,1)S(1)}, u32[]{:S(2)}, u32[]{:S(2)}) collective-permute-start(bf16[4,1,256,256]{3,2,0,1:T(8,128)(2,1)S(1)} %pad_maximum_fusion), channel_id=1, source_target_pairs={{0,4},{4,0},{8,12},{12,8},{16,20},{20,16},{24,28},{28,24},{1,5},{5... | collective-permute-start | bytes 1572872 | tf_op jit(solution)/shard_map/ppermute | solution.py:39
  114.4 14.3 %collective-permute-start.12 = (bf16[256,1024]{1,0:T(8,128)(2,1)}, bf16[256,1024]{1,0:T(8,128)(2,1)}, u32[]{:S(2)}, u32[]{:S(2)}) collective-permute-start(bf16[256,1024]{1,0:T(8,128)(2,1)} %get-tuple-element.412), channel_id=1, source_target_pairs={{0,2},{1,3},{2,0},{3,1},{4,6},{5,7},{6,4},{7,5},{8,10},{9,11},{10,... | collective-permute-start | bytes 1572872 | tf_op jit(solution)/shard_map/ppermute | solution.py:39
  132.0 13.3 %collective-permute-start.13 = (bf16[256,1024]{1,0:T(8,128)(2,1)}, bf16[256,1024]{1,0:T(8,128)(2,1)S(1)}, u32[]{:S(2)}, u32[]{:S(2)}) collective-permute-start(bf16[256,1024]{1,0:T(8,128)(2,1)} %get-tuple-element.415.refs_0_), channel_id=1, source_target_pairs={{0,2},{1,3},{2,0},{3,1},{4,6},{5,7},{6,4},{7,5},{8,10},{9,11},{10,... | collective-permute-start | bytes 1572872 | tf_op jit(solution)/shard_map/ppermute | solution.py:39
  133.5 12.5 %collective-permute-start.14 = (bf16[256,1024]{1,0:T(8,128)(2,1)}, bf16[256,1024]{1,0:T(8,128)(2,1)S(1)}, u32[]{:S(2)}, u32[]{:S(2)}) collective-permute-start(bf16[256,1024]{1,0:T(8,128)(2,1)} %get-tuple-element.415.refs_0_), channel_id=1, source_target_pairs={{0,1},{1,0},{2,3},{3,2},{4,5},{5,4},{6,7},{7,6},{8,9},{9,8},{10,11... | collective-permute-start | bytes 1572872 | tf_op jit(solution)/shard_map/ppermute | solution.py:39
  164.8 14.2 %collective-permute-start.17 = (bf16[256,1024]{1,0:T(8,128)(2,1)}, bf16[256,1024]{1,0:T(8,128)(2,1)S(1)}, u32[]{:S(2)}, u32[]{:S(2)}) collective-permute-start(bf16[256,1024]{1,0:T(8,128)(2,1)} %get-tuple-element.424), channel_id=1, source_target_pairs={{0,2},{1,3},{2,0},{3,1},{4,6},{5,7},{6,4},{7,5},{8,10},{9,11},{10,... | collective-permute-start | bytes 1572872 | tf_op jit(solution)/shard_map/ppermute | solution.py:39
  183.2 13.5 %collective-permute-start.18 = (bf16[256,1024]{1,0:T(8,128)(2,1)}, bf16[256,1024]{1,0:T(8,128)(2,1)}, u32[]{:S(2)}, u32[]{:S(2)}) collective-permute-start(bf16[256,1024]{1,0:T(8,128)(2,1)} %get-tuple-element.427), channel_id=1, source_target_pairs={{0,2},{1,3},{2,0},{3,1},{4,6},{5,7},{6,4},{7,5},{8,10},{9,11},{10,... | collective-permute-start | bytes 1572872 | tf_op jit(solution)/shard_map/ppermute | solution.py:39
  184.7 12.7 %collective-permute-start.19 = (bf16[256,1024]{1,0:T(8,128)(2,1)}, bf16[256,1024]{1,0:T(8,128)(2,1)}, u32[]{:S(2)}, u32[]{:S(2)}) collective-permute-start(bf16[256,1024]{1,0:T(8,128)(2,1)} %get-tuple-element.427), channel_id=1, source_target_pairs={{0,1},{1,0},{2,3},{3,2},{4,5},{5,4},{6,7},{7,6},{8,9},{9,8},{10,11... | collective-permute-start | bytes 1572872 | tf_op jit(solution)/shard_map/ppermute | solution.py:39
  279.5 8.6 %collective-permute-start.22 = (f32[3,4,4,64]{3,2,1,0:T(4,128)S(1)}, f32[3,4,4,64]{3,2,1,0:T(4,128)S(1)}, u32[]{:S(2)}, u32[]{:S(2)}) collective-permute-start(f32[3,4,4,64]{3,2,1,0:T(4,128)S(1)} %pad_maximum_fusion.7), channel_id=1, source_target_pairs={{0,2},{1,3},{2,0},{3,1},{4,6},{5,7},{6,4},{7,5},{8,10},{9,11},{10,... | collective-permute-start | bytes 36872 | tf_op jit(solution)/shard_map/ppermute | solution.py:39
  311.6 14.5 %collective-permute-start.26 = (bf16[512,1024]{1,0:T(8,128)(2,1)S(1)}, bf16[512,1024]{1,0:T(8,128)(2,1)S(1)}, u32[]{:S(2)}, u32[]{:S(2)}) collective-permute-start(bf16[512,1024]{1,0:T(8,128)(2,1)S(1)} %slice.488), channel_id=1, source_target_pairs={{0,1},{1,0},{2,3},{3,2},{4,5},{5,4},{6,7},{7,6},{8,9},{9,8},{10,11... | collective-permute-start | bytes 3145736 | tf_op jit(solution)/shard_map/ppermute | solution.py:39
  325.6 62.7 %collective-permute-start.33 = (bf16[2688,512]{1,0:T(8,128)(2,1)}, bf16[2688,512]{1,0:T(8,128)(2,1)S(1)}, u32[]{:S(2)}, u32[]{:S(2)}) collective-permute-start(bf16[2688,512]{1,0:T(8,128)(2,1)} %get-tuple-element.493), channel_id=1, source_target_pairs={{0,4},{4,0},{8,12},{12,8},{16,20},{20,16},{24,28},{28,24},{1,5},{5... | collective-permute-start | bytes 8257544 | tf_op jit(solution)/shard_map/ppermute | solution.py:39
  330.3 14.3 %collective-permute-start.27 = (bf16[256,1024]{1,0:T(8,128)(2,1)}, bf16[256,1024]{1,0:T(8,128)(2,1)S(1)}, u32[]{:S(2)}, u32[]{:S(2)}) collective-permute-start(bf16[256,1024]{1,0:T(8,128)(2,1)} %get-tuple-element.451), channel_id=1, source_target_pairs={{0,2},{1,3},{2,0},{3,1},{4,6},{5,7},{6,4},{7,5},{8,10},{9,11},{10,... | collective-permute-start | bytes 1572872 | tf_op jit(solution)/shard_map/ppermute | solution.py:39
  349.1 15.3 %collective-permute-start.28 = (bf16[256,1024]{1,0:T(8,128)(2,1)}, bf16[256,1024]{1,0:T(8,128)(2,1)S(1)}, u32[]{:S(2)}, u32[]{:S(2)}) collective-permute-start(bf16[256,1024]{1,0:T(8,128)(2,1)} %get-tuple-element.475.refs_0_), channel_id=1, source_target_pairs={{0,2},{1,3},{2,0},{3,1},{4,6},{5,7},{6,4},{7,5},{8,10},{9,11},{10,... | collective-permute-start | bytes 1572872 | tf_op jit(solution)/shard_map/ppermute | solution.py:39
  349.6 15.3 %collective-permute-start.29 = (bf16[256,1024]{1,0:T(8,128)(2,1)}, bf16[256,1024]{1,0:T(8,128)(2,1)S(1)}, u32[]{:S(2)}, u32[]{:S(2)}) collective-permute-start(bf16[256,1024]{1,0:T(8,128)(2,1)} %get-tuple-element.475.refs_0_), channel_id=1, source_target_pairs={{0,1},{1,0},{2,3},{3,2},{4,5},{5,4},{6,7},{7,6},{8,9},{9,8},{10,11... | collective-permute-start | bytes 1572872 | tf_op jit(solution)/shard_map/ppermute | solution.py:39
  378.8 62.8 %collective-permute-start.35 = (bf16[2688,512]{1,0:T(8,128)(2,1)}, bf16[2688,512]{1,0:T(8,128)(2,1)}, u32[]{:S(2)}, u32[]{:S(2)}) collective-permute-start(bf16[2688,512]{1,0:T(8,128)(2,1)} %get-tuple-element.514), channel_id=1, source_target_pairs={{0,8},{4,12},{8,0},{12,4},{16,24},{20,28},{24,16},{28,20},{1,9},{5... | collective-permute-start | bytes 8257544 | tf_op jit(solution)/shard_map/ppermute | solution.py:39
  380.5 106.0 %collective-permute-start.40 = (bf16[3584,512]{1,0:T(8,128)(2,1)}, bf16[3584,512]{1,0:T(8,128)(2,1)}, u32[]{:S(2)}, u32[]{:S(2)}) collective-permute-start(bf16[3584,512]{1,0:T(8,128)(2,1)} %get-tuple-element.540), channel_id=1, source_target_pairs={{0,4},{4,0},{8,12},{12,8},{16,20},{20,16},{24,28},{28,24},{1,5},{5... | collective-permute-start | bytes 11010056 | tf_op jit(solution)/shard_map/ppermute | solution.py:39
  388.3 13.5 %collective-permute-start.32 = (bf16[256,1024]{1,0:T(8,128)(2,1)}, bf16[256,1024]{1,0:T(8,128)(2,1)S(1)}, u32[]{:S(2)}, u32[]{:S(2)}) collective-permute-start(bf16[256,1024]{1,0:T(8,128)(2,1)} %get-tuple-element.491), channel_id=1, source_target_pairs={{0,2},{1,3},{2,0},{3,1},{4,6},{5,7},{6,4},{7,5},{8,10},{9,11},{10,... | collective-permute-start | bytes 1572872 | tf_op jit(solution)/shard_map/ppermute | solution.py:39
  399.5 84.1 %collective-permute-start.41 = (bf16[2688,256]{1,0:T(8,128)(2,1)S(1)}, bf16[2688,256]{1,0:T(8,128)(2,1)}, u32[]{:S(2)}, u32[]{:S(2)}) collective-permute-start(bf16[2688,256]{1,0:T(8,128)(2,1)S(1)} %get-tuple-element.542), channel_id=1, source_target_pairs={{0,8},{4,12},{8,0},{12,4},{16,24},{20,28},{24,16},{28,20},{1,9},{5... | collective-permute-start | bytes 4128776 | tf_op jit(solution)/shard_map/ppermute | solution.py:39
  406.5 52.8 %collective-permute-start.34 = (bf16[256,1024]{1,0:T(8,128)(2,1)}, bf16[256,1024]{1,0:T(8,128)(2,1)S(1)}, u32[]{:S(2)}, u32[]{:S(2)}) collective-permute-start(bf16[256,1024]{1,0:T(8,128)(2,1)} %get-tuple-element.528.refs_0_), channel_id=1, source_target_pairs={{0,2},{1,3},{2,0},{3,1},{4,6},{5,7},{6,4},{7,5},{8,10},{9,11},{10,... | collective-permute-start | bytes 1572872 | tf_op jit(solution)/shard_map/ppermute | solution.py:39
  407.6 56.1 %collective-permute-start.36 = (bf16[256,1024]{1,0:T(8,128)(2,1)}, bf16[256,1024]{1,0:T(8,128)(2,1)}, u32[]{:S(2)}, u32[]{:S(2)}) collective-permute-start(bf16[256,1024]{1,0:T(8,128)(2,1)} %get-tuple-element.528.refs_0_), channel_id=1, source_target_pairs={{0,1},{1,0},{2,3},{3,2},{4,5},{5,4},{6,7},{7,6},{8,9},{9,8},{10,11... | collective-permute-start | bytes 1572872 | tf_op jit(solution)/shard_map/ppermute | solution.py:39
  462.2 62.0 %collective-permute-start.45 = (bf16[2688,256]{1,0:T(8,128)(2,1)S(1)}, bf16[2688,256]{1,0:T(8,128)(2,1)}, u32[]{:S(2)}, u32[]{:S(2)}) collective-permute-start(bf16[2688,256]{1,0:T(8,128)(2,1)S(1)} %get-tuple-element.571), channel_id=1, source_target_pairs={{0,4},{4,0},{8,12},{12,8},{16,20},{20,16},{24,28},{28,24},{1,5},{5... | collective-permute-start | bytes 4128776 | tf_op jit(solution)/shard_map/ppermute | solution.py:39
  486.5 21.2 %collective-permute-start.38 = (bf16[1024,256]{1,0:T(8,128)(2,1)}, bf16[1024,256]{1,0:T(8,128)(2,1)S(1)}, u32[]{:S(2)}, u32[]{:S(2)}) collective-permute-start(bf16[1024,256]{1,0:T(8,128)(2,1)} %bitcast.52), channel_id=1, source_target_pairs={{0,4},{4,0},{8,12},{12,8},{16,20},{20,16},{24,28},{28,24},{1,5},{5... | collective-permute-start | bytes 1572872 | tf_op jit(solution)/shard_map/ppermute | solution.py:39
  487.0 31.9 %collective-permute-start.39 = (bf16[256,1024]{1,0:T(8,128)(2,1)}, bf16[256,1024]{1,0:T(8,128)(2,1)S(1)}, u32[]{:S(2)}, u32[]{:S(2)}) collective-permute-start(bf16[256,1024]{1,0:T(8,128)(2,1)} %bitcast.54), channel_id=1, source_target_pairs={{0,4},{4,0},{8,12},{12,8},{16,20},{20,16},{24,28},{28,24},{1,5},{5... | collective-permute-start | bytes 1572872 | tf_op jit(solution)/shard_map/ppermute | solution.py:39
  493.0 84.7 %collective-permute-start.48 = (bf16[3584,256]{1,0:T(8,128)(2,1)}, bf16[3584,256]{1,0:T(8,128)(2,1)}, u32[]{:S(2)}, u32[]{:S(2)}) collective-permute-start(bf16[3584,256]{1,0:T(8,128)(2,1)} %get-tuple-element.590), channel_id=1, source_target_pairs={{0,8},{4,12},{8,0},{12,4},{16,24},{20,28},{24,16},{28,20},{1,9},{5... | collective-permute-start | bytes 5505032 | tf_op jit(solution)/shard_map/ppermute | solution.py:39
  500.5 49.7 %collective-permute-start.44 = (bf16[2688,128]{1,0:T(8,128)(2,1)}, bf16[2688,128]{1,0:T(8,128)(2,1)S(1)}, u32[]{:S(2)}, u32[]{:S(2)}) collective-permute-start(bf16[2688,128]{1,0:T(8,128)(2,1)} %get-tuple-element.570), channel_id=1, source_target_pairs={{0,16},{4,20},{8,24},{12,28},{16,0},{20,4},{24,8},{28,12},{1,17},{... | collective-permute-start | bytes 2064392 | tf_op jit(solution)/shard_map/ppermute | solution.py:39
  507.7 164.2 %collective-permute-start.57 = (bf16[3584,512]{1,0:T(8,128)(2,1)}, bf16[3584,512]{1,0:T(8,128)(2,1)}, u32[]{:S(2)}, u32[]{:S(2)}) collective-permute-start(bf16[3584,512]{1,0:T(8,128)(2,1)} %get-tuple-element.642), channel_id=1, source_target_pairs={{0,4},{4,0},{8,12},{12,8},{16,20},{20,16},{24,28},{28,24},{1,5},{5... | collective-permute-start | bytes 11010056 | tf_op jit(solution)/shard_map/ppermute | solution.py:39
  524.2 41.9 %collective-permute-start.42 = (bf16[512,256]{1,0:T(8,128)(2,1)}, bf16[512,256]{1,0:T(8,128)(2,1)S(1)}, u32[]{:S(2)}, u32[]{:S(2)}) collective-permute-start(bf16[512,256]{1,0:T(8,128)(2,1)} %get-tuple-element.568), channel_id=1, source_target_pairs={{0,8},{4,12},{8,0},{12,4},{16,24},{20,28},{24,16},{28,20},{1,9},{5... | collective-permute-start | bytes 786440 | tf_op jit(solution)/shard_map/ppermute | solution.py:39
  525.9 45.8 %collective-permute-start.43 = (bf16[128,1024]{1,0:T(8,128)(2,1)}, bf16[128,1024]{1,0:T(8,128)(2,1)S(1)}, u32[]{:S(2)}, u32[]{:S(2)}) collective-permute-start(bf16[128,1024]{1,0:T(8,128)(2,1)} %get-tuple-element.569), channel_id=1, source_target_pairs={{0,8},{4,12},{8,0},{12,4},{16,24},{20,28},{24,16},{28,20},{1,9},{5... | collective-permute-start | bytes 786440 | tf_op jit(solution)/shard_map/ppermute | solution.py:39
  550.3 84.6 %collective-permute-start.51 = (bf16[2688,128]{1,0:T(8,128)(2,1)}, bf16[2688,128]{1,0:T(8,128)(2,1)S(1)}, u32[]{:S(2)}, u32[]{:S(2)}) collective-permute-start(bf16[2688,128]{1,0:T(8,128)(2,1)} %get-tuple-element.610), channel_id=1, source_target_pairs={{0,16},{4,20},{8,24},{12,28},{16,0},{20,4},{24,8},{28,12},{1,17},{... | collective-permute-start | bytes 2064392 | tf_op jit(solution)/shard_map/ppermute | solution.py:39
  566.1 83.5 %collective-permute-start.53 = (bf16[2048,512]{1,0:T(8,128)(2,1)}, bf16[2048,512]{1,0:T(8,128)(2,1)}, u32[]{:S(2)}, u32[]{:S(2)}) collective-permute-start(bf16[2048,512]{1,0:T(8,128)(2,1)} %get-tuple-element.620), channel_id=1, source_target_pairs={{0,8},{4,12},{8,0},{12,4},{16,24},{20,28},{24,16},{28,20},{1,9},{5... | collective-permute-start | bytes 6291464 | tf_op jit(solution)/shard_map/ppermute | solution.py:39
  576.1 47.8 %collective-permute-start.46 = (bf16[256,256]{1,0:T(8,128)(2,1)}, bf16[256,256]{1,0:T(8,128)(2,1)S(1)}, u32[]{:S(2)}, u32[]{:S(2)}) collective-permute-start(bf16[256,256]{1,0:T(8,128)(2,1)} %get-tuple-element.587), channel_id=1, source_target_pairs={{0,16},{4,20},{8,24},{12,28},{16,0},{20,4},{24,8},{28,12},{1,17},{... | collective-permute-start | bytes 393224 | tf_op jit(solution)/shard_map/ppermute | solution.py:39
  577.8 47.6 %collective-permute-start.47 = (bf16[64,1024]{1,0:T(8,128)(2,1)}, bf16[64,1024]{1,0:T(8,128)(2,1)S(1)}, u32[]{:S(2)}, u32[]{:S(2)}) collective-permute-start(bf16[64,1024]{1,0:T(8,128)(2,1)} %get-tuple-element.588), channel_id=1, source_target_pairs={{0,16},{4,20},{8,24},{12,28},{16,0},{20,4},{24,8},{28,12},{1,17},{... | collective-permute-start | bytes 393224 | tf_op jit(solution)/shard_map/ppermute | solution.py:39
  645.6 53.9 %collective-permute-start.65 = (bf16[3584,128]{1,0:T(8,128)(2,1)}, bf16[3584,128]{1,0:T(8,128)(2,1)S(1)}, u32[]{:S(2)}, u32[]{:S(2)}) collective-permute-start(bf16[3584,128]{1,0:T(8,128)(2,1)} %get-tuple-element.678), channel_id=1, source_target_pairs={{0,16},{4,20},{8,24},{12,28},{16,0},{20,4},{24,8},{28,12},{1,17},{... | collective-permute-start | bytes 2752520 | tf_op jit(solution)/shard_map/ppermute | solution.py:39
  648.9 50.7 %collective-permute-start.64 = (bf16[768,512]{1,0:T(8,128)(2,1)}, bf16[768,512]{1,0:T(8,128)(2,1)}, u32[]{:S(2)}, u32[]{:S(2)}) collective-permute-start(bf16[768,512]{1,0:T(8,128)(2,1)} %get-tuple-element.676), channel_id=1, source_target_pairs={{0,8},{4,12},{8,0},{12,4},{16,24},{20,28},{24,16},{28,20},{1,9},{5... | collective-permute-start | bytes 2359304 | tf_op jit(solution)/shard_map/ppermute | solution.py:39
  657.9 44.2 %collective-permute-start.63 = (bf16[2048,256]{1,0:T(8,128)(2,1)}, bf16[2048,256]{1,0:T(8,128)(2,1)}, u32[]{:S(2)}, u32[]{:S(2)}) collective-permute-start(bf16[2048,256]{1,0:T(8,128)(2,1)} %get-tuple-element.675), channel_id=1, source_target_pairs={{0,4},{4,0},{8,12},{12,8},{16,20},{20,16},{24,28},{28,24},{1,5},{5... | collective-permute-start | bytes 3145736 | tf_op jit(solution)/shard_map/ppermute | solution.py:39
  692.6 53.1 %collective-permute-start.62 = (bf16[3584,256]{1,0:T(8,128)(2,1)}, bf16[3584,256]{1,0:T(8,128)(2,1)}, u32[]{:S(2)}, u32[]{:S(2)}) collective-permute-start(bf16[3584,256]{1,0:T(8,128)(2,1)} %get-tuple-element.674), channel_id=1, source_target_pairs={{0,8},{4,12},{8,0},{12,4},{16,24},{20,28},{24,16},{28,20},{1,9},{5... | collective-permute-start | bytes 5505032 | tf_op jit(solution)/shard_map/ppermute | solution.py:39
  698.2 51.1 %collective-permute-start.61 = (bf16[1296,512]{1,0:T(8,128)(2,1)}, bf16[1296,512]{1,0:T(8,128)(2,1)}, u32[]{:S(2)}, u32[]{:S(2)}) collective-permute-start(bf16[1296,512]{1,0:T(8,128)(2,1)} %get-tuple-element.672), channel_id=1, source_target_pairs={{0,4},{4,0},{8,12},{12,8},{16,20},{20,16},{24,28},{28,24},{1,5},{5... | collective-permute-start | bytes 3981320 | tf_op jit(solution)/shard_map/ppermute | solution.py:39
  704.8 48.9 %collective-permute-start.70 = (bf16[768,256]{1,0:T(8,128)(2,1)}, bf16[768,256]{1,0:T(8,128)(2,1)}, u32[]{:S(2)}, u32[]{:S(2)}) collective-permute-start(bf16[768,256]{1,0:T(8,128)(2,1)} %get-tuple-element.701), channel_id=1, source_target_pairs={{0,4},{4,0},{8,12},{12,8},{16,20},{20,16},{24,28},{28,24},{1,5},{5... | collective-permute-start | bytes 1179656 | tf_op jit(solution)/shard_map/ppermute | solution.py:39
  705.5 71.7 %collective-permute-start.74 = (bf16[2048,128]{1,0:T(8,128)(2,1)}, bf16[2048,128]{1,0:T(8,128)(2,1)}, u32[]{:S(2)}, u32[]{:S(2)}) collective-permute-start(bf16[2048,128]{1,0:T(8,128)(2,1)} %get-tuple-element.713), channel_id=1, source_target_pairs={{0,16},{4,20},{8,24},{12,28},{16,0},{20,4},{24,8},{28,12},{1,17},{... | collective-permute-start | bytes 1572872 | tf_op jit(solution)/shard_map/ppermute | solution.py:39
  751.7 24.5 %collective-permute-start.69 = (bf16[1296,256]{1,0:T(8,128)(2,1)S(1)}, bf16[1296,256]{1,0:T(8,128)(2,1)S(1)}, u32[]{:S(2)}, u32[]{:S(2)}) collective-permute-start(bf16[1296,256]{1,0:T(8,128)(2,1)S(1)} %get-tuple-element.700), channel_id=1, source_target_pairs={{0,8},{4,12},{8,0},{12,4},{16,24},{20,28},{24,16},{28,20},{1,9},{5... | collective-permute-start | bytes 1990664 | tf_op jit(solution)/shard_map/ppermute | solution.py:39
  755.6 55.5 %collective-permute-start.73 = (bf16[3584,128]{1,0:T(8,128)(2,1)}, bf16[3584,128]{1,0:T(8,128)(2,1)}, u32[]{:S(2)}, u32[]{:S(2)}) collective-permute-start(bf16[3584,128]{1,0:T(8,128)(2,1)} %get-tuple-element.712), channel_id=1, source_target_pairs={{0,16},{4,20},{8,24},{12,28},{16,0},{20,4},{24,8},{28,12},{1,17},{... | collective-permute-start | bytes 2752520 | tf_op jit(solution)/shard_map/ppermute | solution.py:39
  756.7 58.5 %collective-permute-start.72 = (bf16[768,128]{1,0:T(8,128)(2,1)}, bf16[768,128]{1,0:T(8,128)(2,1)}, u32[]{:S(2)}, u32[]{:S(2)}) collective-permute-start(bf16[768,128]{1,0:T(8,128)(2,1)} %get-tuple-element.711), channel_id=1, source_target_pairs={{0,16},{4,20},{8,24},{12,28},{16,0},{20,4},{24,8},{28,12},{1,17},{... | collective-permute-start | bytes 589832 | tf_op jit(solution)/shard_map/ppermute | solution.py:39
  777.2 52.1 %collective-permute-start.71 = (bf16[1296,128]{1,0:T(8,128)(2,1)}, bf16[1296,128]{1,0:T(8,128)(2,1)}, u32[]{:S(2)}, u32[]{:S(2)}) collective-permute-start(bf16[1296,128]{1,0:T(8,128)(2,1)} %get-tuple-element.710), channel_id=1, source_target_pairs={{0,16},{4,20},{8,24},{12,28},{16,0},{20,4},{24,8},{28,12},{1,17},{... | collective-permute-start | bytes 995336 | tf_op jit(solution)/shard_map/ppermute | solution.py:39
  (147 other events, 1562.7 us)
Sparse Core Ops, SparseCore 0:
  645.7 35.2 all-reduce.1

commit v3 on v2

--- a/solution.py
+++ b/solution.py
@@ -13,6 +13,34 @@
 ENTROPY_WEIGHT = 0.5
 BRIEF = pl.CostEstimate(flops=0, bytes_accessed=0, transcendentals=0)
 bfloat = jnp.bfloat16
+
+CUTS = (0, 2, 4, 7)
+ORDERS = {"f": "z", "p": "y", "s": "y"}
+PLAN = (
+    (),
+    (("a", "make"), ("a", "send"),),
+    (("b", "make"), ("b", "send"),),
+    (),
+    (("a", "add"),),
+    (("f", "make"), ("f", "send"),),
+    (),
+    (("c", "make"),),
+    (),
+    (),
+    (("t", "step"), ("b", "add"), ("f", "add"),),
+    (("t", "step"),),
+    (("a", "send"), ("b", "send"),),
+    (("c", "send"), ("t", "step"), ("f", "send"),),
+    (),
+    (),
+    (),
+    (),
+    (("p", "make"), ("p", "send"), ("a", "add"), ("a", "send"),),
+    (("s", "make"), ("s", "send"),),
+    (("c", "add"), ("c", "send"), ("b", "add"), ("b", "send"),),
+    (),
+    (("f", "add"), ("f", "send"), ("p", "add"), ("p", "send"), ("c", "add"), ("c", "send"), ("s", "add"), ("s", "send"), ("a", "wait"), ("b", "wait"), ("p", "add"), ("p", "send"), ("f", "wait"), ("s", "add"), ("s", "send"), ("c", "wait"), ("p", "wait"), ("s", "wait"),),
+)
 single = jnp.float32
 
 
@@ -71,18 +99,6 @@
         arrived = tie(*(swap(held, axis, count, bit) for held, bit in zip(helds, bits)))
         helds = [jnp.concatenate([held, more], 0) for held, more in zip(helds, arrived)]
     return helds
-
-
-def scatter_both_steps(values, axis, count, orders, through):
-    for bits in zip(*(order[::-1] for order in orders)):
-        sent = through(*(value[0] for value in values))
-        arrived = [swap(value, axis, count, bit) for value, bit in zip(sent, bits)]
-        yield None
-        arrived = through(*arrived)
-        if bits[0] == orders[0][0]:
-            yield [(value[1], more) for value, more in zip(values, arrived)]
-        else:
-            values = [add_halves(value[1], more) for value, more in zip(values, arrived)]
 
 
 def total_over(value, axis, count, order):
@@ -350,7 +366,7 @@
 def add_columns(kept, arrived):
     rows, width = kept.shape
     block = rows
-    for count in (8, 7, 6, 5, 4, 3, 2):
+    for count in (4, 3, 2):
         if rows % (16 * count) == 0:
             block = rows // count
             break
@@ -493,8 +509,9 @@
         columns == label_ref[...], patch_ref[...], weight_ref[...].astype(single) * factor
     ).astype(bfloat)
     half = width // 2
-    sent_ref[...] = inner_rows(delta, moved[:, half:]).astype(bfloat)
-    kept_ref[...] = inner_rows(delta, moved[:, :half]).astype(bfloat)
+    slope = inner_rows(delta, moved[...])
+    sent_ref[...] = slope[:, half:].astype(bfloat)
+    kept_ref[...] = slope[:, :half].astype(bfloat)
 
 
 def vocab_slope(weights, factors, label, patch, states, order, first, count, tile):
@@ -540,8 +557,9 @@
                 moved[:rows, place * span : (place + 1) * span] = rights[index][:, pl.ds(source, span)]
         right = moved[:rows, :]
         left = lefts[index][...]
-        sent_ref[base : base + entries, :] = inner_rows(left, right[:, half:]).astype(bfloat)
-        kept_ref[base : base + entries, :] = inner_rows(left, right[:, :half]).astype(bfloat)
+        slope = inner_rows(left, right)
+        sent_ref[base : base + entries, :] = slope[:, half:].astype(bfloat)
+        kept_ref[base : base + entries, :] = slope[:, :half].astype(bfloat)
         base += entries
 
 
@@ -734,6 +752,127 @@
         compiler_params=pltpu.CompilerParams(vmem_limit_bytes=40 * 1024 * 1024),
         name="finish_sums",
     )(*kept, *arrived)
+
+
+def order_columns_kernel(count, order_ref, *refs):
+    pieces, (joined_ref, moved_ref) = refs[:count], refs[count:]
+    rows, width = pieces[0].shape
+    span = width // order_ref.shape[0]
+    for index in range(count):
+        part = slice(index * rows, (index + 1) * rows)
+        joined_ref[part, :] = pieces[index][...]
+        for place in range(order_ref.shape[0]):
+            source = pl.multiple_of(order_ref[place] * span, span)
+            moved_ref[part, place * span : (place + 1) * span] = pieces[index][:, pl.ds(source, span)]
+
+
+def order_columns(pieces, order):
+    shape = (len(pieces) * pieces[0].shape[0], pieces[0].shape[1])
+    return pl.pallas_call(
+        functools.partial(order_columns_kernel, len(pieces)),
+        in_specs=[pl.BlockSpec(memory_space=pltpu.SMEM)] + [VMEM] * len(pieces),
+        out_specs=[VMEM, VMEM],
+        out_shape=[jax.ShapeDtypeStruct(shape, bfloat)] * 2,
+        compiler_params=pltpu.CompilerParams(vmem_limit_bytes=40 * 1024 * 1024),
+        cost_estimate=BRIEF,
+        name="order_columns",
+    )(order, *pieces)
+
+
+def half_slope_kernel(
+    first,
+    ratio,
+    base_ref,
+    weight_ref,
+    table_ref,
+    factor_ref,
+    label_ref,
+    patch_ref,
+    far_ref,
+    far_norm_ref,
+    far_scale_ref,
+    far_label_ref,
+    moved_ref,
+    far_moved_ref,
+    sent_ref,
+    kept_ref,
+    delta,
+):
+    rows, tile = weight_ref.shape
+    here = base_ref[0] + first + pl.program_id(0)
+    factors = factor_ref[...]
+    lanes = lax.broadcasted_iota(jnp.int32, factors.shape, 1)
+    factor = jnp.sum(jnp.where(lanes == here // ratio, factors, 0.0), -1, keepdims=True)
+    columns = lax.broadcasted_iota(jnp.int32, weight_ref.shape, 1) + here * tile
+    logits = outer_rows(far_ref[...], table_ref[...])
+    delta[:rows, :] = jnp.where(
+        columns == label_ref[...], patch_ref[...], weight_ref[...].astype(single) * factor
+    ).astype(bfloat)
+    hit = jnp.where(columns == far_label_ref[...], 1.0, 0.0)
+    delta[rows:, :] = (far_scale_ref[...] * (hit - jnp.exp(logits - far_norm_ref[...]))).astype(bfloat)
+    slope = inner_rows(delta[:rows, :], moved_ref[...]) + inner_rows(delta[rows:, :], far_moved_ref[...])
+    half = sent_ref.shape[1]
+    sent_ref[...] = slope[:, half:].astype(bfloat)
+    kept_ref[...] = slope[:, :half].astype(bfloat)
+
+
+def half_slope(base, weights, table, factors, label, patch, far, far_norm, far_scale, far_label, moved, far_moved, first, count, tile):
+    rows, width = far.shape
+    whole = lambda *shape: pl.BlockSpec(shape, lambda i, b: (0,) * len(shape))
+    half = pl.BlockSpec((tile, width // 2), lambda i, b: (i, 0))
+    return pl.pallas_call(
+        functools.partial(half_slope_kernel, first, vocab_tile(weights.shape[1]) // tile),
+        grid_spec=pltpu.PrefetchScalarGridSpec(
+            num_scalar_prefetch=1,
+            grid=(count,),
+            in_specs=[
+                pl.BlockSpec((rows, tile), lambda i, b: (0, i + first + b[0])),
+                pl.BlockSpec((tile, width), lambda i, b: (i + first + b[0], 0)),
+                whole(rows, LANES),
+                whole(rows, 1),
+                whole(rows, 1),
+                whole(rows, width),
+                whole(rows, 1),
+                whole(rows, 1),
+                whole(rows, 1),
+                whole(rows, width),
+                whole(rows, width),
+            ],
+            out_specs=[half, half],
+            scratch_shapes=[pltpu.VMEM((2 * rows, tile), bfloat)],
+        ),
+        out_shape=[jax.ShapeDtypeStruct((count * tile, width // 2), bfloat)] * 2,
+        compiler_params=pltpu.CompilerParams(
+            dimension_semantics=("arbitrary",), vmem_limit_bytes=56 * 1024 * 1024
+        ),
+        cost_estimate=BRIEF,
+        name="half_slope",
+    )(base, weights, table, factors, label, patch, far, far_norm, far_scale, far_label, moved, far_moved)
+
+
+def place_halves_kernel(count, side_ref, *refs):
+    out_ref = refs[-1]
+    half = out_ref.shape[0] // 2
+    for group, side in ((refs[:count], side_ref[0]), (refs[count : 2 * count], 1 - side_ref[0])):
+        offset = 0
+        for ref in group:
+            rows = ref.shape[0]
+            start = pl.multiple_of(side * half + offset, LANES)
+            out_ref[pl.ds(start, rows), :] = ref[...].astype(single)
+            offset += rows
+
+
+def place_halves(side, own, other):
+    total = sum(part.shape[0] for part in own) * 2
+    return pl.pallas_call(
+        functools.partial(place_halves_kernel, len(own)),
+        in_specs=[pl.BlockSpec(memory_space=pltpu.SMEM)] + [VMEM] * (2 * len(own)),
+        out_specs=VMEM,
+        out_shape=jax.ShapeDtypeStruct((total, own[0].shape[1]), single),
+        compiler_params=pltpu.CompilerParams(vmem_limit_bytes=40 * 1024 * 1024),
+        cost_estimate=BRIEF,
+        name="place_halves",
+    )(side, *own, *other)
 
 
 def marginal_objective(seq_values, doc_scores, member, length):
@@ -795,7 +934,7 @@
     quarter = length // mp
     assert own_questions == 1
 
-    token = [score_table[0]]
+    token = [score_table]
 
     def through(*values):
         values = tie(*values, token[0])
@@ -807,6 +946,8 @@
     dp_bits = bits_of(dp)
     dp_order = dp_bits[::-1]
     dp_table = relative_of(dp_order)
+    fast = dp >= 4 and width % (dp * LANES) == 0
+    far = dp_bits[-1]
 
     def to_own(rows, count):
         natural = rows.reshape((count, mp, quarter) + rows.shape[2:])
@@ -834,6 +975,16 @@
         held.append(swap(held[1], "mp", mp, mp_order[1]))
         yield None
         yield through(*held)
+
+    def dp_scatter_steps(halves, order):
+        for bit in reversed(order):
+            sent, kept = through(*halves)
+            arrived = swap(sent, "dp", dp, bit)
+            yield None
+            if bit == order[0]:
+                yield kept, through(arrived)
+            else:
+                halves = add_halves(kept, through(arrived))
 
     def last(steps):
         for value in steps:
@@ -878,6 +1029,10 @@
         )
 
     probe_order = dp_bits[::-1]
+    return_order = dp_bits[:1] + dp_bits[:0:-1]
+    return_bins = where_slots(return_order)
+    state_order = probe_order
+    state_bins = where_slots(state_order)
     first_order = dp_bits[:1] + dp_bits[:0:-1]
     probe_bins = where_slots(probe_order)
     first_bins = where_slots(first_order)
@@ -894,8 +1049,12 @@
     stored_contents = (matmul(passage_rows, content_weight) + content_bias).astype(bfloat)
     stored_addresses = stored_addresses.reshape(store_count, passage_length, local_width)
     stored_contents = stored_contents.reshape(store_count, passage_length, local_width)
-    pair_labels = to_own(jnp.take(labels, my_questions, axis=0, mode="clip"), pair_count).reshape(-1)
-    local_index = pair_labels - member_index * vocab_share
+
+    def label_index(slots):
+        wanted = to_own(jnp.take(labels, slots, axis=0, mode="clip"), pair_count).reshape(-1)
+        return wanted - member_index * vocab_share
+
+    local_index = label_index(my_questions)
     inside = (local_index >= 0) & (local_index < vocab_share)
     label_rows = jnp.take(embedding, jnp.clip(local_index, 0, vocab_share - 1), axis=0, mode="clip")
     probe_all, label_rows = lax.optimization_barrier((probe_all, label_rows))
@@ -915,10 +1074,23 @@
     third_in, third_norm, low = norm_forward(
         kept, arrived, second_norm, shrink_bias, third_gain, third_shift
     )
-    third_low = jnp.concatenate(last(mp_gather_steps(low)), 0)
+    def order_table(order):
+        if not fast:
+            return jnp.arange(width // LANES, dtype=jnp.int32)
+        return group ^ jnp.asarray(relative_of(order), jnp.int32)
+
+    order_a = dp_bits[::-1]
+    order_b = order_a if dp < 4 else [dp_bits[-1], dp_bits[0]] + dp_bits[1:-1]
+    third_low, third_moved = order_columns(last(mp_gather_steps(low)), order_table(order_a))
+    far_low = swap(through(low), "dp", dp, far)
+
 
     label_lanes = jnp.broadcast_to(local_index[:, None], (local_index.shape[0], LANES))
+    third_low = through(third_low)
     entry_weights, entry_sums, entry_mix, entry_tops = vocab_forward(third_low, embedding, label_lanes)
+    entry_tops, entry_sums, entry_mix, far_low = through(
+        entry_tops, entry_sums, entry_mix, far_low
+    )
     entry_tile = vocab_tile(vocab_share)
     local_top = entry_tops[:, vocab_share // entry_tile - 1]
     local_target = jnp.where(
@@ -939,10 +1111,20 @@
     pair_likelihood = jnp.sum((target_logit - log_norm).reshape(mp, pair_count, quarter), -1)
     while pair_likelihood.shape[0] > 1:
         pair_likelihood = pair_likelihood[0::2] + pair_likelihood[1::2]
-    every_likelihood = natural_order(
-        dp_table, group, gather_blocks(pair_likelihood[0], "dp", dp, dp_order), 0
-    ).reshape(-1)
-    doc_scores = jnp.take(score_table, score_index)
+    far_steps = mp_gather_steps(far_low)
+    next(far_steps)
+    shared = jnp.concatenate([pair_likelihood[0], log_norm])
+    arrived = swap(shared, "dp", dp, far)
+    far_norm = arrived[pair_count:]
+    every_likelihood = jnp.stack([shared[:pair_count], arrived[:pair_count]])
+    for bit in dp_order[1:]:
+        every_likelihood = jnp.concatenate(
+            [every_likelihood, swap(every_likelihood, "dp", dp, bit)], 0
+        )
+    every_likelihood = natural_order(dp_table, group, every_likelihood, 0).reshape(-1)
+    next(far_steps)
+    far_third, far_moved = order_columns(next(far_steps), order_table(order_a))
+    doc_scores = jnp.take(token[0], score_index)
     member = slot_question[None, :] == jnp.arange(questions, dtype=jnp.int32)[:, None]
 
     def scored(values_all):
@@ -951,7 +1133,18 @@
     objective, pullback = jax.vjp(scored, every_likelihood)
     likelihood_delta = pullback(jnp.ones_like(objective) * (questions * length))[0]
     pair_delta = lax.dynamic_slice_in_dim(likelihood_delta, group * pair_count, pair_count)
-    row_delta = jnp.broadcast_to(pair_delta[None, :, None], (mp, pair_count, quarter)).reshape(-1)
+
+    def by_row(values):
+        return jnp.broadcast_to(values[None, :, None], (mp, pair_count, quarter)).reshape(-1)
+
+    row_delta = by_row(pair_delta)
+    far_group = group ^ far
+    far_delta = by_row(
+        lax.dynamic_slice_in_dim(likelihood_delta, far_group * pair_count, pair_count)
+    )
+    far_label = label_index(
+        lax.dynamic_slice_in_dim(slot_question, far_group * pair_count, pair_count)
+    )
     surplus = row_delta * (1.0 - jnp.exp(target_logit - log_norm))
     factors = -row_delta[:, None] * jnp.exp(entry_tops - log_norm[:, None])
     third_part = (
@@ -959,13 +1152,6 @@
         - (row_delta * jnp.exp(local_top - log_norm))[:, None] * entry_mix
     )
 
-    fast = width % (dp * LANES) == 0
-
-    def order_table(order):
-        if not fast:
-            return jnp.arange(width // LANES, dtype=jnp.int32)
-        return group ^ jnp.asarray(relative_of(order), jnp.int32)
-
     token[0] = objective
 
     class ColumnSum:
@@ -980,13 +1166,13 @@
                 self.arrived = swap(self.sent, "dp", dp, self.bits[0])
                 self.bits = self.bits[1:]
 
+        def add(self):
+            if fast:
+                self.arrived, self.kept = through(self.arrived, self.kept)
+                self.sent, self.kept = add_columns(self.kept, self.arrived)
+
         def step(self):
-            if not fast or not self.bits:
-                return
-            self.arrived, self.kept = through(self.arrived, self.kept)
-            half = self.kept.shape[1] // 2
-            total = self.kept.astype(single) + self.arrived.astype(single)
-            self.sent, self.kept = total[:, half:].astype(bfloat), total[:, :half].astype(bfloat)
+            self.add()
             self.send()
 
         def wait(self):
@@ -1005,59 +1191,127 @@
         assert not any(part.bits for part in parts)
         return finish_sums([part.kept for part in parts], [part.arrived for part in parts])
 
-    order_a = dp_bits[::-1]
-    order_b = order_a if dp < 4 else [dp_bits[-1], dp_bits[0]] + dp_bits[1:-1]
     slope_tile = entry_tile // 2 if entry_tile % (2 * LANES) == 0 else entry_tile
-    tiles = vocab_share // slope_tile
-    cuts = [tiles * i // 14 for i in (0, 3, 6, 10, 14)]
-    def table_sum(index, order):
-        halves = vocab_slope(
-            entry_weights,
-            through(factors),
-            local_index[:, None],
-            surplus[:, None],
-            third_low,
-            order_table(order),
-            cuts[index],
-            cuts[index + 1] - cuts[index],
-            slope_tile,
-        )
-        return ColumnSum(halves, order)
+    side = (group // far).astype(jnp.int32).reshape(1)
+    tiles = vocab_share // slope_tile // 2 if fast else vocab_share // slope_tile
+    cuts = [-(-tiles * i // 7) for i in CUTS]
+
+    def table_sum(index):
+        first, count = cuts[index], cuts[index + 1] - cuts[index]
+        if fast:
+            halves = half_slope(
+                side * tiles,
+                entry_weights,
+                embedding,
+                through(factors),
+                local_index[:, None],
+                surplus[:, None],
+                far_third,
+                far_norm[:, None],
+                far_delta[:, None],
+                far_label[:, None],
+                third_moved,
+                far_moved,
+                first,
+                count,
+                slope_tile,
+            )
+        else:
+            halves = vocab_slope(
+                entry_weights,
+                through(factors),
+                local_index[:, None],
+                surplus[:, None],
+                third_low,
+                order_table(order_a),
+                first,
+                count,
+                slope_tile,
+            )
+        return ColumnSum(halves, order_a)
 
     def group_sum(pairs, order):
         pairs = [(through(pairs[0][0]), pairs[0][1])] + pairs[1:]
         return ColumnSum(slope_group(pairs, order_table(order)), order)
 
+    sums = {}
+    makers = {
+        "a": lambda: table_sum(0),
+        "b": lambda: table_sum(1),
+        "c": lambda: table_sum(2),
+        "f": lambda: group_sum(
+            [(activated, feed_delta), (expanded_delta, second_low)], orders[ORDERS["f"]]
+        ),
+        "p": lambda: group_sum(
+            [
+                (cross_flat, recall_delta),
+                (address_delta, passage_rows),
+                (content_delta, passage_rows),
+                (probe_flat, first_full),
+                (self_flat, self_delta),
+            ],
+            orders[ORDERS["p"]],
+        ),
+        "s": lambda: group_sum(
+            [
+                (query_flat, inputs),
+                (key_flat, inputs),
+                (value_flat, inputs),
+                (jnp.eye(16, dtype=bfloat), vectors.astype(bfloat)),
+            ],
+            orders[ORDERS["s"]],
+        ),
+    }
+    orders = {"y": order_a, "z": order_b}
+
+    def at(point):
+        for name, action in PLAN[point]:
+            if name == "t":
+                next(state_steps)
+            elif action == "make":
+                sums[name] = makers[name]()
+            else:
+                getattr(sums[name], action)()
+
     half = third_part.shape[0] // 2
     steps = mp_scatter_steps((third_part[half:].astype(bfloat), third_part[:half]))
     next(steps)
-    sum_a1 = table_sum(0, order_a)
-    sum_a1.send()
-    next(steps)
-    sum_b = table_sum(1, order_b)
-    sum_b.send()
+    at(0)
+    next(steps)
+    at(1)
     third_back, feed_low, third_sums = norm_backward(next(steps), third_in, third_gain)
     steps = mp_gather_steps(feed_low)
     next(steps)
-    sum_a2 = table_sum(2, order_a)
-    sum_a2.send()
-    next(steps)
+    at(2)
+    next(steps)
+    at(3)
     feed_delta, expanded_delta, bias_expand, sent, kept = feed_backward(
         next(steps), expand_weight, shrink_weight, expanded
     )
     steps = mp_scatter_steps((sent, kept))
     next(steps)
-    next(steps)
-    sum_a1.step()
-    sum_f = group_sum([(activated, feed_delta), (expanded_delta, second_low)], order_b)
+    at(4)
+    next(steps)
+    at(5)
+    parts = next(steps)
+    at(6)
     second_back, recall_low, second_sums = norm_backward(
-        next(steps) + (third_back,), second_in, second_gain
+        parts + (third_back,), second_in, second_gain
     )
     steps = mp_gather_steps(recall_low)
     next(steps)
-    sum_b.step()
-    sum_a3 = table_sum(3, order_a)
-    next(steps)
+    state_steps = dp_scatter_steps(
+        tuple(
+            value.reshape(-1, width)
+            for value in bin_rows(
+                second_back.reshape(pair_count, quarter, width), state_bins, questions
+            )
+        ),
+        state_order,
+    )
+    at(7)
+    next(steps)
+    at(8)
     recall_delta, mixed_delta = project(
         next(steps), merged_weight, jnp.zeros((local_width,), single), True
     )
@@ -1068,53 +1322,31 @@
         mixed_delta.reshape(mp, pair_count, quarter, local_width),
         probe_bins,
         slot_passage,
-        probe_bins,
+        return_bins,
     )
     address_delta = address_delta.reshape(-1, local_width)
     content_delta = content_delta.reshape(-1, local_width)
 
     half = questions // 2
-    steps = scatter_both_steps(
+    steps = dp_scatter_steps(
         (
-            (
-                probe_binned[half:].reshape(-1, local_width),
-                probe_binned[:half].reshape(-1, local_width),
-            ),
-            tuple(
-                value.reshape(-1, width)
-                for value in bin_rows(
-                    second_back.reshape(pair_count, quarter, width), probe_bins, questions
-                )
-            ),
-        ),
-        "dp",
-        dp,
-        (probe_order, probe_order),
-        through,
-    )
-    next(steps)
-    sum_a1.step()
-    sum_a2.step()
-    sum_a3.send()
-    sum_x = group_sum(
-        [
-            (cross_flat, recall_delta),
-            (address_delta, passage_rows),
-            (content_delta, passage_rows),
-        ],
-        order_b,
-    )
-    next(steps)
-    sum_f.send()
-    sum_b.step()
-    sum_a1.wait()
+            probe_binned[half:].reshape(-1, local_width),
+            probe_binned[:half].reshape(-1, local_width),
+        ),
+        return_order,
+    )
+    at(9)
+    next(steps)
+    at(10)
     for unused in range(len(dp_bits) - 2):
         next(steps)
-    sum_a2.step()
-    sum_x.send()
-    probe_parts, state_parts = next(steps)
+    at(11)
+    next(steps)
+    at(12)
+    probe_parts = next(steps)
+    at(13)
     probe_flat = (
-        probe_parts[0].astype(single) + probe_parts[1].astype(single)
+        probe_parts[0] + probe_parts[1].astype(single)
     ).astype(bfloat)
 
     bias_content = jnp.sum(content_delta, 0, dtype=single)
@@ -1126,15 +1358,18 @@
     bias_probe = jnp.sum(probe_flat, 0, dtype=single)
     steps = mp_scatter_steps(product_halves([probe_flat], [probe_weight], True))
     next(steps)
-    next(steps)
-    sum_b.wait()
+    at(14)
+    next(steps)
+    at(15)
+    state_parts = last(state_steps)
     first_back, self_low, first_sums = norm_backward(
         next(steps) + tuple(state_parts), first_in, first_gain
     )
     steps = mp_gather_steps(self_low)
     next(steps)
-    sum_f.step()
-    next(steps)
+    at(16)
+    next(steps)
+    at(17)
     self_delta, self_mixed_delta = project(
         next(steps), output_weight, jnp.zeros((local_width,), single), True
     )
@@ -1168,56 +1403,44 @@
     quads = quads.reshape(4, dp, local_width // dp).swapaxes(0, 1).reshape(1, width)
     vectors = jnp.concatenate([shared, bias_expand, quads, jnp.zeros((5, width), single)], 0)
     next(steps)
-    sum_a3.step()
-    next(steps)
-    sum_s = group_sum(
-        [
-            (probe_flat, first_full),
-            (self_flat, self_delta),
-            (query_flat, inputs),
-            (key_flat, inputs),
-            (value_flat, inputs),
-            (jnp.eye(16, dtype=bfloat), vectors.astype(bfloat)),
-        ],
-        order_a,
-    )
+    at(18)
+    next(steps)
+    at(19)
     kept, arrived = next(steps)
     input_low = (kept + arrived.astype(single) + first_back).astype(bfloat)
     steps = mp_gather_steps(input_low)
     next(steps)
-    sum_s.send()
-    next(steps)
+    at(20)
+    next(steps)
+    at(21)
     targets_slope = to_natural(jnp.concatenate(next(steps), 0), own_questions)
     targets_slope = targets_slope.reshape(targets.shape).astype(single)
-
-    sum_a2.wait()
-    sum_x.step()
-    sum_f.step()
-    sum_a3.step()
-    sum_s.step()
-    sum_x.step()
-    sum_s.step()
-    sum_f.wait()
-    sum_a3.wait()
-    sum_x.wait()
-    sum_s.wait()
-    embedding_slope = finish([sum_a1, sum_b, sum_a2, sum_a3])
-    feed_slopes = finish([sum_f])
-    cross_slopes = finish([sum_x])
-    self_slopes = finish([sum_s])
+    at(22)
+    table_parts = [sums[name] for name in "abc"]
+    if fast:
+        embedding_slope = place_halves(
+            side, [part.kept for part in table_parts], [part.arrived for part in table_parts]
+        )
+    else:
+        embedding_slope = finish(table_parts)
+    feed_slopes = finish([sums["f"]])
+    probe_slopes = finish([sums["p"]])
+    self_slopes = finish([sums["s"]])
     hidden = expanded.shape[1]
-    shrink_slope = feed_slopes[:hidden]
-    expand_slope = feed_slopes[hidden:].T
-    merged_slope = cross_slopes[:local_width]
-    address_slope = cross_slopes[local_width : 2 * local_width].T
-    content_slope = cross_slopes[2 * local_width :].T
-    probe_slope = self_slopes[:local_width].T
-    output_slope = self_slopes[local_width : 2 * local_width]
-    query_slope = self_slopes[2 * local_width : 3 * local_width].T
-    key_slope = self_slopes[3 * local_width : 4 * local_width].T
-    value_slope = self_slopes[4 * local_width : 5 * local_width].T
-
-    vectors = self_slopes[5 * local_width :]
+
+    def parts_of(slopes, counts):
+        edges = [sum(counts[:i]) for i in range(len(counts) + 1)]
+        return [slopes[a:b] for a, b in zip(edges, edges[1:])]
+
+    shrink_slope, expand_slope = parts_of(feed_slopes, [hidden] * 2)
+    merged_slope, address_slope, content_slope, probe_slope, output_slope = parts_of(
+        probe_slopes, [local_width] * 5
+    )
+    query_slope, key_slope, value_slope, vectors = parts_of(self_slopes, [local_width] * 3 + [16])
+    expand_slope, address_slope, content_slope = expand_slope.T, address_slope.T, content_slope.T
+    probe_slope, query_slope, key_slope, value_slope = (
+        slope.T for slope in (probe_slope, query_slope, key_slope, value_slope)
+    )
     (
         bias_output,
         first_gain_slope,

time: 851 us -> 759 us (0.89)
  waiting for transfers between devices: 318 us -> 206 us
  Pallas kernels: 266 us -> 322 us
  other arithmetic: 69.6 us -> 36.3 us
    ppermute x75 -> x76, waiting for transfers between devices: 318 us -> 183 us  [swap(): return lax.ppermute(value, axis, [(i, i ^ bit) for i in range(count)])]
    pallas_call x4 -> x18, Pallas kernels: 53.6 us -> 116 us  [the longest x3 66.8 us: half_slope(): pl.pallas_call(functools.partial(half_slope_kernel, first, vocab_tile(wei...]
    another operation x16 -> x3, other arithmetic: 28.2 us -> 1.51 us
    psum x1, waiting for transfers between devices: 0.01 us -> 22.9 us  [on_device(): lax.psum((outer_rows(address_delta, address_weight) + outer_rows(content_...]
    slice x17 -> x4, local copies, waits for them, and re-layouts: 17.2 us -> 3.91 us  [the longest x1 2.06 us: on_device(): probe_binned[:half].reshape(-1, local_width)]
    ppermute x75 -> x76, starting transfers between devices: 66.2 us -> 69.3 us  [swap(): return lax.ppermute(value, axis, [(i, i ^ bit) for i in range(count)])]
    unnamed x248 -> x245, local copies, waits for them, and re-layouts: 35.9 us -> 35.1 us
  transfers between devices with their start and end apart: 76 -> 77, of which waited for: 39 -> 35; matrix products, arithmetic and copies ran while one was open for 13% -> 11% of each run, Pallas kernels for 19% -> 36%
where the time goes in v3:
time: 759 us; the launch traced here: 751 us
  Pallas kernels  322 us (42%)
  waiting for transfers between devices  206 us (27%)
  local copies, waits for them, and re-layouts  92.7 us (12%)
  starting transfers between devices  69.3 us (9%)
  other arithmetic  36.3 us (5%)
  between operations  17.3 us (2%)
    ppermute x76, waiting for transfers between devices, swap(): return lax.ppermute(value, axis, [(i, i ^ bit) for i in range(count)])  183 us
    pallas_call x26, Pallas kernels, run_whole(): pl.pallas_call(kernel, in_specs=[VMEM] * len(operands), out_specs=[VMEM]...  85.6 us
    ppermute x76, starting transfers between devices, swap(): return lax.ppermute(value, axis, [(i, i ^ bit) for i in range(count)])  69.3 us
    pallas_call x1, Pallas kernels, vocab_forward(): pl.pallas_call(vocab_forward_kernel, grid=(entries // tile,), in_specs=[w...  69.1 us
    pallas_call x3, Pallas kernels, half_slope(): pl.pallas_call(functools.partial(half_slope_kernel, first, vocab_tile(wei...  66.8 us
    pallas_call x12, Pallas kernels, add_columns(): pl.pallas_call(add_columns_kernel, grid=(rows // block,), in_specs=[whole...  43.3 us
    unnamed x245, local copies, waits for them, and re-layouts  35.1 us
    psum x1, waiting for transfers between devices, on_device(): lax.psum((outer_rows(address_delta, address_weight) + outer_rows(content_...  22.9 us
  transfers between devices with their start and end apart: 77, of which 35 were waited for; matrix products, arithmetic and copies ran while one was open for 11% of the time, Pallas kernels for 36%

profile of v3, /device:TPU:0, one launch (start us, length us, event | category | flops | bytes accessed | tf_op | source)
XLA Modules:
  0.0 750.9 jit_solution(365593017205599536)
XLA Ops:
  25.6 3.7 collective-permute-done.1.arrived_ref
  45.6 6.7 collective-permute-done.5
  54.1 4.0 collective-permute-start.7
  58.1 17.9 %gather_fusion.5 = bf16[1024,1024]{1,0:T(8,128)(2,1)} fusion(bf16[12544,1024]{1,0:T(8,128)(2,1)} %table_ref.7, s32[1024]{0:T(1024)S(1)} %broadcast_clamp_fusion), kind=kCustom, calls=%fused_computation.5 | custom fusion | bytes 4198400 | tf_op jit(solution)/shard_map/jit(_take)/gather | solution.py:1059
  78.6 11.6 %collective-permute-done.10 = bf16[4,1,64,1024]{3,2,0,1:T(8,128)(2,1)S(1)} collective-permute-done((bf16[4,1,64,1024]{3,2,0,1:T(8,128)(2,1)S(1)}, bf16[4,1,64,1024]{3,2,0,1:T(8,128)(2,1)S(1)}, u32[]{:S(2)}, u32[]{:S(2)}) %collective-permute-start.10) | collective-permute-done | bytes 524320 | tf_op jit(solution)/shard_map/ppermute | solution.py:67
  91.1 5.1 attend_forward.3
  97.1 3.3 product_halves.5
  113.9 4.0 pick.1
  117.9 3.7 collective-permute-done.12.arrived_ref
  127.1 11.9 %collective-permute-done.13.refs_1_ = bf16[256,1024]{1,0:T(8,128)(2,1)S(1)} collective-permute-done((bf16[256,1024]{1,0:T(8,128)(2,1)}, bf16[256,1024]{1,0:T(8,128)(2,1)S(1)}, u32[]{:S(2)}, u32[]{:S(2)}) %collective-permute-start.13) | collective-permute-done | bytes 524320 | tf_op jit(solution)/shard_map/ppermute | solution.py:67
  141.6 9.7 %feed_forward.1 = (bf16[1024,1024]{1,0:T(8,128)(2,1)}, f32[1024,1024]{1,0:T(8,128)}, bf16[1024,1024]{1,0:T(8,128)(2,1)}, bf16[512,1024]{1,0:T(8,128)(2,1)}, f32[512,1024]{1,0:T(8,128)}) custom-call(bf16[256,1024]{1,0:T(8,128)(2,1)} %get-tuple-element.496.refs_0_, bf16[256,1024]{1,0:T(8,128)(2,1)} %copy-done.79, bf16[256,1024]{1,0:T(8,128)(2,1)} %copy-done.80, ...), custom_call_target="tpu_custom_call" | custom-call | tf_op jit(solution)/shard_map/feed_forward/pallas_call | solution.py:131
  161.7 10.9 %collective-permute-done.17.arrived_ref = bf16[256,1024]{1,0:T(8,128)(2,1)S(1)} collective-permute-done((bf16[256,1024]{1,0:T(8,128)(2,1)}, bf16[256,1024]{1,0:T(8,128)(2,1)S(1)}, u32[]{:S(2)}, u32[]{:S(2)}) %collective-permute-start.17) | collective-permute-done | bytes 524320 | tf_op jit(solution)/shard_map/ppermute | solution.py:67
  173.4 3.4 norm_forward.5
  178.3 11.9 %collective-permute-done.18.refs_1_ = bf16[256,1024]{1,0:T(8,128)(2,1)S(1)} collective-permute-done((bf16[256,1024]{1,0:T(8,128)(2,1)}, bf16[256,1024]{1,0:T(8,128)(2,1)S(1)}, u32[]{:S(2)}, u32[]{:S(2)}) %collective-permute-start.18) | collective-permute-done | bytes 524320 | tf_op jit(solution)/shard_map/ppermute | solution.py:67
  198.7 69.1 %vocab_forward.1 = (bf16[1024,12544]{1,0:T(8,128)(2,1)}, f32[1024,128]{1,0:T(8,128)}, f32[1024,1024]{1,0:T(8,128)}, f32[1024,128]{1,0:T(8,128)}) custom-call(bf16[1024,1024]{1,0:T(8,128)(2,1)} %copy-done.5, bf16[12544,1024]{1,0:T(8,128)(2,1)} %table_ref.7, s32[1024,128]{1,0:T(8,128)} %broadcast_in_dim.158.label_ref), custom_call_target="tpu_custom_call" | custom-call | tf_op jit(solution)/shard_map/vocab_forward/pallas_call | solution.py:461
  298.6 4.3 select_reduce_fusion
  325.8 19.8 %half_slope.3 = (bf16[1792,512]{1,0:T(8,128)(2,1)}, bf16[1792,512]{1,0:T(8,128)(2,1)}) custom-call(s32[1]{0:T(128)S(6)} %mul.210.base_ref, bf16[1024,12544]{1,0:T(8,128)(2,1)} %get-tuple-element.554.weight_ref, bf16[12544,1024]{1,0:T(8,128)(2,1)} %table_ref.7, f32[1024,128]{1,0:T(8,128)} %exponential_multiply_fusion.factor_ref, s32[1024,1]{1,0:T(8,128)} %copy-done.35, ...), custom_call_target="tpu_custom_call" | custom-call | tf_op jit(solution)/shard_map/half_slope/pallas_call | solution.py:823
  345.6 3.8 norm_backward.3
  351.6 19.9 %half_slope.4 = (bf16[1792,512]{1,0:T(8,128)(2,1)}, bf16[1792,512]{1,0:T(8,128)(2,1)}) custom-call(s32[1]{0:T(128)S(6)} %mul.210.base_ref, bf16[1024,12544]{1,0:T(8,128)(2,1)} %get-tuple-element.554.weight_ref, bf16[12544,1024]{1,0:T(8,128)(2,1)} %table_ref.7, f32[1024,128]{1,0:T(8,128)} %exponential_multiply_fusion.factor_ref, s32[1024,1]{1,0:T(8,128)} %copy-done.35, ...), custom_call_target="tpu_custom_call" | custom-call | tf_op jit(solution)/shard_map/half_slope/pallas_call | solution.py:823
  374.3 11.1 %feed_backward.1 = (bf16[1024,1024]{1,0:T(8,128)(2,1)}, bf16[1024,1024]{1,0:T(8,128)(2,1)}, f32[1,1024]{1,0:T(1,128)}, bf16[512,1024]{1,0:T(8,128)(2,1)}, f32[512,1024]{1,0:T(8,128)}) custom-call(bf16[256,1024]{1,0:T(8,128)(2,1)} %get-tuple-element.585.refs_0_, bf16[256,1024]{1,0:T(8,128)(2,1)} %copy-done.64, bf16[256,1024]{1,0:T(8,128)(2,1)} %copy-done.66, ...), custom_call_target="tpu_custom_call" | custom-call | tf_op jit(solution)/shard_map/feed_backward/pallas_call | solution.py:131
  385.8 6.6 collective-permute-done.36.arrived_ref
  397.1 9.7 %slope_group.3 = (bf16[2048,512]{1,0:T(8,128)(2,1)}, bf16[2048,512]{1,0:T(8,128)(2,1)}) custom-call(s32[8]{0:T(128)} %get-tuple-element.1034.order_ref, bf16[1024,1024]{1,0:T(8,128)(2,1)} %get-tuple-element.607.refs_0_, bf16[1024,1024]{1,0:T(8,128)(2,1)} %get-tuple-element.608.refs_1_, bf16[1024,1024]{1,0:T(8,128)(2,1)} %get-tuple-element.609.refs_2_, ...), custom_call_target="tpu_custom_call" | custom-call | tf_op jit(solution)/shard_map/slope_group/pallas_call | solution.py:573
  410.0 4.0 norm_backward.4
  415.2 27.0 %half_slope.5 = (bf16[2688,512]{1,0:T(8,128)(2,1)}, bf16[2688,512]{1,0:T(8,128)(2,1)}) custom-call(s32[1]{0:T(128)S(6)} %mul.210.base_ref, bf16[1024,12544]{1,0:T(8,128)(2,1)} %get-tuple-element.554.weight_ref, bf16[12544,1024]{1,0:T(8,128)(2,1)} %table_ref.7, f32[1024,128]{1,0:T(8,128)} %exponential_multiply_fusion.factor_ref, s32[1024,1]{1,0:T(8,128)} %copy-done.35, ...), custom_call_target="tpu_custom_call" | custom-call | tf_op jit(solution)/shard_map/half_slope/pallas_call | solution.py:823
  445.2 3.7 project.4
  448.9 13.0 %attend_backward.2 = (bf16[8,256,256]{2,1,0:T(8,128)(2,1)}, bf16[2,256,256]{2,1,0:T(8,128)(2,1)}, bf16[2,256,256]{2,1,0:T(8,128)(2,1)}) custom-call(s32[4]{0:T(128)} %copy-done.28, s32[4]{0:T(128)} %stores_ref.3, s32[4]{0:T(128)} %gather_fusion.2, bf16[8,256,256]{2,1,0:T(8,128)(2,1)} %copy-done.4, bf16[2,256,256]{2,1,0:T(8,128)(2,1)} %bitcast.206, ...), custom_call_target="tpu_custom_call" | custom-call | tf_op jit(solution)/shard_map/attend_backward/pallas_call | solution.py:683
  469.0 9.1 %collective-permute-done.41.arrived_ref = bf16[1024,256]{1,0:T(8,128)(2,1)S(1)} collective-permute-done((bf16[1024,256]{1,0:T(8,128)(2,1)S(1)}, bf16[1024,256]{1,0:T(8,128)(2,1)S(1)}, u32[]{:S(2)}, u32[]{:S(2)}) %collective-permute-start.41) | collective-permute-done | bytes 524320 | tf_op jit(solution)/shard_map/ppermute | solution.py:67
  486.8 8.8 %collective-permute-done.44.arrived_ref = bf16[512,256]{1,0:T(8,128)(2,1)S(1)} collective-permute-done((bf16[512,256]{1,0:T(8,128)(2,1)}, bf16[512,256]{1,0:T(8,128)(2,1)S(1)}, u32[]{:S(2)}, u32[]{:S(2)}) %collective-permute-start.44) | collective-permute-done | bytes 262176 | tf_op jit(solution)/shard_map/ppermute | solution.py:67
  499.6 4.1 add_columns.13
  503.6 4.0 add_columns.12
  508.7 4.3 add_columns.14
  548.6 4.3 attend_backward.3
  552.9 3.5 product_halves.7
  558.4 6.9 slope_group.4
  567.5 3.6 add_columns.15
  575.1 3.8 slope_group.5
  580.5 4.6 add_columns.16
  586.2 3.6 add_columns.17
  595.1 24.6 %collective-permute-done.63.arrived_ref = bf16[2048,256]{1,0:T(8,128)(2,1)} collective-permute-done((bf16[2048,256]{1,0:T(8,128)(2,1)}, bf16[2048,256]{1,0:T(8,128)(2,1)}, u32[]{:S(2)}, u32[]{:S(2)}) %collective-permute-start.63) | collective-permute-done | bytes 1048608 | tf_op jit(solution)/shard_map/ppermute | solution.py:67
  619.7 3.6 add_columns.18
  623.3 3.7 add_columns.19
  630.1 4.7 collective-permute-start.71
  635.6 3.8 add_columns.20
  644.8 22.9 %all-reduce.2.cloned.1.call-done = bf16[2,256,1024]{2,1,0:T(8,128)(2,1)} async-done(((bf16[2,256,1024]{2,1,0:T(8,128)(2,1)}), bf16[2,256,1024]{2,1,0:T(8,128)(2,1)}) %all-reduce.2.cloned.1.call-update) | async-done | bytes 1048592 | tf_op jit(solution)/shard_map/psum | solution.py:1353
  674.8 3.6 add_columns.22
  682.8 19.9 %collective-permute-done.69.refs_1_ = bf16[2048,128]{1,0:T(8,128)(2,1)S(1)} collective-permute-done((bf16[2048,128]{1,0:T(8,128)(2,1)}, bf16[2048,128]{1,0:T(8,128)(2,1)S(1)}, u32[]{:S(2)}, u32[]{:S(2)}) %collective-permute-start.69) | collective-permute-done | bytes 524320 | tf_op jit(solution)/shard_map/ppermute | solution.py:67
  707.8 11.7 %collective-permute-done.75.refs_5_ = bf16[2688,128]{1,0:T(8,128)(2,1)S(1)} collective-permute-done((bf16[2688,128]{1,0:T(8,128)(2,1)}, bf16[2688,128]{1,0:T(8,128)(2,1)S(1)}, u32[]{:S(2)}, u32[]{:S(2)}) %collective-permute-start.75) | collective-permute-done | bytes 688160 | tf_op jit(solution)/shard_map/ppermute | solution.py:67
  719.6 5.6 collective-permute-done.74.refs_1_
  (586 shorter events, 269.1 us)
Async XLA Ops:
  7.2 660.5 %all-reduce.2.cloned.1.call-start = ((), (), s32[]{:S(2)}) async-start(), calls=%async_computation | async-start | bytes 2097152 | tf_op jit(solution)/shard_map/psum | solution.py:1353
  42.7 9.6 %collective-permute-start.5 = (bf16[1,1,256,256]{3,2,0,1:T(8,128)(2,1)}, bf16[1,1,256,256]{3,2,0,1:T(8,128)(2,1)S(1)}, u32[]{:S(2)}, u32[]{:S(2)}) collective-permute-start(bf16[1,1,256,256]{3,2,0,1:T(8,128)(2,1)} %bitcast.231), channel_id=1, source_target_pairs={{0,16},{4,20},{8,24},{12,28},{16,0},{20,4},{24,8},{28,12},{1,17},{... | collective-permute-start | bytes 393224 | tf_op jit(solution)/shard_map/ppermute | solution.py:67
  52.4 24.3 %collective-permute-start.8 = (bf16[2,1,64,1024]{3,2,0,1:T(8,128)(2,1)S(1)}, bf16[2,1,64,1024]{3,2,0,1:T(8,128)(2,1)S(1)}, u32[]{:S(2)}, u32[]{:S(2)}) collective-permute-start(bf16[2,1,64,1024]{3,2,0,1:T(8,128)(2,1)S(1)} %pad_maximum_fusion.4), channel_id=1, source_target_pairs={{0,16},{4,20},{8,24},{12,28},{16,0},{20,4},{24,8},{28,12},{1,17},{... | collective-permute-start | bytes 786440 | tf_op jit(solution)/shard_map/ppermute | solution.py:67
  54.1 22.6 %collective-permute-start.7 = (bf16[2,1,256,256]{3,2,0,1:T(8,128)(2,1)}, bf16[2,1,256,256]{3,2,0,1:T(8,128)(2,1)S(1)}, u32[]{:S(2)}, u32[]{:S(2)}) collective-permute-start(bf16[2,1,256,256]{3,2,0,1:T(8,128)(2,1)} %pad_maximum_fusion.3), channel_id=1, source_target_pairs={{0,8},{4,12},{8,0},{12,4},{16,24},{20,28},{24,16},{28,20},{1,9},{5... | collective-permute-start | bytes 786440 | tf_op jit(solution)/shard_map/ppermute | solution.py:67
  76.8 13.4 %collective-permute-start.10 = (bf16[4,1,64,1024]{3,2,0,1:T(8,128)(2,1)S(1)}, bf16[4,1,64,1024]{3,2,0,1:T(8,128)(2,1)S(1)}, u32[]{:S(2)}, u32[]{:S(2)}) collective-permute-start(bf16[4,1,64,1024]{3,2,0,1:T(8,128)(2,1)S(1)} %pad_maximum_fusion.1), channel_id=1, source_target_pairs={{0,8},{4,12},{8,0},{12,4},{16,24},{20,28},{24,16},{28,20},{1,9},{5... | collective-permute-start | bytes 1572872 | tf_op jit(solution)/shard_map/ppermute | solution.py:67
  76.9 14.1 %collective-permute-start.9 = (bf16[4,1,256,256]{3,2,0,1:T(8,128)(2,1)S(1)}, bf16[4,1,256,256]{3,2,0,1:T(8,128)(2,1)S(1)}, u32[]{:S(2)}, u32[]{:S(2)}) collective-permute-start(bf16[4,1,256,256]{3,2,0,1:T(8,128)(2,1)S(1)} %pad_maximum_fusion), channel_id=1, source_target_pairs={{0,4},{4,0},{8,12},{12,8},{16,20},{20,16},{24,28},{28,24},{1,5},{5... | collective-permute-start | bytes 1572872 | tf_op jit(solution)/shard_map/ppermute | solution.py:67
  107.4 14.2 %collective-permute-start.12 = (bf16[256,1024]{1,0:T(8,128)(2,1)}, bf16[256,1024]{1,0:T(8,128)(2,1)S(1)}, u32[]{:S(2)}, u32[]{:S(2)}) collective-permute-start(bf16[256,1024]{1,0:T(8,128)(2,1)} %get-tuple-element.486), channel_id=1, source_target_pairs={{0,2},{1,3},{2,0},{3,1},{4,6},{5,7},{6,4},{7,5},{8,10},{9,11},{10,... | collective-permute-start | bytes 1572872 | tf_op jit(solution)/shard_map/ppermute | solution.py:67
  125.6 13.3 %collective-permute-start.13 = (bf16[256,1024]{1,0:T(8,128)(2,1)}, bf16[256,1024]{1,0:T(8,128)(2,1)S(1)}, u32[]{:S(2)}, u32[]{:S(2)}) collective-permute-start(bf16[256,1024]{1,0:T(8,128)(2,1)} %get-tuple-element.496.refs_0_), channel_id=1, source_target_pairs={{0,2},{1,3},{2,0},{3,1},{4,6},{5,7},{6,4},{7,5},{8,10},{9,11},{10,... | collective-permute-start | bytes 1572872 | tf_op jit(solution)/shard_map/ppermute | solution.py:67
  127.1 12.5 %collective-permute-start.14 = (bf16[256,1024]{1,0:T(8,128)(2,1)}, bf16[256,1024]{1,0:T(8,128)(2,1)S(1)}, u32[]{:S(2)}, u32[]{:S(2)}) collective-permute-start(bf16[256,1024]{1,0:T(8,128)(2,1)} %get-tuple-element.496.refs_0_), channel_id=1, source_target_pairs={{0,1},{1,0},{2,3},{3,2},{4,5},{5,4},{6,7},{7,6},{8,9},{9,8},{10,11... | collective-permute-start | bytes 1572872 | tf_op jit(solution)/shard_map/ppermute | solution.py:67
  158.4 14.2 %collective-permute-start.17 = (bf16[256,1024]{1,0:T(8,128)(2,1)}, bf16[256,1024]{1,0:T(8,128)(2,1)S(1)}, u32[]{:S(2)}, u32[]{:S(2)}) collective-permute-start(bf16[256,1024]{1,0:T(8,128)(2,1)} %get-tuple-element.511), channel_id=1, source_target_pairs={{0,2},{1,3},{2,0},{3,1},{4,6},{5,7},{6,4},{7,5},{8,10},{9,11},{10,... | collective-permute-start | bytes 1572872 | tf_op jit(solution)/shard_map/ppermute | solution.py:67
  176.8 13.3 %collective-permute-start.18 = (bf16[256,1024]{1,0:T(8,128)(2,1)}, bf16[256,1024]{1,0:T(8,128)(2,1)S(1)}, u32[]{:S(2)}, u32[]{:S(2)}) collective-permute-start(bf16[256,1024]{1,0:T(8,128)(2,1)} %get-tuple-element.532.refs_0_), channel_id=1, source_target_pairs={{0,2},{1,3},{2,0},{3,1},{4,6},{5,7},{6,4},{7,5},{8,10},{9,11},{10,... | collective-permute-start | bytes 1572872 | tf_op jit(solution)/shard_map/ppermute | solution.py:67
  178.3 12.0 %collective-permute-start.19 = (bf16[256,1024]{1,0:T(8,128)(2,1)}, bf16[256,1024]{1,0:T(8,128)(2,1)S(1)}, u32[]{:S(2)}, u32[]{:S(2)}) collective-permute-start(bf16[256,1024]{1,0:T(8,128)(2,1)} %get-tuple-element.532.refs_0_), channel_id=1, source_target_pairs={{0,1},{1,0},{2,3},{3,2},{4,5},{5,4},{6,7},{7,6},{8,9},{9,8},{10,11... | collective-permute-start | bytes 1572872 | tf_op jit(solution)/shard_map/ppermute | solution.py:67
  192.0 76.5 %collective-permute-start.21 = (bf16[256,1024]{1,0:T(8,128)(2,1)}, bf16[256,1024]{1,0:T(8,128)(2,1)S(1)}, u32[]{:S(2)}, u32[]{:S(2)}) collective-permute-start(bf16[256,1024]{1,0:T(8,128)(2,1)} %get-tuple-element.532.refs_0_), channel_id=1, source_target_pairs={{0,16},{4,20},{8,24},{12,28},{16,0},{20,4},{24,8},{28,12},{1,17},{... | collective-permute-start | bytes 1572872 | tf_op jit(solution)/shard_map/ppermute | solution.py:67
  271.0 8.5 %collective-permute-start.26 = (f32[3,4,4,64]{3,2,1,0:T(4,128)S(1)}, f32[3,4,4,64]{3,2,1,0:T(4,128)S(1)}, u32[]{:S(2)}, u32[]{:S(2)}) collective-permute-start(f32[3,4,4,64]{3,2,1,0:T(4,128)S(1)} %pad_maximum_fusion.7), channel_id=1, source_target_pairs={{0,2},{1,3},{2,0},{3,1},{4,6},{5,7},{6,4},{7,5},{8,10},{9,11},{10,... | collective-permute-start | bytes 36872 | tf_op jit(solution)/shard_map/ppermute | solution.py:67
  273.7 13.7 %collective-permute-start.22 = (bf16[256,1024]{1,0:T(8,128)(2,1)S(1)}, bf16[256,1024]{1,0:T(8,128)(2,1)S(1)}, u32[]{:S(2)}, u32[]{:S(2)}) collective-permute-start(bf16[256,1024]{1,0:T(8,128)(2,1)S(1)} %collective-permute-done.21.refs_0_), channel_id=1, source_target_pairs={{0,2},{1,3},{2,0},{3,1},{4,6},{5,7},{6,4},{7,5},{8,10},{9,11},{10,... | collective-permute-start | bytes 1572872 | tf_op jit(solution)/shard_map/ppermute | solution.py:67
  274.3 21.2 %collective-permute-start.23 = (bf16[256,1024]{1,0:T(8,128)(2,1)S(1)}, bf16[256,1024]{1,0:T(8,128)(2,1)S(1)}, u32[]{:S(2)}, u32[]{:S(2)}) collective-permute-start(bf16[256,1024]{1,0:T(8,128)(2,1)S(1)} %collective-permute-done.21.refs_0_), channel_id=1, source_target_pairs={{0,1},{1,0},{2,3},{3,2},{4,5},{5,4},{6,7},{7,6},{8,9},{9,8},{10,11... | collective-permute-start | bytes 1572872 | tf_op jit(solution)/shard_map/ppermute | solution.py:67
  287.5 8.0 %collective-permute-start.24 = (bf16[256,1024]{1,0:T(8,128)(2,1)S(1)}, bf16[256,1024]{1,0:T(8,128)(2,1)S(1)}, u32[]{:S(2)}, u32[]{:S(2)}) collective-permute-start(bf16[256,1024]{1,0:T(8,128)(2,1)S(1)} %collective-permute-done.22.refs_1_), channel_id=1, source_target_pairs={{0,1},{1,0},{2,3},{3,2},{4,5},{5,4},{6,7},{7,6},{8,9},{9,8},{10,11... | collective-permute-start | bytes 1572872 | tf_op jit(solution)/shard_map/ppermute | solution.py:67
  315.2 30.5 %collective-permute-start.31 = (bf16[256,1024]{1,0:T(8,128)(2,1)}, bf16[256,1024]{1,0:T(8,128)(2,1)}, u32[]{:S(2)}, u32[]{:S(2)}) collective-permute-start(bf16[256,1024]{1,0:T(8,128)(2,1)} %get-tuple-element.553), channel_id=1, source_target_pairs={{0,2},{1,3},{2,0},{3,1},{4,6},{5,7},{6,4},{7,5},{8,10},{9,11},{10,... | collective-permute-start | bytes 1572872 | tf_op jit(solution)/shard_map/ppermute | solution.py:67
  349.4 22.0 %collective-permute-start.32 = (bf16[256,1024]{1,0:T(8,128)(2,1)}, bf16[256,1024]{1,0:T(8,128)(2,1)S(1)}, u32[]{:S(2)}, u32[]{:S(2)}) collective-permute-start(bf16[256,1024]{1,0:T(8,128)(2,1)} %get-tuple-element.585.refs_0_), channel_id=1, source_target_pairs={{0,2},{1,3},{2,0},{3,1},{4,6},{5,7},{6,4},{7,5},{8,10},{9,11},{10,... | collective-permute-start | bytes 1572872 | tf_op jit(solution)/shard_map/ppermute | solution.py:67
  350.9 41.5 %collective-permute-start.36 = (bf16[1792,512]{1,0:T(8,128)(2,1)S(1)}, bf16[1792,512]{1,0:T(8,128)(2,1)S(1)}, u32[]{:S(2)}, u32[]{:S(2)}) collective-permute-start(bf16[1792,512]{1,0:T(8,128)(2,1)S(1)} %copy-done.116), channel_id=1, source_target_pairs={{0,4},{4,0},{8,12},{12,8},{16,20},{20,16},{24,28},{28,24},{1,5},{5... | collective-permute-start | bytes 5505032 | tf_op jit(solution)/shard_map/ppermute | solution.py:67
  351.6 20.5 %collective-permute-start.33 = (bf16[256,1024]{1,0:T(8,128)(2,1)}, bf16[256,1024]{1,0:T(8,128)(2,1)S(1)}, u32[]{:S(2)}, u32[]{:S(2)}) collective-permute-start(bf16[256,1024]{1,0:T(8,128)(2,1)} %get-tuple-element.585.refs_0_), channel_id=1, source_target_pairs={{0,1},{1,0},{2,3},{3,2},{4,5},{5,4},{6,7},{7,6},{8,9},{9,8},{10,11... | collective-permute-start | bytes 1572872 | tf_op jit(solution)/shard_map/ppermute | solution.py:67
  396.5 12.7 %collective-permute-start.37 = (bf16[256,1024]{1,0:T(8,128)(2,1)}, bf16[256,1024]{1,0:T(8,128)(2,1)S(1)}, u32[]{:S(2)}, u32[]{:S(2)}) collective-permute-start(bf16[256,1024]{1,0:T(8,128)(2,1)} %get-tuple-element.604), channel_id=1, source_target_pairs={{0,2},{1,3},{2,0},{3,1},{4,6},{5,7},{6,4},{7,5},{8,10},{9,11},{10,... | collective-permute-start | bytes 1572872 | tf_op jit(solution)/shard_map/ppermute | solution.py:67
  406.8 62.3 %collective-permute-start.42 = (bf16[2048,512]{1,0:T(8,128)(2,1)}, bf16[2048,512]{1,0:T(8,128)(2,1)}, u32[]{:S(2)}, u32[]{:S(2)}) collective-permute-start(bf16[2048,512]{1,0:T(8,128)(2,1)} %get-tuple-element.640), channel_id=1, source_target_pairs={{0,8},{4,12},{8,0},{12,4},{16,24},{20,28},{24,16},{28,20},{1,9},{5... | collective-permute-start | bytes 6291464 | tf_op jit(solution)/shard_map/ppermute | solution.py:67
  414.0 28.2 %collective-permute-start.38 = (bf16[256,1024]{1,0:T(8,128)(2,1)}, bf16[256,1024]{1,0:T(8,128)(2,1)S(1)}, u32[]{:S(2)}, u32[]{:S(2)}) collective-permute-start(bf16[256,1024]{1,0:T(8,128)(2,1)} %get-tuple-element.631.refs_0_), channel_id=1, source_target_pairs={{0,2},{1,3},{2,0},{3,1},{4,6},{5,7},{6,4},{7,5},{8,10},{9,11},{10,... | collective-permute-start | bytes 1572872 | tf_op jit(solution)/shard_map/ppermute | solution.py:67
  414.6 54.5 %collective-permute-start.43 = (bf16[1792,512]{1,0:T(8,128)(2,1)S(1)}, bf16[1792,512]{1,0:T(8,128)(2,1)S(1)}, u32[]{:S(2)}, u32[]{:S(2)}) collective-permute-start(bf16[1792,512]{1,0:T(8,128)(2,1)S(1)} %copy-done.115), channel_id=1, source_target_pairs={{0,4},{4,0},{8,12},{12,8},{16,20},{20,16},{24,28},{28,24},{1,5},{5... | collective-permute-start | bytes 5505032 | tf_op jit(solution)/shard_map/ppermute | solution.py:67
  415.2 27.6 %collective-permute-start.39 = (bf16[256,1024]{1,0:T(8,128)(2,1)}, bf16[256,1024]{1,0:T(8,128)(2,1)S(1)}, u32[]{:S(2)}, u32[]{:S(2)}) collective-permute-start(bf16[256,1024]{1,0:T(8,128)(2,1)} %get-tuple-element.631.refs_0_), channel_id=1, source_target_pairs={{0,1},{1,0},{2,3},{3,2},{4,5},{5,4},{6,7},{7,6},{8,9},{9,8},{10,11... | collective-permute-start | bytes 1572872 | tf_op jit(solution)/shard_map/ppermute | solution.py:67
  463.9 14.2 %collective-permute-start.41 = (bf16[1024,256]{1,0:T(8,128)(2,1)S(1)}, bf16[1024,256]{1,0:T(8,128)(2,1)S(1)}, u32[]{:S(2)}, u32[]{:S(2)}) collective-permute-start(bf16[1024,256]{1,0:T(8,128)(2,1)S(1)} %bitcast.244), channel_id=1, source_target_pairs={{0,8},{4,12},{8,0},{12,4},{16,24},{20,28},{24,16},{28,20},{1,9},{5... | collective-permute-start | bytes 1572872 | tf_op jit(solution)/shard_map/ppermute | solution.py:67
  467.6 16.1 %collective-permute-start.45 = (bf16[256,1024]{1,0:T(8,128)(2,1)}, bf16[256,1024]{1,0:T(8,128)(2,1)S(1)}, u32[]{:S(2)}, u32[]{:S(2)}) collective-permute-start(bf16[256,1024]{1,0:T(8,128)(2,1)} %bitcast.288), channel_id=1, source_target_pairs={{0,4},{4,0},{8,12},{12,8},{16,20},{20,16},{24,28},{28,24},{1,5},{5... | collective-permute-start | bytes 1572872 | tf_op jit(solution)/shard_map/ppermute | solution.py:67
  481.1 14.5 %collective-permute-start.44 = (bf16[512,256]{1,0:T(8,128)(2,1)}, bf16[512,256]{1,0:T(8,128)(2,1)S(1)}, u32[]{:S(2)}, u32[]{:S(2)}) collective-permute-start(bf16[512,256]{1,0:T(8,128)(2,1)} %get-tuple-element.656), channel_id=1, source_target_pairs={{0,16},{4,20},{8,24},{12,28},{16,0},{20,4},{24,8},{28,12},{1,17},{... | collective-permute-start | bytes 786440 | tf_op jit(solution)/shard_map/ppermute | solution.py:67
  498.2 9.5 %collective-permute-start.46 = (bf16[256,256]{1,0:T(8,128)(2,1)}, bf16[256,256]{1,0:T(8,128)(2,1)}, u32[]{:S(2)}, u32[]{:S(2)}) collective-permute-start(bf16[256,256]{1,0:T(8,128)(2,1)} %get-tuple-element.670), channel_id=1, source_target_pairs={{0,4},{4,0},{8,12},{12,8},{16,20},{20,16},{24,28},{28,24},{1,5},{5... | collective-permute-start | bytes 393224 | tf_op jit(solution)/shard_map/ppermute | solution.py:67
  507.7 71.3 %collective-permute-start.59 = (bf16[2688,512]{1,0:T(8,128)(2,1)}, bf16[2688,512]{1,0:T(8,128)(2,1)S(1)}, u32[]{:S(2)}, u32[]{:S(2)}) collective-permute-start(bf16[2688,512]{1,0:T(8,128)(2,1)} %get-tuple-element.769), channel_id=1, source_target_pairs={{0,4},{4,0},{8,12},{12,8},{16,20},{20,16},{24,28},{28,24},{1,5},{5... | collective-permute-start | bytes 8257544 | tf_op jit(solution)/shard_map/ppermute | solution.py:67
  521.8 9.9 %collective-permute-start.50 = (bf16[64,1024]{1,0:T(8,128)(2,1)}, bf16[64,1024]{1,0:T(8,128)(2,1)S(1)}, u32[]{:S(2)}, u32[]{:S(2)}) collective-permute-start(bf16[64,1024]{1,0:T(8,128)(2,1)} %get-tuple-element.706), channel_id=1, source_target_pairs={{0,16},{4,20},{8,24},{12,28},{16,0},{20,4},{24,8},{28,12},{1,17},{... | collective-permute-start | bytes 393224 | tf_op jit(solution)/shard_map/ppermute | solution.py:67
  527.8 39.0 %collective-permute-start.55 = (bf16[1792,256]{1,0:T(8,128)(2,1)}, bf16[1792,256]{1,0:T(8,128)(2,1)}, u32[]{:S(2)}, u32[]{:S(2)}) collective-permute-start(bf16[1792,256]{1,0:T(8,128)(2,1)} %get-tuple-element.732), channel_id=1, source_target_pairs={{0,8},{4,12},{8,0},{12,4},{16,24},{20,28},{24,16},{28,20},{1,9},{5... | collective-permute-start | bytes 2752520 | tf_op jit(solution)/shard_map/ppermute | solution.py:67
  543.1 13.5 %collective-permute-start.57 = (f32[9,1024]{1,0:T(8,128)}, f32[9,1024]{1,0:T(8,128)}, u32[]{:S(2)}, u32[]{:S(2)}) collective-permute-start(f32[9,1024]{1,0:T(8,128)} %fusion.57), channel_id=1, source_target_pairs={{0,1},{1,0},{2,3},{3,2},{4,5},{5,4},{6,7},{7,6},{8,9},{9,8},{10,11... | collective-permute-start | bytes 110600 | tf_op jit(solution)/shard_map/ppermute | solution.py:67
  544.6 41.6 %collective-permute-start.65 = (bf16[1792,256]{1,0:T(8,128)(2,1)}, bf16[1792,256]{1,0:T(8,128)(2,1)}, u32[]{:S(2)}, u32[]{:S(2)}) collective-permute-start(bf16[1792,256]{1,0:T(8,128)(2,1)} %get-tuple-element.789), channel_id=1, source_target_pairs={{0,8},{4,12},{8,0},{12,4},{16,24},{20,28},{24,16},{28,20},{1,9},{5... | collective-permute-start | bytes 2752520 | tf_op jit(solution)/shard_map/ppermute | solution.py:67
  556.4 14.7 %collective-permute-start.54 = (bf16[128,1024]{1,0:T(8,128)(2,1)}, bf16[128,1024]{1,0:T(8,128)(2,1)}, u32[]{:S(2)}, u32[]{:S(2)}) collective-permute-start(bf16[128,1024]{1,0:T(8,128)(2,1)} %get-tuple-element.731), channel_id=1, source_target_pairs={{0,1},{1,0},{2,3},{3,2},{4,5},{5,4},{6,7},{7,6},{8,9},{9,8},{10,11... | collective-permute-start | bytes 786440 | tf_op jit(solution)/shard_map/ppermute | solution.py:67
  565.3 58.1 %collective-permute-start.62 = (bf16[1280,512]{1,0:T(8,128)(2,1)}, bf16[1280,512]{1,0:T(8,128)(2,1)}, u32[]{:S(2)}, u32[]{:S(2)}) collective-permute-start(bf16[1280,512]{1,0:T(8,128)(2,1)} %get-tuple-element.784), channel_id=1, source_target_pairs={{0,4},{4,0},{8,12},{12,8},{16,20},{20,16},{24,28},{28,24},{1,5},{5... | collective-permute-start | bytes 3932168 | tf_op jit(solution)/shard_map/ppermute | solution.py:67
  566.9 52.8 %collective-permute-start.63 = (bf16[2048,256]{1,0:T(8,128)(2,1)}, bf16[2048,256]{1,0:T(8,128)(2,1)}, u32[]{:S(2)}, u32[]{:S(2)}) collective-permute-start(bf16[2048,256]{1,0:T(8,128)(2,1)} %get-tuple-element.786), channel_id=1, source_target_pairs={{0,4},{4,0},{8,12},{12,8},{16,20},{20,16},{24,28},{28,24},{1,5},{5... | collective-permute-start | bytes 3145736 | tf_op jit(solution)/shard_map/ppermute | solution.py:67
  585.1 49.7 %collective-permute-start.61 = (bf16[2688,256]{1,0:T(8,128)(2,1)}, bf16[2688,256]{1,0:T(8,128)(2,1)}, u32[]{:S(2)}, u32[]{:S(2)}) collective-permute-start(bf16[2688,256]{1,0:T(8,128)(2,1)} %get-tuple-element.782), channel_id=1, source_target_pairs={{0,8},{4,12},{8,0},{12,4},{16,24},{20,28},{24,16},{28,20},{1,9},{5... | collective-permute-start | bytes 4128776 | tf_op jit(solution)/shard_map/ppermute | solution.py:67
  590.4 48.9 %collective-permute-start.58 = (bf16[784,512]{1,0:T(8,128)(2,1)}, bf16[784,512]{1,0:T(8,128)(2,1)}, u32[]{:S(2)}, u32[]{:S(2)}) collective-permute-start(bf16[784,512]{1,0:T(8,128)(2,1)} %get-tuple-element.767), channel_id=1, source_target_pairs={{0,4},{4,0},{8,12},{12,8},{16,20},{20,16},{24,28},{28,24},{1,5},{5... | collective-permute-start | bytes 2408456 | tf_op jit(solution)/shard_map/ppermute | solution.py:67
  593.4 48.4 %collective-permute-start.72 = (bf16[1792,128]{1,0:T(8,128)(2,1)}, bf16[1792,128]{1,0:T(8,128)(2,1)S(1)}, u32[]{:S(2)}, u32[]{:S(2)}) collective-permute-start(bf16[1792,128]{1,0:T(8,128)(2,1)} %get-tuple-element.825), channel_id=1, source_target_pairs={{0,16},{4,20},{8,24},{12,28},{16,0},{20,4},{24,8},{28,12},{1,17},{... | collective-permute-start | bytes 1376264 | tf_op jit(solution)/shard_map/ppermute | solution.py:67
  627.1 47.7 %collective-permute-start.70 = (bf16[1280,256]{1,0:T(8,128)(2,1)}, bf16[1280,256]{1,0:T(8,128)(2,1)}, u32[]{:S(2)}, u32[]{:S(2)}) collective-permute-start(bf16[1280,256]{1,0:T(8,128)(2,1)} %get-tuple-element.822), channel_id=1, source_target_pairs={{0,8},{4,12},{8,0},{12,4},{16,24},{20,28},{24,16},{28,20},{1,9},{5... | collective-permute-start | bytes 1966088 | tf_op jit(solution)/shard_map/ppermute | solution.py:67
  630.1 44.7 %collective-permute-start.71 = (bf16[1792,128]{1,0:T(8,128)(2,1)}, bf16[1792,128]{1,0:T(8,128)(2,1)S(1)}, u32[]{:S(2)}, u32[]{:S(2)}) collective-permute-start(bf16[1792,128]{1,0:T(8,128)(2,1)} %get-tuple-element.824), channel_id=1, source_target_pairs={{0,16},{4,20},{8,24},{12,28},{16,0},{20,4},{24,8},{28,12},{1,17},{... | collective-permute-start | bytes 1376264 | tf_op jit(solution)/shard_map/ppermute | solution.py:67
  634.8 67.9 %collective-permute-start.69 = (bf16[2048,128]{1,0:T(8,128)(2,1)}, bf16[2048,128]{1,0:T(8,128)(2,1)S(1)}, u32[]{:S(2)}, u32[]{:S(2)}) collective-permute-start(bf16[2048,128]{1,0:T(8,128)(2,1)} %get-tuple-element.821), channel_id=1, source_target_pairs={{0,16},{4,20},{8,24},{12,28},{16,0},{20,4},{24,8},{28,12},{1,17},{... | collective-permute-start | bytes 1572872 | tf_op jit(solution)/shard_map/ppermute | solution.py:67
  641.8 61.0 %collective-permute-start.68 = (bf16[784,256]{1,0:T(8,128)(2,1)}, bf16[784,256]{1,0:T(8,128)(2,1)}, u32[]{:S(2)}, u32[]{:S(2)}) collective-permute-start(bf16[784,256]{1,0:T(8,128)(2,1)} %get-tuple-element.819), channel_id=1, source_target_pairs={{0,8},{4,12},{8,0},{12,4},{16,24},{20,28},{24,16},{28,20},{1,9},{5... | collective-permute-start | bytes 1204232 | tf_op jit(solution)/shard_map/ppermute | solution.py:67
  641.8 77.8 %collective-permute-start.75 = (bf16[2688,128]{1,0:T(8,128)(2,1)}, bf16[2688,128]{1,0:T(8,128)(2,1)S(1)}, u32[]{:S(2)}, u32[]{:S(2)}) collective-permute-start(bf16[2688,128]{1,0:T(8,128)(2,1)} %get-tuple-element.841), channel_id=1, source_target_pairs={{0,16},{4,20},{8,24},{12,28},{16,0},{20,4},{24,8},{28,12},{1,17},{... | collective-permute-start | bytes 2064392 | tf_op jit(solution)/shard_map/ppermute | solution.py:67
  678.3 46.9 %collective-permute-start.74 = (bf16[1280,128]{1,0:T(8,128)(2,1)}, bf16[1280,128]{1,0:T(8,128)(2,1)}, u32[]{:S(2)}, u32[]{:S(2)}) collective-permute-start(bf16[1280,128]{1,0:T(8,128)(2,1)} %get-tuple-element.840), channel_id=1, source_target_pairs={{0,16},{4,20},{8,24},{12,28},{16,0},{20,4},{24,8},{28,12},{1,17},{... | collective-permute-start | bytes 983048 | tf_op jit(solution)/shard_map/ppermute | solution.py:67
  704.7 22.5 %collective-permute-start.73 = (bf16[784,128]{1,0:T(8,128)(2,1)}, bf16[784,128]{1,0:T(8,128)(2,1)S(1)}, u32[]{:S(2)}, u32[]{:S(2)}) collective-permute-start(bf16[784,128]{1,0:T(8,128)(2,1)} %get-tuple-element.839), channel_id=1, source_target_pairs={{0,16},{4,20},{8,24},{12,28},{16,0},{20,4},{24,8},{28,12},{1,17},{... | collective-permute-start | bytes 602120 | tf_op jit(solution)/shard_map/ppermute | solution.py:67
  (148 other events, 1881.1 us)
Sparse Core Ops, SparseCore 0:
  630.2 37.5 all-reduce.1

commit v4 on v3

--- a/solution.py
+++ b/solution.py
@@ -15,31 +15,37 @@
 bfloat = jnp.bfloat16
 
 CUTS = (0, 2, 4, 7)
-ORDERS = {"f": "z", "p": "y", "s": "y"}
+FREE = 99
+ORDERS = {"f": "z", "p": "y", "s": "z"}
+ORDERS = {"f": "z", "p": "y", "s": "z"}
 PLAN = (
     (),
+    (),
     (("a", "make"), ("a", "send"),),
+    (),
+    (),
+    (("f", "make"), ("f", "send"), ("a", "add"), ("a", "send"),),
+    (),
     (("b", "make"), ("b", "send"),),
     (),
-    (("a", "add"),),
-    (("f", "make"), ("f", "send"),),
     (),
-    (("c", "make"),),
-    (),
-    (),
-    (("t", "step"), ("b", "add"), ("f", "add"),),
-    (("t", "step"),),
-    (("a", "send"), ("b", "send"),),
+    (("t", "step"), ("f", "add"),),
+    (("t", "step"), ("c", "make"),),
+    (("a", "add"), ("a", "send"), ("b", "add"), ("b", "send"),),
     (("c", "send"), ("t", "step"), ("f", "send"),),
     (),
     (),
     (),
     (),
-    (("p", "make"), ("p", "send"), ("a", "add"), ("a", "send"),),
+    (("p", "make"), ("p", "send"), ("b", "add"), ("b", "send"),),
     (("s", "make"), ("s", "send"),),
-    (("c", "add"), ("c", "send"), ("b", "add"), ("b", "send"),),
+    (("f", "add"), ("f", "send"), ("c", "add"), ("c", "send"),),
     (),
-    (("f", "add"), ("f", "send"), ("p", "add"), ("p", "send"), ("c", "add"), ("c", "send"), ("s", "add"), ("s", "send"), ("a", "wait"), ("b", "wait"), ("p", "add"), ("p", "send"), ("f", "wait"), ("s", "add"), ("s", "send"), ("c", "wait"), ("p", "wait"), ("s", "wait"),),
+    (("p", "add"), ("p", "send"), ("a", "wait"), ("b", "wait"), ("s", "add"), ("s", "send"), ("c", "add"), ("c", "send"), ("p", "add"), ("p", "send"), ("f", "wait"), ("s", "add"), ("s", "send"), ("c", "wait"), ("p", "wait"), ("s", "wait"),),
+    (),
+    (),
+    (),
+    (),
 )
 single = jnp.float32
 
@@ -93,12 +99,14 @@
     return lax.optimization_barrier(values)
 
 
-def gather_both(owns, axis, count, orders):
+def gather_both_steps(owns, axis, count, orders):
     helds = [own[None] for own in owns]
     for bits in zip(*orders):
-        arrived = tie(*(swap(held, axis, count, bit) for held, bit in zip(helds, bits)))
+        arrived = [swap(held, axis, count, bit) for held, bit in zip(helds, bits)]
+        yield None
+        arrived = tie(*arrived)
         helds = [jnp.concatenate([held, more], 0) for held, more in zip(helds, arrived)]
-    return helds
+    yield helds
 
 
 def total_over(value, axis, count, order):
@@ -134,7 +142,7 @@
         out_specs=[VMEM] * len(outs),
         out_shape=[jax.ShapeDtypeStruct(shape, dtype) for shape, dtype in outs],
         scratch_shapes=list(scratch),
-        compiler_params=pltpu.CompilerParams(vmem_limit_bytes=56 * 1024 * 1024),
+        compiler_params=pltpu.CompilerParams(vmem_limit_bytes=16 * 1024 * 1024),
         cost_estimate=BRIEF,
         name=name,
     )(*operands)
@@ -174,10 +182,13 @@
 
 
 def norm_backward_kernel(count, *refs):
-    hidden_ref, gain_ref, out_ref, low_ref, sums_ref = refs[count:]
     upstream = refs[0][...].astype(single)
     for ref in refs[1:count]:
         upstream = upstream + ref[...].astype(single)
+    norm_backward_rows(upstream, *refs[count:])
+
+
+def norm_backward_rows(upstream, hidden_ref, gain_ref, out_ref, low_ref, sums_ref):
     hidden = hidden_ref[...]
     center = hidden - jnp.mean(hidden, -1, keepdims=True)
     spread = jnp.mean(center * center, -1, keepdims=True)
@@ -365,22 +376,9 @@
 
 def add_columns(kept, arrived):
     rows, width = kept.shape
-    block = rows
-    for count in (4, 3, 2):
-        if rows % (16 * count) == 0:
-            block = rows // count
-            break
-    whole = pl.BlockSpec((block, width), lambda i: (i, 0))
-    half = pl.BlockSpec((block, width // 2), lambda i: (i, 0))
-    return pl.pallas_call(
-        add_columns_kernel,
-        grid=(rows // block,),
-        in_specs=[whole, whole],
-        out_specs=[half, half],
-        out_shape=[jax.ShapeDtypeStruct((rows, width // 2), bfloat)] * 2,
-        cost_estimate=BRIEF,
-        name="add_columns",
-    )(kept, arrived)
+    return run_whole(
+        add_columns_kernel, "add_columns", [((rows, width // 2), bfloat)] * 2, kept, arrived
+    )
 
 
 def bin_rows_kernel(bins_ref, value_ref, sent_ref, kept_ref, sums):
@@ -400,7 +398,9 @@
         out_specs=[VMEM, VMEM],
         out_shape=[jax.ShapeDtypeStruct(shape, bfloat), jax.ShapeDtypeStruct(shape, single)],
         scratch_shapes=[pltpu.VMEM((count,) + value.shape[1:], single)],
-        compiler_params=pltpu.CompilerParams(vmem_limit_bytes=56 * 1024 * 1024),
+        compiler_params=pltpu.CompilerParams(
+            vmem_limit_bytes=8 * 1024 * 1024 + 6 * count * value.shape[1] * value.shape[2]
+        ),
         cost_estimate=BRIEF,
         name="bin_rows",
     )(bins, value)
@@ -413,7 +413,9 @@
     return vocab_share
 
 
-def vocab_forward_kernel(state_ref, table_ref, label_ref, weight_ref, sum_ref, mixed_ref, tops_ref, top):
+def vocab_forward_kernel(
+    state_ref, table_ref, label_ref, label_rows_ref, weight_ref, mixed_ref, tops_ref, stats_ref, top, sum_ref
+):
     step = pl.program_id(0)
     rows = state_ref.shape[0]
     tile = table_ref.shape[0]
@@ -452,8 +454,23 @@
             low, table_ref[...]
         )
 
-
-def vocab_forward(states, table, label):
+    @pl.when(step == pl.num_programs(0) - 1)
+    def finish():
+        label = label_ref[...]
+        entries = tile * pl.num_programs(0)
+        inside = (label >= 0) & (label < entries)
+        target = jnp.sum(
+            state_ref[...].astype(single) * label_rows_ref[...].astype(single), -1, keepdims=True
+        )
+        target = jnp.where(inside, target, 0.0)
+        total = jnp.sum(sum_ref[...], -1, keepdims=True)
+        total = total + jnp.where(inside, jnp.exp(target - top[...]), 0.0)
+        lanes = lax.broadcasted_iota(jnp.int32, label.shape, 1)
+        columns = jnp.where(lanes == 0, top[...], jnp.where(lanes == 1, total, target))
+        stats_ref[...] = jnp.swapaxes(columns, 0, 1)[:8, :]
+
+
+def vocab_forward(states, table, label, label_rows):
     rows, width = states.shape
     entries = table.shape[0]
     tile = vocab_tile(entries)
@@ -465,29 +482,25 @@
             whole(rows, width),
             pl.BlockSpec((tile, width), lambda i: (i, 0)),
             whole(rows, LANES),
+            whole(rows, width),
         ],
-        out_specs=[
-            pl.BlockSpec((rows, tile), lambda i: (0, i)),
-            whole(rows, LANES),
-            whole(rows, width),
-            whole(rows, LANES),
-        ],
+        out_specs=[pl.BlockSpec((rows, tile), lambda i: (0, i)), VMEM, VMEM, VMEM],
         out_shape=[
             jax.ShapeDtypeStruct((rows, entries), bfloat),
-            jax.ShapeDtypeStruct((rows, LANES), single),
             jax.ShapeDtypeStruct((rows, width), single),
             jax.ShapeDtypeStruct((rows, LANES), single),
+            jax.ShapeDtypeStruct((8, rows), single),
         ],
-        scratch_shapes=[pltpu.VMEM((rows, LANES), single)],
+        scratch_shapes=[pltpu.VMEM((rows, LANES), single)] * 2,
         compiler_params=pltpu.CompilerParams(
-            dimension_semantics=("arbitrary",), vmem_limit_bytes=56 * 1024 * 1024
+            dimension_semantics=("arbitrary",), vmem_limit_bytes=40 * 1024 * 1024
         ),
         cost_estimate=BRIEF,
         name="vocab_forward",
-    )(states, table, label)
-
-
-def vocab_slope_kernel(first, ratio, order_ref, weight_ref, factor_ref, label_ref, patch_ref, state_ref, sent_ref, kept_ref, moved):
+    )(states, table, label, label_rows)
+
+
+def vocab_slope_kernel(first, ratio, order_ref, weight_ref, factor_ref, label_ref, column_ref, state_ref, sent_ref, kept_ref, moved):
     step = pl.program_id(0)
     tile = weight_ref.shape[1]
     width = state_ref.shape[1]
@@ -506,7 +519,7 @@
     factor = jnp.sum(jnp.where(lanes == here // ratio, factors, 0.0), -1, keepdims=True)
     columns = lax.broadcasted_iota(jnp.int32, weight_ref.shape, 1) + here * tile
     delta = jnp.where(
-        columns == label_ref[...], patch_ref[...], weight_ref[...].astype(single) * factor
+        columns == label_ref[:, :1], column_ref[:, :1], weight_ref[...].astype(single) * factor
     ).astype(bfloat)
     half = width // 2
     slope = inner_rows(delta, moved[...])
@@ -514,7 +527,7 @@
     kept_ref[...] = slope[:, :half].astype(bfloat)
 
 
-def vocab_slope(weights, factors, label, patch, states, order, first, count, tile):
+def vocab_slope(weights, factors, label, values, states, order, first, count, tile):
     rows, width = states.shape
     whole = lambda *shape: pl.BlockSpec(shape, lambda i, o: (0,) * len(shape))
     half = pl.BlockSpec((tile, width // 2), lambda i, o: (i, 0))
@@ -526,8 +539,8 @@
             in_specs=[
                 pl.BlockSpec((rows, tile), lambda i, o: (0, i + first)),
                 whole(rows, LANES),
-                whole(rows, 1),
-                whole(rows, 1),
+                whole(rows, LANES),
+                whole(rows, LANES),
                 whole(rows, width),
             ],
             out_specs=[half, half],
@@ -539,7 +552,7 @@
         ),
         cost_estimate=BRIEF,
         name="vocab_slope",
-    )(order, weights, factors, label, patch, states)
+    )(order, weights, factors, label, values, states)
 
 
 def slope_group_kernel(count, order_ref, *refs):
@@ -576,7 +589,7 @@
         out_specs=[whole, whole],
         out_shape=[jax.ShapeDtypeStruct((total, width // 2), bfloat)] * 2,
         scratch_shapes=[pltpu.VMEM((rows, width), bfloat)],
-        compiler_params=pltpu.CompilerParams(vmem_limit_bytes=56 * 1024 * 1024),
+        compiler_params=pltpu.CompilerParams(vmem_limit_bytes=16 * 1024 * 1024),
         cost_estimate=BRIEF,
         name="slope_group",
     )(order, *lefts, *rights)
@@ -626,7 +639,7 @@
         ),
         out_shape=jax.ShapeDtypeStruct((parts, count, length // parts, width), bfloat),
         compiler_params=pltpu.CompilerParams(
-            dimension_semantics=("arbitrary",), vmem_limit_bytes=32 * 1024 * 1024
+            dimension_semantics=("arbitrary",), vmem_limit_bytes=12 * 1024 * 1024
         ),
         cost_estimate=BRIEF,
         name="attend_forward",
@@ -705,7 +718,8 @@
             jax.ShapeDtypeStruct(addresses.shape, bfloat),
         ],
         compiler_params=pltpu.CompilerParams(
-            dimension_semantics=("arbitrary",), vmem_limit_bytes=56 * 1024 * 1024
+            dimension_semantics=("arbitrary",),
+            vmem_limit_bytes=12 * 1024 * 1024 + 10 * queries.size,
         ),
         cost_estimate=BRIEF,
         name="attend_backward",
@@ -749,7 +763,7 @@
         in_specs=[whole] * (2 * len(kept)),
         out_specs=whole,
         out_shape=jax.ShapeDtypeStruct((total, kept[0].shape[1]), single),
-        compiler_params=pltpu.CompilerParams(vmem_limit_bytes=40 * 1024 * 1024),
+        compiler_params=pltpu.CompilerParams(vmem_limit_bytes=8 * 1024 * 1024),
         name="finish_sums",
     )(*kept, *arrived)
 
@@ -773,7 +787,7 @@
         in_specs=[pl.BlockSpec(memory_space=pltpu.SMEM)] + [VMEM] * len(pieces),
         out_specs=[VMEM, VMEM],
         out_shape=[jax.ShapeDtypeStruct(shape, bfloat)] * 2,
-        compiler_params=pltpu.CompilerParams(vmem_limit_bytes=40 * 1024 * 1024),
+        compiler_params=pltpu.CompilerParams(vmem_limit_bytes=8 * 1024 * 1024),
         cost_estimate=BRIEF,
         name="order_columns",
     )(order, *pieces)
@@ -787,10 +801,8 @@
     table_ref,
     factor_ref,
     label_ref,
-    patch_ref,
+    column_ref,
     far_ref,
-    far_norm_ref,
-    far_scale_ref,
     far_label_ref,
     moved_ref,
     far_moved_ref,
@@ -806,20 +818,19 @@
     columns = lax.broadcasted_iota(jnp.int32, weight_ref.shape, 1) + here * tile
     logits = outer_rows(far_ref[...], table_ref[...])
     delta[:rows, :] = jnp.where(
-        columns == label_ref[...], patch_ref[...], weight_ref[...].astype(single) * factor
+        columns == label_ref[:, :1], column_ref[:, :1], weight_ref[...].astype(single) * factor
     ).astype(bfloat)
-    hit = jnp.where(columns == far_label_ref[...], 1.0, 0.0)
-    delta[rows:, :] = (far_scale_ref[...] * (hit - jnp.exp(logits - far_norm_ref[...]))).astype(bfloat)
+    hit = jnp.where(columns == far_label_ref[:, :1], 1.0, 0.0)
+    delta[rows:, :] = (column_ref[:, 5:6] * (hit - jnp.exp(logits - column_ref[:, 4:5]))).astype(bfloat)
     slope = inner_rows(delta[:rows, :], moved_ref[...]) + inner_rows(delta[rows:, :], far_moved_ref[...])
     half = sent_ref.shape[1]
-    sent_ref[...] = slope[:, half:].astype(bfloat)
-    kept_ref[...] = slope[:, :half].astype(bfloat)
-
-
-def half_slope(base, weights, table, factors, label, patch, far, far_norm, far_scale, far_label, moved, far_moved, first, count, tile):
+    part = pl.ds(pl.multiple_of(pl.program_id(0) * tile, tile), tile)
+    sent_ref[part, :] = slope[:, half:].astype(bfloat)
+    kept_ref[part, :] = slope[:, :half].astype(bfloat)
+
+
+def half_slope(base, weights, table, factors, label, values, far, far_label, moved, far_moved, first, count, tile):
     rows, width = far.shape
-    whole = lambda *shape: pl.BlockSpec(shape, lambda i, b: (0,) * len(shape))
-    half = pl.BlockSpec((tile, width // 2), lambda i, b: (i, 0))
     return pl.pallas_call(
         functools.partial(half_slope_kernel, first, vocab_tile(weights.shape[1]) // tile),
         grid_spec=pltpu.PrefetchScalarGridSpec(
@@ -828,26 +839,24 @@
             in_specs=[
                 pl.BlockSpec((rows, tile), lambda i, b: (0, i + first + b[0])),
                 pl.BlockSpec((tile, width), lambda i, b: (i + first + b[0], 0)),
-                whole(rows, LANES),
-                whole(rows, 1),
-                whole(rows, 1),
-                whole(rows, width),
-                whole(rows, 1),
-                whole(rows, 1),
-                whole(rows, 1),
-                whole(rows, width),
-                whole(rows, width),
+                VMEM,
+                VMEM,
+                VMEM,
+                VMEM,
+                VMEM,
+                VMEM,
+                VMEM,
             ],
-            out_specs=[half, half],
+            out_specs=[VMEM, VMEM],
             scratch_shapes=[pltpu.VMEM((2 * rows, tile), bfloat)],
         ),
         out_shape=[jax.ShapeDtypeStruct((count * tile, width // 2), bfloat)] * 2,
         compiler_params=pltpu.CompilerParams(
-            dimension_semantics=("arbitrary",), vmem_limit_bytes=56 * 1024 * 1024
+            dimension_semantics=("arbitrary",), vmem_limit_bytes=32 * 1024 * 1024
         ),
         cost_estimate=BRIEF,
         name="half_slope",
-    )(base, weights, table, factors, label, patch, far, far_norm, far_scale, far_label, moved, far_moved)
+    )(base, weights, table, factors, label, values, far, far_label, moved, far_moved)
 
 
 def place_halves_kernel(count, side_ref, *refs):
@@ -869,10 +878,153 @@
         in_specs=[pl.BlockSpec(memory_space=pltpu.SMEM)] + [VMEM] * (2 * len(own)),
         out_specs=VMEM,
         out_shape=jax.ShapeDtypeStruct((total, own[0].shape[1]), single),
-        compiler_params=pltpu.CompilerParams(vmem_limit_bytes=40 * 1024 * 1024),
+        compiler_params=pltpu.CompilerParams(vmem_limit_bytes=8 * 1024 * 1024),
         cost_estimate=BRIEF,
         name="place_halves",
     )(side, *own, *other)
+
+
+def lane_blocks(value, count, index):
+    span = value.shape[1] // count
+    return jnp.concatenate(
+        [value[:, (p ^ (1 << index)) * span : ((p ^ (1 << index)) + 1) * span] for p in range(count)], 1
+    )
+
+
+def merge_stats_kernel(count, index, own_ref, other_ref, out_ref):
+    own, other = own_ref[...], lane_blocks(other_ref[...], count, index)
+    high = jnp.maximum(own[0:1], other[0:1])
+    sums = own[1:2] * jnp.exp(own[0:1] - high) + other[1:2] * jnp.exp(other[0:1] - high)
+    out_ref[...] = jnp.concatenate([high, sums, own[2:3] + other[2:3], own[3:]], 0)
+
+
+def merge_stats(own, other, count, index):
+    return run_whole(
+        functools.partial(merge_stats_kernel, count, index), "merge_stats", [(own.shape, single)], own, other
+    )[0]
+
+
+def row_norms_kernel(count, slots, own_ref, out_ref):
+    own = own_ref[...]
+    norm = own[0:1] + jnp.log(own[1:2])
+    parts = own[2:3] - norm
+    span = parts.shape[1] // count
+    parts = [parts[:, p * span : (p + 1) * span] for p in range(count)]
+    while len(parts) > 1:
+        parts = [parts[p] + parts[p + 1] for p in range(0, len(parts), 2)]
+    lanes = lax.broadcasted_iota(jnp.int32, parts[0].shape, 1)
+    places = lax.broadcasted_iota(jnp.int32, norm.shape, 1)
+    likelihood = jnp.zeros_like(norm)
+    for slot in range(slots):
+        total = jnp.sum(jnp.where(lanes // (span // slots) == slot, parts[0], 0.0), -1, keepdims=True)
+        likelihood = jnp.where(places == slot, total, likelihood)
+    out_ref[...] = jnp.concatenate([norm, likelihood, own[2:]], 0)
+
+
+def row_norms(own, count, slots):
+    return run_whole(
+        functools.partial(row_norms_kernel, count, slots), "row_norms", [(own.shape, single)], own
+    )[0]
+
+
+def as_columns(rows):
+    return jnp.swapaxes(
+        jnp.concatenate([rows, jnp.zeros((LANES - rows.shape[0], rows.shape[1]), single)], 0), 0, 1
+    )
+
+
+def vocab_part_kernel(
+    place_ref, norm_ref, merged_ref, local_ref, label_rows_ref, label_ref, mixed_ref, sent_ref, kept_ref
+):
+    norm = norm_ref[0:1, :]
+    surplus = 1.0 - jnp.exp(merged_ref[2:3, :] - norm)
+    share = jnp.exp(local_ref[0:1, :] - norm)
+    columns = as_columns(jnp.concatenate([surplus, share] + [norm] * 6, 0))
+    label = label_ref[:, 0:1]
+    inside = (label >= 0) & (label < place_ref[3])
+    part = (
+        jnp.where(inside, columns[:, 0:1], 0.0) * label_rows_ref[...].astype(single)
+        - columns[:, 1:2] * mixed_ref[...]
+    )
+    half = kept_ref.shape[0]
+    kept_ref[...] = part[:half]
+    sent_ref[...] = part[half:].astype(bfloat)
+
+
+def vocab_part(place, norm, merged, local, label_rows, label, mixed):
+    rows, width = mixed.shape
+    return pl.pallas_call(
+        vocab_part_kernel,
+        in_specs=[pl.BlockSpec(memory_space=pltpu.SMEM)] + [VMEM] * 6,
+        out_specs=[VMEM] * 2,
+        out_shape=[
+            jax.ShapeDtypeStruct((rows // 2, width), bfloat),
+            jax.ShapeDtypeStruct((rows // 2, width), single),
+        ],
+        compiler_params=pltpu.CompilerParams(vmem_limit_bytes=16 * 1024 * 1024),
+        cost_estimate=BRIEF,
+        name="vocab_part",
+    )(place, norm, merged, local, label_rows, label, mixed)
+
+
+def vocab_scale_kernel(
+    slots, delta_ref, place_ref, norm_ref, merged_ref, far_ref, tops_ref, factor_ref, column_ref
+):
+    norm = norm_ref[0:1, :]
+    lanes = lax.broadcasted_iota(jnp.int32, norm.shape, 1)
+    quarter = norm.shape[1] // slots // place_ref[2]
+    slot_of = lax.rem(lanes // quarter, slots)
+    scale, far_scale = jnp.zeros_like(norm), jnp.zeros_like(norm)
+    for slot in range(slots):
+        scale = jnp.where(slot_of == slot, delta_ref[place_ref[0] + slot], scale)
+        far_scale = jnp.where(slot_of == slot, delta_ref[place_ref[1] + slot], far_scale)
+    surplus = scale * (1.0 - jnp.exp(merged_ref[2:3, :] - norm))
+    columns = as_columns(
+        jnp.concatenate([surplus, norm, scale, norm, far_ref[0:1, :], far_scale, norm, norm], 0)
+    )
+    column_ref[...] = columns
+    factor_ref[...] = -columns[:, 2:3] * jnp.exp(tops_ref[...] - columns[:, 1:2])
+
+
+def vocab_scale(delta, place, norm, merged, far, tops, slots):
+    smem = pl.BlockSpec(memory_space=pltpu.SMEM)
+    return pl.pallas_call(
+        functools.partial(vocab_scale_kernel, slots),
+        in_specs=[smem, smem] + [VMEM] * 4,
+        out_specs=[VMEM] * 2,
+        out_shape=[jax.ShapeDtypeStruct(tops.shape, single)] * 2,
+        compiler_params=pltpu.CompilerParams(vmem_limit_bytes=12 * 1024 * 1024),
+        cost_estimate=BRIEF,
+        name="vocab_scale",
+    )(delta, place, norm, merged, far, tops)
+
+
+def scaled_backward_kernel(slots, delta_ref, place_ref, kept_ref, arrived_ref, *refs):
+    shape = kept_ref.shape
+    slot_of = lax.broadcasted_iota(jnp.int32, (shape[0], LANES), 0) // (shape[0] // slots)
+    scale = jnp.zeros(slot_of.shape, single)
+    for slot in range(slots):
+        scale = jnp.where(slot_of == slot, delta_ref[place_ref[0] + slot], scale)
+    upstream = (kept_ref[...].astype(single) + arrived_ref[...].astype(single)) * scale[:, :1]
+    norm_backward_rows(upstream, *refs)
+
+
+def scaled_backward(delta, place, kept, arrived, hidden, gain, slots):
+    shape = hidden.shape
+    smem = pl.BlockSpec(memory_space=pltpu.SMEM)
+    return pl.pallas_call(
+        functools.partial(scaled_backward_kernel, slots),
+        in_specs=[smem, smem] + [VMEM] * 4,
+        out_specs=[VMEM] * 3,
+        out_shape=[
+            jax.ShapeDtypeStruct(shape, single),
+            jax.ShapeDtypeStruct(shape, bfloat),
+            jax.ShapeDtypeStruct((3, shape[1]), single),
+        ],
+        compiler_params=pltpu.CompilerParams(vmem_limit_bytes=12 * 1024 * 1024),
+        cost_estimate=BRIEF,
+        name="norm_backward",
+    )(delta, place, kept.reshape(shape), arrived.reshape(shape), hidden, row(gain))
 
 
 def marginal_objective(seq_values, doc_scores, member, length):
@@ -936,10 +1088,14 @@
 
     token = [score_table]
 
+    free = [False]
+
     def through(*values):
-        values = tie(*values, token[0])
-        token[0] = values[-1]
-        return values[:-1] if len(values) > 2 else values[0]
+        if not free[0]:
+            values = tie(*values, token[0])
+            token[0] = values[-1]
+            values = values[:-1]
+        return values if len(values) > 1 else values[0]
 
     mp_order = bits_of(mp)[::-1]
     mp_table = relative_of(mp_order)
@@ -1036,12 +1192,23 @@
     first_order = dp_bits[:1] + dp_bits[:0:-1]
     probe_bins = where_slots(probe_order)
     first_bins = where_slots(first_order)
-    probe_all, first_all = gather_both(
+    def label_index(slots):
+        wanted = to_own(jnp.take(labels, slots, axis=0, mode="clip"), pair_count).reshape(-1)
+        return wanted - member_index * vocab_share
+
+    local_index = label_index(my_questions)
+    inside = (local_index >= 0) & (local_index < vocab_share)
+    label_places = jnp.clip(local_index, 0, vocab_share - 1)
+    gather = gather_both_steps(
         (probe_own, first_low.reshape(own_questions, quarter, width)),
         "dp",
         dp,
         (probe_order, first_order),
     )
+    for step in range(len(dp_bits)):
+        next(gather)
+    label_rows = through(jnp.take(embedding, through(label_places), axis=0, mode="clip"))
+    probe_all, first_all = next(gather)
     probe_all = probe_all.reshape(questions, length, local_width)
     first_all = first_all.reshape(questions, quarter, width)
     passage_rows = passages.reshape(-1, width)
@@ -1050,15 +1217,6 @@
     stored_addresses = stored_addresses.reshape(store_count, passage_length, local_width)
     stored_contents = stored_contents.reshape(store_count, passage_length, local_width)
 
-    def label_index(slots):
-        wanted = to_own(jnp.take(labels, slots, axis=0, mode="clip"), pair_count).reshape(-1)
-        return wanted - member_index * vocab_share
-
-    local_index = label_index(my_questions)
-    inside = (local_index >= 0) & (local_index < vocab_share)
-    label_rows = jnp.take(embedding, jnp.clip(local_index, 0, vocab_share - 1), axis=0, mode="clip")
-    probe_all, label_rows = lax.optimization_barrier((probe_all, label_rows))
-
     cross_flat = attend_forward(
         probe_all, stored_addresses, stored_contents, probe_bins, slot_passage, mp
     ).reshape(-1, local_width)
@@ -1081,49 +1239,40 @@
 
     order_a = dp_bits[::-1]
     order_b = order_a if dp < 4 else [dp_bits[-1], dp_bits[0]] + dp_bits[1:-1]
-    third_low, third_moved = order_columns(last(mp_gather_steps(low)), order_table(order_a))
-    far_low = swap(through(low), "dp", dp, far)
-
-
-    label_lanes = jnp.broadcast_to(local_index[:, None], (local_index.shape[0], LANES))
+    third_pieces = last(mp_gather_steps(low))
+    third_low, third_moved = order_columns(third_pieces, order_table(order_a))
+    far_pieces = [swap(piece, "dp", dp, far) for piece in third_pieces[: mp // 2]]
+
+    def label_lanes(index):
+        return jnp.broadcast_to(index[:, None], (index.shape[0], LANES))
+
+    own_labels = label_lanes(local_index)
     third_low = through(third_low)
-    entry_weights, entry_sums, entry_mix, entry_tops = vocab_forward(third_low, embedding, label_lanes)
-    entry_tops, entry_sums, entry_mix, far_low = through(
-        entry_tops, entry_sums, entry_mix, far_low
-    )
+    entry_weights, entry_mix, entry_tops, local_stats = vocab_forward(
+        third_low, embedding, own_labels, label_rows
+    )
+    local_stats, *far_pieces = through(local_stats, *far_pieces)
     entry_tile = vocab_tile(vocab_share)
-    local_top = entry_tops[:, vocab_share // entry_tile - 1]
-    local_target = jnp.where(
-        inside, jnp.sum(third_low.astype(single) * label_rows.astype(single), -1), 0.0
-    )
-    local_total = jnp.sum(entry_sums, -1) + jnp.where(inside, jnp.exp(local_target - local_top), 0.0)
-    stats = jnp.stack([local_top, local_total, local_target]).reshape(3, mp, pair_count, quarter)
+    stats = local_stats
     for index, bit in reversed(list(enumerate(mp_order))):
-        other = swap(stats, "mp", mp, bit)
-        other = jnp.flip(
-            other.reshape(3, mp >> (index + 1), 2, 1 << index, pair_count, quarter), 2
-        ).reshape(stats.shape)
-        high = jnp.maximum(stats[0], other[0])
-        sums = stats[1] * jnp.exp(stats[0] - high) + other[1] * jnp.exp(other[0] - high)
-        stats = jnp.stack([high, sums, stats[2] + other[2]])
-    log_norm = (stats[0] + jnp.log(stats[1])).reshape(-1)
-    target_logit = stats[2].reshape(-1)
-    pair_likelihood = jnp.sum((target_logit - log_norm).reshape(mp, pair_count, quarter), -1)
-    while pair_likelihood.shape[0] > 1:
-        pair_likelihood = pair_likelihood[0::2] + pair_likelihood[1::2]
-    far_steps = mp_gather_steps(far_low)
-    next(far_steps)
-    shared = jnp.concatenate([pair_likelihood[0], log_norm])
-    arrived = swap(shared, "dp", dp, far)
-    far_norm = arrived[pair_count:]
-    every_likelihood = jnp.stack([shared[:pair_count], arrived[:pair_count]])
-    for bit in dp_order[1:]:
-        every_likelihood = jnp.concatenate(
-            [every_likelihood, swap(every_likelihood, "dp", dp, bit)], 0
-        )
+        stats = merge_stats(stats, through(swap(stats, "mp", mp, bit)), mp, index)
+    norms = through(row_norms(stats, mp, pair_count))
+    far_norms = swap(norms, "dp", dp, far)
+    far_group = group ^ far
+    place = jnp.stack([group * pair_count, far_group * pair_count, mp, vocab_share]).astype(jnp.int32)
+    sent, kept = vocab_part(place, norms, stats, local_stats, label_rows, own_labels, entry_mix)
+    steps = mp_scatter_steps((sent, kept))
+    next(steps)
+    far_norms = through(far_norms)
+    every_likelihood = jnp.stack([norms[1, :pair_count], far_norms[1, :pair_count]])
+    arrived = swap(every_likelihood, "dp", dp, dp_order[1])
+    next(steps)
+    for bit in dp_order[2:]:
+        every_likelihood = jnp.concatenate([every_likelihood, through(arrived)], 0)
+        arrived = swap(every_likelihood, "dp", dp, bit)
+    far_pieces += [swap(piece, "mp", mp, mp_order[-1]) for piece in far_pieces]
+    every_likelihood = jnp.concatenate([every_likelihood, through(arrived)], 0)
     every_likelihood = natural_order(dp_table, group, every_likelihood, 0).reshape(-1)
-    next(far_steps)
-    far_third, far_moved = order_columns(next(far_steps), order_table(order_a))
     doc_scores = jnp.take(token[0], score_index)
     member = slot_question[None, :] == jnp.arange(questions, dtype=jnp.int32)[:, None]
 
@@ -1132,27 +1281,15 @@
 
     objective, pullback = jax.vjp(scored, every_likelihood)
     likelihood_delta = pullback(jnp.ones_like(objective) * (questions * length))[0]
-    pair_delta = lax.dynamic_slice_in_dim(likelihood_delta, group * pair_count, pair_count)
-
-    def by_row(values):
-        return jnp.broadcast_to(values[None, :, None], (mp, pair_count, quarter)).reshape(-1)
-
-    row_delta = by_row(pair_delta)
-    far_group = group ^ far
-    far_delta = by_row(
-        lax.dynamic_slice_in_dim(likelihood_delta, far_group * pair_count, pair_count)
-    )
-    far_label = label_index(
-        lax.dynamic_slice_in_dim(slot_question, far_group * pair_count, pair_count)
-    )
-    surplus = row_delta * (1.0 - jnp.exp(target_logit - log_norm))
-    factors = -row_delta[:, None] * jnp.exp(entry_tops - log_norm[:, None])
-    third_part = (
-        jnp.where(inside, surplus, 0.0)[:, None] * label_rows.astype(single)
-        - (row_delta * jnp.exp(local_top - log_norm))[:, None] * entry_mix
-    )
-
-    token[0] = objective
+    far_labels = label_lanes(
+        label_index(lax.dynamic_slice_in_dim(slot_question, far_group * pair_count, pair_count))
+    )
+    factors, values = vocab_scale(
+        likelihood_delta, place, norms, stats, far_norms, entry_tops, pair_count
+    )
+    far_third, far_moved = order_columns(through(*far_pieces), order_table(order_a))
+
+    objective = through(objective)
 
     class ColumnSum:
         def __init__(self, halves, order):
@@ -1204,12 +1341,10 @@
                 entry_weights,
                 embedding,
                 through(factors),
-                local_index[:, None],
-                surplus[:, None],
+                own_labels,
+                values,
                 far_third,
-                far_norm[:, None],
-                far_delta[:, None],
-                far_label[:, None],
+                far_labels,
                 third_moved,
                 far_moved,
                 first,
@@ -1220,8 +1355,8 @@
             halves = vocab_slope(
                 entry_weights,
                 through(factors),
-                local_index[:, None],
-                surplus[:, None],
+                own_labels,
+                values,
                 third_low,
                 order_table(order_a),
                 first,
@@ -1265,6 +1400,7 @@
     orders = {"y": order_a, "z": order_b}
 
     def at(point):
+        free[0] = free[0] or point >= FREE
         for name, action in PLAN[point]:
             if name == "t":
                 next(state_steps)
@@ -1273,13 +1409,12 @@
             else:
                 getattr(sums[name], action)()
 
-    half = third_part.shape[0] // 2
-    steps = mp_scatter_steps((third_part[half:].astype(bfloat), third_part[:half]))
-    next(steps)
     at(0)
-    next(steps)
     at(1)
-    third_back, feed_low, third_sums = norm_backward(next(steps), third_in, third_gain)
+    kept, arrived = next(steps)
+    third_back, feed_low, third_sums = scaled_backward(
+        likelihood_delta, place, kept, arrived, third_in, third_gain, pair_count
+    )
     steps = mp_gather_steps(feed_low)
     next(steps)
     at(2)
@@ -1455,7 +1590,7 @@
     ) = (vectors[i] for i in range(10))
     bias_query, bias_value, bias_probe, bias_content = vectors[10].reshape(4, local_width // dp)
     return (
-        token[0],
+        objective,
         targets_slope,
         passages_slope,
         query_slope,

time: 759 us -> 680 us (0.90)
  Pallas kernels: 322 us -> 228 us
  waiting for transfers between devices: 206 us -> 236 us
  other arithmetic: 36.3 us -> 22.8 us
    ppermute x76, waiting for transfers between devices: 183 us -> 236 us  [swap(): return lax.ppermute(value, axis, [(i, i ^ bit) for i in range(count)])]
    pallas_call x26 -> x40, Pallas kernels: 85.6 us -> 48.5 us  [run_whole(): pl.pallas_call(kernel, in_specs=[VMEM] * len(operands), out_specs=[VMEM]...]
    pallas_call x12 -> x3, Pallas kernels: 43.3 us -> 6.65 us  [the longest x1 2.75 us: scaled_backward(): pl.pallas_call(functools.partial(scaled_backward_kernel, slots), in_specs...]
    psum x1, waiting for transfers between devices: 22.9 us -> 0.02 us  [on_device(): lax.psum((outer_rows(address_delta, address_weight) + outer_rows(content_...]
    unnamed x245 -> x293, local copies, waits for them, and re-layouts: 35.1 us -> 53.7 us
    pallas_call x3, Pallas kernels: 66.8 us -> 57.5 us  [half_slope(): pl.pallas_call(functools.partial(half_slope_kernel, first, vocab_tile(wei...]
    squeeze x11 -> x0, local copies, waits for them, and re-layouts: 8.06 us -> none  [the longest x4 2.73 us: on_device(): other[1] * jnp.exp(other[0] - high)]
  transfers between devices with their start and end apart: 77 -> 77, of which waited for: 35 -> 38; matrix products, arithmetic and copies ran while one was open for 11% -> 10% of each run, Pallas kernels for 36% -> 30%
where the time goes in v4:
time: 680 us; the launch traced here: 672 us
  waiting for transfers between devices  236 us (35%)
  Pallas kernels  228 us (34%)
  local copies, waits for them, and re-layouts  90.7 us (13%)
  starting transfers between devices  68.2 us (10%)
  other arithmetic  22.8 us (3%)
  between operations  17.8 us (3%)
  matrix products  8.59 us (1%)
    ppermute x76, waiting for transfers between devices, swap(): return lax.ppermute(value, axis, [(i, i ^ bit) for i in range(count)])  236 us
    ppermute x76, starting transfers between devices, swap(): return lax.ppermute(value, axis, [(i, i ^ bit) for i in range(count)])  68.2 us
    pallas_call x1, Pallas kernels, vocab_forward(): pl.pallas_call(vocab_forward_kernel, grid=(entries // tile,), in_specs=[w...  67.9 us
    pallas_call x3, Pallas kernels, half_slope(): pl.pallas_call(functools.partial(half_slope_kernel, first, vocab_tile(wei...  57.5 us
    unnamed x293, local copies, waits for them, and re-layouts  53.7 us
    pallas_call x40, Pallas kernels, run_whole(): pl.pallas_call(kernel, in_specs=[VMEM] * len(operands), out_specs=[VMEM]...  48.5 us
    gather x1, local copies, waits for them, and re-layouts, on_device(): jnp.take(embedding, through(label_places), axis=0, mode='clip')  17.8 us
  transfers between devices with their start and end apart: 77, of which 38 were waited for; matrix products, arithmetic and copies ran while one was open for 10% of the time, Pallas kernels for 30%

profile of v4, /device:TPU:0, one launch (start us, length us, event | category | flops | bytes accessed | tf_op | source)
XLA Modules:
  0.0 671.8 jit_solution(6265165094504214201)
XLA Ops:
  18.6 2.7 collective-permute-start.1
  21.3 4.1 collective-permute-done.1.arrived_ref
  36.1 2.7 collective-permute-start.5
  39.7 5.3 collective-permute-done.5
  45.9 3.4 collective-permute-start.8
  50.5 7.1 %collective-permute-done.7 = bf16[2,1,256,256]{3,2,0,1:T(8,128)(2,1)S(1)} collective-permute-done((bf16[2,1,256,256]{3,2,0,1:T(8,128)(2,1)S(1)}, bf16[2,1,256,256]{3,2,0,1:T(8,128)(2,1)S(1)}, u32[]{:S(2)}, u32[]{:S(2)}) %collective-permute-start.7) | collective-permute-done | bytes 262176 | tf_op jit(solution)/shard_map/ppermute | solution.py:73
  57.6 3.6 collective-permute-done.8
  67.5 17.8 %gather_fusion.4 = bf16[1024,1024]{1,0:T(8,128)(2,1)} fusion(bf16[12544,1024]{1,0:T(8,128)(2,1)} %table_ref.7, s32[1024]{0:T(1024)S(1)} %broadcast_clamp_fusion), kind=kCustom, calls=%fused_computation.4 | custom fusion | bytes 4198400 | tf_op jit(solution)/shard_map/jit(_take)/gather | solution.py:1210
  86.7 5.1 attend_forward.3
  92.7 2.6 collective-permute-done.11.arrived_ref
  101.3 4.0 pick.1
  105.2 6.2 collective-permute-done.12.arrived_ref
  115.7 12.6 %collective-permute-done.13.refs_1_ = bf16[256,1024]{1,0:T(8,128)(2,1)S(1)} collective-permute-done((bf16[256,1024]{1,0:T(8,128)(2,1)S(1)}, bf16[256,1024]{1,0:T(8,128)(2,1)S(1)}, u32[]{:S(2)}, u32[]{:S(2)}) %collective-permute-start.13) | collective-permute-done | bytes 524320 | tf_op jit(solution)/shard_map/ppermute | solution.py:73
  131.8 4.7 feed_forward.1
  142.7 13.4 %collective-permute-done.17.arrived_ref = bf16[256,1024]{1,0:T(8,128)(2,1)S(1)} collective-permute-done((bf16[256,1024]{1,0:T(8,128)(2,1)S(1)}, bf16[256,1024]{1,0:T(8,128)(2,1)S(1)}, u32[]{:S(2)}, u32[]{:S(2)}) %collective-permute-start.17) | collective-permute-done | bytes 524320 | tf_op jit(solution)/shard_map/ppermute | solution.py:73
  158.2 12.6 %collective-permute-done.18.refs_1_ = bf16[256,1024]{1,0:T(8,128)(2,1)S(1)} collective-permute-done((bf16[256,1024]{1,0:T(8,128)(2,1)S(1)}, bf16[256,1024]{1,0:T(8,128)(2,1)S(1)}, u32[]{:S(2)}, u32[]{:S(2)}) %collective-permute-start.18) | collective-permute-done | bytes 524320 | tf_op jit(solution)/shard_map/ppermute | solution.py:73
  172.7 2.7 collective-permute-start.21
  178.4 67.9 %vocab_forward.1 = (bf16[1024,12544]{1,0:T(8,128)(2,1)}, f32[1024,1024]{1,0:T(8,128)S(1)}, f32[1024,128]{1,0:T(8,128)S(1)}, f32[8,1024]{1,0:T(8,128)S(1)}) custom-call(bf16[1024,1024]{1,0:T(8,128)(2,1)S(1)} %get-tuple-element.517.state_ref, bf16[12544,1024]{1,0:T(8,128)(2,1)} %table_ref.7, s32[1024,128]{1,0:T(8,128)S(1)} %broadcast_in_dim.125.label_ref, ...), custom_call_target="tpu_custom_call" | custom-call | tf_op jit(solution)/shard_map/vocab_forward/pallas_call | solution.py:478
  248.3 3.3 collective-permute-done.24.other_ref
  256.3 2.8 collective-permute-start.25
  275.1 6.3 collective-permute-done.31.arrived_ref
  283.8 2.7 norm_backward.3
  296.8 16.6 %half_slope.3 = (bf16[1792,512]{1,0:T(8,128)(2,1)S(1)}, bf16[1792,512]{1,0:T(8,128)(2,1)S(1)}) custom-call(s32[1]{0:T(128)S(6)} %mul.72.base_ref, bf16[1024,12544]{1,0:T(8,128)(2,1)} %get-tuple-element.558.weight_ref, bf16[12544,1024]{1,0:T(8,128)(2,1)} %table_ref.7, f32[1024,128]{1,0:T(8,128)S(1)} %get-tuple-element.662.factor_ref, ...), custom_call_target="tpu_custom_call" | custom-call | tf_op jit(solution)/shard_map/half_slope/pallas_call | solution.py:834
  315.8 7.1 %feed_backward.1 = (bf16[1024,1024]{1,0:T(8,128)(2,1)S(1)}, bf16[1024,1024]{1,0:T(8,128)(2,1)S(1)}, f32[1,1024]{1,0:T(1,128)S(1)}, bf16[512,1024]{1,0:T(8,128)(2,1)S(1)}, f32[512,1024]{1,0:T(8,128)S(1)}) custom-call(bf16[256,1024]{1,0:T(8,128)(2,1)} %get-tuple-element.579.refs_0_, bf16[256,1024]{1,0:T(8,128)(2,1)} %collective-permute-done.32.refs_1_, ...), custom_call_target="tpu_custom_call" | custom-call | tf_op jit(solution)/shard_map/feed_backward/pallas_call | solution.py:139
  327.2 6.8 %slope_group.3 = (bf16[2048,512]{1,0:T(8,128)(2,1)}, bf16[2048,512]{1,0:T(8,128)(2,1)S(1)}) custom-call(s32[8]{0:T(128)S(1)} %get-tuple-element.964.order_ref, bf16[1024,1024]{1,0:T(8,128)(2,1)S(1)} %copy-done.29, bf16[1024,1024]{1,0:T(8,128)(2,1)S(1)} %get-tuple-element.601.refs_1_, bf16[1024,1024]{1,0:T(8,128)(2,1)S(1)} %get-tuple-element.602.refs_2_, ...), custom_call_target="tpu_custom_call" | custom-call | tf_op jit(solution)/shard_map/slope_group/pallas_call | solution.py:586
  334.3 21.7 %collective-permute-done.37.arrived_ref = bf16[1792,512]{1,0:T(8,128)(2,1)S(1)} collective-permute-done((bf16[1792,512]{1,0:T(8,128)(2,1)S(1)}, bf16[1792,512]{1,0:T(8,128)(2,1)S(1)}, u32[]{:S(2)}, u32[]{:S(2)}) %collective-permute-start.37) | collective-permute-done | bytes 1835040 | tf_op jit(solution)/shard_map/ppermute | solution.py:73
  359.6 16.2 %half_slope.4 = (bf16[1792,512]{1,0:T(8,128)(2,1)S(1)}, bf16[1792,512]{1,0:T(8,128)(2,1)S(1)}) custom-call(s32[1]{0:T(128)S(6)} %mul.72.base_ref, bf16[1024,12544]{1,0:T(8,128)(2,1)} %get-tuple-element.558.weight_ref, bf16[12544,1024]{1,0:T(8,128)(2,1)} %table_ref.7, f32[1024,128]{1,0:T(8,128)S(1)} %get-tuple-element.662.factor_ref, ...), custom_call_target="tpu_custom_call" | custom-call | tf_op jit(solution)/shard_map/half_slope/pallas_call | solution.py:834
  382.1 10.5 %attend_backward.2 = (bf16[8,256,256]{2,1,0:T(8,128)(2,1)S(1)}, bf16[2,256,256]{2,1,0:T(8,128)(2,1)S(1)}, bf16[2,256,256]{2,1,0:T(8,128)(2,1)S(1)}) custom-call(s32[4]{0:T(128)S(1)} %gather_fusion, s32[4]{0:T(128)S(1)} %copy-done.105, s32[4]{0:T(128)S(1)} %copy-done.101, bf16[8,256,256]{2,1,0:T(8,128)(2,1)S(1)} %maximum_bitcast_fusion.query_ref, ...), custom_call_target="tpu_custom_call" | custom-call | tf_op jit(solution)/shard_map/attend_backward/pallas_call | solution.py:696
  396.3 11.2 %collective-permute-done.41.arrived_ref = bf16[1024,256]{1,0:T(8,128)(2,1)S(1)} collective-permute-done((bf16[1024,256]{1,0:T(8,128)(2,1)S(1)}, bf16[1024,256]{1,0:T(8,128)(2,1)S(1)}, u32[]{:S(2)}, u32[]{:S(2)}) %collective-permute-start.41) | collective-permute-done | bytes 524320 | tf_op jit(solution)/shard_map/ppermute | solution.py:73
  409.0 19.0 %collective-permute-done.44.arrived_ref = bf16[256,1024]{1,0:T(8,128)(2,1)S(1)} collective-permute-done((bf16[256,1024]{1,0:T(8,128)(2,1)S(1)}, bf16[256,1024]{1,0:T(8,128)(2,1)S(1)}, u32[]{:S(2)}, u32[]{:S(2)}) %collective-permute-start.44) | collective-permute-done | bytes 524320 | tf_op jit(solution)/shard_map/ppermute | solution.py:73
  428.1 24.7 %half_slope.5 = (bf16[2688,512]{1,0:T(8,128)(2,1)}, bf16[2688,512]{1,0:T(8,128)(2,1)S(1)}) custom-call(s32[1]{0:T(128)S(6)} %mul.72.base_ref, bf16[1024,12544]{1,0:T(8,128)(2,1)} %get-tuple-element.558.weight_ref, bf16[12544,1024]{1,0:T(8,128)(2,1)} %table_ref.7, f32[1024,128]{1,0:T(8,128)S(1)} %get-tuple-element.662.factor_ref, ...), custom_call_target="tpu_custom_call" | custom-call | tf_op jit(solution)/shard_map/half_slope/pallas_call | solution.py:834
  462.7 3.3 collective-permute-done.48.arrived_ref
  469.8 5.8 collective-permute-done.51.refs_3_
  508.7 4.1 slope_group.4
  520.9 2.9 collective-permute-start.65
  532.0 3.2 add_columns.18
  536.5 6.9 %collective-permute-done.62.arrived_ref = bf16[2048,256]{1,0:T(8,128)(2,1)} collective-permute-done((bf16[2048,256]{1,0:T(8,128)(2,1)}, bf16[2048,256]{1,0:T(8,128)(2,1)}, u32[]{:S(2)}, u32[]{:S(2)}) %collective-permute-start.62) | collective-permute-done | bytes 1048608 | tf_op jit(solution)/shard_map/ppermute | solution.py:73
  546.5 2.6 collective-permute-start.71
  549.1 14.8 %collective-permute-done.65.arrived_ref = bf16[784,512]{1,0:T(8,128)(2,1)} collective-permute-done((bf16[784,512]{1,0:T(8,128)(2,1)}, bf16[784,512]{1,0:T(8,128)(2,1)}, u32[]{:S(2)}, u32[]{:S(2)}) %collective-permute-start.65) | collective-permute-done | bytes 802848 | tf_op jit(solution)/shard_map/ppermute | solution.py:73
  566.7 2.9 reshape.360
  575.5 17.5 %collective-permute-done.71.refs_1_ = bf16[2048,128]{1,0:T(8,128)(2,1)} collective-permute-done((bf16[2048,128]{1,0:T(8,128)(2,1)}, bf16[2048,128]{1,0:T(8,128)(2,1)}, u32[]{:S(2)}, u32[]{:S(2)}) %collective-permute-start.71) | collective-permute-done | bytes 524320 | tf_op jit(solution)/shard_map/ppermute | solution.py:73
  595.3 3.4 collective-permute-start.67
  602.0 7.8 %collective-permute-done.67.refs_1_ = bf16[784,128]{1,0:T(8,128)(2,1)S(1)} collective-permute-done((bf16[784,128]{1,0:T(8,128)(2,1)S(1)}, bf16[784,128]{1,0:T(8,128)(2,1)S(1)}, u32[]{:S(2)}, u32[]{:S(2)}) %collective-permute-start.67) | collective-permute-done | bytes 200736 | tf_op jit(solution)/shard_map/ppermute | solution.py:73
  612.5 3.3 collective-permute-start.70
  615.9 2.5 add_columns.23
  624.8 20.9 %collective-permute-done.70.refs_1_ = bf16[1280,128]{1,0:T(8,128)(2,1)} collective-permute-done((bf16[1280,128]{1,0:T(8,128)(2,1)}, bf16[1280,128]{1,0:T(8,128)(2,1)}, u32[]{:S(2)}, u32[]{:S(2)}) %collective-permute-start.70) | collective-permute-done | bytes 327712 | tf_op jit(solution)/shard_map/ppermute | solution.py:73
  650.7 8.4 %collective-permute-done.75.refs_5_ = bf16[2688,128]{1,0:T(8,128)(2,1)S(1)} collective-permute-done((bf16[2688,128]{1,0:T(8,128)(2,1)}, bf16[2688,128]{1,0:T(8,128)(2,1)S(1)}, u32[]{:S(2)}, u32[]{:S(2)}) %collective-permute-start.75) | collective-permute-done | bytes 688160 | tf_op jit(solution)/shard_map/ppermute | solution.py:73
  659.1 4.3 place_halves.1
  (582 shorter events, 211.8 us)
Async XLA Ops:
  7.2 559.4 %all-reduce.2.cloned.1.call-start = ((), (), s32[]{:S(2)}) async-start(), calls=%async_computation | async-start | bytes 2097152 | tf_op jit(solution)/shard_map/psum | solution.py:1488
  36.1 9.0 %collective-permute-start.5 = (bf16[1,1,256,256]{3,2,0,1:T(8,128)(2,1)S(1)}, bf16[1,1,256,256]{3,2,0,1:T(8,128)(2,1)S(1)}, u32[]{:S(2)}, u32[]{:S(2)}) collective-permute-start(bf16[1,1,256,256]{3,2,0,1:T(8,128)(2,1)S(1)} %bitcast.142), channel_id=1, source_target_pairs={{0,16},{4,20},{8,24},{12,28},{16,0},{20,4},{24,8},{28,12},{1,17},{... | collective-permute-start | bytes 393224 | tf_op jit(solution)/shard_map/ppermute | solution.py:73
  45.1 12.5 %collective-permute-start.7 = (bf16[2,1,256,256]{3,2,0,1:T(8,128)(2,1)S(1)}, bf16[2,1,256,256]{3,2,0,1:T(8,128)(2,1)S(1)}, u32[]{:S(2)}, u32[]{:S(2)}) collective-permute-start(bf16[2,1,256,256]{3,2,0,1:T(8,128)(2,1)S(1)} %pad_maximum_fusion.3), channel_id=1, source_target_pairs={{0,8},{4,12},{8,0},{12,4},{16,24},{20,28},{24,16},{28,20},{1,9},{5... | collective-permute-start | bytes 786440 | tf_op jit(solution)/shard_map/ppermute | solution.py:73
  45.9 15.3 %collective-permute-start.8 = (bf16[2,1,64,1024]{3,2,0,1:T(8,128)(2,1)S(1)}, bf16[2,1,64,1024]{3,2,0,1:T(8,128)(2,1)S(1)}, u32[]{:S(2)}, u32[]{:S(2)}) collective-permute-start(bf16[2,1,64,1024]{3,2,0,1:T(8,128)(2,1)S(1)} %pad_maximum_fusion.4), channel_id=1, source_target_pairs={{0,16},{4,20},{8,24},{12,28},{16,0},{20,4},{24,8},{28,12},{1,17},{... | collective-permute-start | bytes 786440 | tf_op jit(solution)/shard_map/ppermute | solution.py:73
  62.1 23.3 %collective-permute-start.9 = (bf16[4,1,256,256]{3,2,0,1:T(8,128)(2,1)}, bf16[4,1,256,256]{3,2,0,1:T(8,128)(2,1)}, u32[]{:S(2)}, u32[]{:S(2)}) collective-permute-start(bf16[4,1,256,256]{3,2,0,1:T(8,128)(2,1)} %pad_maximum_fusion), channel_id=1, source_target_pairs={{0,4},{4,0},{8,12},{12,8},{16,20},{20,16},{24,28},{28,24},{1,5},{5... | collective-permute-start | bytes 1572872 | tf_op jit(solution)/shard_map/ppermute | solution.py:73
  64.4 21.0 %collective-permute-start.10 = (bf16[4,1,64,1024]{3,2,0,1:T(8,128)(2,1)}, bf16[4,1,64,1024]{3,2,0,1:T(8,128)(2,1)}, u32[]{:S(2)}, u32[]{:S(2)}) collective-permute-start(bf16[4,1,64,1024]{3,2,0,1:T(8,128)(2,1)} %pad_maximum_fusion.1), channel_id=1, source_target_pairs={{0,8},{4,12},{8,0},{12,4},{16,24},{20,28},{24,16},{28,20},{1,9},{5... | collective-permute-start | bytes 1572872 | tf_op jit(solution)/shard_map/ppermute | solution.py:73
  97.2 14.2 %collective-permute-start.12 = (bf16[256,1024]{1,0:T(8,128)(2,1)}, bf16[256,1024]{1,0:T(8,128)(2,1)S(1)}, u32[]{:S(2)}, u32[]{:S(2)}) collective-permute-start(bf16[256,1024]{1,0:T(8,128)(2,1)} %get-tuple-element.476), channel_id=1, source_target_pairs={{0,2},{1,3},{2,0},{3,1},{4,6},{5,7},{6,4},{7,5},{8,10},{9,11},{10,... | collective-permute-start | bytes 1572872 | tf_op jit(solution)/shard_map/ppermute | solution.py:73
  115.2 13.1 %collective-permute-start.13 = (bf16[256,1024]{1,0:T(8,128)(2,1)S(1)}, bf16[256,1024]{1,0:T(8,128)(2,1)S(1)}, u32[]{:S(2)}, u32[]{:S(2)}) collective-permute-start(bf16[256,1024]{1,0:T(8,128)(2,1)S(1)} %get-tuple-element.486.refs_0_), channel_id=1, source_target_pairs={{0,2},{1,3},{2,0},{3,1},{4,6},{5,7},{6,4},{7,5},{8,10},{9,11},{10,... | collective-permute-start | bytes 1572872 | tf_op jit(solution)/shard_map/ppermute | solution.py:73
  115.7 12.6 %collective-permute-start.14 = (bf16[256,1024]{1,0:T(8,128)(2,1)S(1)}, bf16[256,1024]{1,0:T(8,128)(2,1)S(1)}, u32[]{:S(2)}, u32[]{:S(2)}) collective-permute-start(bf16[256,1024]{1,0:T(8,128)(2,1)S(1)} %get-tuple-element.486.refs_0_), channel_id=1, source_target_pairs={{0,1},{1,0},{2,3},{3,2},{4,5},{5,4},{6,7},{7,6},{8,9},{9,8},{10,11... | collective-permute-start | bytes 1572872 | tf_op jit(solution)/shard_map/ppermute | solution.py:73
  142.1 14.0 %collective-permute-start.17 = (bf16[256,1024]{1,0:T(8,128)(2,1)S(1)}, bf16[256,1024]{1,0:T(8,128)(2,1)S(1)}, u32[]{:S(2)}, u32[]{:S(2)}) collective-permute-start(bf16[256,1024]{1,0:T(8,128)(2,1)S(1)} %get-tuple-element.501), channel_id=1, source_target_pairs={{0,2},{1,3},{2,0},{3,1},{4,6},{5,7},{6,4},{7,5},{8,10},{9,11},{10,... | collective-permute-start | bytes 1572872 | tf_op jit(solution)/shard_map/ppermute | solution.py:73
  157.6 13.1 %collective-permute-start.18 = (bf16[256,1024]{1,0:T(8,128)(2,1)S(1)}, bf16[256,1024]{1,0:T(8,128)(2,1)S(1)}, u32[]{:S(2)}, u32[]{:S(2)}) collective-permute-start(bf16[256,1024]{1,0:T(8,128)(2,1)S(1)} %get-tuple-element.511.refs_0_), channel_id=1, source_target_pairs={{0,2},{1,3},{2,0},{3,1},{4,6},{5,7},{6,4},{7,5},{8,10},{9,11},{10,... | collective-permute-start | bytes 1572872 | tf_op jit(solution)/shard_map/ppermute | solution.py:73
  158.1 12.6 %collective-permute-start.19 = (bf16[256,1024]{1,0:T(8,128)(2,1)S(1)}, bf16[256,1024]{1,0:T(8,128)(2,1)S(1)}, u32[]{:S(2)}, u32[]{:S(2)}) collective-permute-start(bf16[256,1024]{1,0:T(8,128)(2,1)S(1)} %get-tuple-element.511.refs_0_), channel_id=1, source_target_pairs={{0,1},{1,0},{2,3},{3,2},{4,5},{5,4},{6,7},{7,6},{8,9},{9,8},{10,11... | collective-permute-start | bytes 1572872 | tf_op jit(solution)/shard_map/ppermute | solution.py:73
  172.7 73.7 %collective-permute-start.21 = (bf16[256,1024]{1,0:T(8,128)(2,1)S(1)}, bf16[256,1024]{1,0:T(8,128)(2,1)S(1)}, u32[]{:S(2)}, u32[]{:S(2)}) collective-permute-start(bf16[256,1024]{1,0:T(8,128)(2,1)S(1)} %get-tuple-element.511.refs_0_), channel_id=1, source_target_pairs={{0,16},{4,20},{8,24},{12,28},{16,0},{20,4},{24,8},{28,12},{1,17},{... | collective-permute-start | bytes 1572872 | tf_op jit(solution)/shard_map/ppermute | solution.py:73
  175.4 71.0 %collective-permute-start.22 = (bf16[256,1024]{1,0:T(8,128)(2,1)S(1)}, bf16[256,1024]{1,0:T(8,128)(2,1)S(1)}, u32[]{:S(2)}, u32[]{:S(2)}) collective-permute-start(bf16[256,1024]{1,0:T(8,128)(2,1)S(1)} %collective-permute-done.18.refs_1_), channel_id=1, source_target_pairs={{0,16},{4,20},{8,24},{12,28},{16,0},{20,4},{24,8},{28,12},{1,17},{... | collective-permute-start | bytes 1572872 | tf_op jit(solution)/shard_map/ppermute | solution.py:73
  259.1 14.5 %collective-permute-start.29 = (bf16[256,1024]{1,0:T(8,128)(2,1)}, bf16[256,1024]{1,0:T(8,128)(2,1)}, u32[]{:S(2)}, u32[]{:S(2)}) collective-permute-start(bf16[256,1024]{1,0:T(8,128)(2,1)} %copy-done.70), channel_id=1, source_target_pairs={{0,1},{1,0},{2,3},{3,2},{4,5},{5,4},{6,7},{7,6},{8,9},{9,8},{10,11... | collective-permute-start | bytes 1572872 | tf_op jit(solution)/shard_map/ppermute | solution.py:73
  259.3 14.3 %collective-permute-start.30 = (bf16[256,1024]{1,0:T(8,128)(2,1)}, bf16[256,1024]{1,0:T(8,128)(2,1)}, u32[]{:S(2)}, u32[]{:S(2)}) collective-permute-start(bf16[256,1024]{1,0:T(8,128)(2,1)} %copy-done.72), channel_id=1, source_target_pairs={{0,1},{1,0},{2,3},{3,2},{4,5},{5,4},{6,7},{7,6},{8,9},{9,8},{10,11... | collective-permute-start | bytes 1572872 | tf_op jit(solution)/shard_map/ppermute | solution.py:73
  268.4 12.9 %collective-permute-start.31 = (bf16[256,1024]{1,0:T(8,128)(2,1)}, bf16[256,1024]{1,0:T(8,128)(2,1)}, u32[]{:S(2)}, u32[]{:S(2)}) collective-permute-start(bf16[256,1024]{1,0:T(8,128)(2,1)} %get-tuple-element.551), channel_id=1, source_target_pairs={{0,2},{1,3},{2,0},{3,1},{4,6},{5,7},{6,4},{7,5},{8,10},{9,11},{10,... | collective-permute-start | bytes 1572872 | tf_op jit(solution)/shard_map/ppermute | solution.py:73
  287.5 25.9 %collective-permute-start.32 = (bf16[256,1024]{1,0:T(8,128)(2,1)}, bf16[256,1024]{1,0:T(8,128)(2,1)}, u32[]{:S(2)}, u32[]{:S(2)}) collective-permute-start(bf16[256,1024]{1,0:T(8,128)(2,1)} %get-tuple-element.579.refs_0_), channel_id=1, source_target_pairs={{0,2},{1,3},{2,0},{3,1},{4,6},{5,7},{6,4},{7,5},{8,10},{9,11},{10,... | collective-permute-start | bytes 1572872 | tf_op jit(solution)/shard_map/ppermute | solution.py:73
  296.5 18.7 %collective-permute-start.33 = (bf16[256,1024]{1,0:T(8,128)(2,1)}, bf16[256,1024]{1,0:T(8,128)(2,1)S(1)}, u32[]{:S(2)}, u32[]{:S(2)}) collective-permute-start(bf16[256,1024]{1,0:T(8,128)(2,1)} %get-tuple-element.579.refs_0_), channel_id=1, source_target_pairs={{0,1},{1,0},{2,3},{3,2},{4,5},{5,4},{6,7},{7,6},{8,9},{9,8},{10,11... | collective-permute-start | bytes 1572872 | tf_op jit(solution)/shard_map/ppermute | solution.py:73
  314.0 42.0 %collective-permute-start.37 = (bf16[1792,512]{1,0:T(8,128)(2,1)S(1)}, bf16[1792,512]{1,0:T(8,128)(2,1)S(1)}, u32[]{:S(2)}, u32[]{:S(2)}) collective-permute-start(bf16[1792,512]{1,0:T(8,128)(2,1)S(1)} %get-tuple-element.596), channel_id=1, source_target_pairs={{0,4},{4,0},{8,12},{12,8},{16,20},{20,16},{24,28},{28,24},{1,5},{5... | collective-permute-start | bytes 5505032 | tf_op jit(solution)/shard_map/ppermute | solution.py:73
  325.9 31.4 %collective-permute-start.36 = (bf16[256,1024]{1,0:T(8,128)(2,1)S(1)}, bf16[256,1024]{1,0:T(8,128)(2,1)S(1)}, u32[]{:S(2)}, u32[]{:S(2)}) collective-permute-start(bf16[256,1024]{1,0:T(8,128)(2,1)S(1)} %get-tuple-element.595), channel_id=1, source_target_pairs={{0,2},{1,3},{2,0},{3,1},{4,6},{5,7},{6,4},{7,5},{8,10},{9,11},{10,... | collective-permute-start | bytes 1572872 | tf_op jit(solution)/shard_map/ppermute | solution.py:73
  334.0 62.3 %collective-permute-start.42 = (bf16[2048,512]{1,0:T(8,128)(2,1)}, bf16[2048,512]{1,0:T(8,128)(2,1)S(1)}, u32[]{:S(2)}, u32[]{:S(2)}) collective-permute-start(bf16[2048,512]{1,0:T(8,128)(2,1)} %get-tuple-element.640), channel_id=1, source_target_pairs={{0,8},{4,12},{8,0},{12,4},{16,24},{20,28},{24,16},{28,20},{1,9},{5... | collective-permute-start | bytes 6291464 | tf_op jit(solution)/shard_map/ppermute | solution.py:73
  358.2 19.1 %collective-permute-start.38 = (bf16[256,1024]{1,0:T(8,128)(2,1)S(1)}, bf16[256,1024]{1,0:T(8,128)(2,1)S(1)}, u32[]{:S(2)}, u32[]{:S(2)}) collective-permute-start(bf16[256,1024]{1,0:T(8,128)(2,1)S(1)} %get-tuple-element.631.refs_0_), channel_id=1, source_target_pairs={{0,2},{1,3},{2,0},{3,1},{4,6},{5,7},{6,4},{7,5},{8,10},{9,11},{10,... | collective-permute-start | bytes 1572872 | tf_op jit(solution)/shard_map/ppermute | solution.py:73
  375.8 79.6 %collective-permute-start.46 = (bf16[1792,512]{1,0:T(8,128)(2,1)S(1)}, bf16[1792,512]{1,0:T(8,128)(2,1)S(1)}, u32[]{:S(2)}, u32[]{:S(2)}) collective-permute-start(bf16[1792,512]{1,0:T(8,128)(2,1)S(1)} %get-tuple-element.673), channel_id=1, source_target_pairs={{0,4},{4,0},{8,12},{12,8},{16,20},{20,16},{24,28},{28,24},{1,5},{5... | collective-permute-start | bytes 5505032 | tf_op jit(solution)/shard_map/ppermute | solution.py:73
  392.7 14.8 %collective-permute-start.41 = (bf16[1024,256]{1,0:T(8,128)(2,1)S(1)}, bf16[1024,256]{1,0:T(8,128)(2,1)S(1)}, u32[]{:S(2)}, u32[]{:S(2)}) collective-permute-start(bf16[1024,256]{1,0:T(8,128)(2,1)S(1)} %bitcast.183), channel_id=1, source_target_pairs={{0,8},{4,12},{8,0},{12,4},{16,24},{20,28},{24,16},{28,20},{1,9},{5... | collective-permute-start | bytes 1572872 | tf_op jit(solution)/shard_map/ppermute | solution.py:73
  393.1 61.3 %collective-permute-start.47 = (bf16[1792,256]{1,0:T(8,128)(2,1)}, bf16[1792,256]{1,0:T(8,128)(2,1)S(1)}, u32[]{:S(2)}, u32[]{:S(2)}) collective-permute-start(bf16[1792,256]{1,0:T(8,128)(2,1)} %get-tuple-element.675), channel_id=1, source_target_pairs={{0,8},{4,12},{8,0},{12,4},{16,24},{20,28},{24,16},{28,20},{1,9},{5... | collective-permute-start | bytes 2752520 | tf_op jit(solution)/shard_map/ppermute | solution.py:73
  395.7 32.3 %collective-permute-start.44 = (bf16[256,1024]{1,0:T(8,128)(2,1)S(1)}, bf16[256,1024]{1,0:T(8,128)(2,1)S(1)}, u32[]{:S(2)}, u32[]{:S(2)}) collective-permute-start(bf16[256,1024]{1,0:T(8,128)(2,1)S(1)} %bitcast.178), channel_id=1, source_target_pairs={{0,4},{4,0},{8,12},{12,8},{16,20},{20,16},{24,28},{28,24},{1,5},{5... | collective-permute-start | bytes 1572872 | tf_op jit(solution)/shard_map/ppermute | solution.py:73
  407.7 45.2 %collective-permute-start.43 = (bf16[512,256]{1,0:T(8,128)(2,1)S(1)}, bf16[512,256]{1,0:T(8,128)(2,1)S(1)}, u32[]{:S(2)}, u32[]{:S(2)}) collective-permute-start(bf16[512,256]{1,0:T(8,128)(2,1)S(1)} %get-tuple-element.653), channel_id=1, source_target_pairs={{0,16},{4,20},{8,24},{12,28},{16,0},{20,4},{24,8},{28,12},{1,17},{... | collective-permute-start | bytes 786440 | tf_op jit(solution)/shard_map/ppermute | solution.py:73
  457.9 72.5 %collective-permute-start.61 = (bf16[2688,512]{1,0:T(8,128)(2,1)}, bf16[2688,512]{1,0:T(8,128)(2,1)}, u32[]{:S(2)}, u32[]{:S(2)}) collective-permute-start(bf16[2688,512]{1,0:T(8,128)(2,1)} %get-tuple-element.782), channel_id=1, source_target_pairs={{0,4},{4,0},{8,12},{12,8},{16,20},{20,16},{24,28},{28,24},{1,5},{5... | collective-permute-start | bytes 8257544 | tf_op jit(solution)/shard_map/ppermute | solution.py:73
  466.2 9.5 %collective-permute-start.51 = (bf16[64,1024]{1,0:T(8,128)(2,1)S(1)}, bf16[64,1024]{1,0:T(8,128)(2,1)S(1)}, u32[]{:S(2)}, u32[]{:S(2)}) collective-permute-start(bf16[64,1024]{1,0:T(8,128)(2,1)S(1)} %get-tuple-element.714), channel_id=1, source_target_pairs={{0,16},{4,20},{8,24},{12,28},{16,0},{20,4},{24,8},{28,12},{1,17},{... | collective-permute-start | bytes 393224 | tf_op jit(solution)/shard_map/ppermute | solution.py:73
  467.7 7.9 %collective-permute-start.50 = (bf16[64,1024]{1,0:T(8,128)(2,1)S(1)}, bf16[64,1024]{1,0:T(8,128)(2,1)S(1)}, u32[]{:S(2)}, u32[]{:S(2)}) collective-permute-start(bf16[64,1024]{1,0:T(8,128)(2,1)S(1)} %get-tuple-element.713), channel_id=1, source_target_pairs={{0,2},{1,3},{2,0},{3,1},{4,6},{5,7},{6,4},{7,5},{8,10},{9,11},{10,... | collective-permute-start | bytes 393224 | tf_op jit(solution)/shard_map/ppermute | solution.py:73
  468.3 47.0 %collective-permute-start.56 = (bf16[1792,256]{1,0:T(8,128)(2,1)}, bf16[1792,256]{1,0:T(8,128)(2,1)}, u32[]{:S(2)}, u32[]{:S(2)}) collective-permute-start(bf16[1792,256]{1,0:T(8,128)(2,1)} %get-tuple-element.740), channel_id=1, source_target_pairs={{0,8},{4,12},{8,0},{12,4},{16,24},{20,28},{24,16},{28,20},{1,9},{5... | collective-permute-start | bytes 2752520 | tf_op jit(solution)/shard_map/ppermute | solution.py:73
  480.0 9.1 %collective-permute-start.53 = (bf16[64,1024]{1,0:T(8,128)(2,1)}, bf16[64,1024]{1,0:T(8,128)(2,1)}, u32[]{:S(2)}, u32[]{:S(2)}) collective-permute-start(bf16[64,1024]{1,0:T(8,128)(2,1)} %get-tuple-element.727.refs_0_), channel_id=1, source_target_pairs={{0,1},{1,0},{2,3},{3,2},{4,5},{5,4},{6,7},{7,6},{8,9},{9,8},{10,11... | collective-permute-start | bytes 393224 | tf_op jit(solution)/shard_map/ppermute | solution.py:73
  481.7 20.8 %collective-permute-start.59 = (f32[9,1024]{1,0:T(8,128)}, f32[9,1024]{1,0:T(8,128)}, u32[]{:S(2)}, u32[]{:S(2)}) collective-permute-start(f32[9,1024]{1,0:T(8,128)} %fusion.26), channel_id=1, source_target_pairs={{0,1},{1,0},{2,3},{3,2},{4,5},{5,4},{6,7},{7,6},{8,9},{9,8},{10,11... | collective-permute-start | bytes 110600 | tf_op jit(solution)/shard_map/ppermute | solution.py:73
  489.1 39.6 %collective-permute-start.73 = (bf16[1792,128]{1,0:T(8,128)(2,1)}, bf16[1792,128]{1,0:T(8,128)(2,1)}, u32[]{:S(2)}, u32[]{:S(2)}) collective-permute-start(bf16[1792,128]{1,0:T(8,128)(2,1)} %copy-done.107), channel_id=1, source_target_pairs={{0,16},{4,20},{8,24},{12,28},{16,0},{20,4},{24,8},{28,12},{1,17},{... | collective-permute-start | bytes 1376264 | tf_op jit(solution)/shard_map/ppermute | solution.py:73
  489.1 54.3 %collective-permute-start.62 = (bf16[2048,256]{1,0:T(8,128)(2,1)}, bf16[2048,256]{1,0:T(8,128)(2,1)}, u32[]{:S(2)}, u32[]{:S(2)}) collective-permute-start(bf16[2048,256]{1,0:T(8,128)(2,1)} %copy-done.106), channel_id=1, source_target_pairs={{0,4},{4,0},{8,12},{12,8},{16,20},{20,16},{24,28},{28,24},{1,5},{5... | collective-permute-start | bytes 3145736 | tf_op jit(solution)/shard_map/ppermute | solution.py:73
  502.5 10.2 %collective-permute-start.55 = (bf16[128,1024]{1,0:T(8,128)(2,1)}, bf16[128,1024]{1,0:T(8,128)(2,1)}, u32[]{:S(2)}, u32[]{:S(2)}) collective-permute-start(bf16[128,1024]{1,0:T(8,128)(2,1)} %get-tuple-element.739), channel_id=1, source_target_pairs={{0,1},{1,0},{2,3},{3,2},{4,5},{5,4},{6,7},{7,6},{8,9},{9,8},{10,11... | collective-permute-start | bytes 786440 | tf_op jit(solution)/shard_map/ppermute | solution.py:73
  512.7 59.3 %collective-permute-start.68 = (bf16[1280,512]{1,0:T(8,128)(2,1)}, bf16[1280,512]{1,0:T(8,128)(2,1)}, u32[]{:S(2)}, u32[]{:S(2)}) collective-permute-start(bf16[1280,512]{1,0:T(8,128)(2,1)} %get-tuple-element.813), channel_id=1, source_target_pairs={{0,4},{4,0},{8,12},{12,8},{16,20},{20,16},{24,28},{28,24},{1,5},{5... | collective-permute-start | bytes 3932168 | tf_op jit(solution)/shard_map/ppermute | solution.py:73
  520.9 43.1 %collective-permute-start.65 = (bf16[784,512]{1,0:T(8,128)(2,1)}, bf16[784,512]{1,0:T(8,128)(2,1)}, u32[]{:S(2)}, u32[]{:S(2)}) collective-permute-start(bf16[784,512]{1,0:T(8,128)(2,1)} %get-tuple-element.803), channel_id=1, source_target_pairs={{0,8},{4,12},{8,0},{12,4},{16,24},{20,28},{24,16},{28,20},{1,9},{5... | collective-permute-start | bytes 2408456 | tf_op jit(solution)/shard_map/ppermute | solution.py:73
  528.7 37.9 %collective-permute-start.74 = (bf16[1792,128]{1,0:T(8,128)(2,1)}, bf16[1792,128]{1,0:T(8,128)(2,1)}, u32[]{:S(2)}, u32[]{:S(2)}) collective-permute-start(bf16[1792,128]{1,0:T(8,128)(2,1)} %get-tuple-element.836), channel_id=1, source_target_pairs={{0,16},{4,20},{8,24},{12,28},{16,0},{20,4},{24,8},{28,12},{1,17},{... | collective-permute-start | bytes 1376264 | tf_op jit(solution)/shard_map/ppermute | solution.py:73
  530.4 13.2 %collective-permute-start.60 = (bf16[64,1024]{1,0:T(8,128)(2,1)S(1)}, bf16[64,1024]{1,0:T(8,128)(2,1)}, u32[]{:S(2)}, u32[]{:S(2)}) collective-permute-start(bf16[64,1024]{1,0:T(8,128)(2,1)S(1)} %add_convert_fusion.1), channel_id=1, source_target_pairs={{0,2},{1,3},{2,0},{3,1},{4,6},{5,7},{6,4},{7,5},{8,10},{9,11},{10,... | collective-permute-start | bytes 393224 | tf_op jit(solution)/shard_map/ppermute | solution.py:73
  543.3 72.6 %collective-permute-start.72 = (bf16[2688,256]{1,0:T(8,128)(2,1)}, bf16[2688,256]{1,0:T(8,128)(2,1)}, u32[]{:S(2)}, u32[]{:S(2)}) collective-permute-start(bf16[2688,256]{1,0:T(8,128)(2,1)} %get-tuple-element.830), channel_id=1, source_target_pairs={{0,8},{4,12},{8,0},{12,4},{16,24},{20,28},{24,16},{28,20},{1,9},{5... | collective-permute-start | bytes 4128776 | tf_op jit(solution)/shard_map/ppermute | solution.py:73
  546.5 46.5 %collective-permute-start.71 = (bf16[2048,128]{1,0:T(8,128)(2,1)}, bf16[2048,128]{1,0:T(8,128)(2,1)}, u32[]{:S(2)}, u32[]{:S(2)}) collective-permute-start(bf16[2048,128]{1,0:T(8,128)(2,1)} %get-tuple-element.827), channel_id=1, source_target_pairs={{0,16},{4,20},{8,24},{12,28},{16,0},{20,4},{24,8},{28,12},{1,17},{... | collective-permute-start | bytes 1572872 | tf_op jit(solution)/shard_map/ppermute | solution.py:73
  566.6 27.5 %collective-permute-start.66 = (bf16[784,256]{1,0:T(8,128)(2,1)}, bf16[784,256]{1,0:T(8,128)(2,1)}, u32[]{:S(2)}, u32[]{:S(2)}) collective-permute-start(bf16[784,256]{1,0:T(8,128)(2,1)} %get-tuple-element.807), channel_id=1, source_target_pairs={{0,4},{4,0},{8,12},{12,8},{16,20},{20,16},{24,28},{28,24},{1,5},{5... | collective-permute-start | bytes 1204232 | tf_op jit(solution)/shard_map/ppermute | solution.py:73
  574.4 36.2 %collective-permute-start.69 = (bf16[1280,256]{1,0:T(8,128)(2,1)}, bf16[1280,256]{1,0:T(8,128)(2,1)}, u32[]{:S(2)}, u32[]{:S(2)}) collective-permute-start(bf16[1280,256]{1,0:T(8,128)(2,1)} %get-tuple-element.820), channel_id=1, source_target_pairs={{0,8},{4,12},{8,0},{12,4},{16,24},{20,28},{24,16},{28,20},{1,9},{5... | collective-permute-start | bytes 1966088 | tf_op jit(solution)/shard_map/ppermute | solution.py:73
  595.3 14.5 %collective-permute-start.67 = (bf16[784,128]{1,0:T(8,128)(2,1)S(1)}, bf16[784,128]{1,0:T(8,128)(2,1)S(1)}, u32[]{:S(2)}, u32[]{:S(2)}) collective-permute-start(bf16[784,128]{1,0:T(8,128)(2,1)S(1)} %get-tuple-element.812), channel_id=1, source_target_pairs={{0,16},{4,20},{8,24},{12,28},{16,0},{20,4},{24,8},{28,12},{1,17},{... | collective-permute-start | bytes 602120 | tf_op jit(solution)/shard_map/ppermute | solution.py:73
  612.5 33.2 %collective-permute-start.70 = (bf16[1280,128]{1,0:T(8,128)(2,1)}, bf16[1280,128]{1,0:T(8,128)(2,1)}, u32[]{:S(2)}, u32[]{:S(2)}) collective-permute-start(bf16[1280,128]{1,0:T(8,128)(2,1)} %get-tuple-element.825), channel_id=1, source_target_pairs={{0,16},{4,20},{8,24},{12,28},{16,0},{20,4},{24,8},{28,12},{1,17},{... | collective-permute-start | bytes 983048 | tf_op jit(solution)/shard_map/ppermute | solution.py:73
  618.4 40.7 %collective-permute-start.75 = (bf16[2688,128]{1,0:T(8,128)(2,1)}, bf16[2688,128]{1,0:T(8,128)(2,1)S(1)}, u32[]{:S(2)}, u32[]{:S(2)}) collective-permute-start(bf16[2688,128]{1,0:T(8,128)(2,1)} %get-tuple-element.837), channel_id=1, source_target_pairs={{0,16},{4,20},{8,24},{12,28},{16,0},{20,4},{24,8},{28,12},{1,17},{... | collective-permute-start | bytes 2064392 | tf_op jit(solution)/shard_map/ppermute | solution.py:73
  (172 other events, 1758.6 us)
Sparse Core Ops, SparseCore 0:
  525.4 36.6 all-reduce.1

commit v5 on v4

--- a/solution.py
+++ b/solution.py
@@ -24,24 +24,24 @@
     (("a", "make"), ("a", "send"),),
     (),
     (),
-    (("f", "make"), ("f", "send"), ("a", "add"), ("a", "send"),),
+    (("f", "make"), ("f", "send"),),
     (),
-    (("b", "make"), ("b", "send"),),
-    (),
+    (("b", "make"), ("a", "add"), ("a", "send"),),
+    (("b", "send"),),
     (),
     (("t", "step"), ("f", "add"),),
-    (("t", "step"), ("c", "make"),),
+    (("c", "make"), ("t", "step"),),
     (("a", "add"), ("a", "send"), ("b", "add"), ("b", "send"),),
     (("c", "send"), ("t", "step"), ("f", "send"),),
     (),
     (),
     (),
     (),
-    (("p", "make"), ("p", "send"), ("b", "add"), ("b", "send"),),
-    (("s", "make"), ("s", "send"),),
+    (("b", "add"), ("b", "send"), ("s", "make"), ("s", "send"),),
+    (("p", "make"), ("p", "send"),),
     (("f", "add"), ("f", "send"), ("c", "add"), ("c", "send"),),
     (),
-    (("p", "add"), ("p", "send"), ("a", "wait"), ("b", "wait"), ("s", "add"), ("s", "send"), ("c", "add"), ("c", "send"), ("p", "add"), ("p", "send"), ("f", "wait"), ("s", "add"), ("s", "send"), ("c", "wait"), ("p", "wait"), ("s", "wait"),),
+    (("p", "add"), ("p", "send"), ("s", "add"), ("s", "send"), ("c", "add"), ("c", "send"), ("s", "add"), ("s", "send"), ("p", "add"), ("p", "send"), ("a", "wait"), ("b", "wait"), ("f", "wait"), ("c", "wait"), ("p", "wait"), ("s", "wait"),),
     (),
     (),
     (),

time: 680 us -> 650 us (0.956)
  waiting for transfers between devices: 236 us -> 214 us
    ppermute x76, waiting for transfers between devices: 236 us -> 211 us  [swap(): return lax.ppermute(value, axis, [(i, i ^ bit) for i in range(count)])]
    unnamed x293 -> x315, local copies, waits for them, and re-layouts: 53.7 us -> 46.8 us
  transfers between devices with their start and end apart: 77 -> 77, of which waited for: 38 -> 41; matrix products, arithmetic and copies ran while one was open for 10% -> 11% of each run, Pallas kernels for 30% -> 30%
where the time goes in v5:
time: 650 us; the launch traced here: 642 us
  Pallas kernels  225 us (35%)
  waiting for transfers between devices  214 us (33%)
  local copies, waits for them, and re-layouts  85.1 us (13%)
  starting transfers between devices  69.2 us (11%)
  other arithmetic  22.5 us (3%)
  between operations  18 us (3%)
  matrix products  7.9 us (1%)
    ppermute x76, waiting for transfers between devices, swap(): return lax.ppermute(value, axis, [(i, i ^ bit) for i in range(count)])  211 us
    ppermute x76, starting transfers between devices, swap(): return lax.ppermute(value, axis, [(i, i ^ bit) for i in range(count)])  69.2 us
    pallas_call x1, Pallas kernels, vocab_forward(): pl.pallas_call(vocab_forward_kernel, grid=(entries // tile,), in_specs=[w...  68 us
    pallas_call x3, Pallas kernels, half_slope(): pl.pallas_call(functools.partial(half_slope_kernel, first, vocab_tile(wei...  59.8 us
    unnamed x315, local copies, waits for them, and re-layouts  46.8 us
    pallas_call x40, Pallas kernels, run_whole(): pl.pallas_call(kernel, in_specs=[VMEM] * len(operands), out_specs=[VMEM]...  45.2 us
    gather x1, local copies, waits for them, and re-layouts, on_device(): jnp.take(embedding, through(label_places), axis=0, mode='clip')  17.8 us
  transfers between devices with their start and end apart: 77, of which 41 were waited for; matrix products, arithmetic and copies ran while one was open for 11% of the time, Pallas kernels for 30%

profile of v5, /device:TPU:0, one launch (start us, length us, event | category | flops | bytes accessed | tf_op | source)
XLA Modules:
  0.0 641.8 jit_solution(11347460233810213230)
XLA Ops:
  17.5 2.9 collective-permute-start.1
  20.4 3.8 collective-permute-done.1.arrived_ref
  33.0 2.7 collective-permute-start.5
  36.9 5.5 collective-permute-done.5
  43.2 3.4 collective-permute-start.8
  47.2 8.3 %collective-permute-done.7 = bf16[2,1,256,256]{3,2,0,1:T(8,128)(2,1)S(1)} collective-permute-done((bf16[2,1,256,256]{3,2,0,1:T(8,128)(2,1)S(1)}, bf16[2,1,256,256]{3,2,0,1:T(8,128)(2,1)S(1)}, u32[]{:S(2)}, u32[]{:S(2)}) %collective-permute-start.7) | collective-permute-done | bytes 262176 | tf_op jit(solution)/shard_map/ppermute | solution.py:73
  55.4 3.2 collective-permute-done.8
  64.6 17.8 %gather_fusion.4 = bf16[1024,1024]{1,0:T(8,128)(2,1)} fusion(bf16[12544,1024]{1,0:T(8,128)(2,1)} %table_ref.7, s32[1024]{0:T(1024)S(1)} %broadcast_clamp_fusion), kind=kCustom, calls=%fused_computation.4 | custom fusion | bytes 4198400 | tf_op jit(solution)/shard_map/jit(_take)/gather | solution.py:1210
  83.8 5.1 attend_forward.3
  89.8 2.6 collective-permute-done.11.arrived_ref
  99.3 4.0 pick.1
  103.3 5.2 collective-permute-done.12.arrived_ref
  113.8 11.6 %collective-permute-done.13.refs_1_ = bf16[256,1024]{1,0:T(8,128)(2,1)S(1)} collective-permute-done((bf16[256,1024]{1,0:T(8,128)(2,1)S(1)}, bf16[256,1024]{1,0:T(8,128)(2,1)S(1)}, u32[]{:S(2)}, u32[]{:S(2)}) %collective-permute-start.13) | collective-permute-done | bytes 524320 | tf_op jit(solution)/shard_map/ppermute | solution.py:73
  128.9 4.7 feed_forward.1
  136.4 2.5 collective-permute-done.16.arrived_ref
  140.8 12.4 %collective-permute-done.17.arrived_ref = bf16[256,1024]{1,0:T(8,128)(2,1)S(1)} collective-permute-done((bf16[256,1024]{1,0:T(8,128)(2,1)S(1)}, bf16[256,1024]{1,0:T(8,128)(2,1)S(1)}, u32[]{:S(2)}, u32[]{:S(2)}) %collective-permute-start.17) | collective-permute-done | bytes 524320 | tf_op jit(solution)/shard_map/ppermute | solution.py:73
  156.2 11.7 %collective-permute-done.18.refs_1_ = bf16[256,1024]{1,0:T(8,128)(2,1)S(1)} collective-permute-done((bf16[256,1024]{1,0:T(8,128)(2,1)S(1)}, bf16[256,1024]{1,0:T(8,128)(2,1)S(1)}, u32[]{:S(2)}, u32[]{:S(2)}) %collective-permute-start.18) | collective-permute-done | bytes 524320 | tf_op jit(solution)/shard_map/ppermute | solution.py:73
  169.8 2.7 collective-permute-start.21
  175.4 68.0 %vocab_forward.1 = (bf16[1024,12544]{1,0:T(8,128)(2,1)}, f32[1024,1024]{1,0:T(8,128)S(1)}, f32[1024,128]{1,0:T(8,128)S(1)}, f32[8,1024]{1,0:T(8,128)S(1)}) custom-call(bf16[1024,1024]{1,0:T(8,128)(2,1)S(1)} %get-tuple-element.517.state_ref, bf16[12544,1024]{1,0:T(8,128)(2,1)} %table_ref.7, s32[1024,128]{1,0:T(8,128)S(1)} %broadcast_in_dim.125.label_ref, ...), custom_call_target="tpu_custom_call" | custom-call | tf_op jit(solution)/shard_map/vocab_forward/pallas_call | solution.py:478
  248.9 2.5 vocab_part.1
  253.4 2.8 collective-permute-start.25
  272.1 6.6 %collective-permute-done.31.arrived_ref = bf16[256,1024]{1,0:T(8,128)(2,1)} collective-permute-done((bf16[256,1024]{1,0:T(8,128)(2,1)}, bf16[256,1024]{1,0:T(8,128)(2,1)}, u32[]{:S(2)}, u32[]{:S(2)}) %collective-permute-start.31) | collective-permute-done | bytes 524320 | tf_op jit(solution)/shard_map/ppermute | solution.py:73
  281.2 2.7 norm_backward.3
  294.9 17.8 %half_slope.3 = (bf16[1792,512]{1,0:T(8,128)(2,1)}, bf16[1792,512]{1,0:T(8,128)(2,1)S(1)}) custom-call(s32[1]{0:T(128)S(6)} %mul.72.base_ref, bf16[1024,12544]{1,0:T(8,128)(2,1)} %get-tuple-element.558.weight_ref, bf16[12544,1024]{1,0:T(8,128)(2,1)} %table_ref.7, f32[1024,128]{1,0:T(8,128)S(1)} %get-tuple-element.657.factor_ref, ...), custom_call_target="tpu_custom_call" | custom-call | tf_op jit(solution)/shard_map/half_slope/pallas_call | solution.py:834
  315.0 7.1 %feed_backward.1 = (bf16[1024,1024]{1,0:T(8,128)(2,1)S(1)}, bf16[1024,1024]{1,0:T(8,128)(2,1)S(1)}, f32[1,1024]{1,0:T(1,128)S(1)}, bf16[512,1024]{1,0:T(8,128)(2,1)S(1)}, f32[512,1024]{1,0:T(8,128)S(1)}) custom-call(bf16[256,1024]{1,0:T(8,128)(2,1)} %get-tuple-element.579.refs_0_, bf16[256,1024]{1,0:T(8,128)(2,1)} %collective-permute-done.32.refs_1_, ...), custom_call_target="tpu_custom_call" | custom-call | tf_op jit(solution)/shard_map/feed_backward/pallas_call | solution.py:139
  325.8 5.5 slope_group.3
  331.7 7.8 %collective-permute-done.36.refs_1_ = bf16[256,1024]{1,0:T(8,128)(2,1)S(1)} collective-permute-done((bf16[256,1024]{1,0:T(8,128)(2,1)S(1)}, bf16[256,1024]{1,0:T(8,128)(2,1)S(1)}, u32[]{:S(2)}, u32[]{:S(2)}) %collective-permute-start.36) | collective-permute-done | bytes 524320 | tf_op jit(solution)/shard_map/ppermute | solution.py:73
  341.0 17.4 %half_slope.4 = (bf16[1792,512]{1,0:T(8,128)(2,1)}, bf16[1792,512]{1,0:T(8,128)(2,1)S(1)}) custom-call(s32[1]{0:T(128)S(6)} %mul.72.base_ref, bf16[1024,12544]{1,0:T(8,128)(2,1)} %get-tuple-element.558.weight_ref, bf16[12544,1024]{1,0:T(8,128)(2,1)} %table_ref.7, f32[1024,128]{1,0:T(8,128)S(1)} %get-tuple-element.657.factor_ref, ...), custom_call_target="tpu_custom_call" | custom-call | tf_op jit(solution)/shard_map/half_slope/pallas_call | solution.py:834
  358.3 6.6 %collective-permute-done.38.arrived_ref = bf16[1792,512]{1,0:T(8,128)(2,1)S(1)} collective-permute-done((bf16[1792,512]{1,0:T(8,128)(2,1)}, bf16[1792,512]{1,0:T(8,128)(2,1)S(1)}, u32[]{:S(2)}, u32[]{:S(2)}) %collective-permute-start.38) | collective-permute-done | bytes 1835040 | tf_op jit(solution)/shard_map/ppermute | solution.py:73
  372.1 10.5 %attend_backward.2 = (bf16[8,256,256]{2,1,0:T(8,128)(2,1)S(1)}, bf16[2,256,256]{2,1,0:T(8,128)(2,1)S(1)}, bf16[2,256,256]{2,1,0:T(8,128)(2,1)S(1)}) custom-call(s32[4]{0:T(128)S(1)} %gather_fusion, s32[4]{0:T(128)S(1)} %copy-done.112, s32[4]{0:T(128)S(1)} %copy-done.110, bf16[8,256,256]{2,1,0:T(8,128)(2,1)S(1)} %maximum_bitcast_fusion.query_ref, ...), custom_call_target="tpu_custom_call" | custom-call | tf_op jit(solution)/shard_map/attend_backward/pallas_call | solution.py:696
  386.7 10.9 %collective-permute-done.41.arrived_ref = bf16[1024,256]{1,0:T(8,128)(2,1)S(1)} collective-permute-done((bf16[1024,256]{1,0:T(8,128)(2,1)S(1)}, bf16[1024,256]{1,0:T(8,128)(2,1)S(1)}, u32[]{:S(2)}, u32[]{:S(2)}) %collective-permute-start.41) | collective-permute-done | bytes 524320 | tf_op jit(solution)/shard_map/ppermute | solution.py:73
  399.0 24.7 %half_slope.5 = (bf16[2688,512]{1,0:T(8,128)(2,1)}, bf16[2688,512]{1,0:T(8,128)(2,1)S(1)}) custom-call(s32[1]{0:T(128)S(6)} %mul.72.base_ref, bf16[1024,12544]{1,0:T(8,128)(2,1)} %get-tuple-element.558.weight_ref, bf16[12544,1024]{1,0:T(8,128)(2,1)} %table_ref.7, f32[1024,128]{1,0:T(8,128)S(1)} %get-tuple-element.657.factor_ref, ...), custom_call_target="tpu_custom_call" | custom-call | tf_op jit(solution)/shard_map/half_slope/pallas_call | solution.py:834
  438.9 7.2 %collective-permute-done.51.refs_3_ = bf16[64,1024]{1,0:T(8,128)(2,1)S(1)} collective-permute-done((bf16[64,1024]{1,0:T(8,128)(2,1)S(1)}, bf16[64,1024]{1,0:T(8,128)(2,1)S(1)}, u32[]{:S(2)}, u32[]{:S(2)}) %collective-permute-start.51) | collective-permute-done | bytes 131104 | tf_op jit(solution)/shard_map/ppermute | solution.py:73
  449.9 2.4 collective-permute-done.52.refs_1_
  454.9 2.4 attend_backward.3
  479.9 4.0 slope_group.5
  485.1 2.5 slope_group.4
  494.1 3.3 add_columns.18
  500.2 14.4 %collective-permute-done.62.arrived_ref = bf16[2048,256]{1,0:T(8,128)(2,1)} collective-permute-done((bf16[2048,256]{1,0:T(8,128)(2,1)}, bf16[2048,256]{1,0:T(8,128)(2,1)}, u32[]{:S(2)}, u32[]{:S(2)}) %collective-permute-start.62) | collective-permute-done | bytes 1048608 | tf_op jit(solution)/shard_map/ppermute | solution.py:73
  526.6 2.5 all-reduce.2.cloned.1.call-done
  529.1 2.8 reshape.360
  536.2 6.4 %collective-permute-done.68.arrived_ref = bf16[1280,512]{1,0:T(8,128)(2,1)} collective-permute-done((bf16[1280,512]{1,0:T(8,128)(2,1)}, bf16[1280,512]{1,0:T(8,128)(2,1)}, u32[]{:S(2)}, u32[]{:S(2)}) %collective-permute-start.68) | collective-permute-done | bytes 1310752 | tf_op jit(solution)/shard_map/ppermute | solution.py:73
  547.7 16.0 %collective-permute-done.74.refs_4_ = bf16[1792,128]{1,0:T(8,128)(2,1)} collective-permute-done((bf16[1792,128]{1,0:T(8,128)(2,1)}, bf16[1792,128]{1,0:T(8,128)(2,1)}, u32[]{:S(2)}, u32[]{:S(2)}) %collective-permute-start.74) | collective-permute-done | bytes 458784 | tf_op jit(solution)/shard_map/ppermute | solution.py:73
  568.3 9.4 %collective-permute-done.67.refs_1_ = bf16[784,128]{1,0:T(8,128)(2,1)S(1)} collective-permute-done((bf16[784,128]{1,0:T(8,128)(2,1)S(1)}, bf16[784,128]{1,0:T(8,128)(2,1)S(1)}, u32[]{:S(2)}, u32[]{:S(2)}) %collective-permute-start.67) | collective-permute-done | bytes 200736 | tf_op jit(solution)/shard_map/ppermute | solution.py:73
  583.9 2.5 add_columns.23
  594.6 20.0 %collective-permute-done.70.refs_1_ = bf16[1280,128]{1,0:T(8,128)(2,1)} collective-permute-done((bf16[1280,128]{1,0:T(8,128)(2,1)}, bf16[1280,128]{1,0:T(8,128)(2,1)}, u32[]{:S(2)}, u32[]{:S(2)}) %collective-permute-start.70) | collective-permute-done | bytes 327712 | tf_op jit(solution)/shard_map/ppermute | solution.py:73
  619.6 9.5 %collective-permute-done.75.refs_5_ = bf16[2688,128]{1,0:T(8,128)(2,1)S(1)} collective-permute-done((bf16[2688,128]{1,0:T(8,128)(2,1)}, bf16[2688,128]{1,0:T(8,128)(2,1)S(1)}, u32[]{:S(2)}, u32[]{:S(2)}) %collective-permute-start.75) | collective-permute-done | bytes 688160 | tf_op jit(solution)/shard_map/ppermute | solution.py:73
  629.1 4.3 place_halves.1
  (604 shorter events, 213.2 us)
Async XLA Ops:
  7.2 521.9 %all-reduce.2.cloned.1.call-start = ((), (), s32[]{:S(2)}) async-start(), calls=%async_computation | async-start | bytes 2097152 | tf_op jit(solution)/shard_map/psum | solution.py:1488
  33.0 9.4 %collective-permute-start.5 = (bf16[1,1,256,256]{3,2,0,1:T(8,128)(2,1)S(1)}, bf16[1,1,256,256]{3,2,0,1:T(8,128)(2,1)S(1)}, u32[]{:S(2)}, u32[]{:S(2)}) collective-permute-start(bf16[1,1,256,256]{3,2,0,1:T(8,128)(2,1)S(1)} %bitcast.142), channel_id=1, source_target_pairs={{0,16},{4,20},{8,24},{12,28},{16,0},{20,4},{24,8},{28,12},{1,17},{... | collective-permute-start | bytes 393224 | tf_op jit(solution)/shard_map/ppermute | solution.py:73
  42.5 13.0 %collective-permute-start.7 = (bf16[2,1,256,256]{3,2,0,1:T(8,128)(2,1)S(1)}, bf16[2,1,256,256]{3,2,0,1:T(8,128)(2,1)S(1)}, u32[]{:S(2)}, u32[]{:S(2)}) collective-permute-start(bf16[2,1,256,256]{3,2,0,1:T(8,128)(2,1)S(1)} %pad_maximum_fusion.3), channel_id=1, source_target_pairs={{0,8},{4,12},{8,0},{12,4},{16,24},{20,28},{24,16},{28,20},{1,9},{5... | collective-permute-start | bytes 786440 | tf_op jit(solution)/shard_map/ppermute | solution.py:73
  43.2 15.3 %collective-permute-start.8 = (bf16[2,1,64,1024]{3,2,0,1:T(8,128)(2,1)S(1)}, bf16[2,1,64,1024]{3,2,0,1:T(8,128)(2,1)S(1)}, u32[]{:S(2)}, u32[]{:S(2)}) collective-permute-start(bf16[2,1,64,1024]{3,2,0,1:T(8,128)(2,1)S(1)} %pad_maximum_fusion.4), channel_id=1, source_target_pairs={{0,16},{4,20},{8,24},{12,28},{16,0},{20,4},{24,8},{28,12},{1,17},{... | collective-permute-start | bytes 786440 | tf_op jit(solution)/shard_map/ppermute | solution.py:73
  59.5 23.0 %collective-permute-start.9 = (bf16[4,1,256,256]{3,2,0,1:T(8,128)(2,1)}, bf16[4,1,256,256]{3,2,0,1:T(8,128)(2,1)}, u32[]{:S(2)}, u32[]{:S(2)}) collective-permute-start(bf16[4,1,256,256]{3,2,0,1:T(8,128)(2,1)} %pad_maximum_fusion), channel_id=1, source_target_pairs={{0,4},{4,0},{8,12},{12,8},{16,20},{20,16},{24,28},{28,24},{1,5},{5... | collective-permute-start | bytes 1572872 | tf_op jit(solution)/shard_map/ppermute | solution.py:73
  61.5 21.0 %collective-permute-start.10 = (bf16[4,1,64,1024]{3,2,0,1:T(8,128)(2,1)}, bf16[4,1,64,1024]{3,2,0,1:T(8,128)(2,1)}, u32[]{:S(2)}, u32[]{:S(2)}) collective-permute-start(bf16[4,1,64,1024]{3,2,0,1:T(8,128)(2,1)} %pad_maximum_fusion.1), channel_id=1, source_target_pairs={{0,8},{4,12},{8,0},{12,4},{16,24},{20,28},{24,16},{28,20},{1,9},{5... | collective-permute-start | bytes 1572872 | tf_op jit(solution)/shard_map/ppermute | solution.py:73
  94.3 14.2 %collective-permute-start.12 = (bf16[256,1024]{1,0:T(8,128)(2,1)}, bf16[256,1024]{1,0:T(8,128)(2,1)S(1)}, u32[]{:S(2)}, u32[]{:S(2)}) collective-permute-start(bf16[256,1024]{1,0:T(8,128)(2,1)} %get-tuple-element.476), channel_id=1, source_target_pairs={{0,2},{1,3},{2,0},{3,1},{4,6},{5,7},{6,4},{7,5},{8,10},{9,11},{10,... | collective-permute-start | bytes 1572872 | tf_op jit(solution)/shard_map/ppermute | solution.py:73
  112.3 13.1 %collective-permute-start.13 = (bf16[256,1024]{1,0:T(8,128)(2,1)S(1)}, bf16[256,1024]{1,0:T(8,128)(2,1)S(1)}, u32[]{:S(2)}, u32[]{:S(2)}) collective-permute-start(bf16[256,1024]{1,0:T(8,128)(2,1)S(1)} %get-tuple-element.486.refs_0_), channel_id=1, source_target_pairs={{0,2},{1,3},{2,0},{3,1},{4,6},{5,7},{6,4},{7,5},{8,10},{9,11},{10,... | collective-permute-start | bytes 1572872 | tf_op jit(solution)/shard_map/ppermute | solution.py:73
  113.8 11.7 %collective-permute-start.14 = (bf16[256,1024]{1,0:T(8,128)(2,1)S(1)}, bf16[256,1024]{1,0:T(8,128)(2,1)S(1)}, u32[]{:S(2)}, u32[]{:S(2)}) collective-permute-start(bf16[256,1024]{1,0:T(8,128)(2,1)S(1)} %get-tuple-element.486.refs_0_), channel_id=1, source_target_pairs={{0,1},{1,0},{2,3},{3,2},{4,5},{5,4},{6,7},{7,6},{8,9},{9,8},{10,11... | collective-permute-start | bytes 1572872 | tf_op jit(solution)/shard_map/ppermute | solution.py:73
  139.2 14.0 %collective-permute-start.17 = (bf16[256,1024]{1,0:T(8,128)(2,1)S(1)}, bf16[256,1024]{1,0:T(8,128)(2,1)S(1)}, u32[]{:S(2)}, u32[]{:S(2)}) collective-permute-start(bf16[256,1024]{1,0:T(8,128)(2,1)S(1)} %get-tuple-element.501), channel_id=1, source_target_pairs={{0,2},{1,3},{2,0},{3,1},{4,6},{5,7},{6,4},{7,5},{8,10},{9,11},{10,... | collective-permute-start | bytes 1572872 | tf_op jit(solution)/shard_map/ppermute | solution.py:73
  154.7 13.1 %collective-permute-start.18 = (bf16[256,1024]{1,0:T(8,128)(2,1)S(1)}, bf16[256,1024]{1,0:T(8,128)(2,1)S(1)}, u32[]{:S(2)}, u32[]{:S(2)}) collective-permute-start(bf16[256,1024]{1,0:T(8,128)(2,1)S(1)} %get-tuple-element.511.refs_0_), channel_id=1, source_target_pairs={{0,2},{1,3},{2,0},{3,1},{4,6},{5,7},{6,4},{7,5},{8,10},{9,11},{10,... | collective-permute-start | bytes 1572872 | tf_op jit(solution)/shard_map/ppermute | solution.py:73
  156.2 11.7 %collective-permute-start.19 = (bf16[256,1024]{1,0:T(8,128)(2,1)S(1)}, bf16[256,1024]{1,0:T(8,128)(2,1)S(1)}, u32[]{:S(2)}, u32[]{:S(2)}) collective-permute-start(bf16[256,1024]{1,0:T(8,128)(2,1)S(1)} %get-tuple-element.511.refs_0_), channel_id=1, source_target_pairs={{0,1},{1,0},{2,3},{3,2},{4,5},{5,4},{6,7},{7,6},{8,9},{9,8},{10,11... | collective-permute-start | bytes 1572872 | tf_op jit(solution)/shard_map/ppermute | solution.py:73
  169.8 73.7 %collective-permute-start.21 = (bf16[256,1024]{1,0:T(8,128)(2,1)S(1)}, bf16[256,1024]{1,0:T(8,128)(2,1)S(1)}, u32[]{:S(2)}, u32[]{:S(2)}) collective-permute-start(bf16[256,1024]{1,0:T(8,128)(2,1)S(1)} %get-tuple-element.511.refs_0_), channel_id=1, source_target_pairs={{0,16},{4,20},{8,24},{12,28},{16,0},{20,4},{24,8},{28,12},{1,17},{... | collective-permute-start | bytes 1572872 | tf_op jit(solution)/shard_map/ppermute | solution.py:73
  172.5 71.0 %collective-permute-start.22 = (bf16[256,1024]{1,0:T(8,128)(2,1)S(1)}, bf16[256,1024]{1,0:T(8,128)(2,1)S(1)}, u32[]{:S(2)}, u32[]{:S(2)}) collective-permute-start(bf16[256,1024]{1,0:T(8,128)(2,1)S(1)} %collective-permute-done.18.refs_1_), channel_id=1, source_target_pairs={{0,16},{4,20},{8,24},{12,28},{16,0},{20,4},{24,8},{28,12},{1,17},{... | collective-permute-start | bytes 1572872 | tf_op jit(solution)/shard_map/ppermute | solution.py:73
  256.2 14.5 %collective-permute-start.29 = (bf16[256,1024]{1,0:T(8,128)(2,1)}, bf16[256,1024]{1,0:T(8,128)(2,1)}, u32[]{:S(2)}, u32[]{:S(2)}) collective-permute-start(bf16[256,1024]{1,0:T(8,128)(2,1)} %copy-done.76), channel_id=1, source_target_pairs={{0,1},{1,0},{2,3},{3,2},{4,5},{5,4},{6,7},{7,6},{8,9},{9,8},{10,11... | collective-permute-start | bytes 1572872 | tf_op jit(solution)/shard_map/ppermute | solution.py:73
  256.4 14.3 %collective-permute-start.30 = (bf16[256,1024]{1,0:T(8,128)(2,1)}, bf16[256,1024]{1,0:T(8,128)(2,1)}, u32[]{:S(2)}, u32[]{:S(2)}) collective-permute-start(bf16[256,1024]{1,0:T(8,128)(2,1)} %copy-done.78), channel_id=1, source_target_pairs={{0,1},{1,0},{2,3},{3,2},{4,5},{5,4},{6,7},{7,6},{8,9},{9,8},{10,11... | collective-permute-start | bytes 1572872 | tf_op jit(solution)/shard_map/ppermute | solution.py:73
  265.8 12.9 %collective-permute-start.31 = (bf16[256,1024]{1,0:T(8,128)(2,1)}, bf16[256,1024]{1,0:T(8,128)(2,1)}, u32[]{:S(2)}, u32[]{:S(2)}) collective-permute-start(bf16[256,1024]{1,0:T(8,128)(2,1)} %get-tuple-element.551), channel_id=1, source_target_pairs={{0,2},{1,3},{2,0},{3,1},{4,6},{5,7},{6,4},{7,5},{8,10},{9,11},{10,... | collective-permute-start | bytes 1572872 | tf_op jit(solution)/shard_map/ppermute | solution.py:73
  284.9 27.8 %collective-permute-start.32 = (bf16[256,1024]{1,0:T(8,128)(2,1)}, bf16[256,1024]{1,0:T(8,128)(2,1)}, u32[]{:S(2)}, u32[]{:S(2)}) collective-permute-start(bf16[256,1024]{1,0:T(8,128)(2,1)} %get-tuple-element.579.refs_0_), channel_id=1, source_target_pairs={{0,2},{1,3},{2,0},{3,1},{4,6},{5,7},{6,4},{7,5},{8,10},{9,11},{10,... | collective-permute-start | bytes 1572872 | tf_op jit(solution)/shard_map/ppermute | solution.py:73
  294.6 18.7 %collective-permute-start.33 = (bf16[256,1024]{1,0:T(8,128)(2,1)}, bf16[256,1024]{1,0:T(8,128)(2,1)S(1)}, u32[]{:S(2)}, u32[]{:S(2)}) collective-permute-start(bf16[256,1024]{1,0:T(8,128)(2,1)} %get-tuple-element.579.refs_0_), channel_id=1, source_target_pairs={{0,1},{1,0},{2,3},{3,2},{4,5},{5,4},{6,7},{7,6},{8,9},{9,8},{10,11... | collective-permute-start | bytes 1572872 | tf_op jit(solution)/shard_map/ppermute | solution.py:73
  322.6 42.3 %collective-permute-start.38 = (bf16[1792,512]{1,0:T(8,128)(2,1)}, bf16[1792,512]{1,0:T(8,128)(2,1)S(1)}, u32[]{:S(2)}, u32[]{:S(2)}) collective-permute-start(bf16[1792,512]{1,0:T(8,128)(2,1)} %get-tuple-element.614), channel_id=1, source_target_pairs={{0,4},{4,0},{8,12},{12,8},{16,20},{20,16},{24,28},{28,24},{1,5},{5... | collective-permute-start | bytes 5505032 | tf_op jit(solution)/shard_map/ppermute | solution.py:73
  325.2 14.3 %collective-permute-start.36 = (bf16[256,1024]{1,0:T(8,128)(2,1)S(1)}, bf16[256,1024]{1,0:T(8,128)(2,1)S(1)}, u32[]{:S(2)}, u32[]{:S(2)}) collective-permute-start(bf16[256,1024]{1,0:T(8,128)(2,1)S(1)} %get-tuple-element.595), channel_id=1, source_target_pairs={{0,2},{1,3},{2,0},{3,1},{4,6},{5,7},{6,4},{7,5},{8,10},{9,11},{10,... | collective-permute-start | bytes 1572872 | tf_op jit(solution)/shard_map/ppermute | solution.py:73
  331.3 55.4 %collective-permute-start.42 = (bf16[2048,512]{1,0:T(8,128)(2,1)S(1)}, bf16[2048,512]{1,0:T(8,128)(2,1)S(1)}, u32[]{:S(2)}, u32[]{:S(2)}) collective-permute-start(bf16[2048,512]{1,0:T(8,128)(2,1)S(1)} %get-tuple-element.640), channel_id=1, source_target_pairs={{0,8},{4,12},{8,0},{12,4},{16,24},{20,28},{24,16},{28,20},{1,9},{5... | collective-permute-start | bytes 6291464 | tf_op jit(solution)/shard_map/ppermute | solution.py:73
  340.4 25.8 %collective-permute-start.37 = (bf16[256,1024]{1,0:T(8,128)(2,1)S(1)}, bf16[256,1024]{1,0:T(8,128)(2,1)S(1)}, u32[]{:S(2)}, u32[]{:S(2)}) collective-permute-start(bf16[256,1024]{1,0:T(8,128)(2,1)S(1)} %get-tuple-element.631.refs_0_), channel_id=1, source_target_pairs={{0,2},{1,3},{2,0},{3,1},{4,6},{5,7},{6,4},{7,5},{8,10},{9,11},{10,... | collective-permute-start | bytes 1572872 | tf_op jit(solution)/shard_map/ppermute | solution.py:73
  366.2 59.9 %collective-permute-start.46 = (bf16[1792,512]{1,0:T(8,128)(2,1)}, bf16[1792,512]{1,0:T(8,128)(2,1)S(1)}, u32[]{:S(2)}, u32[]{:S(2)}) collective-permute-start(bf16[1792,512]{1,0:T(8,128)(2,1)} %get-tuple-element.673), channel_id=1, source_target_pairs={{0,4},{4,0},{8,12},{12,8},{16,20},{20,16},{24,28},{28,24},{1,5},{5... | collective-permute-start | bytes 5505032 | tf_op jit(solution)/shard_map/ppermute | solution.py:73
  382.7 14.8 %collective-permute-start.41 = (bf16[1024,256]{1,0:T(8,128)(2,1)S(1)}, bf16[1024,256]{1,0:T(8,128)(2,1)S(1)}, u32[]{:S(2)}, u32[]{:S(2)}) collective-permute-start(bf16[1024,256]{1,0:T(8,128)(2,1)S(1)} %bitcast.183), channel_id=1, source_target_pairs={{0,8},{4,12},{8,0},{12,4},{16,24},{20,28},{24,16},{28,20},{1,9},{5... | collective-permute-start | bytes 1572872 | tf_op jit(solution)/shard_map/ppermute | solution.py:73
  383.1 41.7 %collective-permute-start.47 = (bf16[1792,256]{1,0:T(8,128)(2,1)}, bf16[1792,256]{1,0:T(8,128)(2,1)S(1)}, u32[]{:S(2)}, u32[]{:S(2)}) collective-permute-start(bf16[1792,256]{1,0:T(8,128)(2,1)} %get-tuple-element.675), channel_id=1, source_target_pairs={{0,8},{4,12},{8,0},{12,4},{16,24},{20,28},{24,16},{28,20},{1,9},{5... | collective-permute-start | bytes 2752520 | tf_op jit(solution)/shard_map/ppermute | solution.py:73
  385.7 38.0 %collective-permute-start.44 = (bf16[256,1024]{1,0:T(8,128)(2,1)S(1)}, bf16[256,1024]{1,0:T(8,128)(2,1)S(1)}, u32[]{:S(2)}, u32[]{:S(2)}) collective-permute-start(bf16[256,1024]{1,0:T(8,128)(2,1)S(1)} %bitcast.178), channel_id=1, source_target_pairs={{0,4},{4,0},{8,12},{12,8},{16,20},{20,16},{24,28},{28,24},{1,5},{5... | collective-permute-start | bytes 1572872 | tf_op jit(solution)/shard_map/ppermute | solution.py:73
  397.7 26.2 %collective-permute-start.43 = (bf16[512,256]{1,0:T(8,128)(2,1)S(1)}, bf16[512,256]{1,0:T(8,128)(2,1)S(1)}, u32[]{:S(2)}, u32[]{:S(2)}) collective-permute-start(bf16[512,256]{1,0:T(8,128)(2,1)S(1)} %get-tuple-element.653), channel_id=1, source_target_pairs={{0,16},{4,20},{8,24},{12,28},{16,0},{20,4},{24,8},{28,12},{1,17},{... | collective-permute-start | bytes 786440 | tf_op jit(solution)/shard_map/ppermute | solution.py:73
  429.1 62.9 %collective-permute-start.61 = (bf16[2688,512]{1,0:T(8,128)(2,1)}, bf16[2688,512]{1,0:T(8,128)(2,1)}, u32[]{:S(2)}, u32[]{:S(2)}) collective-permute-start(bf16[2688,512]{1,0:T(8,128)(2,1)} %get-tuple-element.782), channel_id=1, source_target_pairs={{0,4},{4,0},{8,12},{12,8},{16,20},{20,16},{24,28},{28,24},{1,5},{5... | collective-permute-start | bytes 8257544 | tf_op jit(solution)/shard_map/ppermute | solution.py:73
  436.5 9.6 %collective-permute-start.51 = (bf16[64,1024]{1,0:T(8,128)(2,1)S(1)}, bf16[64,1024]{1,0:T(8,128)(2,1)S(1)}, u32[]{:S(2)}, u32[]{:S(2)}) collective-permute-start(bf16[64,1024]{1,0:T(8,128)(2,1)S(1)} %get-tuple-element.714), channel_id=1, source_target_pairs={{0,16},{4,20},{8,24},{12,28},{16,0},{20,4},{24,8},{28,12},{1,17},{... | collective-permute-start | bytes 393224 | tf_op jit(solution)/shard_map/ppermute | solution.py:73
  438.3 7.8 %collective-permute-start.50 = (bf16[64,1024]{1,0:T(8,128)(2,1)S(1)}, bf16[64,1024]{1,0:T(8,128)(2,1)S(1)}, u32[]{:S(2)}, u32[]{:S(2)}) collective-permute-start(bf16[64,1024]{1,0:T(8,128)(2,1)S(1)} %get-tuple-element.713), channel_id=1, source_target_pairs={{0,2},{1,3},{2,0},{3,1},{4,6},{5,7},{6,4},{7,5},{8,10},{9,11},{10,... | collective-permute-start | bytes 393224 | tf_op jit(solution)/shard_map/ppermute | solution.py:73
  453.7 13.7 %collective-permute-start.58 = (f32[9,1024]{1,0:T(8,128)}, f32[9,1024]{1,0:T(8,128)}, u32[]{:S(2)}, u32[]{:S(2)}) collective-permute-start(f32[9,1024]{1,0:T(8,128)} %fusion.26), channel_id=1, source_target_pairs={{0,1},{1,0},{2,3},{3,2},{4,5},{5,4},{6,7},{7,6},{8,9},{9,8},{10,11... | collective-permute-start | bytes 110600 | tf_op jit(solution)/shard_map/ppermute | solution.py:73
  461.4 27.1 %collective-permute-start.73 = (bf16[1792,128]{1,0:T(8,128)(2,1)}, bf16[1792,128]{1,0:T(8,128)(2,1)}, u32[]{:S(2)}, u32[]{:S(2)}) collective-permute-start(bf16[1792,128]{1,0:T(8,128)(2,1)} %copy-done.115), channel_id=1, source_target_pairs={{0,16},{4,20},{8,24},{12,28},{16,0},{20,4},{24,8},{28,12},{1,17},{... | collective-permute-start | bytes 1376264 | tf_op jit(solution)/shard_map/ppermute | solution.py:73
  461.5 53.1 %collective-permute-start.62 = (bf16[2048,256]{1,0:T(8,128)(2,1)}, bf16[2048,256]{1,0:T(8,128)(2,1)}, u32[]{:S(2)}, u32[]{:S(2)}) collective-permute-start(bf16[2048,256]{1,0:T(8,128)(2,1)} %copy-done.113), channel_id=1, source_target_pairs={{0,4},{4,0},{8,12},{12,8},{16,20},{20,16},{24,28},{28,24},{1,5},{5... | collective-permute-start | bytes 3145736 | tf_op jit(solution)/shard_map/ppermute | solution.py:73
  462.7 37.5 %collective-permute-start.56 = (bf16[1792,256]{1,0:T(8,128)(2,1)}, bf16[1792,256]{1,0:T(8,128)(2,1)}, u32[]{:S(2)}, u32[]{:S(2)}) collective-permute-start(bf16[1792,256]{1,0:T(8,128)(2,1)} %copy-done.114), channel_id=1, source_target_pairs={{0,8},{4,12},{8,0},{12,4},{16,24},{20,28},{24,16},{28,20},{1,9},{5... | collective-permute-start | bytes 2752520 | tf_op jit(solution)/shard_map/ppermute | solution.py:73
  467.4 16.6 %collective-permute-start.59 = (bf16[64,1024]{1,0:T(8,128)(2,1)S(1)}, bf16[64,1024]{1,0:T(8,128)(2,1)}, u32[]{:S(2)}, u32[]{:S(2)}) collective-permute-start(bf16[64,1024]{1,0:T(8,128)(2,1)S(1)} %get-tuple-element.765), channel_id=1, source_target_pairs={{0,2},{1,3},{2,0},{3,1},{4,6},{5,7},{6,4},{7,5},{8,10},{9,11},{10,... | collective-permute-start | bytes 393224 | tf_op jit(solution)/shard_map/ppermute | solution.py:73
  484.0 58.6 %collective-permute-start.68 = (bf16[1280,512]{1,0:T(8,128)(2,1)}, bf16[1280,512]{1,0:T(8,128)(2,1)}, u32[]{:S(2)}, u32[]{:S(2)}) collective-permute-start(bf16[1280,512]{1,0:T(8,128)(2,1)} %get-tuple-element.813), channel_id=1, source_target_pairs={{0,4},{4,0},{8,12},{12,8},{16,20},{20,16},{24,28},{28,24},{1,5},{5... | collective-permute-start | bytes 3932168 | tf_op jit(solution)/shard_map/ppermute | solution.py:73
  488.4 28.7 %collective-permute-start.65 = (bf16[784,512]{1,0:T(8,128)(2,1)}, bf16[784,512]{1,0:T(8,128)(2,1)}, u32[]{:S(2)}, u32[]{:S(2)}) collective-permute-start(bf16[784,512]{1,0:T(8,128)(2,1)} %get-tuple-element.803), channel_id=1, source_target_pairs={{0,8},{4,12},{8,0},{12,4},{16,24},{20,28},{24,16},{28,20},{1,9},{5... | collective-permute-start | bytes 2408456 | tf_op jit(solution)/shard_map/ppermute | solution.py:73
  498.5 85.4 %collective-permute-start.72 = (bf16[2688,256]{1,0:T(8,128)(2,1)}, bf16[2688,256]{1,0:T(8,128)(2,1)}, u32[]{:S(2)}, u32[]{:S(2)}) collective-permute-start(bf16[2688,256]{1,0:T(8,128)(2,1)} %get-tuple-element.830), channel_id=1, source_target_pairs={{0,8},{4,12},{8,0},{12,4},{16,24},{20,28},{24,16},{28,20},{1,9},{5... | collective-permute-start | bytes 4128776 | tf_op jit(solution)/shard_map/ppermute | solution.py:73
  500.2 24.3 %collective-permute-start.63 = (bf16[64,1024]{1,0:T(8,128)(2,1)}, bf16[64,1024]{1,0:T(8,128)(2,1)S(1)}, u32[]{:S(2)}, u32[]{:S(2)}) collective-permute-start(bf16[64,1024]{1,0:T(8,128)(2,1)} %add_convert_fusion.1), channel_id=1, source_target_pairs={{0,1},{1,0},{2,3},{3,2},{4,5},{5,4},{6,7},{7,6},{8,9},{9,8},{10,11... | collective-permute-start | bytes 393224 | tf_op jit(solution)/shard_map/ppermute | solution.py:73
  514.5 11.2 %collective-permute-start.64 = (bf16[64,1024]{1,0:T(8,128)(2,1)}, bf16[64,1024]{1,0:T(8,128)(2,1)}, u32[]{:S(2)}, u32[]{:S(2)}) collective-permute-start(bf16[64,1024]{1,0:T(8,128)(2,1)} %collective-permute-done.60), channel_id=1, source_target_pairs={{0,1},{1,0},{2,3},{3,2},{4,5},{5,4},{6,7},{7,6},{8,9},{9,8},{10,11... | collective-permute-start | bytes 393224 | tf_op jit(solution)/shard_map/ppermute | solution.py:73
  517.1 46.6 %collective-permute-start.71 = (bf16[2048,128]{1,0:T(8,128)(2,1)}, bf16[2048,128]{1,0:T(8,128)(2,1)}, u32[]{:S(2)}, u32[]{:S(2)}) collective-permute-start(bf16[2048,128]{1,0:T(8,128)(2,1)} %get-tuple-element.827), channel_id=1, source_target_pairs={{0,16},{4,20},{8,24},{12,28},{16,0},{20,4},{24,8},{28,12},{1,17},{... | collective-permute-start | bytes 1572872 | tf_op jit(solution)/shard_map/ppermute | solution.py:73
  524.4 39.3 %collective-permute-start.74 = (bf16[1792,128]{1,0:T(8,128)(2,1)}, bf16[1792,128]{1,0:T(8,128)(2,1)}, u32[]{:S(2)}, u32[]{:S(2)}) collective-permute-start(bf16[1792,128]{1,0:T(8,128)(2,1)} %get-tuple-element.836), channel_id=1, source_target_pairs={{0,16},{4,20},{8,24},{12,28},{16,0},{20,4},{24,8},{28,12},{1,17},{... | collective-permute-start | bytes 1376264 | tf_op jit(solution)/shard_map/ppermute | solution.py:73
  525.8 39.1 %collective-permute-start.66 = (bf16[784,256]{1,0:T(8,128)(2,1)}, bf16[784,256]{1,0:T(8,128)(2,1)S(1)}, u32[]{:S(2)}, u32[]{:S(2)}) collective-permute-start(bf16[784,256]{1,0:T(8,128)(2,1)} %get-tuple-element.807), channel_id=1, source_target_pairs={{0,4},{4,0},{8,12},{12,8},{16,20},{20,16},{24,28},{28,24},{1,5},{5... | collective-permute-start | bytes 1204232 | tf_op jit(solution)/shard_map/ppermute | solution.py:73
  545.0 36.0 %collective-permute-start.69 = (bf16[1280,256]{1,0:T(8,128)(2,1)}, bf16[1280,256]{1,0:T(8,128)(2,1)}, u32[]{:S(2)}, u32[]{:S(2)}) collective-permute-start(bf16[1280,256]{1,0:T(8,128)(2,1)} %get-tuple-element.820), channel_id=1, source_target_pairs={{0,8},{4,12},{8,0},{12,4},{16,24},{20,28},{24,16},{28,20},{1,9},{5... | collective-permute-start | bytes 1966088 | tf_op jit(solution)/shard_map/ppermute | solution.py:73
  565.0 12.7 %collective-permute-start.67 = (bf16[784,128]{1,0:T(8,128)(2,1)S(1)}, bf16[784,128]{1,0:T(8,128)(2,1)S(1)}, u32[]{:S(2)}, u32[]{:S(2)}) collective-permute-start(bf16[784,128]{1,0:T(8,128)(2,1)S(1)} %get-tuple-element.812), channel_id=1, source_target_pairs={{0,16},{4,20},{8,24},{12,28},{16,0},{20,4},{24,8},{28,12},{1,17},{... | collective-permute-start | bytes 602120 | tf_op jit(solution)/shard_map/ppermute | solution.py:73
  582.9 31.7 %collective-permute-start.70 = (bf16[1280,128]{1,0:T(8,128)(2,1)}, bf16[1280,128]{1,0:T(8,128)(2,1)}, u32[]{:S(2)}, u32[]{:S(2)}) collective-permute-start(bf16[1280,128]{1,0:T(8,128)(2,1)} %get-tuple-element.825), channel_id=1, source_target_pairs={{0,16},{4,20},{8,24},{12,28},{16,0},{20,4},{24,8},{28,12},{1,17},{... | collective-permute-start | bytes 983048 | tf_op jit(solution)/shard_map/ppermute | solution.py:73
  586.4 42.7 %collective-permute-start.75 = (bf16[2688,128]{1,0:T(8,128)(2,1)}, bf16[2688,128]{1,0:T(8,128)(2,1)S(1)}, u32[]{:S(2)}, u32[]{:S(2)}) collective-permute-start(bf16[2688,128]{1,0:T(8,128)(2,1)} %get-tuple-element.837), channel_id=1, source_target_pairs={{0,16},{4,20},{8,24},{12,28},{16,0},{20,4},{24,8},{28,12},{1,17},{... | collective-permute-start | bytes 2064392 | tf_op jit(solution)/shard_map/ppermute | solution.py:73
  (183 other events, 2021.5 us)
Sparse Core Ops, SparseCore 0:
  494.2 34.8 all-reduce.1
